TPU v7x, 32 devices: a whole 2x2x4 slice. The times are simulated.
32 devices in a mesh: dp: 2 (over x), expert: 16 (over z, y, core).
Axes of the slice: x: 2, y: 2, z: 4, core: 2. Of those that a mesh axis runs over, the one named last changes fastest.
Arguments:
- head_outputs: bfloat16 [4096, 8, 128], P(('dp', 'expert')), may hold values from -6 to 6
- out_grad: bfloat16 [4096, 4096], P(('dp', 'expert')), may hold values from -0.29882812 to 0.29882812
- gate_weights: bfloat16 [4096, 8], P(('dp', 'expert')), may hold values from 0.099609375 to 1
- route_ids: int32 [4096, 8], P(('dp', 'expert')), may hold values from 0 to 15, all different within a row; in each aligned block of 128 rows (0 to 127, 128 to 255, ...) at most 72 rows name the same one
- out_proj: bfloat16 [16, 128, 4096], P('expert'), may hold values from -0.5 to 0.5
Outputs:
- grad_head: bfloat16 [4096, 8, 128], P(('dp', 'expert'))
- grad_gate: bfloat16 [4096, 8], P(('dp', 'expert'))
- grad_proj: float32 [16, 128, 4096], P('expert', 'dp')
Inputs may be any that keep to these rules, and one draw needn't show every extreme that they name: `route_ids`: each row names 8 different head experts. Within the 128 rows of one device no head expert is named by more than 72 rows, and in some devices' rows one is named by exactly 72.
All inputs are finite; a program needn't handle non-finite values.
Results may differ from a plain program's by a relative error of at most 0.0049.
Values may be sent and summed in bfloat16 or wider, within the bound.
No kernel may reach another device: no remote copies, remote signals or barrier semaphores. Data moves between devices by JAX's collectives and lax.ppermute only.
A program may use at most 128 MiB of HBM per device.

v0:
```python
import jax
import jax.numpy as jnp
from jax import lax
from jax.sharding import PartitionSpec as P

soft_cap = 1.5


def block_rows(row_total):
    for block_size in (512, 384, 256, 128):
        if row_total % block_size == 0:
            return block_size
    return row_total


def owner_work(received_grad, received_head, received_gate, weights):
    row_count, slot_width, features = received_grad.shape
    local_experts, head_dim, _ = weights.shape
    sources = row_count // local_experts
    grad_all = received_grad.reshape(sources, local_experts, slot_width, features)
    head_all = received_head.reshape(sources, local_experts, slot_width, head_dim)
    gate_all = received_gate.reshape(sources, local_experts, slot_width)
    heads_back, gates_back, weight_sums = ([], [], [])
    row_total = sources * slot_width
    block_size = block_rows(row_total)
    blocks = row_total // block_size
    grad_rows = grad_all[:, 0].reshape(row_total, features)
    head_rows = head_all[:, 0].reshape(row_total, head_dim)
    gate_rows = gate_all[:, 0].reshape(row_total)
    weight = weights[0]

    def advance(
        index,
        carry,
        grad_rows=grad_rows,
        head_rows=head_rows,
        gate_rows=gate_rows,
        weight=weight,
        block_size=block_size,
    ):
        running, head_out, gate_out = carry
        start_row = index * block_size
        grad_block = lax.dynamic_slice_in_dim(grad_rows, start_row, block_size, 0)
        head_block = lax.dynamic_slice_in_dim(head_rows, start_row, block_size, 0)
        gate_block = lax.dynamic_slice_in_dim(gate_rows, start_row, block_size, 0)
        pre_cap = jnp.dot(head_block, weight, preferred_element_type=jnp.float32)
        capped = jnp.tanh(pre_cap / soft_cap)
        grad_pre = (
            gate_block[:, None].astype(jnp.float32)
            * grad_block.astype(jnp.float32)
            * (1.0 - capped * capped)
        ).astype(jnp.bfloat16)
        head_grad = lax.dot_general(
            grad_pre, weight, (((1,), (1,)), ((), ())), preferred_element_type=jnp.float32
        ).astype(jnp.bfloat16)
        gate_grad = jnp.sum(grad_block.astype(jnp.float32) * (soft_cap * capped), axis=1).astype(
            jnp.bfloat16
        )
        running = running + lax.dot_general(
            head_block, grad_pre, (((0,), (0,)), ((), ())), preferred_element_type=jnp.float32
        )
        head_out = lax.dynamic_update_slice_in_dim(head_out, head_grad, start_row, 0)
        gate_out = lax.dynamic_update_slice_in_dim(gate_out, gate_grad, start_row, 0)
        return (running, head_out, gate_out)

    start_carry = (
        jnp.zeros((head_dim, features), jnp.float32),
        jnp.zeros((row_total, head_dim), jnp.bfloat16),
        jnp.zeros((row_total,), jnp.bfloat16),
    )
    weight_sum, head_grad, gate_grad = lax.fori_loop(0, blocks, advance, start_carry)
    heads_back.append(head_grad.reshape(sources, slot_width, head_dim))
    gates_back.append(gate_grad.reshape(sources, slot_width))
    weight_sums.append(weight_sum)
    back_head = jnp.stack(heads_back, axis=1).reshape(row_count, slot_width, head_dim)
    back_gate = jnp.stack(gates_back, axis=1).reshape(row_count, slot_width)
    return (back_head, back_gate, jnp.stack(weight_sums))


def local(head_outputs, out_grad, gate_weights, route_ids, out_proj):
    tok_rows, top_count, head_dim = head_outputs.shape
    features = out_grad.shape[1]
    local_experts = out_proj.shape[0]
    experts = local_experts * lax.axis_size("expert")
    capacity = 9 * tok_rows * top_count // (8 * experts)
    pair_count = tok_rows * top_count
    flat_routes = route_ids.reshape(pair_count)
    one_hot = (flat_routes[:, None] == jnp.arange(experts, dtype=jnp.int32)[None, :]).astype(
        jnp.int32
    )
    before = jnp.cumsum(one_hot, axis=0) - one_hot
    position = jnp.sum(before * one_hot, axis=1)
    target = flat_routes * capacity + position
    source = (
        jnp.full((experts * capacity,), pair_count, jnp.int32)
        .at[target]
        .set(jnp.arange(pair_count, dtype=jnp.int32))
    )
    send_grad = jnp.take(out_grad, source // top_count, axis=0, mode="fill", fill_value=0).reshape(
        experts, capacity, features
    )
    send_head = jnp.take(
        head_outputs.reshape(pair_count, head_dim), source, axis=0, mode="fill", fill_value=0
    ).reshape(experts, capacity, head_dim)
    send_gate = jnp.take(
        gate_weights.reshape(pair_count), source, axis=0, mode="fill", fill_value=0
    ).reshape(experts, capacity)
    received = (
        lax.all_to_all(send_grad, "expert", split_axis=0, concat_axis=0, tiled=True),
        lax.all_to_all(send_head, "expert", split_axis=0, concat_axis=0, tiled=True),
        lax.all_to_all(send_gate, "expert", split_axis=0, concat_axis=0, tiled=True),
    )
    back_head, back_gate, weight_sum = owner_work(received[0], received[1], received[2], out_proj)
    got_head, got_gate = (
        lax.all_to_all(back_head, "expert", split_axis=0, concat_axis=0, tiled=True),
        lax.all_to_all(back_gate, "expert", split_axis=0, concat_axis=0, tiled=True),
    )
    grad_head = jnp.take(got_head.reshape(experts * capacity, head_dim), target, axis=0).reshape(
        tok_rows, top_count, head_dim
    )
    grad_gate = jnp.take(got_gate.reshape(experts * capacity), target, axis=0).reshape(
        tok_rows, top_count
    )
    proj_parts = [lax.psum_scatter(weight_sum[0], "dp", scatter_dimension=0, tiled=True)]
    return (grad_head, grad_gate, jnp.stack(proj_parts))


def solution(mesh):
    return jax.shard_map(
        local,
        mesh=mesh,
        in_specs=(
            P(("dp", "expert"), None, None),
            P(("dp", "expert"), None),
            P(("dp", "expert"), None),
            P(("dp", "expert"), None),
            P("expert", None, None),
        ),
        out_specs=(
            P(("dp", "expert"), None, None),
            P(("dp", "expert"), None),
            P("expert", "dp", None),
        ),
        check_vma=False,
    )
```

profile of v0, /device:TPU:0, one launch (start us, length us, event | category | flops | bytes accessed | tf_op | source)
XLA Modules:
  0.0 347.6 jit_solution(13561740484808579513)
XLA Ops:
  7.2 0.0 copy-start
  7.2 0.0 copy-start.3
  7.2 0.9 copy.18
  8.1 0.1 eq.26
  8.2 0.1 reshape.139
  8.3 4.5 %reduce-window.6 = s32[16,8,128]{2,1,0:T(8,128)S(1)} reduce-window(s32[16,8,128]{2,1,0:T(8,128)S(1)} %fusion.11, s32[]{:T(128)} %constant.134.clone.1), window={size=1x1x128 pad=0_0x0_0x127_0}, to_apply=%region_0.0 | reduce-window | flops 2080768 | bytes 131076 | tf_op jit(solution)/shard_map/reduce-window
  12.8 0.1 slice.18
  12.9 0.1 copy.21
  13.1 0.1 copy.22
  13.1 0.1 broadcast_add_fusion
  13.2 0.1 mul.81
  13.4 4.3 %scatter_custom_fusion = s32[1152]{0:T(1024)S(1)} fusion(s32[1024]{0:T(1024)S(1)} %bitcast.52, s32[1024]{0:T(1024)S(1)} %iota.11, s32[]{:T(128)} %constant.139.clone.1), kind=kCustom, calls=%fused_computation.49 | custom fusion | bytes 4612 | tf_op jit(solution)/shard_map/scatter | solution.py:97
  17.7 0.8 copy.23
  18.5 0.1 reshape.142
  18.6 7.3 %gather_fusion.1 = bf16[1152]{0:T(1024)(128)(2,1)S(1)} fusion(bf16[1024]{0:T(1024)(128)(2,1)S(1)} %reshape.142, s32[2048]{0:T(1024)S(1)} %pad_clamp_fusion.1), kind=kCustom, calls=%fused_computation.1 | custom fusion | bytes 9216 | tf_op jit(solution)/shard_map/jit(_take)/gather | solution.py:105
  25.9 0.7 select_n.94
  26.6 7.4 %all-to-all-start.1 = ((bf16[16,1,72]{2,1,0:T(2,128)(2,1)}), bf16[16,1,72]{2,1,0:T(2,128)(2,1)S(1)}, u32[]{:S(2)}, u32[]{:S(2)}) async-start(bf16[16,1,72]{2,1,0:T(2,128)(2,1)} %select_n.94), calls=%async_computation.1 | async-start | bytes 16384 | tf_op jit(solution)/shard_map/all_to_all | solution.py:111
  34.0 0.1 broadcast_in_dim.70
  34.1 0.0 copy-done.3
  34.2 2.9 gather_fusion
  37.1 0.9 broadcast_select_fusion.1
  38.0 0.1 broadcast_in_dim.74
  38.1 0.0 copy-done
  38.1 8.0 %gather_fusion.2 = bf16[1152,4096]{1,0:T(8,128)(2,1)} fusion(bf16[128,4096]{1,0:T(8,128)(2,1)S(1)} %copy-done, s32[2048]{0:T(1024)S(1)} %pad_clamp_fusion), kind=kCustom, calls=%fused_computation.2 | custom fusion | bytes 18878976 | tf_op jit(solution)/shard_map/jit(_take)/gather | solution.py:99
  46.2 0.0 all-to-all-done.1
  46.2 6.0 %all-to-all-start = ((bf16[16,72,128]{2,1,0:T(8,128)(2,1)}), bf16[16,72,128]{2,1,0:T(8,128)(2,1)S(1)}, u32[]{:S(2)}, u32[]{:S(2)}) async-start(bf16[16,72,128]{2,1,0:T(8,128)(2,1)} %broadcast_select_fusion.1), calls=%async_computation | async-start | bytes 589824 | tf_op jit(solution)/shard_map/all_to_all | solution.py:110
  52.2 8.0 %broadcast_select_fusion = bf16[16,72,4096]{2,1,0:T(8,128)(2,1)} fusion(bf16[16,72,4096]{2,1,0:T(8,128)(2,1)} %bitcast.43, pred[16,72]{1,0:T(8,128)(4,1)S(1)} %broadcast_in_dim.74), kind=kLoop, calls=%fused_computation.20 | loop fusion | flops 4718592 | bytes 18875520 | tf_op jit(solution)/shard_map/jit(_take)/select_n | solution.py:99
  60.2 2.5 all-to-all-done
  62.8 4.8 %all-to-all-start.2 = ((bf16[16,72,4096]{2,1,0:T(8,128)(2,1)}), bf16[16,72,4096]{2,1,0:T(8,128)(2,1)}, u32[]{:S(2)}, u32[]{:S(2)}) async-start(bf16[16,72,4096]{2,1,0:T(8,128)(2,1)} %broadcast_select_fusion), calls=%async_computation.2 | async-start | bytes 18874368 | tf_op jit(solution)/shard_map/all_to_all | solution.py:109
  67.6 0.0 reduce-scatter.2.cloned.1.call-start
  67.7 0.1 reshape_squeeze_reshape.10
  67.8 168.7 %all-to-all-done.2 = bf16[16,72,4096]{2,1,0:T(8,128)(2,1)} async-done(((bf16[16,72,4096]{2,1,0:T(8,128)(2,1)}), bf16[16,72,4096]{2,1,0:T(8,128)(2,1)}, u32[]{:S(2)}, u32[]{:S(2)}) %all-to-all-start.2) | async-done | bytes 9437216 | tf_op jit(solution)/shard_map/all_to_all | solution.py:109
  236.5 0.8 broadcast_in_dim.67
  237.2 34.2 %while.18 = (s32[]{:T(128)}, f32[128,4096]{1,0:T(8,128)S(1)}, bf16[1152,128]{1,0:T(8,128)(2,1)}, bf16[1152]{0:T(1024)(128)(2,1)S(1)}, bf16[1152,128]{1,0:T(8,128...) while((s32[]{:T(128)}, f32[128,4096]{1,0:T(8,128)S(1)}, ...), condition=%wide.region_6.7_spmd.clone, body=%wide.region_4.6_spmd.clone.sunk | while | flops 1224785920 | bytes 35954420 | solution.py:71
  237.2 0.1 dynamic-slice_convert_fusion.2
  237.3 6.4 %fusion.32 = (bf16[384]{0:T(512)(128)(2,1)S(1)}, bf16[384,4096]{1,0:T(8,128)(2,1)}) fusion(bf16[1152,4096]{1,0:T(8,128)(2,1)} %get-tuple-element.287, s32[]{:T(128)S(6)} %select_n.116, f32[384]{0:T(512)S(1)} %dynamic-slice_convert_fusion.2, bf16[128,4096]{1,0:T(8,128)(2,1)} %get-tuple-element.288, bf16[1152,128]{1,0:T(8,128)(2,1)S(1)} %get-tuple-element.285), kind=kOutput, calls=%fused_computation.10.clone.1 | convolution fusion | flops 418381440 | bytes 7442176 | tf_op jit(solution)/shard_map/while/body/eval_jaxpr/dot_general | solution.py:46
  243.7 3.1 convolution_add_fusion.2
  246.8 0.0 copy-done.1
  246.8 1.6 fusion.33
  248.4 0.2 dynamic_update_slice.20
  248.6 0.1 dynamic-slice_convert_fusion.2
  248.7 6.4 %fusion.32 = (bf16[384]{0:T(512)(128)(2,1)S(1)}, bf16[384,4096]{1,0:T(8,128)(2,1)}) fusion(bf16[1152,4096]{1,0:T(8,128)(2,1)} %get-tuple-element.287, s32[]{:T(128)S(6)} %select_n.116, f32[384]{0:T(512)S(1)} %dynamic-slice_convert_fusion.2, bf16[128,4096]{1,0:T(8,128)(2,1)} %get-tuple-element.288, bf16[1152,128]{1,0:T(8,128)(2,1)S(1)} %get-tuple-element.285), kind=kOutput, calls=%fused_computation.10.clone.1 | convolution fusion | flops 418381440 | bytes 7442176 | tf_op jit(solution)/shard_map/while/body/eval_jaxpr/dot_general | solution.py:46
  255.1 3.1 convolution_add_fusion.2
  258.2 1.6 fusion.33
  259.8 0.2 dynamic_update_slice.20
  260.0 0.1 dynamic-slice_convert_fusion.2
  260.1 6.4 %fusion.32 = (bf16[384]{0:T(512)(128)(2,1)S(1)}, bf16[384,4096]{1,0:T(8,128)(2,1)}) fusion(bf16[1152,4096]{1,0:T(8,128)(2,1)} %get-tuple-element.287, s32[]{:T(128)S(6)} %select_n.116, f32[384]{0:T(512)S(1)} %dynamic-slice_convert_fusion.2, bf16[128,4096]{1,0:T(8,128)(2,1)} %get-tuple-element.288, bf16[1152,128]{1,0:T(8,128)(2,1)S(1)} %get-tuple-element.285), kind=kOutput, calls=%fused_computation.10.clone.1 | convolution fusion | flops 418381440 | bytes 7442176 | tf_op jit(solution)/shard_map/while/body/eval_jaxpr/dot_general | solution.py:46
  266.5 3.1 convolution_add_fusion.2
  269.6 1.6 fusion.33
  271.2 0.2 dynamic_update_slice.20
  271.4 1.3 copy-done.2
  272.8 0.0 reduce-scatter.2.cloned.1.call-update
  272.8 0.1 all_to_all.25
  272.9 46.9 %all_to_all.31 = bf16[16,1,72]{2,1,0:T(2,128)(2,1)S(1)} all-to-all(bf16[16,1,72]{2,1,0:T(2,128)(2,1)S(1)} %all_to_all.25), channel_id=1, replica_groups=mesh['dp'=2,'expert'=16] {'expert'}, dimensions={0} | all-to-all | bytes 4608 | tf_op jit(solution)/shard_map/all_to_all | solution.py:116
  319.8 3.5 %all-to-all-start.3 = ((bf16[16,72,128]{2,1,0:T(8,128)(2,1)}), bf16[16,72,128]{2,1,0:T(8,128)(2,1)S(1)}, u32[]{:S(2)}, u32[]{:S(2)}) async-start(bf16[16,72,128]{2,1,0:T(8,128)(2,1)} %bitcast.47), calls=%async_computation.3 | async-start | bytes 589824 | tf_op jit(solution)/shard_map/all_to_all | solution.py:115
  323.3 0.1 reduce_sum.27
  323.5 0.1 reshape.144
  323.6 6.8 %gather_fusion.4 = bf16[1024]{0:T(1024)(128)(2,1)S(1)} fusion(bf16[1152]{0:T(1024)(128)(2,1)S(1)} %reshape.144, s32[1024]{0:T(1024)S(1)} %broadcast_clamp_fusion), kind=kCustom, calls=%fused_computation.4 | custom fusion | bytes 8192 | tf_op jit(solution)/shard_map/jit(_take)/gather | solution.py:121
  330.4 0.1 gather.36
  330.5 0.7 copy.26
  331.2 2.7 all-to-all-done.3
  333.9 3.2 gather_fusion.3
  337.1 0.9 bitcast_select_fusion
  338.0 2.8 reduce-scatter.2.cloned.1.call-done
  (30 shorter events, 0.3 us)
Async XLA Ops:
  7.2 31.0 %copy-start = (bf16[128,4096]{1,0:T(8,128)(2,1)S(1)}, bf16[128,4096]{1,0:T(8,128)(2,1)}, u32[]{:S(2)}) copy-start(bf16[128,4096]{1,0:T(8,128)(2,1)} %param.8) | copy-start | bytes 3145732
  7.2 27.0 %copy-start.3 = (bf16[128,8,128]{2,1,0:T(8,128)(2,1)S(1)}, bf16[128,8,128]{2,1,0:T(8,128)(2,1)}, u32[]{:S(2)}) copy-start(bf16[128,8,128]{2,1,0:T(8,128)(2,1)} %param.7) | copy-start | bytes 786436
  26.6 19.6 %all-to-all-start.1 = ((bf16[16,1,72]{2,1,0:T(2,128)(2,1)}), bf16[16,1,72]{2,1,0:T(2,128)(2,1)S(1)}, u32[]{:S(2)}, u32[]{:S(2)}) async-start(bf16[16,1,72]{2,1,0:T(2,128)(2,1)} %select_n.94), calls=%async_computation.1 | async-start | bytes 16384 | tf_op jit(solution)/shard_map/all_to_all | solution.py:111
  46.2 16.6 %all-to-all-start = ((bf16[16,72,128]{2,1,0:T(8,128)(2,1)}), bf16[16,72,128]{2,1,0:T(8,128)(2,1)S(1)}, u32[]{:S(2)}, u32[]{:S(2)}) async-start(bf16[16,72,128]{2,1,0:T(8,128)(2,1)} %broadcast_select_fusion.1), calls=%async_computation | async-start | bytes 589824 | tf_op jit(solution)/shard_map/all_to_all | solution.py:110
  62.8 173.7 %all-to-all-start.2 = ((bf16[16,72,4096]{2,1,0:T(8,128)(2,1)}), bf16[16,72,4096]{2,1,0:T(8,128)(2,1)}, u32[]{:S(2)}, u32[]{:S(2)}) async-start(bf16[16,72,4096]{2,1,0:T(8,128)(2,1)} %broadcast_select_fusion), calls=%async_computation.2 | async-start | bytes 18874368 | tf_op jit(solution)/shard_map/all_to_all | solution.py:109
  67.6 273.2 %reduce-scatter.2.cloned.1.call-start = ((), (), s32[]{:S(2)}) async-start(), calls=%async_computation.6 | async-start | bytes 3145728 | tf_op jit(solution)/shard_map/reduce_scatter | solution.py:124
  243.7 3.1 copy-start.1
  243.7 3.1 copy-start.4
  255.1 3.1 copy-start.1
  255.1 3.1 copy-start.4
  266.5 3.1 copy-start.1
  266.5 3.1 copy-start.4
  271.4 1.4 copy-start.2
  319.8 14.1 %all-to-all-start.3 = ((bf16[16,72,128]{2,1,0:T(8,128)(2,1)}), bf16[16,72,128]{2,1,0:T(8,128)(2,1)S(1)}, u32[]{:S(2)}, u32[]{:S(2)}) async-start(bf16[16,72,128]{2,1,0:T(8,128)(2,1)} %bitcast.47), calls=%async_computation.3 | async-start | bytes 589824 | tf_op jit(solution)/shard_map/all_to_all | solution.py:115
Sparse Core Ops, SparseCore 0:
  272.9 67.8 reduce-scatter.1
where the time goes:
time: 348 us
  waiting for transfers between devices  177 us (51%)
  blocking collectives  46.9 us (13%)
  local copies, waits for them, and re-layouts  39.6 us (11%)
  matrix products  33.3 us (10%)
  starting transfers between devices  21.7 us (6%)
  other arithmetic  15 us (4%)
  between operations  14.3 us (4%)
    all_to_all x1, waiting for transfers between devices, local(): lax.all_to_all(send_grad, 'expert', split_axis=0, concat_axis=0, tiled=True)  169 us
    all_to_all x1, blocking collectives, local(): lax.all_to_all(back_gate, 'expert', split_axis=0, concat_axis=0, tiled=True)  46.9 us
    dot_general x3, matrix products, advance(): pre_cap = jnp.dot(head_block, weight, preferred_element_type=jnp.float32)  19.2 us
    dot_general x3, matrix products, advance(): lax.dot_general(head_block, grad_pre, (((0,), (0,)), ((), ())), preferred...  9.3 us
    gather x1, local copies, waits for them, and re-layouts, local(): jnp.take(out_grad, source // top_count, axis=0, mode='fill', fill_value=0)  8.04 us
    select_n x1, other arithmetic, local(): jnp.take(out_grad, source // top_count, axis=0, mode='fill', fill_value=0)  8.04 us
    all_to_all x1, starting transfers between devices, local(): lax.all_to_all(send_gate, 'expert', split_axis=0, concat_axis=0, tiled=True)  7.39 us
    gather x1, local copies, waits for them, and re-layouts, local(): jnp.take(gate_weights.reshape(pair_count), source, axis=0, mode='fill', f...  7.27 us
  transfers between devices with their start and end apart: 5, of which 4 were waited for; matrix products, arithmetic and copies ran while one was open for 9% of the time, Pallas kernels for 0%

commit v1 on v0

v1 whole, which is shorter than its diff:
```python
import functools

import jax
import jax.numpy as jnp
from jax import lax
from jax.experimental import pallas as pl
from jax.experimental.pallas import tpu as pltpu
from jax.sharding import PartitionSpec as P

soft_cap = 1.5
AXES = ("dp", "expert")
GROUP = 4
LANES = 128


class Plan:
    def __init__(self, mesh, tokens, top, head_dim, features):
        self.dp = mesh.shape["dp"]
        self.experts = mesh.shape["expert"]
        self.rows = GROUP // 2
        self.planes = self.experts // GROUP
        self.splits = self.dp * self.rows
        self.sources = self.splits * 2
        self.tokens, self.top, self.head_dim = tokens, top, head_dim
        self.part = features // self.splits
        cap = 9 * tokens * top // (8 * self.experts)
        self.cap = -(-cap // 8) * 8
        self.back = self.rows * self.cap + 16
        self.width = self.part + top * head_dim + LANES

    def index(self, x, z, y, c):
        return x * self.experts + z * GROUP + y * 2 + c

    def pairs(self, dx=0, dz=0, dy=0, dc=0):
        out = []
        for x in range(self.dp):
            for z in range(self.planes):
                for y in range(self.rows):
                    for c in range(2):
                        target = self.index(
                            (x + dx) % self.dp,
                            (z + dz) % self.planes,
                            (y + dy) % self.rows,
                            c ^ dc,
                        )
                        out.append((self.index(x, z, y, c), target))
        return out

    def shift(self, value, **by):
        if not any(by.values()):
            return value
        return lax.ppermute(value, AXES, self.pairs(**by))

    def splits_list(self):
        return [(dx, dy) for dx in range(self.dp) for dy in range(self.rows)]


def slot_kernel(plan, ids, *refs):
    packs = refs[: plan.sources]
    w_ref, p_ref, back_ref, buf, grads, heads, sems = refs[plan.sources :]
    tokens, cap, part, top, head_dim = plan.tokens, plan.cap, plan.part, plan.top, plan.head_dim
    pair_rows = 2 * cap
    pair_total = plan.sources // 2

    def copies(q):
        slot = q % 2
        return [
            pltpu.make_async_copy(
                packs[2 * q + b], buf.at[slot, pl.ds(b * tokens, tokens), :], sems.at[slot, b]
            )
            for b in range(2)
        ]

    for copy in copies(0):
        copy.start()
    row_of = lax.broadcasted_iota(jnp.int32, (cap, tokens), 0)
    lane_of = lax.broadcasted_iota(jnp.int32, (cap, tokens), 1)
    diagonal = (row_of == lane_of).astype(jnp.float32)
    before = (
        lax.broadcasted_iota(jnp.int32, (tokens, tokens), 0)
        < lax.broadcasted_iota(jnp.int32, (tokens, tokens), 1)
    ).astype(jnp.bfloat16)
    block_row = lax.broadcasted_iota(jnp.int32, (16, LANES), 0)
    chunk = min(part, 512)
    for q in range(pair_total):
        slot = q % 2
        if q + 1 < pair_total:
            for copy in copies(q + 1):
                copy.start()
        for copy in copies(q):
            copy.wait()
        masks, gate_rows, occupied = {}, {}, []
        for b in range(2):
            meta = buf[slot, pl.ds(b * tokens, 16), pl.ds(part + top * head_dim, LANES)].astype(
                jnp.float32
            )
            for i in range(plan.rows):
                mask = (meta[top : 2 * top] == ids[i].astype(jnp.float32)).astype(jnp.float32)
                masks[i, b] = mask
                gate_rows[i, b] = jnp.sum(mask * meta[:top], axis=0, keepdims=True)
                occupied.append(jnp.sum(mask, axis=0, keepdims=True))
        count = len(occupied)
        padded = jnp.concatenate(
            occupied + [jnp.zeros((-count % 16, tokens), jnp.float32)] * (count % 16 > 0), axis=0
        )
        places = jnp.dot(
            padded.astype(jnp.bfloat16), before, preferred_element_type=jnp.float32
        )
        ones, gates = [], []
        for i in range(plan.rows):
            halves, columns = [], []
            for b in range(2):
                at = b * plan.rows + i
                place = places[at : at + 1].astype(jnp.int32)
                hot = jnp.where(row_of == place, occupied[at], 0.0)
                columns.append(jnp.sum(hot * gate_rows[i, b], axis=1, keepdims=True))
                pieces = [(hot * masks[i, b][k : k + 1]).astype(jnp.bfloat16) for k in range(top)]
                wide = jnp.concatenate(pieces, axis=1)
                raw = jnp.concatenate(
                    [
                        buf[slot, pl.ds(b * tokens, tokens), pl.ds(part + k * head_dim, head_dim)]
                        for k in range(top)
                    ],
                    axis=0,
                )
                chosen = jnp.dot(wide, raw, preferred_element_type=jnp.float32)
                halves.append((hot, chosen))
            empty = jnp.zeros((cap, tokens), jnp.float32)
            ones.append(
                jnp.concatenate(
                    [
                        jnp.concatenate([halves[0][0], empty], axis=1),
                        jnp.concatenate([empty, halves[1][0]], axis=1),
                    ],
                    axis=0,
                ).astype(jnp.bfloat16)
            )
            gates.append(jnp.concatenate(columns, axis=0))
            heads[i, pl.ds(q * pair_rows, pair_rows), :] = jnp.concatenate(
                [halves[0][1], halves[1][1]], axis=0
            ).astype(jnp.bfloat16)
        all_ones = jnp.concatenate(ones, axis=0)
        sums = [jnp.zeros((pair_rows, 1), jnp.float32) for _ in range(plan.rows)]
        for start in range(0, part, chunk):
            grad = jnp.dot(
                all_ones, buf[slot, :, pl.ds(start, chunk)], preferred_element_type=jnp.float32
            )
            for i in range(plan.rows):
                grad_block = grad[i * pair_rows : (i + 1) * pair_rows]
                weight = w_ref[pl.ds(pl.multiple_of(ids[plan.rows + i], 128), head_dim), pl.ds(start, chunk)]
                pre = jnp.dot(
                    heads[i, pl.ds(q * pair_rows, pair_rows), :],
                    weight,
                    preferred_element_type=jnp.float32,
                )
                capped = jnp.tanh(pre * (1.0 / soft_cap))
                sums[i] = sums[i] + jnp.sum(grad_block * capped, axis=1, keepdims=True)
                grads[i, pl.ds(q * pair_rows, pair_rows), pl.ds(start, chunk)] = (
                    gates[i] * grad_block * (1.0 - capped * capped)
                ).astype(jnp.bfloat16)
        for b in range(2):
            block = jnp.zeros((16, LANES), jnp.float32)
            for i in range(plan.rows):
                column = soft_cap * sums[i][b * cap : (b + 1) * cap]
                line = jnp.sum(diagonal * column, axis=0, keepdims=True)
                block = jnp.where(block_row == i, line, block)
            back_ref[2 * q + b, pl.ds(plan.rows * cap, 16), :] = block.astype(jnp.bfloat16)
    for i in range(plan.rows):
        weight = w_ref[pl.ds(pl.multiple_of(ids[plan.rows + i], 128), head_dim), :]
        grad_all = grads[i]
        p_ref[pl.ds(i * head_dim, head_dim), :] = lax.dot_general(
            heads[i], grad_all, (((0,), (0,)), ((), ())), preferred_element_type=jnp.float32
        ).astype(p_ref.dtype)
        rows = lax.dot_general(
            grad_all, weight, (((1,), (1,)), ((), ())), preferred_element_type=jnp.float32
        ).astype(jnp.bfloat16)
        for s in range(plan.sources):
            back_ref[s, pl.ds(i * cap, cap), :] = rows[s * cap : (s + 1) * cap]


def slot_work(plan, ids, packs, weight, kind):
    rows = plan.sources * plan.cap
    flops = 6 * plan.rows * rows * plan.head_dim * plan.part
    return pl.pallas_call(
        functools.partial(slot_kernel, plan),
        out_shape=(
            jax.ShapeDtypeStruct((plan.rows * plan.head_dim, plan.part), kind),
            jax.ShapeDtypeStruct((plan.sources, plan.back, LANES), jnp.bfloat16),
        ),
        in_specs=[pl.BlockSpec(memory_space=pltpu.SMEM)]
        + [pl.BlockSpec(memory_space=pl.ANY)] * plan.sources
        + [pl.BlockSpec(memory_space=pltpu.VMEM)],
        out_specs=(
            pl.BlockSpec(memory_space=pltpu.VMEM),
            pl.BlockSpec(memory_space=pltpu.VMEM),
        ),
        scratch_shapes=[
            pltpu.VMEM((2, 2 * plan.tokens, plan.width), jnp.bfloat16),
            pltpu.VMEM((plan.rows, rows, plan.part), jnp.bfloat16),
            pltpu.VMEM((plan.rows, rows, plan.head_dim), jnp.bfloat16),
            pltpu.SemaphoreType.DMA((2, 2)),
        ],
        compiler_params=pltpu.CompilerParams(vmem_limit_bytes=32 * 1024 * 1024),
        cost_estimate=pl.CostEstimate(
            flops=flops,
            bytes_accessed=plan.sources * plan.tokens * plan.width * 2,
            transcendentals=plan.rows * rows * plan.part,
        ),
    )(ids, *packs, weight)


def final_kernel(plan, target_ref, gate_ref, place_ref, *refs):
    parts = refs[: plan.sources]
    head_ref, out_gate_ref, table = refs[plan.sources :]
    length = plan.planes * plan.back
    for dc in range(2):
        total = None
        for s in range(plan.splits):
            piece = parts[2 * s + dc][...].astype(jnp.float32)
            total = piece if total is None else total + piece
        table[pl.ds(dc * length, length), :] = total.astype(jnp.bfloat16)
    block = 256
    count = plan.tokens * plan.top
    for start in range(0, count, block):
        slot_of = lax.broadcasted_iota(jnp.int32, (block, 2 * length), 1)
        hot = (slot_of == target_ref[pl.ds(start, block), :]).astype(jnp.bfloat16)
        head_ref[pl.ds(start, block), :] = jnp.dot(
            hot, table[...], preferred_element_type=jnp.float32
        ).astype(jnp.bfloat16)
        hot = (slot_of == gate_ref[pl.ds(start, block), :]).astype(jnp.bfloat16)
        lines = jnp.dot(hot, table[...], preferred_element_type=jnp.float32)
        lane_of = lax.broadcasted_iota(jnp.int32, (block, LANES), 1)
        out_gate_ref[pl.ds(start, block), :] = jnp.sum(
            jnp.where(lane_of == place_ref[pl.ds(start, block), :], lines, 0.0),
            axis=1,
            keepdims=True,
        )


def final_work(plan, target, gate_line, place, parts):
    count = plan.tokens * plan.top
    return pl.pallas_call(
        functools.partial(final_kernel, plan),
        out_shape=(
            jax.ShapeDtypeStruct((count, plan.head_dim), jnp.bfloat16),
            jax.ShapeDtypeStruct((count, 1), jnp.float32),
        ),
        in_specs=[pl.BlockSpec(memory_space=pltpu.VMEM)] * (3 + plan.sources),
        out_specs=(
            pl.BlockSpec(memory_space=pltpu.VMEM),
            pl.BlockSpec(memory_space=pltpu.VMEM),
        ),
        scratch_shapes=[pltpu.VMEM((2 * plan.planes * plan.back, LANES), jnp.bfloat16)],
        compiler_params=pltpu.CompilerParams(vmem_limit_bytes=48 * 1024 * 1024),
    )(target, gate_line, place, *parts)


def local(mesh, head_outputs, out_grad, gate_weights, route_ids, out_proj):
    tokens, top, head_dim = head_outputs.shape
    features = out_grad.shape[1]
    plan = Plan(mesh, tokens, top, head_dim, features)
    x = lax.axis_index("dp")
    me = lax.axis_index("expert")
    z, y, c = me // GROUP, (me % GROUP) // 2, me % 2

    flat_heads = head_outputs.reshape(tokens, top * head_dim)
    meta = jnp.concatenate(
        [
            gate_weights.T,
            route_ids.T.astype(jnp.bfloat16),
            jnp.zeros((LANES - 2 * top, tokens), jnp.bfloat16),
        ],
        axis=0,
    )

    def pack(dx, dy):
        split = ((x + dx) % plan.dp) * plan.rows + (y + dy) % plan.rows
        piece = lax.dynamic_slice_in_dim(out_grad, split * plan.part, plan.part, 1)
        return jnp.concatenate([piece, flat_heads, meta], axis=1)

    near = [plan.shift(pack(dx, dy), dx=dx, dy=dy) for dx, dy in plan.splits_list()]
    packs = []
    for value in near:
        packs += [value, plan.shift(value, dc=1)]

    weight_parts = []
    for dy in range(plan.rows):
        split = x * plan.rows + (y + dy) % plan.rows
        piece = lax.dynamic_slice_in_dim(out_proj[0], split * plan.part, plan.part, 1)
        weight_parts.append(plan.shift(piece, dy=dy))
    own_weights = jnp.concatenate(weight_parts, axis=0)
    weights = [plan.shift(own_weights, dz=-k % plan.planes) for k in range(plan.planes)]

    rows_at = jnp.arange(plan.rows, dtype=jnp.int32)
    weight_at = ((y - rows_at) % plan.rows) * head_dim
    projections, backs = [None] * plan.planes, [None] * plan.planes
    order = list(range(1, plan.planes)) + [0]
    for k in order:
        expert_ids = ((z + k) % plan.planes) * GROUP + rows_at * 2 + c
        ids = jnp.concatenate([expert_ids, weight_at]).astype(jnp.int32)
        kind = jnp.float32 if k == 0 else jnp.bfloat16
        projections[k], backs[k] = slot_work(plan, ids, packs, weights[k], kind)

    total = projections[0]
    for k in range(1, plan.planes):
        total = total + plan.shift(projections[k], dz=k).astype(jnp.float32)
    own_rows = head_dim // plan.dp
    grad_proj = jnp.zeros((own_rows, features), jnp.float32)
    for dx, dy in plan.splits_list():
        start = ((y + dy) % plan.rows) * head_dim + ((x + dx) % plan.dp) * own_rows
        piece = lax.dynamic_slice_in_dim(total, start, own_rows, 0)
        if dx or dy:
            piece = plan.shift(piece.astype(jnp.bfloat16), dx=dx, dy=dy).astype(jnp.float32)
        split = ((x - dx) % plan.dp) * plan.rows + (y - dy) % plan.rows
        grad_proj = lax.dynamic_update_slice_in_dim(grad_proj, piece, split * plan.part, 1)

    parts = []
    source = 0
    for dx, dy in plan.splits_list():
        for dc in range(2):
            rows = jnp.concatenate([backs[k][source] for k in range(plan.planes)], axis=0)
            parts.append(
                plan.shift(rows, dx=-dx % plan.dp, dy=-dy % plan.rows, dc=dc)
            )
            source += 1
    routes = route_ids.reshape(tokens * top)
    hot = (routes[:, None] == jnp.arange(plan.experts, dtype=jnp.int32)[None, :]).astype(jnp.float32)
    per_token = hot.reshape(tokens, top, plan.experts).sum(axis=1)
    earlier = jnp.tril(jnp.ones((tokens, tokens), jnp.float32), -1)
    places = jnp.dot(earlier, per_token)
    place = jnp.sum(
        hot.reshape(tokens, top, plan.experts) * places[:, None, :], axis=2
    ).astype(jnp.int32).reshape(tokens * top)
    plane = (routes // GROUP - z) % plan.planes
    row = (routes % GROUP) // 2
    side = (routes % 2) ^ c
    base = side * (plan.planes * plan.back) + plane * plan.back
    target = base + row * plan.cap + place
    gate_line = base + plan.rows * plan.cap + row
    grad_head, grad_gate = final_work(
        plan, target[:, None], gate_line[:, None], place[:, None], parts
    )
    return (
        grad_head.reshape(tokens, top, head_dim),
        grad_gate.reshape(tokens, top).astype(jnp.bfloat16),
        grad_proj[None],
    )


def solution(mesh):
    return jax.shard_map(
        functools.partial(local, mesh),
        mesh=mesh,
        in_specs=(
            P(("dp", "expert"), None, None),
            P(("dp", "expert"), None),
            P(("dp", "expert"), None),
            P(("dp", "expert"), None),
            P("expert", None, None),
        ),
        out_specs=(
            P(("dp", "expert"), None, None),
            P(("dp", "expert"), None),
            P("expert", "dp", None),
        ),
        check_vma=False,
    )
```

time: 348 us -> 170 us (0.49)
  the two profiles are of different devices: /device:TPU:0 before, /device:TPU:8 now
where the time goes in v1:
time: 170 us
  waiting for transfers between devices  86.7 us (51%)
  starting transfers between devices  36.3 us (21%)
  Pallas kernels  30 us (18%)
  local copies, waits for them, and re-layouts  7.82 us (5%)
  other arithmetic  7.54 us (4%)
    ppermute x24, waiting for transfers between devices, shift(): return lax.ppermute(value, AXES, self.pairs(**by))  86.7 us
    ppermute x24, starting transfers between devices, shift(): return lax.ppermute(value, AXES, self.pairs(**by))  36.3 us
    pallas_call x4, Pallas kernels, slot_work(): pl.pallas_call(functools.partial(slot_kernel, plan), out_shape=(jax.Shape...  27.8 us
  transfers between devices with their start and end apart: 24, of which 10 were waited for; matrix products, arithmetic and copies ran while one was open for 6% of the time, Pallas kernels for 14%

profile of v1, /device:TPU:8, one launch (start us, length us, event | category | flops | bytes accessed | tf_op | source)
XLA Modules:
  0.0 169.9 jit_solution(12673778290929148470)
XLA Ops:
  0.7 2.0 %dynamic-slice_bitcast_fusion.1 = (bf16[128,1024]{1,0:T(8,128)(2,1)}, bf16[128,1024]{1,0:T(8,128)(2,1)}) fusion(bf16[1,128,4096]{2,1,0:T(8,128)(2,1)} %param.9, s32[]{:T(128)S(6)} %select_n.245, s32[]{:T(128)S(6)} %select_n.246), kind=kLoop, calls=%fused_computation.50 | loop fusion | bytes 1048584 | tf_op jit(solution)/shard_map/dynamic_slice | solution.py:289
  2.7 1.5 collective-permute-start.7
  4.3 0.0 copy-start.8
  4.3 0.1 constant_dynamic-slice_fusion
  4.5 0.6 copy-done.8
  5.0 1.1 fusion.3
  6.1 0.5 collective-permute-start.1
  6.6 1.5 collective-permute-start.3
  8.1 1.5 collective-permute-start.5
  9.6 0.1 collective-permute-start
  9.9 0.2 fusion.15
  10.1 24.8 %collective-permute-done.1.refs_2_ = bf16[128,2176]{1,0:T(8,128)(2,1)S(1)} collective-permute-done((bf16[128,2176]{1,0:T(8,128)(2,1)S(1)}, bf16[128,2176]{1,0:T(8,128)(2,1)S(1)}, u32[]{:S(2)}, u32[]{:S(2)}) %collective-permute-start.1) | collective-permute-done | bytes 557088 | tf_op jit(solution)/shard_map/ppermute | solution.py:52
  34.8 0.5 collective-permute-start.4
  35.4 0.1 collective-permute-start.6
  35.4 1.9 %pad_maximum_fusion.5.refs_8_ = bf16[256,1024]{1,0:T(8,128)(2,1)} fusion(bf16[128,1024]{1,0:T(8,128)(2,1)} %collective-permute-done.7, bf16[128,1024]{1,0:T(8,128)(2,1)} %get-tuple-element.38), kind=kLoop, calls=%fused_computation.31 | loop fusion | flops 1048576 | bytes 1048576 | tf_op jit(solution)/shard_map/concatenate | solution.py:291
  37.3 0.2 collective-permute-start.8
  37.5 0.0 collective-permute-done.refs_1_
  37.5 2.9 %collective-permute-start.9 = (bf16[256,1024]{1,0:T(8,128)(2,1)}, bf16[256,1024]{1,0:T(8,128)(2,1)}, u32[]{:S(2)}, u32[]{:S(2)}) collective-permute-start(bf16[256,1024]{1,0:T(8,128)(2,1)} %pad_maximum_fusion.5.refs_8_), channel_id=1, source_target_pairs={{0,8},{1,9},{2,10},{3,11},{4,12},{5,13},{6,14},{7,15},{8,0},{9,1},... | collective-permute-start | bytes 1572872 | tf_op jit(solution)/shard_map/ppermute | solution.py:52
  40.4 0.1 copy.31
  40.5 0.1 copy.37
  40.6 1.0 convert_element_type.68.place_ref
  41.6 1.0 reshape.320
  42.6 0.1 pad_add_fusion
  42.7 2.5 %collective-permute-start.10 = (bf16[256,1024]{1,0:T(8,128)(2,1)}, bf16[256,1024]{1,0:T(8,128)(2,1)S(1)}, u32[]{:S(2)}, u32[]{:S(2)}) collective-permute-start(bf16[256,1024]{1,0:T(8,128)(2,1)} %pad_maximum_fusion.5.refs_8_), channel_id=1, source_target_pairs={{0,4},{1,5},{2,6},{3,7},{4,8},{5,9},{6,10},{7,11},{8,12},{9,13},{1... | collective-permute-start | bytes 1572872 | tf_op jit(solution)/shard_map/ppermute | solution.py:52
  45.2 0.0 collective-permute-done.4.refs_5_
  45.2 6.8 %shard_map.76 = (f32[256,1024]{1,0:T(8,128)S(1)}, bf16[8,160,128]{2,1,0:T(8,128)(2,1)S(1)}) custom-call(s32[4]{0:T(128)S(1)} %get-tuple-element.81.ids, bf16[128,2176]{1,0:T(8,128)(2,1)S(1)} %fusion.refs_0_, bf16[128,2176]{1,0:T(8,128)(2,1)S(1)} %collective-permute-done.refs_1_, bf16[128,2176]{1,0:T(8,128)(2,1)S(1)} %collective-permute-done.1.refs_2_, ...), custom_call_target="tpu_custom_call" | custom-call | flops 905969664 | bytes 4456448 | tf_op jit(solution)/shard_map/pallas_call | solution.py:184
  52.0 0.0 copy-start.1
  52.0 1.0 copy-done.1
  53.0 7.1 %shard_map.77 = (bf16[256,1024]{1,0:T(8,128)(2,1)}, bf16[8,160,128]{2,1,0:T(8,128)(2,1)S(1)}) custom-call(s32[4]{0:T(128)S(1)} %get-tuple-element.82.ids, bf16[128,2176]{1,0:T(8,128)(2,1)S(1)} %fusion.refs_0_, bf16[128,2176]{1,0:T(8,128)(2,1)S(1)} %collective-permute-done.refs_1_, bf16[128,2176]{1,0:T(8,128)(2,1)S(1)} %collective-permute-done.1.refs_2_, ...), custom_call_target="tpu_custom_call" | custom-call | flops 905969664 | bytes 4456448 | tf_op jit(solution)/shard_map/pallas_call | solution.py:184
  60.1 15.3 %collective-permute-done.9.refs_8_ = bf16[256,1024]{1,0:T(8,128)(2,1)} collective-permute-done((bf16[256,1024]{1,0:T(8,128)(2,1)}, bf16[256,1024]{1,0:T(8,128)(2,1)}, u32[]{:S(2)}, u32[]{:S(2)}) %collective-permute-start.9) | collective-permute-done | bytes 524320 | tf_op jit(solution)/shard_map/ppermute | solution.py:52
  75.5 7.3 %shard_map.78 = (bf16[256,1024]{1,0:T(8,128)(2,1)}, bf16[8,160,128]{2,1,0:T(8,128)(2,1)S(1)}) custom-call(s32[4]{0:T(128)S(1)} %get-tuple-element.83.ids, bf16[128,2176]{1,0:T(8,128)(2,1)S(1)} %fusion.refs_0_, bf16[128,2176]{1,0:T(8,128)(2,1)S(1)} %collective-permute-done.refs_1_, bf16[128,2176]{1,0:T(8,128)(2,1)S(1)} %collective-permute-done.1.refs_2_, ...), custom_call_target="tpu_custom_call" | custom-call | flops 905969664 | bytes 4456448 | tf_op jit(solution)/shard_map/pallas_call | solution.py:184
  82.8 3.2 %collective-permute-done.10.refs_8_ = bf16[256,1024]{1,0:T(8,128)(2,1)S(1)} collective-permute-done((bf16[256,1024]{1,0:T(8,128)(2,1)}, bf16[256,1024]{1,0:T(8,128)(2,1)S(1)}, u32[]{:S(2)}, u32[]{:S(2)}) %collective-permute-start.10) | collective-permute-done | bytes 524320 | tf_op jit(solution)/shard_map/ppermute | solution.py:52
  86.0 6.6 %shard_map.79 = (bf16[256,1024]{1,0:T(8,128)(2,1)}, bf16[8,160,128]{2,1,0:T(8,128)(2,1)S(1)}) custom-call(s32[4]{0:T(128)S(1)} %get-tuple-element.84.ids, bf16[128,2176]{1,0:T(8,128)(2,1)S(1)} %fusion.refs_0_, bf16[128,2176]{1,0:T(8,128)(2,1)S(1)} %collective-permute-done.refs_1_, bf16[128,2176]{1,0:T(8,128)(2,1)S(1)} %collective-permute-done.1.refs_2_, ...), custom_call_target="tpu_custom_call" | custom-call | flops 905969664 | bytes 4456448 | tf_op jit(solution)/shard_map/pallas_call | solution.py:184
  92.7 1.5 collective-permute-start.17
  94.3 1.1 collective-permute-start.16
  95.3 1.5 collective-permute-start.15
  96.8 0.6 collective-permute-start.14
  97.4 0.8 collective-permute-start.13
  98.2 0.7 pad_maximum_fusion.8
  98.9 1.2 collective-permute-done.17.refs_7_
  100.1 6.5 %collective-permute-start.18 = (bf16[256,1024]{1,0:T(8,128)(2,1)}, bf16[256,1024]{1,0:T(8,128)(2,1)S(1)}, u32[]{:S(2)}, u32[]{:S(2)}) collective-permute-start(bf16[256,1024]{1,0:T(8,128)(2,1)} %get-tuple-element.20), channel_id=1, source_target_pairs={{0,4},{1,5},{2,6},{3,7},{4,8},{5,9},{6,10},{7,11},{8,12},{9,13},{1... | collective-permute-start | bytes 1572872 | tf_op jit(solution)/shard_map/ppermute | solution.py:52
  106.6 4.3 %collective-permute-start.19 = (bf16[256,1024]{1,0:T(8,128)(2,1)}, bf16[256,1024]{1,0:T(8,128)(2,1)}, u32[]{:S(2)}, u32[]{:S(2)}) collective-permute-start(bf16[256,1024]{1,0:T(8,128)(2,1)} %get-tuple-element.21), channel_id=1, source_target_pairs={{0,8},{1,9},{2,10},{3,11},{4,12},{5,13},{6,14},{7,15},{8,0},{9,1},... | collective-permute-start | bytes 1572872 | tf_op jit(solution)/shard_map/ppermute | solution.py:52
  110.9 4.8 %collective-permute-start.20 = (bf16[256,1024]{1,0:T(8,128)(2,1)}, bf16[256,1024]{1,0:T(8,128)(2,1)}, u32[]{:S(2)}, u32[]{:S(2)}) collective-permute-start(bf16[256,1024]{1,0:T(8,128)(2,1)} %get-tuple-element.22), channel_id=1, source_target_pairs={{0,12},{1,13},{2,14},{3,15},{4,0},{5,1},{6,2},{7,3},{8,4},{9,5},{1... | collective-permute-start | bytes 1572872 | tf_op jit(solution)/shard_map/ppermute | solution.py:52
  115.7 0.7 pad_maximum_fusion.7
  116.4 0.4 collective-permute-start.12
  116.8 1.2 add_add_fusion
  118.2 4.0 %collective-permute-done.12.refs_2_ = bf16[640,128]{1,0:T(8,128)(2,1)S(1)} collective-permute-done((bf16[640,128]{1,0:T(8,128)(2,1)}, bf16[640,128]{1,0:T(8,128)(2,1)S(1)}, u32[]{:S(2)}, u32[]{:S(2)}) %collective-permute-start.12) | collective-permute-done | bytes 163872 | tf_op jit(solution)/shard_map/ppermute | solution.py:52
  122.2 2.2 %shard_map.80 = (bf16[1024,128]{1,0:T(8,128)(2,1)}, f32[1024,1]{1,0:T(8,128)S(1)}) custom-call(s32[1024,1]{1,0:T(8,128)S(1)} %get-tuple-element.45.target_ref, s32[1024,1]{1,0:T(8,128)S(1)} %get-tuple-element.44.gate_ref, s32[1024,1]{1,0:T(8,128)S(1)} %copy-done, bf16[640,128]{1,0:T(8,128)(2,1)S(1)} %pad_maximum_fusion.6.refs_0_, ...), custom_call_target="tpu_custom_call" | custom-call | tf_op jit(solution)/shard_map/pallas_call | solution.py:242
  124.4 27.6 %collective-permute-done.19 = bf16[256,1024]{1,0:T(8,128)(2,1)} collective-permute-done((bf16[256,1024]{1,0:T(8,128)(2,1)}, bf16[256,1024]{1,0:T(8,128)(2,1)}, u32[]{:S(2)}, u32[]{:S(2)}) %collective-permute-start.19) | collective-permute-done | bytes 524320 | tf_op jit(solution)/shard_map/ppermute | solution.py:52
  152.0 4.8 %collective-permute-done.20 = bf16[256,1024]{1,0:T(8,128)(2,1)} collective-permute-done((bf16[256,1024]{1,0:T(8,128)(2,1)}, bf16[256,1024]{1,0:T(8,128)(2,1)}, u32[]{:S(2)}, u32[]{:S(2)}) %collective-permute-start.20) | collective-permute-done | bytes 524320 | tf_op jit(solution)/shard_map/ppermute | solution.py:52
  156.9 1.5 convert_add_fusion
  158.3 0.1 dynamic-slice_convert_fusion
  158.4 1.3 collective-permute-start.21
  159.7 0.2 convert_reduce_fusion
  160.0 0.1 convert_element_type.61
  160.1 0.7 copy.40
  160.7 1.5 collective-permute-start.22
  162.2 0.7 collective-permute-start.23
  162.9 0.1 broadcast_in_dim.35
  163.1 0.8 collective-permute-done.21
  163.9 3.2 %collective-permute-done.22 = bf16[64,1024]{1,0:T(8,128)(2,1)S(1)} collective-permute-done((bf16[64,1024]{1,0:T(8,128)(2,1)S(1)}, bf16[64,1024]{1,0:T(8,128)(2,1)S(1)}, u32[]{:S(2)}, u32[]{:S(2)}) %collective-permute-start.22) | collective-permute-done | bytes 131104 | tf_op jit(solution)/shard_map/ppermute | solution.py:52
  167.1 1.7 %collective-permute-done.23 = bf16[64,1024]{1,0:T(8,128)(2,1)S(1)} collective-permute-done((bf16[64,1024]{1,0:T(8,128)(2,1)S(1)}, bf16[64,1024]{1,0:T(8,128)(2,1)S(1)}, u32[]{:S(2)}, u32[]{:S(2)}) %collective-permute-start.23) | collective-permute-done | bytes 131104 | tf_op jit(solution)/shard_map/ppermute | solution.py:52
  168.9 0.0 copy-start.5
  168.9 1.0 copy-done.5
  (51 shorter events, 0.5 us)
Async XLA Ops:
  0.6 3.6 %copy-start.6 = (bf16[128,8,128]{2,1,0:T(8,128)(2,1)S(1)}, bf16[128,8,128]{2,1,0:T(8,128)(2,1)}, u32[]{:S(2)}) copy-start(bf16[128,8,128]{2,1,0:T(8,128)(2,1)} %param.5) | copy-start | bytes 786436
  0.6 3.6 %copy-start.7 = (s32[128,8]{0,1:T(8,128)S(1)}, s32[128,8]{0,1:T(8,128)}, u32[]{:S(2)}) copy-start(s32[128,8]{0,1:T(8,128)} %param.8) | copy-start | bytes 12292
  0.7 3.7 %copy-start.4 = (bf16[128,4096]{1,0:T(8,128)(2,1)S(1)}, bf16[128,4096]{1,0:T(8,128)(2,1)}, u32[]{:S(2)}) copy-start(bf16[128,4096]{1,0:T(8,128)(2,1)} %param.6) | copy-start | bytes 3145732
  2.7 32.7 %collective-permute-start.7 = (bf16[128,1024]{1,0:T(8,128)(2,1)}, bf16[128,1024]{1,0:T(8,128)(2,1)}, u32[]{:S(2)}, u32[]{:S(2)}) collective-permute-start(bf16[128,1024]{1,0:T(8,128)(2,1)} %get-tuple-element.39), channel_id=1, source_target_pairs={{0,2},{1,3},{2,0},{3,1},{4,6},{5,7},{6,4},{7,5},{8,10},{9,11},{10,... | collective-permute-start | bytes 786440 | tf_op jit(solution)/shard_map/ppermute | solution.py:52
  4.3 0.7 copy-start.8
  6.1 28.7 %collective-permute-start.1 = (bf16[128,2176]{1,0:T(8,128)(2,1)S(1)}, bf16[128,2176]{1,0:T(8,128)(2,1)S(1)}, u32[]{:S(2)}, u32[]{:S(2)}) collective-permute-start(bf16[128,2176]{1,0:T(8,128)(2,1)S(1)} %get-tuple-element.79), channel_id=1, source_target_pairs={{0,2},{1,3},{2,0},{3,1},{4,6},{5,7},{6,4},{7,5},{8,10},{9,11},{10,... | collective-permute-start | bytes 1671176 | tf_op jit(solution)/shard_map/ppermute | solution.py:52
  6.6 28.2 %collective-permute-start.3 = (bf16[128,2176]{1,0:T(8,128)(2,1)}, bf16[128,2176]{1,0:T(8,128)(2,1)S(1)}, u32[]{:S(2)}, u32[]{:S(2)}) collective-permute-start(bf16[128,2176]{1,0:T(8,128)(2,1)} %get-tuple-element.80), channel_id=1, source_target_pairs={{0,16},{1,17},{2,18},{3,19},{4,20},{5,21},{6,22},{7,23},{8,24},{9,... | collective-permute-start | bytes 1671176 | tf_op jit(solution)/shard_map/ppermute | solution.py:52
  8.1 27.2 %collective-permute-start.5 = (bf16[128,2176]{1,0:T(8,128)(2,1)}, bf16[128,2176]{1,0:T(8,128)(2,1)S(1)}, u32[]{:S(2)}, u32[]{:S(2)}) collective-permute-start(bf16[128,2176]{1,0:T(8,128)(2,1)} %get-tuple-element.78), channel_id=1, source_target_pairs={{0,18},{1,19},{2,16},{3,17},{4,22},{5,23},{6,20},{7,21},{8,26},{9,... | collective-permute-start | bytes 1671176 | tf_op jit(solution)/shard_map/ppermute | solution.py:52
  9.6 27.9 %collective-permute-start = (bf16[128,2176]{1,0:T(8,128)(2,1)S(1)}, bf16[128,2176]{1,0:T(8,128)(2,1)S(1)}, u32[]{:S(2)}, u32[]{:S(2)}) collective-permute-start(bf16[128,2176]{1,0:T(8,128)(2,1)S(1)} %fusion.refs_0_), channel_id=1, source_target_pairs={{0,1},{1,0},{2,3},{3,2},{4,5},{5,4},{6,7},{7,6},{8,9},{9,8},{10,11... | collective-permute-start | bytes 1671176 | tf_op jit(solution)/shard_map/ppermute | solution.py:52
  34.8 7.9 %collective-permute-start.2 = (bf16[128,2176]{1,0:T(8,128)(2,1)S(1)}, bf16[128,2176]{1,0:T(8,128)(2,1)S(1)}, u32[]{:S(2)}, u32[]{:S(2)}) collective-permute-start(bf16[128,2176]{1,0:T(8,128)(2,1)S(1)} %collective-permute-done.1.refs_2_), channel_id=1, source_target_pairs={{0,1},{1,0},{2,3},{3,2},{4,5},{5,4},{6,7},{7,6},{8,9},{9,8},{10,11... | collective-permute-start | bytes 1671176 | tf_op jit(solution)/shard_map/ppermute | solution.py:52
  34.8 10.3 %collective-permute-start.4 = (bf16[128,2176]{1,0:T(8,128)(2,1)S(1)}, bf16[128,2176]{1,0:T(8,128)(2,1)}, u32[]{:S(2)}, u32[]{:S(2)}) collective-permute-start(bf16[128,2176]{1,0:T(8,128)(2,1)S(1)} %collective-permute-done.3.refs_4_), channel_id=1, source_target_pairs={{0,1},{1,0},{2,3},{3,2},{4,5},{5,4},{6,7},{7,6},{8,9},{9,8},{10,11... | collective-permute-start | bytes 1671176 | tf_op jit(solution)/shard_map/ppermute | solution.py:52
  35.4 9.8 %collective-permute-start.6 = (bf16[128,2176]{1,0:T(8,128)(2,1)S(1)}, bf16[128,2176]{1,0:T(8,128)(2,1)}, u32[]{:S(2)}, u32[]{:S(2)}) collective-permute-start(bf16[128,2176]{1,0:T(8,128)(2,1)S(1)} %collective-permute-done.5.refs_6_), channel_id=1, source_target_pairs={{0,1},{1,0},{2,3},{3,2},{4,5},{5,4},{6,7},{7,6},{8,9},{9,8},{10,11... | collective-permute-start | bytes 1671176 | tf_op jit(solution)/shard_map/ppermute | solution.py:52
  37.3 15.7 %collective-permute-start.8 = (bf16[256,1024]{1,0:T(8,128)(2,1)}, bf16[256,1024]{1,0:T(8,128)(2,1)}, u32[]{:S(2)}, u32[]{:S(2)}) collective-permute-start(bf16[256,1024]{1,0:T(8,128)(2,1)} %pad_maximum_fusion.5.refs_8_), channel_id=1, source_target_pairs={{0,12},{1,13},{2,14},{3,15},{4,0},{5,1},{6,2},{7,3},{8,4},{9,5},{1... | collective-permute-start | bytes 1572872 | tf_op jit(solution)/shard_map/ppermute | solution.py:52
  37.5 37.9 %collective-permute-start.9 = (bf16[256,1024]{1,0:T(8,128)(2,1)}, bf16[256,1024]{1,0:T(8,128)(2,1)}, u32[]{:S(2)}, u32[]{:S(2)}) collective-permute-start(bf16[256,1024]{1,0:T(8,128)(2,1)} %pad_maximum_fusion.5.refs_8_), channel_id=1, source_target_pairs={{0,8},{1,9},{2,10},{3,11},{4,12},{5,13},{6,14},{7,15},{8,0},{9,1},... | collective-permute-start | bytes 1572872 | tf_op jit(solution)/shard_map/ppermute | solution.py:52
  42.7 43.3 %collective-permute-start.10 = (bf16[256,1024]{1,0:T(8,128)(2,1)}, bf16[256,1024]{1,0:T(8,128)(2,1)S(1)}, u32[]{:S(2)}, u32[]{:S(2)}) collective-permute-start(bf16[256,1024]{1,0:T(8,128)(2,1)} %pad_maximum_fusion.5.refs_8_), channel_id=1, source_target_pairs={{0,4},{1,5},{2,6},{3,7},{4,8},{5,9},{6,10},{7,11},{8,12},{9,13},{1... | collective-permute-start | bytes 1572872 | tf_op jit(solution)/shard_map/ppermute | solution.py:52
  52.0 1.0 copy-start.1
  92.7 24.1 %copy-start = (s32[1024,1]{1,0:T(8,128)S(1)}, s32[1024,1]{1,0:T(8,128)}, u32[]{:S(2)}) copy-start(s32[1024,1]{1,0:T(8,128)} %convert_element_type.68.place_ref) | copy-start | bytes 12292
  92.7 24.1 %copy-start.3 = (s32[1024,1]{1,0:T(8,128)S(1)}, s32[1024,1]{1,0:T(8,128)}, u32[]{:S(2)}) copy-start(s32[1024,1]{1,0:T(8,128)} %reshape.320) | copy-start | bytes 12292
  92.7 7.4 %collective-permute-start.17 = (bf16[640,128]{1,0:T(8,128)(2,1)S(1)}, bf16[640,128]{1,0:T(8,128)(2,1)S(1)}, u32[]{:S(2)}, u32[]{:S(2)}) collective-permute-start(bf16[640,128]{1,0:T(8,128)(2,1)S(1)} %pad_maximum_fusion.13), channel_id=1, source_target_pairs={{0,19},{1,18},{2,17},{3,16},{4,23},{5,22},{6,21},{7,20},{8,27},{9,... | collective-permute-start | bytes 491528 | tf_op jit(solution)/shard_map/ppermute | solution.py:52
  94.3 12.3 %collective-permute-start.16 = (bf16[640,128]{1,0:T(8,128)(2,1)S(1)}, bf16[640,128]{1,0:T(8,128)(2,1)S(1)}, u32[]{:S(2)}, u32[]{:S(2)}) collective-permute-start(bf16[640,128]{1,0:T(8,128)(2,1)S(1)} %pad_maximum_fusion.12), channel_id=1, source_target_pairs={{0,18},{1,19},{2,16},{3,17},{4,22},{5,23},{6,20},{7,21},{8,26},{9,... | collective-permute-start | bytes 491528 | tf_op jit(solution)/shard_map/ppermute | solution.py:52
  95.3 15.5 %collective-permute-start.15 = (bf16[640,128]{1,0:T(8,128)(2,1)S(1)}, bf16[640,128]{1,0:T(8,128)(2,1)S(1)}, u32[]{:S(2)}, u32[]{:S(2)}) collective-permute-start(bf16[640,128]{1,0:T(8,128)(2,1)S(1)} %pad_maximum_fusion.11), channel_id=1, source_target_pairs={{0,17},{1,16},{2,19},{3,18},{4,21},{5,20},{6,23},{7,22},{8,25},{9,... | collective-permute-start | bytes 491528 | tf_op jit(solution)/shard_map/ppermute | solution.py:52
  96.8 19.6 %collective-permute-start.14 = (bf16[640,128]{1,0:T(8,128)(2,1)S(1)}, bf16[640,128]{1,0:T(8,128)(2,1)S(1)}, u32[]{:S(2)}, u32[]{:S(2)}) collective-permute-start(bf16[640,128]{1,0:T(8,128)(2,1)S(1)} %pad_maximum_fusion.10), channel_id=1, source_target_pairs={{0,16},{1,17},{2,18},{3,19},{4,20},{5,21},{6,22},{7,23},{8,24},{9,... | collective-permute-start | bytes 491528 | tf_op jit(solution)/shard_map/ppermute | solution.py:52
  97.4 19.4 %collective-permute-start.13 = (bf16[640,128]{1,0:T(8,128)(2,1)S(1)}, bf16[640,128]{1,0:T(8,128)(2,1)S(1)}, u32[]{:S(2)}, u32[]{:S(2)}) collective-permute-start(bf16[640,128]{1,0:T(8,128)(2,1)S(1)} %pad_maximum_fusion.9), channel_id=1, source_target_pairs={{0,3},{1,2},{2,1},{3,0},{4,7},{5,6},{6,5},{7,4},{8,11},{9,10},{10,... | collective-permute-start | bytes 491528 | tf_op jit(solution)/shard_map/ppermute | solution.py:52
  100.1 24.4 %collective-permute-start.18 = (bf16[256,1024]{1,0:T(8,128)(2,1)}, bf16[256,1024]{1,0:T(8,128)(2,1)S(1)}, u32[]{:S(2)}, u32[]{:S(2)}) collective-permute-start(bf16[256,1024]{1,0:T(8,128)(2,1)} %get-tuple-element.20), channel_id=1, source_target_pairs={{0,4},{1,5},{2,6},{3,7},{4,8},{5,9},{6,10},{7,11},{8,12},{9,13},{1... | collective-permute-start | bytes 1572872 | tf_op jit(solution)/shard_map/ppermute | solution.py:52
  106.6 45.5 %collective-permute-start.19 = (bf16[256,1024]{1,0:T(8,128)(2,1)}, bf16[256,1024]{1,0:T(8,128)(2,1)}, u32[]{:S(2)}, u32[]{:S(2)}) collective-permute-start(bf16[256,1024]{1,0:T(8,128)(2,1)} %get-tuple-element.21), channel_id=1, source_target_pairs={{0,8},{1,9},{2,10},{3,11},{4,12},{5,13},{6,14},{7,15},{8,0},{9,1},... | collective-permute-start | bytes 1572872 | tf_op jit(solution)/shard_map/ppermute | solution.py:52
  110.9 46.0 %collective-permute-start.20 = (bf16[256,1024]{1,0:T(8,128)(2,1)}, bf16[256,1024]{1,0:T(8,128)(2,1)}, u32[]{:S(2)}, u32[]{:S(2)}) collective-permute-start(bf16[256,1024]{1,0:T(8,128)(2,1)} %get-tuple-element.22), channel_id=1, source_target_pairs={{0,12},{1,13},{2,14},{3,15},{4,0},{5,1},{6,2},{7,3},{8,4},{9,5},{1... | collective-permute-start | bytes 1572872 | tf_op jit(solution)/shard_map/ppermute | solution.py:52
  116.4 5.8 %collective-permute-start.12 = (bf16[640,128]{1,0:T(8,128)(2,1)}, bf16[640,128]{1,0:T(8,128)(2,1)S(1)}, u32[]{:S(2)}, u32[]{:S(2)}) collective-permute-start(bf16[640,128]{1,0:T(8,128)(2,1)} %pad_maximum_fusion.8), channel_id=1, source_target_pairs={{0,2},{1,3},{2,0},{3,1},{4,6},{5,7},{6,4},{7,5},{8,10},{9,11},{10,... | collective-permute-start | bytes 491528 | tf_op jit(solution)/shard_map/ppermute | solution.py:52
  116.8 5.4 %collective-permute-start.11 = (bf16[640,128]{1,0:T(8,128)(2,1)}, bf16[640,128]{1,0:T(8,128)(2,1)S(1)}, u32[]{:S(2)}, u32[]{:S(2)}) collective-permute-start(bf16[640,128]{1,0:T(8,128)(2,1)} %pad_maximum_fusion.7), channel_id=1, source_target_pairs={{0,1},{1,0},{2,3},{3,2},{4,5},{5,4},{6,7},{7,6},{8,9},{9,8},{10,11... | collective-permute-start | bytes 491528 | tf_op jit(solution)/shard_map/ppermute | solution.py:52
  122.2 34.6 %copy-start.2 = (f32[256,1024]{1,0:T(8,128)S(1)}, f32[256,1024]{1,0:T(8,128)}, u32[]{:S(2)}) copy-start(f32[256,1024]{1,0:T(8,128)} %copy-done.1) | copy-start | bytes 3145732
  158.4 5.5 %collective-permute-start.21 = (bf16[64,1024]{1,0:T(8,128)(2,1)S(1)}, bf16[64,1024]{1,0:T(8,128)(2,1)S(1)}, u32[]{:S(2)}, u32[]{:S(2)}) collective-permute-start(bf16[64,1024]{1,0:T(8,128)(2,1)S(1)} %get-tuple-element.37), channel_id=1, source_target_pairs={{0,2},{1,3},{2,0},{3,1},{4,6},{5,7},{6,4},{7,5},{8,10},{9,11},{10,... | collective-permute-start | bytes 393224 | tf_op jit(solution)/shard_map/ppermute | solution.py:52
  160.7 6.4 %collective-permute-start.22 = (bf16[64,1024]{1,0:T(8,128)(2,1)S(1)}, bf16[64,1024]{1,0:T(8,128)(2,1)S(1)}, u32[]{:S(2)}, u32[]{:S(2)}) collective-permute-start(bf16[64,1024]{1,0:T(8,128)(2,1)S(1)} %get-tuple-element.36), channel_id=1, source_target_pairs={{0,16},{1,17},{2,18},{3,19},{4,20},{5,21},{6,22},{7,23},{8,24},{9,... | collective-permute-start | bytes 393224 | tf_op jit(solution)/shard_map/ppermute | solution.py:52
  162.2 6.7 %collective-permute-start.23 = (bf16[64,1024]{1,0:T(8,128)(2,1)S(1)}, bf16[64,1024]{1,0:T(8,128)(2,1)S(1)}, u32[]{:S(2)}, u32[]{:S(2)}) collective-permute-start(bf16[64,1024]{1,0:T(8,128)(2,1)S(1)} %get-tuple-element.35), channel_id=1, source_target_pairs={{0,18},{1,19},{2,16},{3,17},{4,22},{5,23},{6,20},{7,21},{8,26},{9,... | collective-permute-start | bytes 393224 | tf_op jit(solution)/shard_map/ppermute | solution.py:52
  168.9 1.0 copy-start.5

commit v2 on v1

--- a/solution.py
+++ b/solution.py
@@ -50,6 +50,14 @@
         if not any(by.values()):
             return value
         return lax.ppermute(value, AXES, self.pairs(**by))
+
+    def along(self, value, moves):
+        out = []
+        for x in range(self.dp):
+            for a, b in moves:
+                for r in range(GROUP):
+                    out.append((self.index(x, a, 0, 0) + r, self.index(x, b, 0, 0) + r))
+        return lax.ppermute(value, AXES, out)
 
     def splits_list(self):
         return [(dx, dy) for dx in range(self.dp) for dy in range(self.rows)]
@@ -180,7 +188,6 @@
 
 def slot_work(plan, ids, packs, weight, kind):
     rows = plan.sources * plan.cap
-    flops = 6 * plan.rows * rows * plan.head_dim * plan.part
     return pl.pallas_call(
         functools.partial(slot_kernel, plan),
         out_shape=(
@@ -201,11 +208,6 @@
             pltpu.SemaphoreType.DMA((2, 2)),
         ],
         compiler_params=pltpu.CompilerParams(vmem_limit_bytes=32 * 1024 * 1024),
-        cost_estimate=pl.CostEstimate(
-            flops=flops,
-            bytes_accessed=plan.sources * plan.tokens * plan.width * 2,
-            transcendentals=plan.rows * rows * plan.part,
-        ),
     )(ids, *packs, weight)
 
 
@@ -289,21 +291,54 @@
         piece = lax.dynamic_slice_in_dim(out_proj[0], split * plan.part, plan.part, 1)
         weight_parts.append(plan.shift(piece, dy=dy))
     own_weights = jnp.concatenate(weight_parts, axis=0)
-    weights = [plan.shift(own_weights, dz=-k % plan.planes) for k in range(plan.planes)]
-
     rows_at = jnp.arange(plan.rows, dtype=jnp.int32)
     weight_at = ((y - rows_at) % plan.rows) * head_dim
-    projections, backs = [None] * plan.planes, [None] * plan.planes
-    order = list(range(1, plan.planes)) + [0]
-    for k in order:
-        expert_ids = ((z + k) % plan.planes) * GROUP + rows_at * 2 + c
-        ids = jnp.concatenate([expert_ids, weight_at]).astype(jnp.int32)
-        kind = jnp.float32 if k == 0 else jnp.bfloat16
-        projections[k], backs[k] = slot_work(plan, ids, packs, weights[k], kind)
-
-    total = projections[0]
-    for k in range(1, plan.planes):
-        total = total + plan.shift(projections[k], dz=k).astype(jnp.float32)
+
+    def work(plane, weight, kind, after=None):
+        ids = jnp.concatenate([plane * GROUP + rows_at * 2 + c, weight_at]).astype(jnp.int32)
+        if after is not None:
+            ids, _ = lax.optimization_barrier((ids, after))
+        return slot_work(plan, ids, packs, weight, kind)
+
+    if plan.planes == 4:
+        inner = (z == 1) | (z == 2)
+        mates, middle = [(0, 1), (1, 0), (2, 3), (3, 2)], [(1, 2), (2, 1)]
+        outward, inward, across = [(1, 0), (2, 3)], [(0, 1), (3, 2)], [(1, 3), (2, 0)]
+        at = {"own": z, "mate": z ^ 1, "near": jnp.where(z < 2, 2, 1), "far": jnp.where(z < 2, 3, 0)}
+        weights = {"own": own_weights, "mate": plan.along(own_weights, mates)}
+        near_in = plan.along(own_weights, middle)
+        near_out = plan.along(near_in, outward)
+        far_in = plan.along(weights["mate"], middle)
+        far_out = plan.along(far_in, outward)
+        weights["near"] = jnp.where(inner, near_in, near_out)
+        weights["far"] = jnp.where(inner, far_in, far_out)
+        sums, back_at, back = {}, {}, None
+        for name in ("near", "far", "mate", "own"):
+            kind = jnp.float32 if name == "own" else jnp.bfloat16
+            sums[name], back = work(at[name], weights[name], kind, back)
+            back_at[name] = back
+        near_sum = sums["near"] + plan.along(sums["near"], inward)
+        far_sum = sums["far"] + plan.along(sums["far"], inward)
+        total = (
+            sums["own"]
+            + plan.along(sums["mate"], mates).astype(jnp.float32)
+            + plan.along(near_sum, middle).astype(jnp.float32)
+            + plan.along(far_sum, across).astype(jnp.float32)
+        )
+        names = ("own", "mate", "near", "far")
+        backs = [back_at[name] for name in names]
+        backs, _ = lax.optimization_barrier((backs, (near_sum, far_sum)))
+        plane_of = jnp.stack([at[name] for name in names])
+    else:
+        backs, total = [], None
+        for k in range(plan.planes):
+            weight = plan.shift(own_weights, dz=-k % plan.planes)
+            part, back = work((z + k) % plan.planes, weight, jnp.bfloat16 if k else jnp.float32)
+            backs.append(back)
+            part = plan.shift(part, dz=k).astype(jnp.float32)
+            total = part if total is None else total + part
+        plane_of = (z + jnp.arange(plan.planes, dtype=jnp.int32)) % plan.planes
+
     own_rows = head_dim // plan.dp
     grad_proj = jnp.zeros((own_rows, features), jnp.float32)
     for dx, dy in plan.splits_list():
@@ -331,12 +366,16 @@
     place = jnp.sum(
         hot.reshape(tokens, top, plan.experts) * places[:, None, :], axis=2
     ).astype(jnp.int32).reshape(tokens * top)
-    plane = (routes // GROUP - z) % plan.planes
+    slots = jnp.arange(plan.planes, dtype=jnp.int32)
+    plane = jnp.sum(
+        jnp.where((routes // GROUP)[:, None] == plane_of[None, :], slots[None, :], 0), axis=1
+    )
     row = (routes % GROUP) // 2
     side = (routes % 2) ^ c
     base = side * (plan.planes * plan.back) + plane * plan.back
     target = base + row * plan.cap + place
     gate_line = base + plan.rows * plan.cap + row
+    target, _ = lax.optimization_barrier((target, total))
     grad_head, grad_gate = final_work(
         plan, target[:, None], gate_line[:, None], place[:, None], parts
     )

time: 170 us -> 125 us (0.74)
  the two profiles are of different devices: /device:TPU:8 before, /device:TPU:0 now
where the time goes in v2:
time: 125 us; the launch traced here: 124 us
  waiting for transfers between devices  34.5 us (28%)
  starting transfers between devices  33.1 us (26%)
  Pallas kernels  28 us (22%)
  other arithmetic  13.5 us (11%)
  local copies, waits for them, and re-layouts  13.3 us (11%)
  between operations  1.37 us (1%)
    pallas_call x4, Pallas kernels, slot_work(): pl.pallas_call(functools.partial(slot_kernel, plan), out_shape=(jax.Shape...  25.8 us
    ppermute x10, waiting for transfers between devices, along(): return lax.ppermute(value, AXES, out)  18.7 us
    ppermute x10, starting transfers between devices, along(): return lax.ppermute(value, AXES, out)  17.5 us
    ppermute x18, waiting for transfers between devices, shift(): return lax.ppermute(value, AXES, self.pairs(**by))  15.8 us
    ppermute x18, starting transfers between devices, shift(): return lax.ppermute(value, AXES, self.pairs(**by))  15.6 us
    unnamed x37, local copies, waits for them, and re-layouts  4.59 us
    add x1, other arithmetic, local(): gate_line = base + plan.rows * plan.cap + row  2.75 us
  transfers between devices with their start and end apart: 28, of which 8 were waited for; matrix products, arithmetic and copies ran while one was open for 17% of the time, Pallas kernels for 23%

profile of v2, /device:TPU:0, one launch (start us, length us, event | category | flops | bytes accessed | tf_op | source)
XLA Modules:
  0.0 124.0 jit_solution(37815478769526957)
XLA Ops:
  0.7 1.9 %dynamic-slice_bitcast_fusion.1 = (bf16[128,1024]{1,0:T(8,128)(2,1)S(1)}, bf16[128,1024]{1,0:T(8,128)(2,1)}) fusion(bf16[1,128,4096]{2,1,0:T(8,128)(2,1)} %param.9, s32[]{:T(128)S(6)} %select_n.226, s32[]{:T(128)S(6)} %select_n.227), kind=kLoop, calls=%fused_computation.41 | loop fusion | bytes 1048584 | tf_op jit(solution)/shard_map/dynamic_slice | solution.py:291
  2.6 3.0 %collective-permute-start.7 = (bf16[128,1024]{1,0:T(8,128)(2,1)}, bf16[128,1024]{1,0:T(8,128)(2,1)}, u32[]{:S(2)}, u32[]{:S(2)}) collective-permute-start(bf16[128,1024]{1,0:T(8,128)(2,1)} %get-tuple-element.55), channel_id=1, source_target_pairs={{0,2},{1,3},{2,0},{3,1},{4,6},{5,7},{6,4},{7,5},{8,10},{9,11},{10,... | collective-permute-start | bytes 786440 | tf_op jit(solution)/shard_map/ppermute | solution.py:52
  5.7 0.1 constant_dynamic-slice_fusion
  5.8 0.6 copy-done.16
  6.4 1.1 fusion.3
  7.5 2.0 %collective-permute-start.3 = (bf16[128,2176]{1,0:T(8,128)(2,1)S(1)}, bf16[128,2176]{1,0:T(8,128)(2,1)S(1)}, u32[]{:S(2)}, u32[]{:S(2)}) collective-permute-start(bf16[128,2176]{1,0:T(8,128)(2,1)S(1)} %get-tuple-element.94), channel_id=1, source_target_pairs={{0,16},{1,17},{2,18},{3,19},{4,20},{5,21},{6,22},{7,23},{8,24},{9,... | collective-permute-start | bytes 1671176 | tf_op jit(solution)/shard_map/ppermute | solution.py:52
  9.5 1.5 %collective-permute-start.5 = (bf16[128,2176]{1,0:T(8,128)(2,1)}, bf16[128,2176]{1,0:T(8,128)(2,1)S(1)}, u32[]{:S(2)}, u32[]{:S(2)}) collective-permute-start(bf16[128,2176]{1,0:T(8,128)(2,1)} %get-tuple-element.92), channel_id=1, source_target_pairs={{0,18},{1,19},{2,16},{3,17},{4,22},{5,23},{6,20},{7,21},{8,26},{9,... | collective-permute-start | bytes 1671176 | tf_op jit(solution)/shard_map/ppermute | solution.py:52
  11.0 2.0 %collective-permute-done.7 = bf16[128,1024]{1,0:T(8,128)(2,1)} collective-permute-done((bf16[128,1024]{1,0:T(8,128)(2,1)}, bf16[128,1024]{1,0:T(8,128)(2,1)}, u32[]{:S(2)}, u32[]{:S(2)}) %collective-permute-start.7) | collective-permute-done | bytes 262176 | tf_op jit(solution)/shard_map/ppermute | solution.py:52
  13.0 1.0 pad_maximum_fusion.5.refs_8_
  14.0 2.2 %collective-permute-start.10 = (bf16[256,1024]{1,0:T(8,128)(2,1)S(1)}, bf16[256,1024]{1,0:T(8,128)(2,1)S(1)}, u32[]{:S(2)}, u32[]{:S(2)}) collective-permute-start(bf16[256,1024]{1,0:T(8,128)(2,1)S(1)} %pad_maximum_fusion.5.refs_8_), channel_id=1, source_target_pairs={{0,4},{1,5},{2,6},{3,7},{4,0},{5,1},{6,2},{7,3},{8,12},{9,13},{10,... | collective-permute-start | bytes 1572872 | tf_op jit(solution)/shard_map/ppermute | solution.py:60
  16.2 0.7 collective-permute-start.8
  16.9 0.2 fusion.12
  17.1 9.2 %collective-permute-done.10.refs_8_ = bf16[256,1024]{1,0:T(8,128)(2,1)S(1)} collective-permute-done((bf16[256,1024]{1,0:T(8,128)(2,1)S(1)}, bf16[256,1024]{1,0:T(8,128)(2,1)S(1)}, u32[]{:S(2)}, u32[]{:S(2)}) %collective-permute-start.10) | collective-permute-done | bytes 524320 | tf_op jit(solution)/shard_map/ppermute | solution.py:60
  26.4 1.5 %collective-permute-start.11 = (bf16[256,1024]{1,0:T(8,128)(2,1)S(1)}, bf16[256,1024]{1,0:T(8,128)(2,1)}, u32[]{:S(2)}, u32[]{:S(2)}) collective-permute-start(bf16[256,1024]{1,0:T(8,128)(2,1)S(1)} %collective-permute-done.10.refs_8_), channel_id=1, source_target_pairs={{4,8},{5,9},{6,10},{7,11},{8,4},{9,5},{10,6},{11,7},{20,24},{21,25... | collective-permute-start | bytes 1572872 | tf_op jit(solution)/shard_map/ppermute | solution.py:60
  27.8 1.3 %collective-permute-start.9 = (bf16[256,1024]{1,0:T(8,128)(2,1)S(1)}, bf16[256,1024]{1,0:T(8,128)(2,1)S(1)}, u32[]{:S(2)}, u32[]{:S(2)}) collective-permute-start(bf16[256,1024]{1,0:T(8,128)(2,1)S(1)} %collective-permute-done.8), channel_id=1, source_target_pairs={{4,0},{5,1},{6,2},{7,3},{8,12},{9,13},{10,14},{11,15},{20,16},{21,... | collective-permute-start | bytes 1572872 | tf_op jit(solution)/shard_map/ppermute | solution.py:60
  29.3 6.7 %collective-permute-done.1.refs_2_ = bf16[128,2176]{1,0:T(8,128)(2,1)S(1)} collective-permute-done((bf16[128,2176]{1,0:T(8,128)(2,1)}, bf16[128,2176]{1,0:T(8,128)(2,1)S(1)}, u32[]{:S(2)}, u32[]{:S(2)}) %collective-permute-start.1) | collective-permute-done | bytes 557088 | tf_op jit(solution)/shard_map/ppermute | solution.py:52
  36.0 0.5 collective-permute-start.2
  36.6 0.5 collective-permute-start.6
  37.1 4.3 %collective-permute-done.9 = bf16[256,1024]{1,0:T(8,128)(2,1)S(1)} collective-permute-done((bf16[256,1024]{1,0:T(8,128)(2,1)S(1)}, bf16[256,1024]{1,0:T(8,128)(2,1)S(1)}, u32[]{:S(2)}, u32[]{:S(2)}) %collective-permute-start.9) | collective-permute-done | bytes 524320 | tf_op jit(solution)/shard_map/ppermute | solution.py:60
  41.3 0.8 copy-done.13
  42.1 1.3 %collective-permute-start.12 = (bf16[256,1024]{1,0:T(8,128)(2,1)}, bf16[256,1024]{1,0:T(8,128)(2,1)}, u32[]{:S(2)}, u32[]{:S(2)}) collective-permute-start(bf16[256,1024]{1,0:T(8,128)(2,1)} %collective-permute-done.11), channel_id=1, source_target_pairs={{4,0},{5,1},{6,2},{7,3},{8,12},{9,13},{10,14},{11,15},{20,16},{21,... | collective-permute-start | bytes 1572872 | tf_op jit(solution)/shard_map/ppermute | solution.py:60
  43.5 0.1 copy.34
  43.6 0.1 reshape.241
  43.7 1.1 broadcast_select_fusion.1.refs_8_
  44.9 6.6 %shard_map.76 = (bf16[256,1024]{1,0:T(8,128)(2,1)}, bf16[8,160,128]{2,1,0:T(8,128)(2,1)S(1)}) custom-call(s32[4]{0:T(128)S(1)} %get-tuple-element.99.ids, bf16[128,2176]{1,0:T(8,128)(2,1)S(1)} %fusion.refs_0_, bf16[128,2176]{1,0:T(8,128)(2,1)S(1)} %collective-permute-done.refs_1_, bf16[128,2176]{1,0:T(8,128)(2,1)S(1)} %collective-permute-done.1.refs_2_, ...), custom_call_target="tpu_custom_call" | custom-call | tf_op jit(solution)/shard_map/pallas_call | solution.py:191
  51.5 0.7 copy-done.6
  52.2 6.1 %collective-permute-start.14 = (bf16[256,1024]{1,0:T(8,128)(2,1)}, bf16[256,1024]{1,0:T(8,128)(2,1)}, u32[]{:S(2)}, u32[]{:S(2)}) collective-permute-start(bf16[256,1024]{1,0:T(8,128)(2,1)} %get-tuple-element.29), channel_id=1, source_target_pairs={{0,4},{1,5},{2,6},{3,7},{12,8},{13,9},{14,10},{15,11},{16,20},{17,... | collective-permute-start | bytes 1572872 | tf_op jit(solution)/shard_map/ppermute | solution.py:60
  58.3 1.1 broadcast_select_fusion.refs_8_
  59.4 6.6 %shard_map.77 = (bf16[256,1024]{1,0:T(8,128)(2,1)}, bf16[8,160,128]{2,1,0:T(8,128)(2,1)S(1)}) custom-call(s32[4]{0:T(128)S(1)} %get-tuple-element.22.ids, bf16[128,2176]{1,0:T(8,128)(2,1)S(1)} %fusion.refs_0_, bf16[128,2176]{1,0:T(8,128)(2,1)S(1)} %collective-permute-done.refs_1_, bf16[128,2176]{1,0:T(8,128)(2,1)S(1)} %collective-permute-done.1.refs_2_, ...), custom_call_target="tpu_custom_call" | custom-call | tf_op jit(solution)/shard_map/pallas_call | solution.py:191
  66.0 0.7 copy-done.8
  66.8 2.1 %collective-permute-start.16 = (bf16[256,1024]{1,0:T(8,128)(2,1)}, bf16[256,1024]{1,0:T(8,128)(2,1)}, u32[]{:S(2)}, u32[]{:S(2)}) collective-permute-start(bf16[256,1024]{1,0:T(8,128)(2,1)} %get-tuple-element.30), channel_id=1, source_target_pairs={{0,4},{1,5},{2,6},{3,7},{12,8},{13,9},{14,10},{15,11},{16,20},{17,... | collective-permute-start | bytes 1572872 | tf_op jit(solution)/shard_map/ppermute | solution.py:60
  69.0 1.0 reshape.248
  70.0 0.1 copy.35
  70.2 1.0 convert_element_type.68.place_ref
  71.2 1.0 copy.41
  72.2 2.8 %fusion.8.gate_ref = s32[1024,1]{1,0:T(8,128)} fusion(s32[1024,1]{1,0:T(8,128)} %copy.41, s32[1024,1]{1,0:T(8,128)} %reshape.248, s32[]{:T(128)S(6)} %select_n.205), kind=kLoop, calls=%fused_computation.23 | loop fusion | flops 39936 | bytes 12292 | tf_op jit(solution)/shard_map/add | solution.py:377
  75.0 6.3 %shard_map.78 = (bf16[256,1024]{1,0:T(8,128)(2,1)S(1)}, bf16[8,160,128]{2,1,0:T(8,128)(2,1)S(1)}) custom-call(s32[4]{0:T(128)S(1)} %get-tuple-element.24.ids, bf16[128,2176]{1,0:T(8,128)(2,1)S(1)} %fusion.refs_0_, bf16[128,2176]{1,0:T(8,128)(2,1)S(1)} %collective-permute-done.refs_1_, bf16[128,2176]{1,0:T(8,128)(2,1)S(1)} %collective-permute-done.1.refs_2_, ...), custom_call_target="tpu_custom_call" | custom-call | tf_op jit(solution)/shard_map/pallas_call | solution.py:191
  81.4 1.4 %add.338 = bf16[256,1024]{1,0:T(8,128)(2,1)S(1)} add(bf16[256,1024]{1,0:T(8,128)(2,1)} %get-tuple-element.29, bf16[256,1024]{1,0:T(8,128)(2,1)} %collective-permute-done.14) | non-fusion elementwise | flops 262144 | bytes 1572864 | tf_op jit(solution)/shard_map/add | solution.py:320
  82.8 0.7 collective-permute-start.15
  83.5 6.3 %shard_map.79 = (f32[256,1024]{1,0:T(8,128)S(1)}, bf16[8,160,128]{2,1,0:T(8,128)(2,1)S(1)}) custom-call(s32[4]{0:T(128)S(1)} %get-tuple-element.26.ids, bf16[128,2176]{1,0:T(8,128)(2,1)S(1)} %fusion.refs_0_, bf16[128,2176]{1,0:T(8,128)(2,1)S(1)} %collective-permute-done.refs_1_, bf16[128,2176]{1,0:T(8,128)(2,1)S(1)} %collective-permute-done.1.refs_2_, ...), custom_call_target="tpu_custom_call" | custom-call | tf_op jit(solution)/shard_map/pallas_call | solution.py:191
  89.8 1.4 %add.340 = bf16[256,1024]{1,0:T(8,128)(2,1)S(1)} add(bf16[256,1024]{1,0:T(8,128)(2,1)} %get-tuple-element.30, bf16[256,1024]{1,0:T(8,128)(2,1)} %collective-permute-done.16) | non-fusion elementwise | flops 262144 | bytes 1572864 | tf_op jit(solution)/shard_map/add | solution.py:321
  91.2 1.6 %collective-permute-start.17 = (bf16[256,1024]{1,0:T(8,128)(2,1)S(1)}, bf16[256,1024]{1,0:T(8,128)(2,1)S(1)}, u32[]{:S(2)}, u32[]{:S(2)}) collective-permute-start(bf16[256,1024]{1,0:T(8,128)(2,1)S(1)} %add.340), channel_id=1, source_target_pairs={{4,12},{5,13},{6,14},{7,15},{8,0},{9,1},{10,2},{11,3},{20,28},{21,... | collective-permute-start | bytes 1572872 | tf_op jit(solution)/shard_map/ppermute | solution.py:60
  93.1 0.6 collective-permute-start.24
  93.7 2.0 %collective-permute-start.23 = (bf16[640,128]{1,0:T(8,128)(2,1)S(1)}, bf16[640,128]{1,0:T(8,128)(2,1)S(1)}, u32[]{:S(2)}, u32[]{:S(2)}) collective-permute-start(bf16[640,128]{1,0:T(8,128)(2,1)S(1)} %pad_maximum_fusion.12), channel_id=1, source_target_pairs={{0,18},{1,19},{2,16},{3,17},{4,22},{5,23},{6,20},{7,21},{8,26},{9,... | collective-permute-start | bytes 491528 | tf_op jit(solution)/shard_map/ppermute | solution.py:52
  95.7 0.7 pad_maximum_fusion.11
  96.5 1.5 %collective-permute-start.22 = (bf16[640,128]{1,0:T(8,128)(2,1)}, bf16[640,128]{1,0:T(8,128)(2,1)S(1)}, u32[]{:S(2)}, u32[]{:S(2)}) collective-permute-start(bf16[640,128]{1,0:T(8,128)(2,1)} %pad_maximum_fusion.11), channel_id=1, source_target_pairs={{0,17},{1,16},{2,19},{3,18},{4,21},{5,20},{6,23},{7,22},{8,25},{9,... | collective-permute-start | bytes 491528 | tf_op jit(solution)/shard_map/ppermute | solution.py:52
  97.9 0.5 collective-permute-start.21
  98.5 2.0 %collective-permute-done.24.refs_7_ = bf16[640,128]{1,0:T(8,128)(2,1)S(1)} collective-permute-done((bf16[640,128]{1,0:T(8,128)(2,1)S(1)}, bf16[640,128]{1,0:T(8,128)(2,1)S(1)}, u32[]{:S(2)}, u32[]{:S(2)}) %collective-permute-start.24) | collective-permute-done | bytes 163872 | tf_op jit(solution)/shard_map/ppermute | solution.py:52
  100.4 3.7 %collective-permute-done.23.refs_6_ = bf16[640,128]{1,0:T(8,128)(2,1)S(1)} collective-permute-done((bf16[640,128]{1,0:T(8,128)(2,1)S(1)}, bf16[640,128]{1,0:T(8,128)(2,1)S(1)}, u32[]{:S(2)}, u32[]{:S(2)}) %collective-permute-start.23) | collective-permute-done | bytes 163872 | tf_op jit(solution)/shard_map/ppermute | solution.py:52
  104.1 5.2 %collective-permute-done.17 = bf16[256,1024]{1,0:T(8,128)(2,1)S(1)} collective-permute-done((bf16[256,1024]{1,0:T(8,128)(2,1)S(1)}, bf16[256,1024]{1,0:T(8,128)(2,1)S(1)}, u32[]{:S(2)}, u32[]{:S(2)}) %collective-permute-start.17) | collective-permute-done | bytes 524320 | tf_op jit(solution)/shard_map/ppermute | solution.py:60
  109.4 1.3 %convert_add_fusion = f32[256,1024]{1,0:T(8,128)} fusion(bf16[256,1024]{1,0:T(8,128)(2,1)S(1)} %collective-permute-done.17, bf16[256,1024]{1,0:T(8,128)(2,1)S(1)} %collective-permute-done.15, f32[256,1024]{1,0:T(8,128)S(1)} %get-tuple-element.27, bf16[256,1024]{1,0:T(8,128)(2,1)S(1)} %collective-permute-done.13), kind=kLoop, calls=%fused_computation | loop fusion | flops 1572864 | bytes 3670016 | tf_op jit(solution)/shard_map/add | solution.py:323
  110.7 0.2 copy.43.target_ref
  110.9 2.0 %dynamic-slice_convert_fusion = (bf16[64,1024]{1,0:T(8,128)(2,1)}, bf16[64,1024]{1,0:T(8,128)(2,1)}, bf16[64,1024]{1,0:T(8,128)(2,1)}) fusion(f32[256,1024]{1,0:T(8,128)} %convert_add_fusion, s32[]{:T(128)S(6)} %select_n.240, s32[]{:T(128)S(6)} %select_n.237, s32[]{:T(128)S(6)} %select_n.234), kind=kLoop, calls=%fused_computation.36 | loop fusion | bytes 786444 | tf_op jit(solution)/shard_map/convert_element_type | solution.py:348
  112.9 1.5 %collective-permute-start.25 = (bf16[64,1024]{1,0:T(8,128)(2,1)}, bf16[64,1024]{1,0:T(8,128)(2,1)}, u32[]{:S(2)}, u32[]{:S(2)}) collective-permute-start(bf16[64,1024]{1,0:T(8,128)(2,1)} %get-tuple-element.53), channel_id=1, source_target_pairs={{0,2},{1,3},{2,0},{3,1},{4,6},{5,7},{6,4},{7,5},{8,10},{9,11},{10,... | collective-permute-start | bytes 393224 | tf_op jit(solution)/shard_map/ppermute | solution.py:52
  114.4 1.5 %collective-permute-start.26 = (bf16[64,1024]{1,0:T(8,128)(2,1)}, bf16[64,1024]{1,0:T(8,128)(2,1)S(1)}, u32[]{:S(2)}, u32[]{:S(2)}) collective-permute-start(bf16[64,1024]{1,0:T(8,128)(2,1)} %get-tuple-element.52), channel_id=1, source_target_pairs={{0,16},{1,17},{2,18},{3,19},{4,20},{5,21},{6,22},{7,23},{8,24},{9,... | collective-permute-start | bytes 393224 | tf_op jit(solution)/shard_map/ppermute | solution.py:52
  115.9 0.5 collective-permute-start.27
  116.4 2.2 %shard_map.80 = (bf16[1024,128]{1,0:T(8,128)(2,1)}, f32[1024,1]{1,0:T(8,128)S(1)}) custom-call(s32[1024,1]{1,0:T(8,128)S(1)} %copy.43.target_ref, s32[1024,1]{1,0:T(8,128)S(1)} %copy-done.3, s32[1024,1]{1,0:T(8,128)S(1)} %copy-done.2, bf16[640,128]{1,0:T(8,128)(2,1)S(1)} %pad_maximum_fusion.6.refs_0_, bf16[640,128]{1,0:T(8,128)(2,1)S(1)} %collective-permute-done.18.refs_1_, ...), custom_call_target="tpu_custom_call" | custom-call | tf_op jit(solution)/shard_map/pallas_call | solution.py:244
  118.6 0.2 convert_reduce_fusion
  118.8 0.1 convert_element_type.64
  118.9 0.7 copy.45
  119.7 1.0 bitcast_dynamic-update-slice_fusion
  120.7 0.9 convert_dynamic-update-slice_fusion.2
  121.6 1.4 %collective-permute-done.27 = bf16[64,1024]{1,0:T(8,128)(2,1)S(1)} collective-permute-done((bf16[64,1024]{1,0:T(8,128)(2,1)}, bf16[64,1024]{1,0:T(8,128)(2,1)S(1)}, u32[]{:S(2)}, u32[]{:S(2)}) %collective-permute-start.27) | collective-permute-done | bytes 131104 | tf_op jit(solution)/shard_map/ppermute | solution.py:52
  123.0 1.0 copy-done.11
  (87 shorter events, 1.1 us)
Async XLA Ops:
  0.6 4.9 %copy-start.14 = (bf16[128,8,128]{2,1,0:T(8,128)(2,1)S(1)}, bf16[128,8,128]{2,1,0:T(8,128)(2,1)}, u32[]{:S(2)}) copy-start(bf16[128,8,128]{2,1,0:T(8,128)(2,1)} %param.5) | copy-start | bytes 786436
  0.6 5.0 %copy-start.15 = (s32[128,8]{0,1:T(8,128)S(1)}, s32[128,8]{0,1:T(8,128)}, u32[]{:S(2)}) copy-start(s32[128,8]{0,1:T(8,128)} %param.8) | copy-start | bytes 12292
  0.7 5.0 %copy-start.10 = (bf16[128,4096]{1,0:T(8,128)(2,1)S(1)}, bf16[128,4096]{1,0:T(8,128)(2,1)}, u32[]{:S(2)}) copy-start(bf16[128,4096]{1,0:T(8,128)(2,1)} %param.6) | copy-start | bytes 3145732
  2.6 10.4 %collective-permute-start.7 = (bf16[128,1024]{1,0:T(8,128)(2,1)}, bf16[128,1024]{1,0:T(8,128)(2,1)}, u32[]{:S(2)}, u32[]{:S(2)}) collective-permute-start(bf16[128,1024]{1,0:T(8,128)(2,1)} %get-tuple-element.55), channel_id=1, source_target_pairs={{0,2},{1,3},{2,0},{3,1},{4,6},{5,7},{6,4},{7,5},{8,10},{9,11},{10,... | collective-permute-start | bytes 786440 | tf_op jit(solution)/shard_map/ppermute | solution.py:52
  5.7 0.7 copy-start.16
  7.5 28.5 %collective-permute-start.1 = (bf16[128,2176]{1,0:T(8,128)(2,1)}, bf16[128,2176]{1,0:T(8,128)(2,1)S(1)}, u32[]{:S(2)}, u32[]{:S(2)}) collective-permute-start(bf16[128,2176]{1,0:T(8,128)(2,1)} %get-tuple-element.93), channel_id=1, source_target_pairs={{0,2},{1,3},{2,0},{3,1},{4,6},{5,7},{6,4},{7,5},{8,10},{9,11},{10,... | collective-permute-start | bytes 1671176 | tf_op jit(solution)/shard_map/ppermute | solution.py:52
  7.5 28.5 %collective-permute-start.3 = (bf16[128,2176]{1,0:T(8,128)(2,1)S(1)}, bf16[128,2176]{1,0:T(8,128)(2,1)S(1)}, u32[]{:S(2)}, u32[]{:S(2)}) collective-permute-start(bf16[128,2176]{1,0:T(8,128)(2,1)S(1)} %get-tuple-element.94), channel_id=1, source_target_pairs={{0,16},{1,17},{2,18},{3,19},{4,20},{5,21},{6,22},{7,23},{8,24},{9,... | collective-permute-start | bytes 1671176 | tf_op jit(solution)/shard_map/ppermute | solution.py:52
  9.5 27.0 %collective-permute-start.5 = (bf16[128,2176]{1,0:T(8,128)(2,1)}, bf16[128,2176]{1,0:T(8,128)(2,1)S(1)}, u32[]{:S(2)}, u32[]{:S(2)}) collective-permute-start(bf16[128,2176]{1,0:T(8,128)(2,1)} %get-tuple-element.92), channel_id=1, source_target_pairs={{0,18},{1,19},{2,16},{3,17},{4,22},{5,23},{6,20},{7,21},{8,26},{9,... | collective-permute-start | bytes 1671176 | tf_op jit(solution)/shard_map/ppermute | solution.py:52
  14.0 22.5 %copy-start = (bf16[256,1024]{1,0:T(8,128)(2,1)}, bf16[256,1024]{1,0:T(8,128)(2,1)S(1)}, u32[]{:S(2)}) copy-start(bf16[256,1024]{1,0:T(8,128)(2,1)S(1)} %pad_maximum_fusion.5.refs_8_) | copy-start | bytes 1572868
  14.0 12.3 %collective-permute-start.10 = (bf16[256,1024]{1,0:T(8,128)(2,1)S(1)}, bf16[256,1024]{1,0:T(8,128)(2,1)S(1)}, u32[]{:S(2)}, u32[]{:S(2)}) collective-permute-start(bf16[256,1024]{1,0:T(8,128)(2,1)S(1)} %pad_maximum_fusion.5.refs_8_), channel_id=1, source_target_pairs={{0,4},{1,5},{2,6},{3,7},{4,0},{5,1},{6,2},{7,3},{8,12},{9,13},{10,... | collective-permute-start | bytes 1572872 | tf_op jit(solution)/shard_map/ppermute | solution.py:60
  16.2 11.6 %collective-permute-start.8 = (bf16[256,1024]{1,0:T(8,128)(2,1)S(1)}, bf16[256,1024]{1,0:T(8,128)(2,1)S(1)}, u32[]{:S(2)}, u32[]{:S(2)}) collective-permute-start(bf16[256,1024]{1,0:T(8,128)(2,1)S(1)} %pad_maximum_fusion.5.refs_8_), channel_id=1, source_target_pairs={{4,8},{5,9},{6,10},{7,11},{8,4},{9,5},{10,6},{11,7},{20,24},{21,25... | collective-permute-start | bytes 1572872 | tf_op jit(solution)/shard_map/ppermute | solution.py:60
  26.4 10.2 %copy-start.4 = (bf16[256,1024]{1,0:T(8,128)(2,1)}, bf16[256,1024]{1,0:T(8,128)(2,1)S(1)}, u32[]{:S(2)}) copy-start(bf16[256,1024]{1,0:T(8,128)(2,1)S(1)} %collective-permute-done.10.refs_8_) | copy-start | bytes 1572868
  26.4 10.2 %collective-permute-start.11 = (bf16[256,1024]{1,0:T(8,128)(2,1)S(1)}, bf16[256,1024]{1,0:T(8,128)(2,1)}, u32[]{:S(2)}, u32[]{:S(2)}) collective-permute-start(bf16[256,1024]{1,0:T(8,128)(2,1)S(1)} %collective-permute-done.10.refs_8_), channel_id=1, source_target_pairs={{4,8},{5,9},{6,10},{7,11},{8,4},{9,5},{10,6},{11,7},{20,24},{21,25... | collective-permute-start | bytes 1572872 | tf_op jit(solution)/shard_map/ppermute | solution.py:60
  27.8 9.2 %copy-start.12 = (bf16[256,1024]{1,0:T(8,128)(2,1)}, bf16[256,1024]{1,0:T(8,128)(2,1)S(1)}, u32[]{:S(2)}) copy-start(bf16[256,1024]{1,0:T(8,128)(2,1)S(1)} %collective-permute-done.8) | copy-start | bytes 1572868
  27.8 13.5 %collective-permute-start.9 = (bf16[256,1024]{1,0:T(8,128)(2,1)S(1)}, bf16[256,1024]{1,0:T(8,128)(2,1)S(1)}, u32[]{:S(2)}, u32[]{:S(2)}) collective-permute-start(bf16[256,1024]{1,0:T(8,128)(2,1)S(1)} %collective-permute-done.8), channel_id=1, source_target_pairs={{4,0},{5,1},{6,2},{7,3},{8,12},{9,13},{10,14},{11,15},{20,16},{21,... | collective-permute-start | bytes 1572872 | tf_op jit(solution)/shard_map/ppermute | solution.py:60
  36.0 8.9 %collective-permute-start = (bf16[128,2176]{1,0:T(8,128)(2,1)S(1)}, bf16[128,2176]{1,0:T(8,128)(2,1)S(1)}, u32[]{:S(2)}, u32[]{:S(2)}) collective-permute-start(bf16[128,2176]{1,0:T(8,128)(2,1)S(1)} %fusion.refs_0_), channel_id=1, source_target_pairs={{0,1},{1,0},{2,3},{3,2},{4,5},{5,4},{6,7},{7,6},{8,9},{9,8},{10,11... | collective-permute-start | bytes 1671176 | tf_op jit(solution)/shard_map/ppermute | solution.py:52
  36.0 8.9 %collective-permute-start.2 = (bf16[128,2176]{1,0:T(8,128)(2,1)S(1)}, bf16[128,2176]{1,0:T(8,128)(2,1)S(1)}, u32[]{:S(2)}, u32[]{:S(2)}) collective-permute-start(bf16[128,2176]{1,0:T(8,128)(2,1)S(1)} %collective-permute-done.1.refs_2_), channel_id=1, source_target_pairs={{0,1},{1,0},{2,3},{3,2},{4,5},{5,4},{6,7},{7,6},{8,9},{9,8},{10,11... | collective-permute-start | bytes 1671176 | tf_op jit(solution)/shard_map/ppermute | solution.py:52
  36.5 8.4 %collective-permute-start.4 = (bf16[128,2176]{1,0:T(8,128)(2,1)S(1)}, bf16[128,2176]{1,0:T(8,128)(2,1)}, u32[]{:S(2)}, u32[]{:S(2)}) collective-permute-start(bf16[128,2176]{1,0:T(8,128)(2,1)S(1)} %collective-permute-done.3.refs_4_), channel_id=1, source_target_pairs={{0,1},{1,0},{2,3},{3,2},{4,5},{5,4},{6,7},{7,6},{8,9},{9,8},{10,11... | collective-permute-start | bytes 1671176 | tf_op jit(solution)/shard_map/ppermute | solution.py:52
  36.6 8.3 %collective-permute-start.6 = (bf16[128,2176]{1,0:T(8,128)(2,1)S(1)}, bf16[128,2176]{1,0:T(8,128)(2,1)}, u32[]{:S(2)}, u32[]{:S(2)}) collective-permute-start(bf16[128,2176]{1,0:T(8,128)(2,1)S(1)} %collective-permute-done.5.refs_6_), channel_id=1, source_target_pairs={{0,1},{1,0},{2,3},{3,2},{4,5},{5,4},{6,7},{7,6},{8,9},{9,8},{10,11... | collective-permute-start | bytes 1671176 | tf_op jit(solution)/shard_map/ppermute | solution.py:52
  41.3 0.8 copy-start.13
  42.1 16.2 %collective-permute-start.12 = (bf16[256,1024]{1,0:T(8,128)(2,1)}, bf16[256,1024]{1,0:T(8,128)(2,1)}, u32[]{:S(2)}, u32[]{:S(2)}) collective-permute-start(bf16[256,1024]{1,0:T(8,128)(2,1)} %collective-permute-done.11), channel_id=1, source_target_pairs={{4,0},{5,1},{6,2},{7,3},{8,12},{9,13},{10,14},{11,15},{20,16},{21,... | collective-permute-start | bytes 1572872 | tf_op jit(solution)/shard_map/ppermute | solution.py:60
  51.5 0.7 copy-start.6
  52.2 29.2 %collective-permute-start.14 = (bf16[256,1024]{1,0:T(8,128)(2,1)}, bf16[256,1024]{1,0:T(8,128)(2,1)}, u32[]{:S(2)}, u32[]{:S(2)}) collective-permute-start(bf16[256,1024]{1,0:T(8,128)(2,1)} %get-tuple-element.29), channel_id=1, source_target_pairs={{0,4},{1,5},{2,6},{3,7},{12,8},{13,9},{14,10},{15,11},{16,20},{17,... | collective-permute-start | bytes 1572872 | tf_op jit(solution)/shard_map/ppermute | solution.py:60
  66.0 0.7 copy-start.8
  66.8 23.1 %collective-permute-start.16 = (bf16[256,1024]{1,0:T(8,128)(2,1)}, bf16[256,1024]{1,0:T(8,128)(2,1)}, u32[]{:S(2)}, u32[]{:S(2)}) collective-permute-start(bf16[256,1024]{1,0:T(8,128)(2,1)} %get-tuple-element.30), channel_id=1, source_target_pairs={{0,4},{1,5},{2,6},{3,7},{12,8},{13,9},{14,10},{15,11},{16,20},{17,... | collective-permute-start | bytes 1572872 | tf_op jit(solution)/shard_map/ppermute | solution.py:60
  72.2 2.8 %copy-start.5 = (bf16[256,1024]{1,0:T(8,128)(2,1)S(1)}, bf16[256,1024]{1,0:T(8,128)(2,1)}, u32[]{:S(2)}) copy-start(bf16[256,1024]{1,0:T(8,128)(2,1)} %copy-done.4) | copy-start | bytes 1572868
  81.3 2.3 %copy-start.1 = (bf16[256,1024]{1,0:T(8,128)(2,1)S(1)}, bf16[256,1024]{1,0:T(8,128)(2,1)}, u32[]{:S(2)}) copy-start(bf16[256,1024]{1,0:T(8,128)(2,1)} %copy-done) | copy-start | bytes 1572868
  81.3 15.2 %collective-permute-start.13 = (bf16[256,1024]{1,0:T(8,128)(2,1)S(1)}, bf16[256,1024]{1,0:T(8,128)(2,1)S(1)}, u32[]{:S(2)}, u32[]{:S(2)}) collective-permute-start(bf16[256,1024]{1,0:T(8,128)(2,1)S(1)} %get-tuple-element.28), channel_id=1, source_target_pairs={{0,4},{1,5},{2,6},{3,7},{4,0},{5,1},{6,2},{7,3},{8,12},{9,13},{10,... | collective-permute-start | bytes 1572872 | tf_op jit(solution)/shard_map/ppermute | solution.py:60
  82.8 15.1 %collective-permute-start.15 = (bf16[256,1024]{1,0:T(8,128)(2,1)S(1)}, bf16[256,1024]{1,0:T(8,128)(2,1)S(1)}, u32[]{:S(2)}, u32[]{:S(2)}) collective-permute-start(bf16[256,1024]{1,0:T(8,128)(2,1)S(1)} %add.338), channel_id=1, source_target_pairs={{4,8},{5,9},{6,10},{7,11},{8,4},{9,5},{10,6},{11,7},{20,24},{21,25... | collective-permute-start | bytes 1572872 | tf_op jit(solution)/shard_map/ppermute | solution.py:60
  91.2 1.7 %copy-start.7 = (bf16[8,160,128]{2,1,0:T(8,128)(2,1)S(1)}, bf16[8,160,128]{2,1,0:T(8,128)(2,1)}, u32[]{:S(2)}) copy-start(bf16[8,160,128]{2,1,0:T(8,128)(2,1)} %copy-done.6) | copy-start | bytes 983044
  91.2 1.8 %copy-start.9 = (bf16[8,160,128]{2,1,0:T(8,128)(2,1)S(1)}, bf16[8,160,128]{2,1,0:T(8,128)(2,1)}, u32[]{:S(2)}) copy-start(bf16[8,160,128]{2,1,0:T(8,128)(2,1)} %copy-done.8) | copy-start | bytes 983044
  91.2 18.1 %collective-permute-start.17 = (bf16[256,1024]{1,0:T(8,128)(2,1)S(1)}, bf16[256,1024]{1,0:T(8,128)(2,1)S(1)}, u32[]{:S(2)}, u32[]{:S(2)}) collective-permute-start(bf16[256,1024]{1,0:T(8,128)(2,1)S(1)} %add.340), channel_id=1, source_target_pairs={{4,12},{5,13},{6,14},{7,15},{8,0},{9,1},{10,2},{11,3},{20,28},{21,... | collective-permute-start | bytes 1572872 | tf_op jit(solution)/shard_map/ppermute | solution.py:60
  93.1 7.4 %collective-permute-start.24 = (bf16[640,128]{1,0:T(8,128)(2,1)S(1)}, bf16[640,128]{1,0:T(8,128)(2,1)S(1)}, u32[]{:S(2)}, u32[]{:S(2)}) collective-permute-start(bf16[640,128]{1,0:T(8,128)(2,1)S(1)} %pad_maximum_fusion.13), channel_id=1, source_target_pairs={{0,19},{1,18},{2,17},{3,16},{4,23},{5,22},{6,21},{7,20},{8,27},{9,... | collective-permute-start | bytes 491528 | tf_op jit(solution)/shard_map/ppermute | solution.py:52
  93.7 10.5 %collective-permute-start.23 = (bf16[640,128]{1,0:T(8,128)(2,1)S(1)}, bf16[640,128]{1,0:T(8,128)(2,1)S(1)}, u32[]{:S(2)}, u32[]{:S(2)}) collective-permute-start(bf16[640,128]{1,0:T(8,128)(2,1)S(1)} %pad_maximum_fusion.12), channel_id=1, source_target_pairs={{0,18},{1,19},{2,16},{3,17},{4,22},{5,23},{6,20},{7,21},{8,26},{9,... | collective-permute-start | bytes 491528 | tf_op jit(solution)/shard_map/ppermute | solution.py:52
  96.5 16.4 %collective-permute-start.22 = (bf16[640,128]{1,0:T(8,128)(2,1)}, bf16[640,128]{1,0:T(8,128)(2,1)S(1)}, u32[]{:S(2)}, u32[]{:S(2)}) collective-permute-start(bf16[640,128]{1,0:T(8,128)(2,1)} %pad_maximum_fusion.11), channel_id=1, source_target_pairs={{0,17},{1,16},{2,19},{3,18},{4,21},{5,20},{6,23},{7,22},{8,25},{9,... | collective-permute-start | bytes 491528 | tf_op jit(solution)/shard_map/ppermute | solution.py:52
  97.9 16.5 %collective-permute-start.21 = (bf16[640,128]{1,0:T(8,128)(2,1)S(1)}, bf16[640,128]{1,0:T(8,128)(2,1)S(1)}, u32[]{:S(2)}, u32[]{:S(2)}) collective-permute-start(bf16[640,128]{1,0:T(8,128)(2,1)S(1)} %pad_maximum_fusion.10), channel_id=1, source_target_pairs={{0,16},{1,17},{2,18},{3,19},{4,20},{5,21},{6,22},{7,23},{8,24},{9,... | collective-permute-start | bytes 491528 | tf_op jit(solution)/shard_map/ppermute | solution.py:52
  100.4 15.5 %collective-permute-start.20 = (bf16[640,128]{1,0:T(8,128)(2,1)S(1)}, bf16[640,128]{1,0:T(8,128)(2,1)S(1)}, u32[]{:S(2)}, u32[]{:S(2)}) collective-permute-start(bf16[640,128]{1,0:T(8,128)(2,1)S(1)} %pad_maximum_fusion.9), channel_id=1, source_target_pairs={{0,3},{1,2},{2,1},{3,0},{4,7},{5,6},{6,5},{7,4},{8,11},{9,10},{10,... | collective-permute-start | bytes 491528 | tf_op jit(solution)/shard_map/ppermute | solution.py:52
  104.1 12.2 %collective-permute-start.19 = (bf16[640,128]{1,0:T(8,128)(2,1)S(1)}, bf16[640,128]{1,0:T(8,128)(2,1)S(1)}, u32[]{:S(2)}, u32[]{:S(2)}) collective-permute-start(bf16[640,128]{1,0:T(8,128)(2,1)S(1)} %pad_maximum_fusion.8), channel_id=1, source_target_pairs={{0,2},{1,3},{2,0},{3,1},{4,6},{5,7},{6,4},{7,5},{8,10},{9,11},{10,... | collective-permute-start | bytes 491528 | tf_op jit(solution)/shard_map/ppermute | solution.py:52
  109.4 7.0 %collective-permute-start.18 = (bf16[640,128]{1,0:T(8,128)(2,1)S(1)}, bf16[640,128]{1,0:T(8,128)(2,1)S(1)}, u32[]{:S(2)}, u32[]{:S(2)}) collective-permute-start(bf16[640,128]{1,0:T(8,128)(2,1)S(1)} %pad_maximum_fusion.7), channel_id=1, source_target_pairs={{0,1},{1,0},{2,3},{3,2},{4,5},{5,4},{6,7},{7,6},{8,9},{9,8},{10,11... | collective-permute-start | bytes 491528 | tf_op jit(solution)/shard_map/ppermute | solution.py:52
  110.7 5.7 %copy-start.2 = (s32[1024,1]{1,0:T(8,128)S(1)}, s32[1024,1]{1,0:T(8,128)}, u32[]{:S(2)}) copy-start(s32[1024,1]{1,0:T(8,128)} %convert_element_type.68.place_ref) | copy-start | bytes 12292
  110.7 5.7 %copy-start.3 = (s32[1024,1]{1,0:T(8,128)S(1)}, s32[1024,1]{1,0:T(8,128)}, u32[]{:S(2)}) copy-start(s32[1024,1]{1,0:T(8,128)} %fusion.8.gate_ref) | copy-start | bytes 12292
  112.9 7.8 %collective-permute-start.25 = (bf16[64,1024]{1,0:T(8,128)(2,1)}, bf16[64,1024]{1,0:T(8,128)(2,1)}, u32[]{:S(2)}, u32[]{:S(2)}) collective-permute-start(bf16[64,1024]{1,0:T(8,128)(2,1)} %get-tuple-element.53), channel_id=1, source_target_pairs={{0,2},{1,3},{2,0},{3,1},{4,6},{5,7},{6,4},{7,5},{8,10},{9,11},{10,... | collective-permute-start | bytes 393224 | tf_op jit(solution)/shard_map/ppermute | solution.py:52
  114.4 7.2 %collective-permute-start.26 = (bf16[64,1024]{1,0:T(8,128)(2,1)}, bf16[64,1024]{1,0:T(8,128)(2,1)S(1)}, u32[]{:S(2)}, u32[]{:S(2)}) collective-permute-start(bf16[64,1024]{1,0:T(8,128)(2,1)} %get-tuple-element.52), channel_id=1, source_target_pairs={{0,16},{1,17},{2,18},{3,19},{4,20},{5,21},{6,22},{7,23},{8,24},{9,... | collective-permute-start | bytes 393224 | tf_op jit(solution)/shard_map/ppermute | solution.py:52
  115.9 7.1 %collective-permute-start.27 = (bf16[64,1024]{1,0:T(8,128)(2,1)}, bf16[64,1024]{1,0:T(8,128)(2,1)S(1)}, u32[]{:S(2)}, u32[]{:S(2)}) collective-permute-start(bf16[64,1024]{1,0:T(8,128)(2,1)} %get-tuple-element.51), channel_id=1, source_target_pairs={{0,18},{1,19},{2,16},{3,17},{4,22},{5,23},{6,20},{7,21},{8,26},{9,... | collective-permute-start | bytes 393224 | tf_op jit(solution)/shard_map/ppermute | solution.py:52
  123.0 1.0 copy-start.11

commit v3 on v1

v3 whole, which is shorter than its diff:
```python
import functools

import jax
import jax.numpy as jnp
from jax import lax
from jax.experimental import pallas as pl
from jax.experimental.pallas import tpu as pltpu
from jax.sharding import PartitionSpec as P

soft_cap = 1.5
AXES = ("dp", "expert")
GROUP = 4
LANES = 128


class Plan:
    def __init__(self, mesh, tokens, top, head_dim, features):
        self.dp = mesh.shape["dp"]
        self.experts = mesh.shape["expert"]
        self.rows = GROUP // 2
        self.planes = self.experts // GROUP
        self.splits = self.dp * self.rows
        self.sources = self.splits * 2
        self.tokens, self.top, self.head_dim = tokens, top, head_dim
        self.part = features // self.splits
        cap = 9 * tokens * top // (8 * self.experts)
        self.cap = -(-cap // 8) * 8
        self.back = self.rows * self.cap + 16

    def index(self, x, z, y, c):
        return x * self.experts + z * GROUP + y * 2 + c

    def pairs(self, dx=0, dz=0, dy=0, dc=0):
        out = []
        for x in range(self.dp):
            for z in range(self.planes):
                for y in range(self.rows):
                    for c in range(2):
                        target = self.index(
                            (x + dx) % self.dp,
                            (z + dz) % self.planes,
                            (y + dy) % self.rows,
                            c ^ dc,
                        )
                        out.append((self.index(x, z, y, c), target))
        return out

    def shift(self, value, **by):
        if not any(by.values()):
            return value
        return lax.ppermute(value, AXES, self.pairs(**by))

    def along(self, value, moves):
        out = []
        for x in range(self.dp):
            for a, b in moves:
                for r in range(GROUP):
                    out.append((self.index(x, a, 0, 0) + r, self.index(x, b, 0, 0) + r))
        return lax.ppermute(value, AXES, out)

    def splits_list(self):
        return [(dx, dy) for dx in range(self.dp) for dy in range(self.rows)]


def select_kernel(plan, ids, pack_ref, hot_ref, head_ref, gate_ref):
    tokens, cap, top, head_dim = plan.tokens, plan.cap, plan.top, plan.head_dim
    experts = plan.planes * plan.rows
    row_of = lax.broadcasted_iota(jnp.int32, (cap, tokens), 0)
    before = (
        lax.broadcasted_iota(jnp.int32, (tokens, tokens), 0)
        < lax.broadcasted_iota(jnp.int32, (tokens, tokens), 1)
    ).astype(jnp.bfloat16)
    empty = jnp.zeros((cap, tokens), jnp.bfloat16)

    def pair(q, carry):
        for b in range(2):
            start = pl.multiple_of((2 * q + b) * tokens, tokens)
            meta = pack_ref[pl.ds(start, 2 * top), pl.ds(top * head_dim, LANES)].astype(jnp.float32)
            masks, gate_rows, occupied = [], [], []
            for e in range(experts):
                mask = (meta[top:] == ids[e].astype(jnp.float32)).astype(jnp.float32)
                masks.append(mask)
                gate_rows.append(jnp.sum(mask * meta[:top], axis=0, keepdims=True))
                occupied.append(jnp.sum(mask, axis=0, keepdims=True))
            filled = occupied + [jnp.zeros((1, tokens), jnp.float32)] * (-experts % 16)
            places = jnp.dot(
                jnp.concatenate(filled, axis=0).astype(jnp.bfloat16),
                before,
                preferred_element_type=jnp.float32,
            )
            wide = []
            for e in range(experts):
                place = places[e : e + 1].astype(jnp.int32)
                hot = jnp.where(row_of == place, occupied[e], 0.0)
                gates = jnp.sum(hot * gate_rows[e], axis=1, keepdims=True)
                slot, i = divmod(e, plan.rows)
                at = (2 * i + b) * cap
                hot_ref[slot, q, pl.ds(at, cap), :] = jnp.concatenate(
                    [hot.astype(jnp.bfloat16), empty] if b == 0 else [empty, hot.astype(jnp.bfloat16)],
                    axis=1,
                )
                gate_ref[slot, q, pl.ds(at, cap), :] = jnp.broadcast_to(gates, (cap, LANES)).astype(
                    jnp.bfloat16
                )
                wide.append(
                    jnp.concatenate(
                        [(hot * masks[e][k : k + 1]).astype(jnp.bfloat16) for k in range(top)], axis=1
                    )
                )
            raw = jnp.concatenate(
                [
                    pack_ref[pl.ds(start, tokens), pl.ds(k * head_dim, head_dim)]
                    for k in range(top)
                ],
                axis=0,
            )
            chosen = jnp.dot(
                jnp.concatenate(wide, axis=0), raw, preferred_element_type=jnp.float32
            ).astype(jnp.bfloat16)
            for e in range(experts):
                slot, i = divmod(e, plan.rows)
                head_ref[slot, q, pl.ds((2 * i + b) * cap, cap), :] = chosen[e * cap : (e + 1) * cap]
        return carry

    lax.fori_loop(0, plan.sources // 2, pair, 0)


def select_work(plan, ids, packs):
    rows = plan.rows * 2 * plan.cap
    lead = (plan.planes, plan.sources // 2, rows)
    return pl.pallas_call(
        functools.partial(select_kernel, plan),
        out_shape=(
            jax.ShapeDtypeStruct((*lead, 2 * plan.tokens), jnp.bfloat16),
            jax.ShapeDtypeStruct((*lead, plan.head_dim), jnp.bfloat16),
            jax.ShapeDtypeStruct((*lead, LANES), jnp.bfloat16),
        ),
        in_specs=[
            pl.BlockSpec(memory_space=pltpu.SMEM),
            pl.BlockSpec(memory_space=pltpu.VMEM),
        ],
        out_specs=(pl.BlockSpec(memory_space=pltpu.VMEM),) * 3,
        compiler_params=pltpu.CompilerParams(vmem_limit_bytes=56 * 1024 * 1024),
    )(ids, packs)


def slot_kernel(plan, slot_index, earlier, ids, *refs):
    packs = refs[: plan.sources]
    hot_any, head_any, gate_any, w_ref = refs[plan.sources : plan.sources + 4]
    rest = refs[plan.sources + 4 :]
    earlier_refs, rest = rest[:earlier], rest[earlier:]
    count = plan.sources if earlier else 1
    p_ref, back_refs, (buf, hots, heads, gates, grads, sems) = rest[0], rest[1 : 1 + count], rest[1 + count :]
    tokens, cap, part, head_dim = plan.tokens, plan.cap, plan.part, plan.head_dim
    pair_rows = 2 * cap
    pair_total = plan.sources // 2
    base = (plan.planes - 1) * plan.back if earlier else 0

    def copies(q):
        slot = q % 2
        return [
            pltpu.make_async_copy(
                packs[2 * q + b], buf.at[slot, pl.ds(b * tokens, tokens), :], sems.at[slot, b]
            )
            for b in range(2)
        ]

    chosen = [
        pltpu.make_async_copy(hot_any.at[slot_index], hots, sems.at[2, 0]),
        pltpu.make_async_copy(head_any.at[slot_index], heads, sems.at[2, 1]),
        pltpu.make_async_copy(gate_any.at[slot_index], gates, sems.at[3, 0]),
    ]
    for copy in chosen + copies(0):
        copy.start()
    lines = lax.broadcasted_iota(jnp.int32, (cap, LANES), 0)
    lanes = lax.broadcasted_iota(jnp.int32, (cap, LANES), 1)
    diagonal = (lines == lanes).astype(jnp.float32)
    block_row = lax.broadcasted_iota(jnp.int32, (16, LANES), 0)
    chunk = min(part, 512)
    for copy in chosen:
        copy.wait()
    for q in range(pair_total):
        slot = q % 2
        if q + 1 < pair_total:
            for copy in copies(q + 1):
                copy.start()
        for copy in copies(q):
            copy.wait()
        sums = [jnp.zeros((pair_rows, LANES), jnp.float32) for _ in range(plan.rows)]
        for start in range(0, part, chunk):
            grad = jnp.dot(
                hots[q], buf[slot, :, pl.ds(start, chunk)], preferred_element_type=jnp.float32
            )
            for i in range(plan.rows):
                at = i * pair_rows
                weight = w_ref[
                    pl.ds(pl.multiple_of(ids[plan.rows + i], 128), head_dim), pl.ds(start, chunk)
                ]
                pre = jnp.dot(
                    heads[q, pl.ds(at, pair_rows), :], weight, preferred_element_type=jnp.float32
                )
                gate = gates[q, pl.ds(at, pair_rows), :].astype(jnp.float32)
                for lane in range(0, chunk, LANES):
                    grad_block = grad[at : at + pair_rows, lane : lane + LANES]
                    capped = jnp.tanh(pre[:, lane : lane + LANES] * (1.0 / soft_cap))
                    sums[i] = sums[i] + grad_block * capped
                    grads[i, pl.ds(q * pair_rows, pair_rows), pl.ds(start + lane, LANES)] = (
                        gate * grad_block * (1.0 - capped * capped)
                    ).astype(jnp.bfloat16)
        for b in range(2):
            block = jnp.zeros((16, LANES), jnp.float32)
            for i in range(plan.rows):
                column = jnp.sum(sums[i][b * cap : (b + 1) * cap], axis=1, keepdims=True) * soft_cap
                line = jnp.sum(diagonal * column, axis=0, keepdims=True)
                block = jnp.where(block_row == i, line, block)
            s = 2 * q + b
            at = base + plan.rows * cap
            if earlier:
                back_refs[s][pl.ds(at, 16), :] = block.astype(jnp.bfloat16)
            else:
                back_refs[0][s, pl.ds(at, 16), :] = block.astype(jnp.bfloat16)
    for i in range(plan.rows):
        weight = w_ref[pl.ds(pl.multiple_of(ids[plan.rows + i], 128), head_dim), :]
        grad_all = grads[i]
        head_all = jnp.concatenate(
            [heads[q, pl.ds(i * pair_rows, pair_rows), :] for q in range(pair_total)], axis=0
        )
        p_ref[pl.ds(i * head_dim, head_dim), :] = lax.dot_general(
            head_all, grad_all, (((0,), (0,)), ((), ())), preferred_element_type=jnp.float32
        ).astype(p_ref.dtype)
        rows = lax.dot_general(
            grad_all, weight, (((1,), (1,)), ((), ())), preferred_element_type=jnp.float32
        ).astype(jnp.bfloat16)
        for s in range(plan.sources):
            value = rows[s * cap : (s + 1) * cap]
            if earlier:
                back_refs[s][pl.ds(base + i * cap, cap), :] = value
            else:
                back_refs[0][s, pl.ds(i * cap, cap), :] = value
    for j, ref in enumerate(earlier_refs):
        for s in range(plan.sources):
            back_refs[s][pl.ds(j * plan.back, plan.back), :] = ref[s]


def slot_work(plan, slot_index, ids, packs, selected, weight, kind, earlier=()):
    rows = plan.rows * 2 * plan.cap
    pair_total = plan.sources // 2
    if earlier:
        backs = (
            jax.ShapeDtypeStruct((plan.planes * plan.back, LANES), jnp.bfloat16),
        ) * plan.sources
    else:
        backs = (jax.ShapeDtypeStruct((plan.sources, plan.back, LANES), jnp.bfloat16),)
    vmem = pl.BlockSpec(memory_space=pltpu.VMEM)
    return pl.pallas_call(
        functools.partial(slot_kernel, plan, slot_index, len(earlier)),
        out_shape=(jax.ShapeDtypeStruct((plan.rows * plan.head_dim, plan.part), kind), *backs),
        in_specs=[pl.BlockSpec(memory_space=pltpu.SMEM)]
        + [pl.BlockSpec(memory_space=pl.ANY)] * (plan.sources + 3)
        + [vmem] * (1 + len(earlier)),
        out_specs=(vmem,) * (1 + len(backs)),
        scratch_shapes=[
            pltpu.VMEM((2, 2 * plan.tokens, plan.part), jnp.bfloat16),
            pltpu.VMEM((pair_total, rows, 2 * plan.tokens), jnp.bfloat16),
            pltpu.VMEM((pair_total, rows, plan.head_dim), jnp.bfloat16),
            pltpu.VMEM((pair_total, rows, LANES), jnp.bfloat16),
            pltpu.VMEM((plan.rows, plan.sources * plan.cap, plan.part), jnp.bfloat16),
            pltpu.SemaphoreType.DMA((4, 2)),
        ],
        compiler_params=pltpu.CompilerParams(vmem_limit_bytes=32 * 1024 * 1024),
    )(ids, *packs, *selected, weight, *earlier)


def sum_kernel(plan, starts, own_ref, *refs):
    received = refs[: len(refs) - plan.splits]
    pieces = refs[len(refs) - plan.splits :]
    rows = plan.head_dim // plan.dp
    for j, piece in enumerate(pieces):
        at = pl.ds(pl.multiple_of(starts[j], rows), rows)
        total = own_ref[at, :]
        for ref in received:
            total = total + ref[at, :].astype(jnp.float32)
        piece[...] = total.astype(piece.dtype)


def sum_work(plan, starts, own, received):
    rows = plan.head_dim // plan.dp
    vmem = pl.BlockSpec(memory_space=pltpu.VMEM)
    return pl.pallas_call(
        functools.partial(sum_kernel, plan),
        out_shape=tuple(
            jax.ShapeDtypeStruct((rows, plan.part), jnp.bfloat16 if j else jnp.float32)
            for j in range(plan.splits)
        ),
        in_specs=[pl.BlockSpec(memory_space=pltpu.SMEM)] + [vmem] * (1 + len(received)),
        out_specs=(vmem,) * plan.splits,
    )(starts, own, *received)


def layout_kernel(plan, starts, *refs):
    out_ref = refs[-1]
    for j, piece in enumerate(refs[:-1]):
        at = pl.ds(pl.multiple_of(starts[j], plan.part), plan.part)
        out_ref[:, at] = piece[...].astype(jnp.float32)


def layout_work(plan, starts, pieces):
    rows = plan.head_dim // plan.dp
    vmem = pl.BlockSpec(memory_space=pltpu.VMEM)
    return pl.pallas_call(
        functools.partial(layout_kernel, plan),
        out_shape=jax.ShapeDtypeStruct((rows, plan.part * plan.splits), jnp.float32),
        in_specs=[pl.BlockSpec(memory_space=pltpu.SMEM)] + [vmem] * plan.splits,
        out_specs=vmem,
    )(starts, *pieces)


def final_kernel(plan, target_ref, gate_ref, place_ref, *refs):
    parts = refs[: plan.sources]
    head_ref, out_gate_ref, table = refs[plan.sources :]
    length = plan.planes * plan.back
    for dc in range(2):
        total = None
        for s in range(plan.splits):
            piece = parts[2 * s + dc][...].astype(jnp.float32)
            total = piece if total is None else total + piece
        table[pl.ds(dc * length, length), :] = total.astype(jnp.bfloat16)
    block = 256
    count = plan.tokens * plan.top
    for start in range(0, count, block):
        slot_of = lax.broadcasted_iota(jnp.int32, (block, 2 * length), 1)
        hot = (slot_of == target_ref[pl.ds(start, block), :]).astype(jnp.bfloat16)
        head_ref[pl.ds(start, block), :] = jnp.dot(
            hot, table[...], preferred_element_type=jnp.float32
        ).astype(jnp.bfloat16)
        hot = (slot_of == gate_ref[pl.ds(start, block), :]).astype(jnp.bfloat16)
        lines = jnp.dot(hot, table[...], preferred_element_type=jnp.float32)
        lane_of = lax.broadcasted_iota(jnp.int32, (block, LANES), 1)
        out_gate_ref[pl.ds(start, block), :] = jnp.sum(
            jnp.where(lane_of == place_ref[pl.ds(start, block), :], lines, 0.0),
            axis=1,
            keepdims=True,
        )


def final_work(plan, target, gate_line, place, parts):
    count = plan.tokens * plan.top
    return pl.pallas_call(
        functools.partial(final_kernel, plan),
        out_shape=(
            jax.ShapeDtypeStruct((count, plan.head_dim), jnp.bfloat16),
            jax.ShapeDtypeStruct((count, 1), jnp.float32),
        ),
        in_specs=[pl.BlockSpec(memory_space=pltpu.VMEM)] * (3 + plan.sources),
        out_specs=(
            pl.BlockSpec(memory_space=pltpu.VMEM),
            pl.BlockSpec(memory_space=pltpu.VMEM),
        ),
        scratch_shapes=[pltpu.VMEM((2 * plan.planes * plan.back, LANES), jnp.bfloat16)],
        compiler_params=pltpu.CompilerParams(vmem_limit_bytes=48 * 1024 * 1024),
    )(target, gate_line, place, *parts)


def local(mesh, head_outputs, out_grad, gate_weights, route_ids, out_proj):
    tokens, top, head_dim = head_outputs.shape
    features = out_grad.shape[1]
    plan = Plan(mesh, tokens, top, head_dim, features)
    x = lax.axis_index("dp")
    me = lax.axis_index("expert")
    z, y, c = me // GROUP, (me % GROUP) // 2, me % 2

    weight_parts = []
    for dy in range(plan.rows):
        split = x * plan.rows + (y + dy) % plan.rows
        piece = lax.dynamic_slice_in_dim(out_proj[0], split * plan.part, plan.part, 1)
        weight_parts.append(plan.shift(piece, dy=dy))
    own_weights = jnp.concatenate(weight_parts, axis=0)

    meta = jnp.concatenate(
        [
            gate_weights.T,
            route_ids.T.astype(jnp.bfloat16),
            jnp.zeros((LANES - 2 * top, tokens), jnp.bfloat16),
        ],
        axis=0,
    )
    head_pack = jnp.concatenate([head_outputs.reshape(tokens, top * head_dim), meta], axis=1)

    def grad_part(dx, dy):
        split = ((x + dx) % plan.dp) * plan.rows + (y + dy) % plan.rows
        return lax.dynamic_slice_in_dim(out_grad, split * plan.part, plan.part, 1)

    def plane_gather(piece_of):
        out = []
        for dx, dy in plan.splits_list():
            value = plan.shift(piece_of(dx, dy), dx=dx, dy=dy)
            out += [value, plan.shift(value, dc=1)]
        return out

    head_packs = jnp.concatenate(plane_gather(lambda dx, dy: head_pack), axis=0)
    packs = plane_gather(grad_part)

    if plan.planes == 4:
        inner = (z == 1) | (z == 2)
        mates, middle = [(0, 1), (1, 0), (2, 3), (3, 2)], [(1, 2), (2, 1)]
        outward, inward, across = [(1, 0), (2, 3)], [(0, 1), (3, 2)], [(1, 3), (2, 0)]
        plane_of = jnp.stack([jnp.where(z < 2, 2, 1), jnp.where(z < 2, 3, 0), z ^ 1, z])
        mate = plan.along(own_weights, mates)
        near_in = plan.along(own_weights, middle)
        near_out = plan.along(near_in, outward)
        far_in = plan.along(mate, middle)
        far_out = plan.along(far_in, outward)
        weights = [
            jnp.where(inner, near_in, near_out),
            jnp.where(inner, far_in, far_out),
            mate,
            own_weights,
        ]
    else:
        steps = [k % plan.planes for k in range(1, plan.planes + 1)]
        plane_of = (z + jnp.array(steps, jnp.int32)) % plan.planes
        weights = [plan.shift(own_weights, dz=-k % plan.planes) for k in steps]

    routes = route_ids.reshape(tokens * top)
    hot = (routes[:, None] == jnp.arange(plan.experts, dtype=jnp.int32)[None, :]).astype(jnp.float32)
    per_token = hot.reshape(tokens, top, plan.experts).sum(axis=1)
    earlier = jnp.tril(jnp.ones((tokens, tokens), jnp.float32), -1)
    places = jnp.dot(earlier, per_token)
    place = jnp.sum(
        hot.reshape(tokens, top, plan.experts) * places[:, None, :], axis=2
    ).astype(jnp.int32).reshape(tokens * top)
    slots = jnp.arange(plan.planes, dtype=jnp.int32)
    slot = jnp.sum(
        jnp.where((routes // GROUP)[:, None] == plane_of[None, :], slots[None, :], 0), axis=1
    )
    row = (routes % GROUP) // 2
    side = (routes % 2) ^ c
    base = side * (plan.planes * plan.back) + slot * plan.back
    target = (base + row * plan.cap + place)[:, None]
    gate_line = (base + plan.rows * plan.cap + row)[:, None]
    place = place[:, None]

    rows_at = jnp.arange(plan.rows, dtype=jnp.int32)
    weight_at = ((y - rows_at) % plan.rows) * head_dim
    expert_ids = (plane_of[:, None] * GROUP + rows_at[None, :] * 2 + c).astype(jnp.int32)
    selected = select_work(plan, expert_ids.reshape(-1), head_packs)
    selected, (target, gate_line, place) = lax.optimization_barrier(
        (selected, (target, gate_line, place))
    )
    sums, backs = [], []
    for j in range(plan.planes):
        last = j == plan.planes - 1
        ids = jnp.concatenate([expert_ids[j], weight_at]).astype(jnp.int32)
        if backs:
            ids, _ = lax.optimization_barrier((ids, backs[-1]))
        part, *back = slot_work(
            plan,
            j,
            ids,
            packs,
            selected,
            weights[j],
            jnp.float32 if last else jnp.bfloat16,
            backs if last else (),
        )
        sums.append(part)
        backs = back if last else backs + back

    if plan.planes == 4:
        near_sum = sums[0] + plan.along(sums[0], inward)
        far_sum = sums[1] + plan.along(sums[1], inward)
        received = [
            plan.along(sums[2], mates),
            plan.along(near_sum, middle),
            plan.along(far_sum, across),
        ]
        backs, _ = lax.optimization_barrier((backs, (near_sum, far_sum)))
    else:
        received = [plan.shift(sums[j], dz=steps[j]) for j in range(plan.planes - 1)]
    own_rows = head_dim // plan.dp
    starts = jnp.stack(
        [
            ((y + dy) % plan.rows) * head_dim + ((x + dx) % plan.dp) * own_rows
            for dx, dy in plan.splits_list()
        ]
    ).astype(jnp.int32)
    pieces = sum_work(plan, starts, sums[-1], received)
    target, _ = lax.optimization_barrier((target, pieces[0]))
    pieces = [
        plan.shift(piece, dx=dx, dy=dy) for piece, (dx, dy) in zip(pieces, plan.splits_list())
    ]
    starts = jnp.stack(
        [
            (((x - dx) % plan.dp) * plan.rows + (y - dy) % plan.rows) * plan.part
            for dx, dy in plan.splits_list()
        ]
    ).astype(jnp.int32)
    grad_proj = layout_work(plan, starts, pieces)

    parts = []
    for dx, dy in plan.splits_list():
        for dc in range(2):
            parts.append(
                plan.shift(backs[len(parts)], dx=-dx % plan.dp, dy=-dy % plan.rows, dc=dc)
            )
    grad_head, grad_gate = final_work(plan, target, gate_line, place, parts)
    return (
        grad_head.reshape(tokens, top, head_dim),
        grad_gate.reshape(tokens, top).astype(jnp.bfloat16),
        grad_proj[None],
    )


def solution(mesh):
    return jax.shard_map(
        functools.partial(local, mesh),
        mesh=mesh,
        in_specs=(
            P(("dp", "expert"), None, None),
            P(("dp", "expert"), None),
            P(("dp", "expert"), None),
            P(("dp", "expert"), None),
            P("expert", None, None),
        ),
        out_specs=(
            P(("dp", "expert"), None, None),
            P(("dp", "expert"), None),
            P("expert", "dp", None),
        ),
        check_vma=False,
    )
```

time: 170 us -> 145 us (0.85)
  the two profiles are of different devices: /device:TPU:8 before, /device:TPU:0 now
where the time goes in v3:
time: 145 us; the launch traced here: 143 us
  starting transfers between devices  39.7 us (27%)
  waiting for transfers between devices  37 us (26%)
  Pallas kernels  35.6 us (25%)
  local copies, waits for them, and re-layouts  22.3 us (15%)
  other arithmetic  7.1 us (5%)
    ppermute x25, waiting for transfers between devices, shift(): return lax.ppermute(value, AXES, self.pairs(**by))  21.5 us
    pallas_call x4, Pallas kernels, slot_work(): pl.pallas_call(functools.partial(slot_kernel, plan, slot_index, len(earli...  21.3 us
    ppermute x25, starting transfers between devices, shift(): return lax.ppermute(value, AXES, self.pairs(**by))  20.6 us
    ppermute x10, starting transfers between devices, along(): return lax.ppermute(value, AXES, out)  19.2 us
    unnamed x33, local copies, waits for them, and re-layouts  15.9 us
    ppermute x10, waiting for transfers between devices, along(): return lax.ppermute(value, AXES, out)  15.5 us
    pallas_call x1, Pallas kernels, select_work(): pl.pallas_call(functools.partial(select_kernel, plan), out_shape=(jax.Sha...  7.26 us
  transfers between devices with their start and end apart: 35, of which 11 were waited for; matrix products, arithmetic and copies ran while one was open for 14% of the time, Pallas kernels for 23%

profile of v3, /device:TPU:0, one launch (start us, length us, event | category | flops | bytes accessed | tf_op | source)
XLA Modules:
  0.0 143.0 jit_solution(9613217646437892614)
XLA Ops:
  0.6 0.8 convert_bitcast_fusion
  1.4 1.0 copy.46
  2.4 1.4 %fusion.5 = (bf16[128,1152]{1,0:T(8,128)(2,1)S(1)}, bf16[1024,1152]{1,0:T(8,128)(2,1)}) fusion(bf16[112,128]{1,0:T(8,128)(2,1)S(1)} %broadcast_in_dim.34, bf16[8,128]{1,0:T(8,128)(2,1)S(1)} %convert_bitcast_fusion, bf16[8,128]{1,0:T(8,128)(2,1)} %bitcast.39, bf16[128,1024]{1,0:T(8,128)(2,1)S(1)} %bitcast.36), kind=kLoop, calls=%fused_computation.21 | loop fusion | flops 1179647 | bytes 884736 | tf_op jit(solution)/shard_map/concatenate | solution.py:387
  3.8 2.9 %collective-permute-start.3 = (bf16[128,1152]{1,0:T(8,128)(2,1)S(1)}, bf16[128,1152]{1,0:T(8,128)(2,1)}, u32[]{:S(2)}, u32[]{:S(2)}) collective-permute-start(bf16[128,1152]{1,0:T(8,128)(2,1)S(1)} %get-tuple-element.109), channel_id=1, source_target_pairs={{0,16},{1,17},{2,18},{3,19},{4,20},{5,21},{6,22},{7,23},{8,24},{9,... | collective-permute-start | bytes 884744 | tf_op jit(solution)/shard_map/ppermute | solution.py:51
  6.8 1.5 %collective-permute-start.1 = (bf16[128,1152]{1,0:T(8,128)(2,1)S(1)}, bf16[128,1152]{1,0:T(8,128)(2,1)}, u32[]{:S(2)}, u32[]{:S(2)}) collective-permute-start(bf16[128,1152]{1,0:T(8,128)(2,1)S(1)} %get-tuple-element.109), channel_id=1, source_target_pairs={{0,2},{1,3},{2,0},{3,1},{4,6},{5,7},{6,4},{7,5},{8,10},{9,11},{10,... | collective-permute-start | bytes 884744 | tf_op jit(solution)/shard_map/ppermute | solution.py:51
  8.3 1.8 %dynamic-slice_bitcast_fusion.1 = (bf16[128,1024]{1,0:T(8,128)(2,1)S(1)}, bf16[128,1024]{1,0:T(8,128)(2,1)}) fusion(bf16[1,128,4096]{2,1,0:T(8,128)(2,1)} %param.9, s32[]{:T(128)S(6)} %select_n.210, s32[]{:T(128)S(6)} %select_n.211), kind=kLoop, calls=%fused_computation.26 | loop fusion | bytes 1048584 | tf_op jit(solution)/shard_map/dynamic_slice | solution.py:375
  10.1 2.0 %collective-permute-start.14 = (bf16[128,1024]{1,0:T(8,128)(2,1)}, bf16[128,1024]{1,0:T(8,128)(2,1)}, u32[]{:S(2)}, u32[]{:S(2)}) collective-permute-start(bf16[128,1024]{1,0:T(8,128)(2,1)} %get-tuple-element.102), channel_id=1, source_target_pairs={{0,2},{1,3},{2,0},{3,1},{4,6},{5,7},{6,4},{7,5},{8,10},{9,11},{10,... | collective-permute-start | bytes 786440 | tf_op jit(solution)/shard_map/ppermute | solution.py:51
  13.7 0.8 add_add_fusion
  14.5 2.1 %constant_dynamic-slice_fusion = (bf16[128,1024]{1,0:T(8,128)(2,1)}, bf16[128,1024]{1,0:T(8,128)(2,1)}, bf16[128,1024]{1,0:T(8,128)(2,1)S(1)}, bf16[128,1024]{1,0:T(8,128)(2,1)}) fusion(bf16[128,4096]{1,0:T(8,128)(2,1)} %param.6, s32[]{:T(128)S(6)} %select_n.208, s32[]{:T(128)S(6)} %select_n.206, s32[]{:T(128)S(6)} %select_n.205, s32[]{:T(128)S(6)} %select_n.207), kind=kLoop, calls=%fused_computation.58 | loop fusion | bytes 2097168 | tf_op jit(solution)/shard_map/dynamic_slice | solution.py:391
  16.6 10.7 %collective-permute-done.14 = bf16[128,1024]{1,0:T(8,128)(2,1)} collective-permute-done((bf16[128,1024]{1,0:T(8,128)(2,1)}, bf16[128,1024]{1,0:T(8,128)(2,1)}, u32[]{:S(2)}, u32[]{:S(2)}) %collective-permute-start.14) | collective-permute-done | bytes 262176 | tf_op jit(solution)/shard_map/ppermute | solution.py:51
  27.3 1.0 pad_maximum_fusion.refs_11_
  28.3 1.6 %collective-permute-start.17 = (bf16[256,1024]{1,0:T(8,128)(2,1)S(1)}, bf16[256,1024]{1,0:T(8,128)(2,1)S(1)}, u32[]{:S(2)}, u32[]{:S(2)}) collective-permute-start(bf16[256,1024]{1,0:T(8,128)(2,1)S(1)} %pad_maximum_fusion.refs_11_), channel_id=1, source_target_pairs={{0,4},{1,5},{2,6},{3,7},{4,0},{5,1},{6,2},{7,3},{8,12},{9,13},{10,... | collective-permute-start | bytes 1572872 | tf_op jit(solution)/shard_map/ppermute | solution.py:59
  30.0 0.6 add.278.ids
  30.6 0.8 collective-permute-start.15
  31.5 1.7 %constant_dynamic-update-slice_fusion.6 = bf16[1024,1152]{1,0:T(8,128)(2,1)} fusion(bf16[1024,1152]{1,0:T(8,128)(2,1)} %get-tuple-element.110, bf16[128,1152]{1,0:T(8,128)(2,1)} %collective-permute-done), kind=kLoop, calls=%fused_computation.42 | loop fusion | bytes 589824
  33.2 1.7 %constant_dynamic-update-slice_fusion.5 = bf16[1024,1152]{1,0:T(8,128)(2,1)} fusion(bf16[1024,1152]{1,0:T(8,128)(2,1)} %constant_dynamic-update-slice_fusion.6, bf16[128,1152]{1,0:T(8,128)(2,1)} %collective-permute-done.1), kind=kLoop, calls=%fused_computation.41 | loop fusion | bytes 589824
  34.9 1.5 %collective-permute-start.12 = (bf16[128,1024]{1,0:T(8,128)(2,1)}, bf16[128,1024]{1,0:T(8,128)(2,1)S(1)}, u32[]{:S(2)}, u32[]{:S(2)}) collective-permute-start(bf16[128,1024]{1,0:T(8,128)(2,1)} %get-tuple-element.103), channel_id=1, source_target_pairs={{0,18},{1,19},{2,16},{3,17},{4,22},{5,23},{6,20},{7,21},{8,26},{9,... | collective-permute-start | bytes 786440 | tf_op jit(solution)/shard_map/ppermute | solution.py:51
  36.9 3.9 %collective-permute-done.17.refs_11_ = bf16[256,1024]{1,0:T(8,128)(2,1)S(1)} collective-permute-done((bf16[256,1024]{1,0:T(8,128)(2,1)S(1)}, bf16[256,1024]{1,0:T(8,128)(2,1)S(1)}, u32[]{:S(2)}, u32[]{:S(2)}) %collective-permute-start.17) | collective-permute-done | bytes 524320 | tf_op jit(solution)/shard_map/ppermute | solution.py:59
  40.8 0.7 collective-permute-start.18
  41.5 0.7 constant_dynamic-update-slice_fusion.4
  42.2 1.7 %constant_dynamic-update-slice_fusion.3 = bf16[1024,1152]{1,0:T(8,128)(2,1)} fusion(bf16[1024,1152]{1,0:T(8,128)(2,1)} %constant_dynamic-update-slice_fusion.4, bf16[128,1152]{1,0:T(8,128)(2,1)} %collective-permute-done.3), kind=kLoop, calls=%fused_computation.39 | loop fusion | bytes 589824
  44.0 1.5 %collective-permute-start.8 = (bf16[128,1024]{1,0:T(8,128)(2,1)S(1)}, bf16[128,1024]{1,0:T(8,128)(2,1)S(1)}, u32[]{:S(2)}, u32[]{:S(2)}) collective-permute-start(bf16[128,1024]{1,0:T(8,128)(2,1)S(1)} %copy-done.8), channel_id=1, source_target_pairs={{0,2},{1,3},{2,0},{3,1},{4,6},{5,7},{6,4},{7,5},{8,10},{9,11},{10,... | collective-permute-start | bytes 786440 | tf_op jit(solution)/shard_map/ppermute | solution.py:51
  45.5 1.3 collective-permute-start.16
  46.8 0.7 constant_dynamic-update-slice_fusion.2
  47.5 1.0 collective-permute-start.10
  48.5 1.3 collective-permute-start.19
  49.8 1.7 %constant_dynamic-update-slice_fusion.1 = bf16[1024,1152]{1,0:T(8,128)(2,1)} fusion(bf16[1024,1152]{1,0:T(8,128)(2,1)} %constant_dynamic-update-slice_fusion.2, bf16[128,1152]{1,0:T(8,128)(2,1)} %copy-done.6), kind=kLoop, calls=%fused_computation.37 | loop fusion | bytes 589824
  51.5 0.8 constant_dynamic-update-slice_fusion.pack_ref
  52.2 7.3 %shard_map.76 = (bf16[4,4,288,256]{3,2,1,0:T(8,128)(2,1)}, bf16[4,4,288,128]{3,2,1,0:T(8,128)(2,1)}, bf16[4,4,288,128]{3,2,1,0:T(8,128)(2,1)}) custom-call(s32[8]{0:T(128)} %add.278.ids, bf16[1024,1152]{1,0:T(8,128)(2,1)} %constant_dynamic-update-slice_fusion.pack_ref), custom_call_target="tpu_custom_call" | custom-call | tf_op jit(solution)/shard_map/pallas_call | solution.py:131
  59.5 0.5 collective-permute-start.13
  60.1 2.5 %collective-permute-done.16 = bf16[256,1024]{1,0:T(8,128)(2,1)S(1)} collective-permute-done((bf16[256,1024]{1,0:T(8,128)(2,1)S(1)}, bf16[256,1024]{1,0:T(8,128)(2,1)S(1)}, u32[]{:S(2)}, u32[]{:S(2)}) %collective-permute-start.16) | collective-permute-done | bytes 524320 | tf_op jit(solution)/shard_map/ppermute | solution.py:59
  62.7 1.4 %collective-permute-done.11.refs_5_ = bf16[128,1024]{1,0:T(8,128)(2,1)S(1)} collective-permute-done((bf16[128,1024]{1,0:T(8,128)(2,1)S(1)}, bf16[128,1024]{1,0:T(8,128)(2,1)S(1)}, u32[]{:S(2)}, u32[]{:S(2)}) %collective-permute-start.11) | collective-permute-done | bytes 262176 | tf_op jit(solution)/shard_map/ppermute | solution.py:51
  64.2 1.7 %copy-done = bf16[4,4,288,256]{3,2,1,0:T(8,128)(2,1)S(1)} copy-done((bf16[4,4,288,256]{3,2,1,0:T(8,128)(2,1)S(1)}, bf16[4,4,288,256]{3,2,1,0:T(8,128)(2,1)}, u32[]{:S(2)}) %copy-start) | copy-done | bytes 2359320
  65.9 1.3 copy-done.2
  67.1 5.1 %shard_map.77 = (bf16[256,1024]{1,0:T(8,128)(2,1)S(1)}, bf16[8,160,128]{2,1,0:T(8,128)(2,1)S(1)}) custom-call(s32[4]{0:T(128)S(1)} %get-tuple-element.115.ids, bf16[128,1024]{1,0:T(8,128)(2,1)S(1)} %get-tuple-element.105.refs_0_, bf16[128,1024]{1,0:T(8,128)(2,1)S(1)} %collective-permute-done.7.refs_1_, bf16[128,1024]{1,0:T(8,128)(2,1)S(1)} %collective-permute-done.8.refs_2_, ...), custom_call_target="tpu_custom_call" | custom-call | tf_op jit(solution)/shard_map/pallas_call | solution.py:255
  72.3 9.1 %collective-permute-start.21 = (bf16[256,1024]{1,0:T(8,128)(2,1)S(1)}, bf16[256,1024]{1,0:T(8,128)(2,1)S(1)}, u32[]{:S(2)}, u32[]{:S(2)}) collective-permute-start(bf16[256,1024]{1,0:T(8,128)(2,1)S(1)} %get-tuple-element.60), channel_id=1, source_target_pairs={{0,4},{1,5},{2,6},{3,7},{12,8},{13,9},{14,10},{15,11},{16,20},{17,... | collective-permute-start | bytes 1572872 | tf_op jit(solution)/shard_map/ppermute | solution.py:59
  81.4 5.1 %shard_map.78 = (bf16[256,1024]{1,0:T(8,128)(2,1)S(1)}, bf16[8,160,128]{2,1,0:T(8,128)(2,1)S(1)}) custom-call(s32[4]{0:T(128)S(1)} %get-tuple-element.53.ids, bf16[128,1024]{1,0:T(8,128)(2,1)S(1)} %get-tuple-element.105.refs_0_, bf16[128,1024]{1,0:T(8,128)(2,1)S(1)} %collective-permute-done.7.refs_1_, bf16[128,1024]{1,0:T(8,128)(2,1)S(1)} %collective-permute-done.8.refs_2_, ...), custom_call_target="tpu_custom_call" | custom-call | tf_op jit(solution)/shard_map/pallas_call | solution.py:255
  86.6 1.3 collective-permute-start.23
  87.9 5.1 %shard_map.79 = (bf16[256,1024]{1,0:T(8,128)(2,1)S(1)}, bf16[8,160,128]{2,1,0:T(8,128)(2,1)S(1)}) custom-call(s32[4]{0:T(128)S(1)} %get-tuple-element.55.ids, bf16[128,1024]{1,0:T(8,128)(2,1)S(1)} %get-tuple-element.105.refs_0_, bf16[128,1024]{1,0:T(8,128)(2,1)S(1)} %collective-permute-done.7.refs_1_, bf16[128,1024]{1,0:T(8,128)(2,1)S(1)} %collective-permute-done.8.refs_2_, ...), custom_call_target="tpu_custom_call" | custom-call | tf_op jit(solution)/shard_map/pallas_call | solution.py:255
  93.4 1.0 add.313
  94.4 1.5 %collective-permute-start.22 = (bf16[256,1024]{1,0:T(8,128)(2,1)}, bf16[256,1024]{1,0:T(8,128)(2,1)}, u32[]{:S(2)}, u32[]{:S(2)}) collective-permute-start(bf16[256,1024]{1,0:T(8,128)(2,1)} %add.313), channel_id=1, source_target_pairs={{4,8},{5,9},{6,10},{7,11},{8,4},{9,5},{10,6},{11,7},{20,24},{21,25... | collective-permute-start | bytes 1572872 | tf_op jit(solution)/shard_map/ppermute | solution.py:59
  95.9 8.7 %collective-permute-done.23 = bf16[256,1024]{1,0:T(8,128)(2,1)S(1)} collective-permute-done((bf16[256,1024]{1,0:T(8,128)(2,1)S(1)}, bf16[256,1024]{1,0:T(8,128)(2,1)S(1)}, u32[]{:S(2)}, u32[]{:S(2)}) %collective-permute-start.23) | collective-permute-done | bytes 524320 | tf_op jit(solution)/shard_map/ppermute | solution.py:59
  104.9 1.5 %collective-permute-start.24 = (bf16[256,1024]{1,0:T(8,128)(2,1)S(1)}, bf16[256,1024]{1,0:T(8,128)(2,1)}, u32[]{:S(2)}, u32[]{:S(2)}) collective-permute-start(bf16[256,1024]{1,0:T(8,128)(2,1)S(1)} %add.314), channel_id=1, source_target_pairs={{4,12},{5,13},{6,14},{7,15},{8,0},{9,1},{10,2},{11,3},{20,28},{21,... | collective-permute-start | bytes 1572872 | tf_op jit(solution)/shard_map/ppermute | solution.py:59
  106.4 5.9 %shard_map.80 = (f32[256,1024]{1,0:T(8,128)S(1)}, bf16[640,128]{1,0:T(8,128)(2,1)S(1)}, bf16[640,128]{1,0:T(8,128)(2,1)}, bf16[640,128]{1,0:T(8,128)(2,1)}, bf16...) custom-call(s32[4]{0:T(128)S(1)} %get-tuple-element.57.ids, ...), custom_call_target="tpu_custom_call" | custom-call | tf_op jit(solution)/shard_map/pallas_call | solution.py:255
  112.3 1.0 copy-done.3
  113.2 0.7 copy-done.4
  113.9 0.7 copy-done.5
  114.6 1.5 %collective-permute-start.26 = (bf16[640,128]{1,0:T(8,128)(2,1)}, bf16[640,128]{1,0:T(8,128)(2,1)S(1)}, u32[]{:S(2)}, u32[]{:S(2)}) collective-permute-start(bf16[640,128]{1,0:T(8,128)(2,1)} %get-tuple-element.76), channel_id=1, source_target_pairs={{0,2},{1,3},{2,0},{3,1},{4,6},{5,7},{6,4},{7,5},{8,10},{9,11},{10,... | collective-permute-start | bytes 491528 | tf_op jit(solution)/shard_map/ppermute | solution.py:51
  116.4 1.4 collective-permute-start.28
  118.1 3.7 %collective-permute-done.26.refs_2_ = bf16[640,128]{1,0:T(8,128)(2,1)S(1)} collective-permute-done((bf16[640,128]{1,0:T(8,128)(2,1)}, bf16[640,128]{1,0:T(8,128)(2,1)S(1)}, u32[]{:S(2)}, u32[]{:S(2)}) %collective-permute-start.26) | collective-permute-done | bytes 163872 | tf_op jit(solution)/shard_map/ppermute | solution.py:51
  121.8 1.9 %collective-permute-start.30 = (bf16[640,128]{1,0:T(8,128)(2,1)S(1)}, bf16[640,128]{1,0:T(8,128)(2,1)S(1)}, u32[]{:S(2)}, u32[]{:S(2)}) collective-permute-start(bf16[640,128]{1,0:T(8,128)(2,1)S(1)} %get-tuple-element.80), channel_id=1, source_target_pairs={{0,18},{1,19},{2,16},{3,17},{4,22},{5,23},{6,20},{7,21},{8,26},{9,... | collective-permute-start | bytes 491528 | tf_op jit(solution)/shard_map/ppermute | solution.py:51
  123.7 0.6 pad_add_fusion.1.starts
  124.4 0.6 pad_add_fusion.6.starts
  125.2 2.7 %shard_map.81 = (f32[64,1024]{1,0:T(8,128)}, bf16[64,1024]{1,0:T(8,128)(2,1)}, bf16[64,1024]{1,0:T(8,128)(2,1)}, bf16[64,1024]{1,0:T(8,128)(2,1)}) custom-call(s32[4]{0:T(128)} %pad_add_fusion.1.starts, f32[256,1024]{1,0:T(8,128)} %copy-done.3, bf16[256,1024]{1,0:T(8,128)(2,1)} %collective-permute-done.20.refs_0_, ...), custom_call_target="tpu_custom_call" | custom-call | tf_op jit(solution)/shard_map/pallas_call | solution.py:289
  127.9 1.3 collective-permute-start.32
  129.2 1.0 collective-permute-start.33
  130.1 1.2 collective-permute-start.34
  131.7 2.3 %collective-permute-done.31.refs_7_ = bf16[640,128]{1,0:T(8,128)(2,1)S(1)} collective-permute-done((bf16[640,128]{1,0:T(8,128)(2,1)S(1)}, bf16[640,128]{1,0:T(8,128)(2,1)S(1)}, u32[]{:S(2)}, u32[]{:S(2)}) %collective-permute-start.31) | collective-permute-done | bytes 163872 | tf_op jit(solution)/shard_map/ppermute | solution.py:51
  134.0 2.2 %shard_map.82 = (bf16[1024,128]{1,0:T(8,128)(2,1)}, f32[1024,1]{1,0:T(8,128)S(1)}) custom-call(s32[1024,1]{1,0:T(8,128)S(1)} %get-tuple-element.63.target_ref, s32[1024,1]{1,0:T(8,128)S(1)} %get-tuple-element.64.gate_ref, s32[1024,1]{1,0:T(8,128)S(1)} %copy.42.place_ref, bf16[640,128]{1,0:T(8,128)(2,1)S(1)} %get-tuple-element.74.refs_0_, ...), custom_call_target="tpu_custom_call" | custom-call | tf_op jit(solution)/shard_map/pallas_call | solution.py:348
  136.5 0.7 copy.43
  137.2 0.7 collective-permute-done.32.refs_1_
  137.9 2.3 %collective-permute-done.34.refs_3_ = bf16[64,1024]{1,0:T(8,128)(2,1)S(1)} collective-permute-done((bf16[64,1024]{1,0:T(8,128)(2,1)}, bf16[64,1024]{1,0:T(8,128)(2,1)S(1)}, u32[]{:S(2)}, u32[]{:S(2)}) %collective-permute-start.34) | collective-permute-done | bytes 131104 | tf_op jit(solution)/shard_map/ppermute | solution.py:51
  140.2 0.6 copy-done.10
  140.8 2.2 %shard_map.83 = f32[64,4096]{1,0:T(8,128)} custom-call(s32[4]{0:T(128)} %pad_add_fusion.6.starts, f32[64,1024]{1,0:T(8,128)} %get-tuple-element.62.refs_0_, bf16[64,1024]{1,0:T(8,128)(2,1)} %copy-done.9, bf16[64,1024]{1,0:T(8,128)(2,1)} %collective-permute-done.33.refs_2_, bf16[64,1024]{1,0:T(8,128)(2,1)} %copy-done.10), custom_call_target="tpu_custom_call" | custom-call | tf_op jit(solution)/shard_map/pallas_call | solution.py:310
  (85 shorter events, 4.5 us)
Async XLA Ops:
  0.6 11.4 %copy-start.11 = (s32[128,8]{0,1:T(8,128)S(1)}, s32[128,8]{0,1:T(8,128)}, u32[]{:S(2)}) copy-start(s32[128,8]{0,1:T(8,128)} %param.8) | copy-start | bytes 12292
  3.8 31.1 %collective-permute-start.3 = (bf16[128,1152]{1,0:T(8,128)(2,1)S(1)}, bf16[128,1152]{1,0:T(8,128)(2,1)}, u32[]{:S(2)}, u32[]{:S(2)}) collective-permute-start(bf16[128,1152]{1,0:T(8,128)(2,1)S(1)} %get-tuple-element.109), channel_id=1, source_target_pairs={{0,16},{1,17},{2,18},{3,19},{4,20},{5,21},{6,22},{7,23},{8,24},{9,... | collective-permute-start | bytes 884744 | tf_op jit(solution)/shard_map/ppermute | solution.py:51
  6.8 23.8 %collective-permute-start.1 = (bf16[128,1152]{1,0:T(8,128)(2,1)S(1)}, bf16[128,1152]{1,0:T(8,128)(2,1)}, u32[]{:S(2)}, u32[]{:S(2)}) collective-permute-start(bf16[128,1152]{1,0:T(8,128)(2,1)S(1)} %get-tuple-element.109), channel_id=1, source_target_pairs={{0,2},{1,3},{2,0},{3,1},{4,6},{5,7},{6,4},{7,5},{8,10},{9,11},{10,... | collective-permute-start | bytes 884744 | tf_op jit(solution)/shard_map/ppermute | solution.py:51
  8.3 23.1 %collective-permute-start = (bf16[128,1152]{1,0:T(8,128)(2,1)S(1)}, bf16[128,1152]{1,0:T(8,128)(2,1)}, u32[]{:S(2)}, u32[]{:S(2)}) collective-permute-start(bf16[128,1152]{1,0:T(8,128)(2,1)S(1)} %get-tuple-element.109), channel_id=1, source_target_pairs={{0,1},{1,0},{2,3},{3,2},{4,5},{5,4},{6,7},{7,6},{8,9},{9,8},{10,11... | collective-permute-start | bytes 884744 | tf_op jit(solution)/shard_map/ppermute | solution.py:51
  8.3 28.1 %collective-permute-start.5 = (bf16[128,1152]{1,0:T(8,128)(2,1)S(1)}, bf16[128,1152]{1,0:T(8,128)(2,1)S(1)}, u32[]{:S(2)}, u32[]{:S(2)}) collective-permute-start(bf16[128,1152]{1,0:T(8,128)(2,1)S(1)} %get-tuple-element.109), channel_id=1, source_target_pairs={{0,18},{1,19},{2,16},{3,17},{4,22},{5,23},{6,20},{7,21},{8,26},{9,... | collective-permute-start | bytes 884744 | tf_op jit(solution)/shard_map/ppermute | solution.py:51
  10.1 17.2 %collective-permute-start.14 = (bf16[128,1024]{1,0:T(8,128)(2,1)}, bf16[128,1024]{1,0:T(8,128)(2,1)}, u32[]{:S(2)}, u32[]{:S(2)}) collective-permute-start(bf16[128,1024]{1,0:T(8,128)(2,1)} %get-tuple-element.102), channel_id=1, source_target_pairs={{0,2},{1,3},{2,0},{3,1},{4,6},{5,7},{6,4},{7,5},{8,10},{9,11},{10,... | collective-permute-start | bytes 786440 | tf_op jit(solution)/shard_map/ppermute | solution.py:51
  28.3 12.5 %collective-permute-start.17 = (bf16[256,1024]{1,0:T(8,128)(2,1)S(1)}, bf16[256,1024]{1,0:T(8,128)(2,1)S(1)}, u32[]{:S(2)}, u32[]{:S(2)}) collective-permute-start(bf16[256,1024]{1,0:T(8,128)(2,1)S(1)} %pad_maximum_fusion.refs_11_), channel_id=1, source_target_pairs={{0,4},{1,5},{2,6},{3,7},{4,0},{5,1},{6,2},{7,3},{8,12},{9,13},{10,... | collective-permute-start | bytes 1572872 | tf_op jit(solution)/shard_map/ppermute | solution.py:59
  30.6 13.4 %copy-start.8 = (bf16[128,1024]{1,0:T(8,128)(2,1)S(1)}, bf16[128,1024]{1,0:T(8,128)(2,1)}, u32[]{:S(2)}) copy-start(bf16[128,1024]{1,0:T(8,128)(2,1)} %get-tuple-element.104) | copy-start | bytes 786436
  30.6 16.9 %copy-start.7 = (bf16[128,1024]{1,0:T(8,128)(2,1)S(1)}, bf16[128,1024]{1,0:T(8,128)(2,1)}, u32[]{:S(2)}) copy-start(bf16[128,1024]{1,0:T(8,128)(2,1)} %get-tuple-element.106) | copy-start | bytes 786436
  30.6 14.9 %collective-permute-start.15 = (bf16[256,1024]{1,0:T(8,128)(2,1)S(1)}, bf16[256,1024]{1,0:T(8,128)(2,1)S(1)}, u32[]{:S(2)}, u32[]{:S(2)}) collective-permute-start(bf16[256,1024]{1,0:T(8,128)(2,1)S(1)} %pad_maximum_fusion.refs_11_), channel_id=1, source_target_pairs={{4,8},{5,9},{6,10},{7,11},{8,4},{9,5},{10,6},{11,7},{20,24},{21,25... | collective-permute-start | bytes 1572872 | tf_op jit(solution)/shard_map/ppermute | solution.py:59
  31.4 5.2 %collective-permute-start.2 = (bf16[128,1152]{1,0:T(8,128)(2,1)}, bf16[128,1152]{1,0:T(8,128)(2,1)S(1)}, u32[]{:S(2)}, u32[]{:S(2)}) collective-permute-start(bf16[128,1152]{1,0:T(8,128)(2,1)} %collective-permute-done.1), channel_id=1, source_target_pairs={{0,1},{1,0},{2,3},{3,2},{4,5},{5,4},{6,7},{7,6},{8,9},{9,8},{10,11... | collective-permute-start | bytes 884744 | tf_op jit(solution)/shard_map/ppermute | solution.py:51
  34.9 24.6 %collective-permute-start.12 = (bf16[128,1024]{1,0:T(8,128)(2,1)}, bf16[128,1024]{1,0:T(8,128)(2,1)S(1)}, u32[]{:S(2)}, u32[]{:S(2)}) collective-permute-start(bf16[128,1024]{1,0:T(8,128)(2,1)} %get-tuple-element.103), channel_id=1, source_target_pairs={{0,18},{1,19},{2,16},{3,17},{4,22},{5,23},{6,20},{7,21},{8,26},{9,... | collective-permute-start | bytes 786440 | tf_op jit(solution)/shard_map/ppermute | solution.py:51
  36.4 12.1 %copy-start.6 = (bf16[128,1152]{1,0:T(8,128)(2,1)}, bf16[128,1152]{1,0:T(8,128)(2,1)S(1)}, u32[]{:S(2)}) copy-start(bf16[128,1152]{1,0:T(8,128)(2,1)S(1)} %collective-permute-done.5) | copy-start | bytes 884740
  36.4 7.6 %collective-permute-start.4 = (bf16[128,1152]{1,0:T(8,128)(2,1)}, bf16[128,1152]{1,0:T(8,128)(2,1)S(1)}, u32[]{:S(2)}, u32[]{:S(2)}) collective-permute-start(bf16[128,1152]{1,0:T(8,128)(2,1)} %collective-permute-done.3), channel_id=1, source_target_pairs={{0,1},{1,0},{2,3},{3,2},{4,5},{5,4},{6,7},{7,6},{8,9},{9,8},{10,11... | collective-permute-start | bytes 884744 | tf_op jit(solution)/shard_map/ppermute | solution.py:51
  36.6 10.9 %collective-permute-start.6 = (bf16[128,1152]{1,0:T(8,128)(2,1)S(1)}, bf16[128,1152]{1,0:T(8,128)(2,1)S(1)}, u32[]{:S(2)}, u32[]{:S(2)}) collective-permute-start(bf16[128,1152]{1,0:T(8,128)(2,1)S(1)} %collective-permute-done.5), channel_id=1, source_target_pairs={{0,1},{1,0},{2,3},{3,2},{4,5},{5,4},{6,7},{7,6},{8,9},{9,8},{10,11... | collective-permute-start | bytes 884744 | tf_op jit(solution)/shard_map/ppermute | solution.py:51
  40.8 7.7 %collective-permute-start.18 = (bf16[256,1024]{1,0:T(8,128)(2,1)S(1)}, bf16[256,1024]{1,0:T(8,128)(2,1)S(1)}, u32[]{:S(2)}, u32[]{:S(2)}) collective-permute-start(bf16[256,1024]{1,0:T(8,128)(2,1)S(1)} %collective-permute-done.17.refs_11_), channel_id=1, source_target_pairs={{4,8},{5,9},{6,10},{7,11},{8,4},{9,5},{10,6},{11,7},{20,24},{21,25... | collective-permute-start | bytes 1572872 | tf_op jit(solution)/shard_map/ppermute | solution.py:59
  44.0 15.6 %collective-permute-start.8 = (bf16[128,1024]{1,0:T(8,128)(2,1)S(1)}, bf16[128,1024]{1,0:T(8,128)(2,1)S(1)}, u32[]{:S(2)}, u32[]{:S(2)}) collective-permute-start(bf16[128,1024]{1,0:T(8,128)(2,1)S(1)} %copy-done.8), channel_id=1, source_target_pairs={{0,2},{1,3},{2,0},{3,1},{4,6},{5,7},{6,4},{7,5},{8,10},{9,11},{10,... | collective-permute-start | bytes 786440 | tf_op jit(solution)/shard_map/ppermute | solution.py:51
  45.5 17.2 %collective-permute-start.16 = (bf16[256,1024]{1,0:T(8,128)(2,1)S(1)}, bf16[256,1024]{1,0:T(8,128)(2,1)S(1)}, u32[]{:S(2)}, u32[]{:S(2)}) collective-permute-start(bf16[256,1024]{1,0:T(8,128)(2,1)S(1)} %collective-permute-done.15), channel_id=1, source_target_pairs={{4,0},{5,1},{6,2},{7,3},{8,12},{9,13},{10,14},{11,15},{20,16},{21,... | collective-permute-start | bytes 1572872 | tf_op jit(solution)/shard_map/ppermute | solution.py:59
  47.5 12.5 %collective-permute-start.10 = (bf16[128,1024]{1,0:T(8,128)(2,1)S(1)}, bf16[128,1024]{1,0:T(8,128)(2,1)S(1)}, u32[]{:S(2)}, u32[]{:S(2)}) collective-permute-start(bf16[128,1024]{1,0:T(8,128)(2,1)S(1)} %copy-done.7), channel_id=1, source_target_pairs={{0,16},{1,17},{2,18},{3,19},{4,20},{5,21},{6,22},{7,23},{8,24},{9,... | collective-permute-start | bytes 786440 | tf_op jit(solution)/shard_map/ppermute | solution.py:51
  48.5 32.9 %collective-permute-start.19 = (bf16[256,1024]{1,0:T(8,128)(2,1)S(1)}, bf16[256,1024]{1,0:T(8,128)(2,1)S(1)}, u32[]{:S(2)}, u32[]{:S(2)}) collective-permute-start(bf16[256,1024]{1,0:T(8,128)(2,1)S(1)} %collective-permute-done.18), channel_id=1, source_target_pairs={{4,0},{5,1},{6,2},{7,3},{8,12},{9,13},{10,14},{11,15},{20,16},{21,... | collective-permute-start | bytes 1572872 | tf_op jit(solution)/shard_map/ppermute | solution.py:59
  59.5 4.7 %copy-start.1 = (bf16[4,4,288,128]{3,2,1,0:T(8,128)(2,1)S(1)}, bf16[4,4,288,128]{3,2,1,0:T(8,128)(2,1)}, u32[]{:S(2)}) copy-start(bf16[4,4,288,128]{3,2,1,0:T(8,128)(2,1)} %get-tuple-element.50.refs_9_) | copy-start | bytes 3538948
  59.5 3.2 %collective-permute-start.7 = (bf16[128,1024]{1,0:T(8,128)(2,1)S(1)}, bf16[128,1024]{1,0:T(8,128)(2,1)S(1)}, u32[]{:S(2)}, u32[]{:S(2)}) collective-permute-start(bf16[128,1024]{1,0:T(8,128)(2,1)S(1)} %get-tuple-element.105.refs_0_), channel_id=1, source_target_pairs={{0,1},{1,0},{2,3},{3,2},{4,5},{5,4},{6,7},{7,6},{8,9},{9,8},{10,11... | collective-permute-start | bytes 786440 | tf_op jit(solution)/shard_map/ppermute | solution.py:51
  59.5 3.2 %collective-permute-start.13 = (bf16[128,1024]{1,0:T(8,128)(2,1)S(1)}, bf16[128,1024]{1,0:T(8,128)(2,1)S(1)}, u32[]{:S(2)}, u32[]{:S(2)}) collective-permute-start(bf16[128,1024]{1,0:T(8,128)(2,1)S(1)} %collective-permute-done.12.refs_6_), channel_id=1, source_target_pairs={{0,1},{1,0},{2,3},{3,2},{4,5},{5,4},{6,7},{7,6},{8,9},{9,8},{10,11... | collective-permute-start | bytes 786440 | tf_op jit(solution)/shard_map/ppermute | solution.py:51
  60.0 2.7 %collective-permute-start.9 = (bf16[128,1024]{1,0:T(8,128)(2,1)S(1)}, bf16[128,1024]{1,0:T(8,128)(2,1)S(1)}, u32[]{:S(2)}, u32[]{:S(2)}) collective-permute-start(bf16[128,1024]{1,0:T(8,128)(2,1)S(1)} %collective-permute-done.8.refs_2_), channel_id=1, source_target_pairs={{0,1},{1,0},{2,3},{3,2},{4,5},{5,4},{6,7},{7,6},{8,9},{9,8},{10,11... | collective-permute-start | bytes 786440 | tf_op jit(solution)/shard_map/ppermute | solution.py:51
  62.6 1.5 %collective-permute-start.11 = (bf16[128,1024]{1,0:T(8,128)(2,1)S(1)}, bf16[128,1024]{1,0:T(8,128)(2,1)S(1)}, u32[]{:S(2)}, u32[]{:S(2)}) collective-permute-start(bf16[128,1024]{1,0:T(8,128)(2,1)S(1)} %collective-permute-done.10.refs_4_), channel_id=1, source_target_pairs={{0,1},{1,0},{2,3},{3,2},{4,5},{5,4},{6,7},{7,6},{8,9},{9,8},{10,11... | collective-permute-start | bytes 786440 | tf_op jit(solution)/shard_map/ppermute | solution.py:51
  64.2 1.7 %copy-start = (bf16[4,4,288,256]{3,2,1,0:T(8,128)(2,1)S(1)}, bf16[4,4,288,256]{3,2,1,0:T(8,128)(2,1)}, u32[]{:S(2)}) copy-start(bf16[4,4,288,256]{3,2,1,0:T(8,128)(2,1)} %get-tuple-element.49.refs_8_) | copy-start | bytes 7077892
  65.9 1.3 copy-start.2
  72.3 21.2 %collective-permute-start.21 = (bf16[256,1024]{1,0:T(8,128)(2,1)S(1)}, bf16[256,1024]{1,0:T(8,128)(2,1)S(1)}, u32[]{:S(2)}, u32[]{:S(2)}) collective-permute-start(bf16[256,1024]{1,0:T(8,128)(2,1)S(1)} %get-tuple-element.60), channel_id=1, source_target_pairs={{0,4},{1,5},{2,6},{3,7},{12,8},{13,9},{14,10},{15,11},{16,20},{17,... | collective-permute-start | bytes 1572872 | tf_op jit(solution)/shard_map/ppermute | solution.py:59
  86.6 18.1 %collective-permute-start.23 = (bf16[256,1024]{1,0:T(8,128)(2,1)S(1)}, bf16[256,1024]{1,0:T(8,128)(2,1)S(1)}, u32[]{:S(2)}, u32[]{:S(2)}) collective-permute-start(bf16[256,1024]{1,0:T(8,128)(2,1)S(1)} %get-tuple-element.61), channel_id=1, source_target_pairs={{0,4},{1,5},{2,6},{3,7},{12,8},{13,9},{14,10},{15,11},{16,20},{17,... | collective-permute-start | bytes 1572872 | tf_op jit(solution)/shard_map/ppermute | solution.py:59
  93.1 23.0 %collective-permute-start.20 = (bf16[256,1024]{1,0:T(8,128)(2,1)S(1)}, bf16[256,1024]{1,0:T(8,128)(2,1)}, u32[]{:S(2)}, u32[]{:S(2)}) collective-permute-start(bf16[256,1024]{1,0:T(8,128)(2,1)S(1)} %get-tuple-element.59), channel_id=1, source_target_pairs={{0,4},{1,5},{2,6},{3,7},{4,0},{5,1},{6,2},{7,3},{8,12},{9,13},{10,... | collective-permute-start | bytes 1572872 | tf_op jit(solution)/shard_map/ppermute | solution.py:59
  94.4 22.0 %collective-permute-start.22 = (bf16[256,1024]{1,0:T(8,128)(2,1)}, bf16[256,1024]{1,0:T(8,128)(2,1)}, u32[]{:S(2)}, u32[]{:S(2)}) collective-permute-start(bf16[256,1024]{1,0:T(8,128)(2,1)} %add.313), channel_id=1, source_target_pairs={{4,8},{5,9},{6,10},{7,11},{8,4},{9,5},{10,6},{11,7},{20,24},{21,25... | collective-permute-start | bytes 1572872 | tf_op jit(solution)/shard_map/ppermute | solution.py:59
  104.9 18.9 %collective-permute-start.24 = (bf16[256,1024]{1,0:T(8,128)(2,1)S(1)}, bf16[256,1024]{1,0:T(8,128)(2,1)}, u32[]{:S(2)}, u32[]{:S(2)}) collective-permute-start(bf16[256,1024]{1,0:T(8,128)(2,1)S(1)} %add.314), channel_id=1, source_target_pairs={{4,12},{5,13},{6,14},{7,15},{8,0},{9,1},{10,2},{11,3},{20,28},{21,... | collective-permute-start | bytes 1572872 | tf_op jit(solution)/shard_map/ppermute | solution.py:59
  112.3 1.0 copy-start.3
  113.2 0.7 copy-start.4
  113.9 0.7 copy-start.5
  114.6 3.2 %collective-permute-start.25 = (bf16[640,128]{1,0:T(8,128)(2,1)}, bf16[640,128]{1,0:T(8,128)(2,1)S(1)}, u32[]{:S(2)}, u32[]{:S(2)}) collective-permute-start(bf16[640,128]{1,0:T(8,128)(2,1)} %get-tuple-element.75), channel_id=1, source_target_pairs={{0,1},{1,0},{2,3},{3,2},{4,5},{5,4},{6,7},{7,6},{8,9},{9,8},{10,11... | collective-permute-start | bytes 491528 | tf_op jit(solution)/shard_map/ppermute | solution.py:51
  114.6 7.2 %collective-permute-start.26 = (bf16[640,128]{1,0:T(8,128)(2,1)}, bf16[640,128]{1,0:T(8,128)(2,1)S(1)}, u32[]{:S(2)}, u32[]{:S(2)}) collective-permute-start(bf16[640,128]{1,0:T(8,128)(2,1)} %get-tuple-element.76), channel_id=1, source_target_pairs={{0,2},{1,3},{2,0},{3,1},{4,6},{5,7},{6,4},{7,5},{8,10},{9,11},{10,... | collective-permute-start | bytes 491528 | tf_op jit(solution)/shard_map/ppermute | solution.py:51
  116.1 11.8 %collective-permute-start.27 = (bf16[640,128]{1,0:T(8,128)(2,1)}, bf16[640,128]{1,0:T(8,128)(2,1)S(1)}, u32[]{:S(2)}, u32[]{:S(2)}) collective-permute-start(bf16[640,128]{1,0:T(8,128)(2,1)} %copy-done.5), channel_id=1, source_target_pairs={{0,3},{1,2},{2,1},{3,0},{4,7},{5,6},{6,5},{7,4},{8,11},{9,10},{10,... | collective-permute-start | bytes 491528 | tf_op jit(solution)/shard_map/ppermute | solution.py:51
  116.4 12.7 %collective-permute-start.28 = (bf16[640,128]{1,0:T(8,128)(2,1)}, bf16[640,128]{1,0:T(8,128)(2,1)S(1)}, u32[]{:S(2)}, u32[]{:S(2)}) collective-permute-start(bf16[640,128]{1,0:T(8,128)(2,1)} %copy-done.4), channel_id=1, source_target_pairs={{0,16},{1,17},{2,18},{3,19},{4,20},{5,21},{6,22},{7,23},{8,24},{9,... | collective-permute-start | bytes 491528 | tf_op jit(solution)/shard_map/ppermute | solution.py:51
  117.8 12.3 %collective-permute-start.29 = (bf16[640,128]{1,0:T(8,128)(2,1)S(1)}, bf16[640,128]{1,0:T(8,128)(2,1)S(1)}, u32[]{:S(2)}, u32[]{:S(2)}) collective-permute-start(bf16[640,128]{1,0:T(8,128)(2,1)S(1)} %get-tuple-element.79), channel_id=1, source_target_pairs={{0,17},{1,16},{2,19},{3,18},{4,21},{5,20},{6,23},{7,22},{8,25},{9,... | collective-permute-start | bytes 491528 | tf_op jit(solution)/shard_map/ppermute | solution.py:51
  121.8 9.9 %collective-permute-start.30 = (bf16[640,128]{1,0:T(8,128)(2,1)S(1)}, bf16[640,128]{1,0:T(8,128)(2,1)S(1)}, u32[]{:S(2)}, u32[]{:S(2)}) collective-permute-start(bf16[640,128]{1,0:T(8,128)(2,1)S(1)} %get-tuple-element.80), channel_id=1, source_target_pairs={{0,18},{1,19},{2,16},{3,17},{4,22},{5,23},{6,20},{7,21},{8,26},{9,... | collective-permute-start | bytes 491528 | tf_op jit(solution)/shard_map/ppermute | solution.py:51
  123.7 10.3 %collective-permute-start.31 = (bf16[640,128]{1,0:T(8,128)(2,1)S(1)}, bf16[640,128]{1,0:T(8,128)(2,1)S(1)}, u32[]{:S(2)}, u32[]{:S(2)}) collective-permute-start(bf16[640,128]{1,0:T(8,128)(2,1)S(1)} %get-tuple-element.81), channel_id=1, source_target_pairs={{0,19},{1,18},{2,17},{3,16},{4,23},{5,22},{6,21},{7,20},{8,27},{9,... | collective-permute-start | bytes 491528 | tf_op jit(solution)/shard_map/ppermute | solution.py:51
  127.9 10.0 %collective-permute-start.32 = (bf16[64,1024]{1,0:T(8,128)(2,1)}, bf16[64,1024]{1,0:T(8,128)(2,1)S(1)}, u32[]{:S(2)}, u32[]{:S(2)}) collective-permute-start(bf16[64,1024]{1,0:T(8,128)(2,1)} %get-tuple-element.84), channel_id=1, source_target_pairs={{0,2},{1,3},{2,0},{3,1},{4,6},{5,7},{6,4},{7,5},{8,10},{9,11},{10,... | collective-permute-start | bytes 393224 | tf_op jit(solution)/shard_map/ppermute | solution.py:51
  129.2 8.8 %collective-permute-start.33 = (bf16[64,1024]{1,0:T(8,128)(2,1)}, bf16[64,1024]{1,0:T(8,128)(2,1)}, u32[]{:S(2)}, u32[]{:S(2)}) collective-permute-start(bf16[64,1024]{1,0:T(8,128)(2,1)} %get-tuple-element.85), channel_id=1, source_target_pairs={{0,16},{1,17},{2,18},{3,19},{4,20},{5,21},{6,22},{7,23},{8,24},{9,... | collective-permute-start | bytes 393224 | tf_op jit(solution)/shard_map/ppermute | solution.py:51
  130.1 10.0 %collective-permute-start.34 = (bf16[64,1024]{1,0:T(8,128)(2,1)}, bf16[64,1024]{1,0:T(8,128)(2,1)S(1)}, u32[]{:S(2)}, u32[]{:S(2)}) collective-permute-start(bf16[64,1024]{1,0:T(8,128)(2,1)} %get-tuple-element.86), channel_id=1, source_target_pairs={{0,18},{1,19},{2,16},{3,17},{4,22},{5,23},{6,20},{7,21},{8,26},{9,... | collective-permute-start | bytes 393224 | tf_op jit(solution)/shard_map/ppermute | solution.py:51
  137.9 2.3 %copy-start.9 = (bf16[64,1024]{1,0:T(8,128)(2,1)}, bf16[64,1024]{1,0:T(8,128)(2,1)S(1)}, u32[]{:S(2)}) copy-start(bf16[64,1024]{1,0:T(8,128)(2,1)S(1)} %collective-permute-done.32.refs_1_) | copy-start | bytes 393220
  140.2 0.6 copy-start.10

commit v4 on v3

--- a/solution.py
+++ b/solution.py
@@ -62,144 +62,97 @@
         return [(dx, dy) for dx in range(self.dp) for dy in range(self.rows)]
 
 
-def select_kernel(plan, ids, pack_ref, hot_ref, head_ref, gate_ref):
-    tokens, cap, top, head_dim = plan.tokens, plan.cap, plan.top, plan.head_dim
-    experts = plan.planes * plan.rows
+def slot_kernel(plan, weight_count, earlier, ids, *refs):
+    packs, rest = refs[: plan.sources], refs[plan.sources :]
+    weight_refs, rest = rest[:weight_count], rest[weight_count:]
+    earlier_refs, rest = rest[:earlier], rest[earlier:]
+    count = plan.sources if earlier else 1
+    p_ref, back_refs, (grads, heads, weights) = rest[0], rest[1 : 1 + count], rest[1 + count :]
+    tokens, cap, part, top, head_dim = plan.tokens, plan.cap, plan.part, plan.top, plan.head_dim
+    pair_rows = 2 * cap
+    pair_total = plan.sources // 2
+    base = (plan.planes - 1) * plan.back if earlier else 0
+
+    for i in range(plan.rows):
+        at = pl.ds(pl.multiple_of(ids[plan.rows + i], head_dim), head_dim)
+        if weight_count == 1:
+            weights[i] = weight_refs[0][at, :]
+        else:
+            for j in range(2):
+
+                @pl.when(ids[2 * plan.rows] == j)
+                def _():
+                    weights[i] = weight_refs[j][at, :]
+
     row_of = lax.broadcasted_iota(jnp.int32, (cap, tokens), 0)
+    diagonal = (row_of == lax.broadcasted_iota(jnp.int32, (cap, tokens), 1)).astype(jnp.float32)
     before = (
         lax.broadcasted_iota(jnp.int32, (tokens, tokens), 0)
         < lax.broadcasted_iota(jnp.int32, (tokens, tokens), 1)
     ).astype(jnp.bfloat16)
+    block_row = lax.broadcasted_iota(jnp.int32, (16, LANES), 0)
     empty = jnp.zeros((cap, tokens), jnp.bfloat16)
-
-    def pair(q, carry):
+    chunk = min(part, 512)
+    for q in range(pair_total):
+        hots, gates, chosen = {}, {}, {}
         for b in range(2):
-            start = pl.multiple_of((2 * q + b) * tokens, tokens)
-            meta = pack_ref[pl.ds(start, 2 * top), pl.ds(top * head_dim, LANES)].astype(jnp.float32)
-            masks, gate_rows, occupied = [], [], []
-            for e in range(experts):
-                mask = (meta[top:] == ids[e].astype(jnp.float32)).astype(jnp.float32)
+            pack = packs[2 * q + b]
+            meta = pack[pl.ds(0, 2 * top), pl.ds(part + top * head_dim, LANES)].astype(jnp.float32)
+            masks, occupied = [], []
+            for i in range(plan.rows):
+                mask = (meta[top:] == ids[i].astype(jnp.float32)).astype(jnp.float32)
                 masks.append(mask)
-                gate_rows.append(jnp.sum(mask * meta[:top], axis=0, keepdims=True))
                 occupied.append(jnp.sum(mask, axis=0, keepdims=True))
-            filled = occupied + [jnp.zeros((1, tokens), jnp.float32)] * (-experts % 16)
+            filled = occupied + [jnp.zeros((1, tokens), jnp.float32)] * (-plan.rows % 16)
             places = jnp.dot(
                 jnp.concatenate(filled, axis=0).astype(jnp.bfloat16),
                 before,
                 preferred_element_type=jnp.float32,
             )
             wide = []
-            for e in range(experts):
-                place = places[e : e + 1].astype(jnp.int32)
-                hot = jnp.where(row_of == place, occupied[e], 0.0)
-                gates = jnp.sum(hot * gate_rows[e], axis=1, keepdims=True)
-                slot, i = divmod(e, plan.rows)
-                at = (2 * i + b) * cap
-                hot_ref[slot, q, pl.ds(at, cap), :] = jnp.concatenate(
-                    [hot.astype(jnp.bfloat16), empty] if b == 0 else [empty, hot.astype(jnp.bfloat16)],
-                    axis=1,
-                )
-                gate_ref[slot, q, pl.ds(at, cap), :] = jnp.broadcast_to(gates, (cap, LANES)).astype(
-                    jnp.bfloat16
-                )
+            for i in range(plan.rows):
+                place = places[i : i + 1].astype(jnp.int32)
+                hot = jnp.where(row_of == place, occupied[i], 0.0)
+                gate_row = jnp.sum(masks[i] * meta[:top], axis=0, keepdims=True)
+                gates[i, b] = jnp.sum(hot * gate_row, axis=1, keepdims=True)
+                hots[i, b] = hot.astype(jnp.bfloat16)
                 wide.append(
                     jnp.concatenate(
-                        [(hot * masks[e][k : k + 1]).astype(jnp.bfloat16) for k in range(top)], axis=1
+                        [(hot * masks[i][k : k + 1]).astype(jnp.bfloat16) for k in range(top)], axis=1
                     )
                 )
             raw = jnp.concatenate(
-                [
-                    pack_ref[pl.ds(start, tokens), pl.ds(k * head_dim, head_dim)]
-                    for k in range(top)
-                ],
-                axis=0,
+                [pack[:, pl.ds(part + k * head_dim, head_dim)] for k in range(top)], axis=0
             )
-            chosen = jnp.dot(
+            rows = jnp.dot(
                 jnp.concatenate(wide, axis=0), raw, preferred_element_type=jnp.float32
             ).astype(jnp.bfloat16)
-            for e in range(experts):
-                slot, i = divmod(e, plan.rows)
-                head_ref[slot, q, pl.ds((2 * i + b) * cap, cap), :] = chosen[e * cap : (e + 1) * cap]
-        return carry
-
-    lax.fori_loop(0, plan.sources // 2, pair, 0)
-
-
-def select_work(plan, ids, packs):
-    rows = plan.rows * 2 * plan.cap
-    lead = (plan.planes, plan.sources // 2, rows)
-    return pl.pallas_call(
-        functools.partial(select_kernel, plan),
-        out_shape=(
-            jax.ShapeDtypeStruct((*lead, 2 * plan.tokens), jnp.bfloat16),
-            jax.ShapeDtypeStruct((*lead, plan.head_dim), jnp.bfloat16),
-            jax.ShapeDtypeStruct((*lead, LANES), jnp.bfloat16),
-        ),
-        in_specs=[
-            pl.BlockSpec(memory_space=pltpu.SMEM),
-            pl.BlockSpec(memory_space=pltpu.VMEM),
-        ],
-        out_specs=(pl.BlockSpec(memory_space=pltpu.VMEM),) * 3,
-        compiler_params=pltpu.CompilerParams(vmem_limit_bytes=56 * 1024 * 1024),
-    )(ids, packs)
-
-
-def slot_kernel(plan, slot_index, earlier, ids, *refs):
-    packs = refs[: plan.sources]
-    hot_any, head_any, gate_any, w_ref = refs[plan.sources : plan.sources + 4]
-    rest = refs[plan.sources + 4 :]
-    earlier_refs, rest = rest[:earlier], rest[earlier:]
-    count = plan.sources if earlier else 1
-    p_ref, back_refs, (buf, hots, heads, gates, grads, sems) = rest[0], rest[1 : 1 + count], rest[1 + count :]
-    tokens, cap, part, head_dim = plan.tokens, plan.cap, plan.part, plan.head_dim
-    pair_rows = 2 * cap
-    pair_total = plan.sources // 2
-    base = (plan.planes - 1) * plan.back if earlier else 0
-
-    def copies(q):
-        slot = q % 2
-        return [
-            pltpu.make_async_copy(
-                packs[2 * q + b], buf.at[slot, pl.ds(b * tokens, tokens), :], sems.at[slot, b]
-            )
-            for b in range(2)
-        ]
-
-    chosen = [
-        pltpu.make_async_copy(hot_any.at[slot_index], hots, sems.at[2, 0]),
-        pltpu.make_async_copy(head_any.at[slot_index], heads, sems.at[2, 1]),
-        pltpu.make_async_copy(gate_any.at[slot_index], gates, sems.at[3, 0]),
-    ]
-    for copy in chosen + copies(0):
-        copy.start()
-    lines = lax.broadcasted_iota(jnp.int32, (cap, LANES), 0)
-    lanes = lax.broadcasted_iota(jnp.int32, (cap, LANES), 1)
-    diagonal = (lines == lanes).astype(jnp.float32)
-    block_row = lax.broadcasted_iota(jnp.int32, (16, LANES), 0)
-    chunk = min(part, 512)
-    for copy in chosen:
-        copy.wait()
-    for q in range(pair_total):
-        slot = q % 2
-        if q + 1 < pair_total:
-            for copy in copies(q + 1):
-                copy.start()
-        for copy in copies(q):
-            copy.wait()
+            for i in range(plan.rows):
+                heads[i, pl.ds(q * pair_rows + b * cap, cap), :] = rows[i * cap : (i + 1) * cap]
+        all_hots = jnp.concatenate(
+            [
+                jnp.concatenate([hots[i, b], empty] if b == 0 else [empty, hots[i, b]], axis=1)
+                for i in range(plan.rows)
+                for b in range(2)
+            ],
+            axis=0,
+        )
         sums = [jnp.zeros((pair_rows, LANES), jnp.float32) for _ in range(plan.rows)]
         for start in range(0, part, chunk):
-            grad = jnp.dot(
-                hots[q], buf[slot, :, pl.ds(start, chunk)], preferred_element_type=jnp.float32
+            both = jnp.concatenate(
+                [packs[2 * q + b][:, pl.ds(start, chunk)] for b in range(2)], axis=0
             )
+            grad = jnp.dot(all_hots, both, preferred_element_type=jnp.float32)
             for i in range(plan.rows):
                 at = i * pair_rows
-                weight = w_ref[
-                    pl.ds(pl.multiple_of(ids[plan.rows + i], 128), head_dim), pl.ds(start, chunk)
-                ]
                 pre = jnp.dot(
-                    heads[q, pl.ds(at, pair_rows), :], weight, preferred_element_type=jnp.float32
+                    heads[i, pl.ds(q * pair_rows, pair_rows), :],
+                    weights[i, :, pl.ds(start, chunk)],
+                    preferred_element_type=jnp.float32,
                 )
-                gate = gates[q, pl.ds(at, pair_rows), :].astype(jnp.float32)
+                gate = jnp.broadcast_to(
+                    jnp.concatenate([gates[i, 0], gates[i, 1]], axis=0), (pair_rows, LANES)
+                )
                 for lane in range(0, chunk, LANES):
                     grad_block = grad[at : at + pair_rows, lane : lane + LANES]
                     capped = jnp.tanh(pre[:, lane : lane + LANES] * (1.0 / soft_cap))
@@ -220,16 +173,12 @@
             else:
                 back_refs[0][s, pl.ds(at, 16), :] = block.astype(jnp.bfloat16)
     for i in range(plan.rows):
-        weight = w_ref[pl.ds(pl.multiple_of(ids[plan.rows + i], 128), head_dim), :]
         grad_all = grads[i]
-        head_all = jnp.concatenate(
-            [heads[q, pl.ds(i * pair_rows, pair_rows), :] for q in range(pair_total)], axis=0
-        )
         p_ref[pl.ds(i * head_dim, head_dim), :] = lax.dot_general(
-            head_all, grad_all, (((0,), (0,)), ((), ())), preferred_element_type=jnp.float32
+            heads[i], grad_all, (((0,), (0,)), ((), ())), preferred_element_type=jnp.float32
         ).astype(p_ref.dtype)
         rows = lax.dot_general(
-            grad_all, weight, (((1,), (1,)), ((), ())), preferred_element_type=jnp.float32
+            grad_all, weights[i], (((1,), (1,)), ((), ())), preferred_element_type=jnp.float32
         ).astype(jnp.bfloat16)
         for s in range(plan.sources):
             value = rows[s * cap : (s + 1) * cap]
@@ -242,9 +191,8 @@
             back_refs[s][pl.ds(j * plan.back, plan.back), :] = ref[s]
 
 
-def slot_work(plan, slot_index, ids, packs, selected, weight, kind, earlier=()):
-    rows = plan.rows * 2 * plan.cap
-    pair_total = plan.sources // 2
+def slot_work(plan, ids, packs, weights, kind, earlier=()):
+    rows = plan.sources * plan.cap
     if earlier:
         backs = (
             jax.ShapeDtypeStruct((plan.planes * plan.back, LANES), jnp.bfloat16),
@@ -253,22 +201,18 @@
         backs = (jax.ShapeDtypeStruct((plan.sources, plan.back, LANES), jnp.bfloat16),)
     vmem = pl.BlockSpec(memory_space=pltpu.VMEM)
     return pl.pallas_call(
-        functools.partial(slot_kernel, plan, slot_index, len(earlier)),
+        functools.partial(slot_kernel, plan, len(weights), len(earlier)),
         out_shape=(jax.ShapeDtypeStruct((plan.rows * plan.head_dim, plan.part), kind), *backs),
         in_specs=[pl.BlockSpec(memory_space=pltpu.SMEM)]
-        + [pl.BlockSpec(memory_space=pl.ANY)] * (plan.sources + 3)
-        + [vmem] * (1 + len(earlier)),
+        + [vmem] * (plan.sources + len(weights) + len(earlier)),
         out_specs=(vmem,) * (1 + len(backs)),
         scratch_shapes=[
-            pltpu.VMEM((2, 2 * plan.tokens, plan.part), jnp.bfloat16),
-            pltpu.VMEM((pair_total, rows, 2 * plan.tokens), jnp.bfloat16),
-            pltpu.VMEM((pair_total, rows, plan.head_dim), jnp.bfloat16),
-            pltpu.VMEM((pair_total, rows, LANES), jnp.bfloat16),
-            pltpu.VMEM((plan.rows, plan.sources * plan.cap, plan.part), jnp.bfloat16),
-            pltpu.SemaphoreType.DMA((4, 2)),
+            pltpu.VMEM((plan.rows, rows, plan.part), jnp.bfloat16),
+            pltpu.VMEM((plan.rows, rows, plan.head_dim), jnp.bfloat16),
+            pltpu.VMEM((plan.rows, plan.head_dim, plan.part), jnp.bfloat16),
         ],
-        compiler_params=pltpu.CompilerParams(vmem_limit_bytes=32 * 1024 * 1024),
-    )(ids, *packs, *selected, weight, *earlier)
+        compiler_params=pltpu.CompilerParams(vmem_limit_bytes=20 * 1024 * 1024),
+    )(ids, *packs, *weights, *earlier)
 
 
 def sum_kernel(plan, starts, own_ref, *refs):
@@ -372,9 +316,11 @@
     weight_parts = []
     for dy in range(plan.rows):
         split = x * plan.rows + (y + dy) % plan.rows
-        piece = lax.dynamic_slice_in_dim(out_proj[0], split * plan.part, plan.part, 1)
-        weight_parts.append(plan.shift(piece, dy=dy))
-    own_weights = jnp.concatenate(weight_parts, axis=0)
+        weight_parts.append(lax.dynamic_slice_in_dim(out_proj[0], split * plan.part, plan.part, 1))
+    out_grad, weight_parts = lax.optimization_barrier((out_grad, weight_parts))
+    own_weights = jnp.concatenate(
+        [plan.shift(piece, dy=dy) for dy, piece in enumerate(weight_parts)], axis=0
+    )
 
     meta = jnp.concatenate(
         [
@@ -384,21 +330,17 @@
         ],
         axis=0,
     )
-    head_pack = jnp.concatenate([head_outputs.reshape(tokens, top * head_dim), meta], axis=1)
-
-    def grad_part(dx, dy):
+    flat_heads = head_outputs.reshape(tokens, top * head_dim)
+    near_packs = []
+    for dx, dy in plan.splits_list():
         split = ((x + dx) % plan.dp) * plan.rows + (y + dy) % plan.rows
-        return lax.dynamic_slice_in_dim(out_grad, split * plan.part, plan.part, 1)
-
-    def plane_gather(piece_of):
-        out = []
-        for dx, dy in plan.splits_list():
-            value = plan.shift(piece_of(dx, dy), dx=dx, dy=dy)
-            out += [value, plan.shift(value, dc=1)]
-        return out
-
-    head_packs = jnp.concatenate(plane_gather(lambda dx, dy: head_pack), axis=0)
-    packs = plane_gather(grad_part)
+        piece = lax.dynamic_slice_in_dim(out_grad, split * plan.part, plan.part, 1)
+        value = jnp.concatenate([piece, flat_heads, meta], axis=1)
+        if dx or dy:
+            value = plan.shift(value, dx=dx, dy=dy)
+        else:
+            value, own_weights = lax.optimization_barrier((value, own_weights))
+        near_packs.append(value)
 
     if plan.planes == 4:
         inner = (z == 1) | (z == 2)
@@ -408,20 +350,21 @@
         mate = plan.along(own_weights, mates)
         near_in = plan.along(own_weights, middle)
         near_out = plan.along(near_in, outward)
-        far_in = plan.along(mate, middle)
+        far_in, near_out = lax.optimization_barrier((plan.along(mate, middle), near_out))
         far_out = plan.along(far_in, outward)
-        weights = [
-            jnp.where(inner, near_in, near_out),
-            jnp.where(inner, far_in, far_out),
-            mate,
-            own_weights,
-        ]
+        near_packs[1:], near_in = lax.optimization_barrier((near_packs[1:], near_in))
+        weights = [(near_in, near_out), (far_in, far_out), (mate,), (own_weights,)]
+        which = jnp.where(inner, 0, 1)
     else:
         steps = [k % plan.planes for k in range(1, plan.planes + 1)]
         plane_of = (z + jnp.array(steps, jnp.int32)) % plan.planes
-        weights = [plan.shift(own_weights, dz=-k % plan.planes) for k in steps]
-
-    routes = route_ids.reshape(tokens * top)
+        weights = [(plan.shift(own_weights, dz=-k % plan.planes),) for k in steps]
+        which = z * 0
+    packs = []
+    for value in near_packs:
+        packs += [value, plan.shift(value, dc=1)]
+
+    routes, own_weights = lax.optimization_barrier((route_ids.reshape(tokens * top), own_weights))
     hot = (routes[:, None] == jnp.arange(plan.experts, dtype=jnp.int32)[None, :]).astype(jnp.float32)
     per_token = hot.reshape(tokens, top, plan.experts).sum(axis=1)
     earlier = jnp.tril(jnp.ones((tokens, tokens), jnp.float32), -1)
@@ -443,38 +386,30 @@
     rows_at = jnp.arange(plan.rows, dtype=jnp.int32)
     weight_at = ((y - rows_at) % plan.rows) * head_dim
     expert_ids = (plane_of[:, None] * GROUP + rows_at[None, :] * 2 + c).astype(jnp.int32)
-    selected = select_work(plan, expert_ids.reshape(-1), head_packs)
-    selected, (target, gate_line, place) = lax.optimization_barrier(
-        (selected, (target, gate_line, place))
-    )
-    sums, backs = [], []
+    sums, backs, done = [], [], (target, gate_line, place)
     for j in range(plan.planes):
         last = j == plan.planes - 1
-        ids = jnp.concatenate([expert_ids[j], weight_at]).astype(jnp.int32)
-        if backs:
-            ids, _ = lax.optimization_barrier((ids, backs[-1]))
-        part, *back = slot_work(
-            plan,
-            j,
-            ids,
-            packs,
-            selected,
-            weights[j],
-            jnp.float32 if last else jnp.bfloat16,
-            backs if last else (),
-        )
+        ids = jnp.concatenate([expert_ids[j], weight_at, which[None]]).astype(jnp.int32)
+        if last and plan.planes == 4:
+            near_sum = sums[0] + plan.along(sums[0], inward)
+            done = (done, near_sum)
+        ids, done = lax.optimization_barrier((ids, done))
+        if j == 0:
+            target, gate_line, place = done
+        kind = jnp.float32 if last else jnp.bfloat16
+        part, *back = slot_work(plan, ids, packs, weights[j], kind, backs if last else ())
         sums.append(part)
         backs = back if last else backs + back
+        done = back[0]
 
     if plan.planes == 4:
-        near_sum = sums[0] + plan.along(sums[0], inward)
         far_sum = sums[1] + plan.along(sums[1], inward)
         received = [
             plan.along(sums[2], mates),
             plan.along(near_sum, middle),
             plan.along(far_sum, across),
         ]
-        backs, _ = lax.optimization_barrier((backs, (near_sum, far_sum)))
+        backs, _ = lax.optimization_barrier((backs, far_sum))
     else:
         received = [plan.shift(sums[j], dz=steps[j]) for j in range(plan.planes - 1)]
     own_rows = head_dim // plan.dp

time: 145 us -> 121 us (0.83)
  local copies, waits for them, and re-layouts: 22.3 us -> 7.83 us
  starting transfers between devices: 39.7 us -> 34.1 us
  Pallas kernels: 35.6 us -> 31.8 us
  waiting for transfers between devices: 37 us -> 35.4 us
    ppermute x25 -> x18, waiting for transfers between devices: 21.5 us -> 9.25 us  [shift(): return lax.ppermute(value, AXES, self.pairs(**by))]
    ppermute x10, waiting for transfers between devices: 15.5 us -> 26.2 us  [along(): return lax.ppermute(value, AXES, out)]
    unnamed x33 -> x25, local copies, waits for them, and re-layouts: 15.9 us -> 5.3 us
    ppermute x25 -> x18, starting transfers between devices: 20.6 us -> 15.8 us  [shift(): return lax.ppermute(value, AXES, self.pairs(**by))]
    pallas_call x5 -> x4, Pallas kernels: 28.5 us -> 24.7 us  [slot_work(): pl.pallas_call(functools.partial(slot_kernel, plan, len(weights), len(ear...]
    dynamic_slice x1, local copies, waits for them, and re-layouts: 2.07 us -> 0.09 us  [local(): piece = lax.dynamic_slice_in_dim(out_grad, split * plan.part, plan.part, 1)]
  transfers between devices with their start and end apart: 35 -> 28, of which waited for: 11 -> 10; matrix products, arithmetic and copies ran while one was open for 14% -> 10% of each run, Pallas kernels for 23% -> 25%
where the time goes in v4:
time: 121 us; the launch traced here: 119 us
  waiting for transfers between devices  35.4 us (29%)
  starting transfers between devices  34.1 us (28%)
  Pallas kernels  31.8 us (26%)
  local copies, waits for them, and re-layouts  7.83 us (6%)
  other arithmetic  7.68 us (6%)
    ppermute x10, waiting for transfers between devices, along(): return lax.ppermute(value, AXES, out)  26.2 us
    pallas_call x4, Pallas kernels, slot_work(): pl.pallas_call(functools.partial(slot_kernel, plan, len(weights), len(ear...  24.7 us
    ppermute x10, starting transfers between devices, along(): return lax.ppermute(value, AXES, out)  18.3 us
    ppermute x18, starting transfers between devices, shift(): return lax.ppermute(value, AXES, self.pairs(**by))  15.8 us
    ppermute x18, waiting for transfers between devices, shift(): return lax.ppermute(value, AXES, self.pairs(**by))  9.25 us
    unnamed x25, local copies, waits for them, and re-layouts  5.3 us
    pallas_call x1, Pallas kernels, sum_work(): pl.pallas_call(functools.partial(sum_kernel, plan), out_shape=tuple((jax....  2.66 us
  transfers between devices with their start and end apart: 28, of which 10 were waited for; matrix products, arithmetic and copies ran while one was open for 10% of the time, Pallas kernels for 25%

profile of v4, /device:TPU:0, one launch (start us, length us, event | category | flops | bytes accessed | tf_op | source)
XLA Modules:
  0.0 118.6 jit_solution(3853681943779876197)
XLA Ops:
  0.7 1.1 dynamic-slice_bitcast_fusion
  1.9 3.0 %collective-permute-start = (bf16[128,1024]{1,0:T(8,128)(2,1)S(1)}, bf16[128,1024]{1,0:T(8,128)(2,1)S(1)}, u32[]{:S(2)}, u32[]{:S(2)}) collective-permute-start(bf16[128,1024]{1,0:T(8,128)(2,1)S(1)} %get-tuple-element.54), channel_id=1, source_target_pairs={{0,2},{1,3},{2,0},{3,1},{4,6},{5,7},{6,4},{7,5},{8,10},{9,11},{10,... | collective-permute-start | bytes 786440 | tf_op jit(solution)/shard_map/ppermute | solution.py:51
  4.9 1.0 copy.26
  6.1 0.6 copy-done.8
  6.6 1.3 %fusion.3 = (bf16[128,2176]{1,0:T(8,128)(2,1)}, bf16[128,2176]{1,0:T(8,128)(2,1)}, bf16[128,2176]{1,0:T(8,128)(2,1)}) fusion(bf16[128,1024]{1,0:T(8,128)(2,1)S(1)} %bitcast.37, bf16[128,1024]{1,0:T(8,128)(2,1)S(1)} %get-tuple-element.112, bf16[112,128]{1,0:T(8,128)(2,1)S(1)} %broadcast_in_dim.46, bf16[8,128]{1,0:T(8,128)(2,1)S(1)} %convert_bitcast_fusion, ...), kind=kLoop, calls=%fused_computation.7 | loop fusion | flops 5013504 | bytes 2752512 | tf_op jit(solution)/shard_map/concatenate | solution.py:338
  8.0 1.9 %collective-permute-start.3 = (bf16[128,2176]{1,0:T(8,128)(2,1)}, bf16[128,2176]{1,0:T(8,128)(2,1)S(1)}, u32[]{:S(2)}, u32[]{:S(2)}) collective-permute-start(bf16[128,2176]{1,0:T(8,128)(2,1)} %get-tuple-element.120), channel_id=1, source_target_pairs={{0,16},{1,17},{2,18},{3,19},{4,20},{5,21},{6,22},{7,23},{8,24},{9,... | collective-permute-start | bytes 1671176 | tf_op jit(solution)/shard_map/ppermute | solution.py:51
  9.9 1.5 %collective-permute-start.4 = (bf16[128,2176]{1,0:T(8,128)(2,1)}, bf16[128,2176]{1,0:T(8,128)(2,1)S(1)}, u32[]{:S(2)}, u32[]{:S(2)}) collective-permute-start(bf16[128,2176]{1,0:T(8,128)(2,1)} %get-tuple-element.118), channel_id=1, source_target_pairs={{0,18},{1,19},{2,16},{3,17},{4,22},{5,23},{6,20},{7,21},{8,26},{9,... | collective-permute-start | bytes 1671176 | tf_op jit(solution)/shard_map/ppermute | solution.py:51
  11.4 0.5 iota_multiply_fusion
  12.0 0.5 fusion.16
  12.5 0.1 copy.16
  12.6 0.5 iota_add_fusion
  13.3 0.8 fusion.refs_0_
  14.2 1.5 %collective-permute-start.5 = (bf16[256,1024]{1,0:T(8,128)(2,1)S(1)}, bf16[256,1024]{1,0:T(8,128)(2,1)}, u32[]{:S(2)}, u32[]{:S(2)}) collective-permute-start(bf16[256,1024]{1,0:T(8,128)(2,1)S(1)} %pad_maximum_fusion.5.refs_8_), channel_id=1, source_target_pairs={{4,8},{5,9},{6,10},{7,11},{8,4},{9,5},{10,6},{11,7},{20,24},{21,25... | collective-permute-start | bytes 1572872 | tf_op jit(solution)/shard_map/ppermute | solution.py:59
  15.6 3.7 %collective-permute-start.9 = (bf16[256,1024]{1,0:T(8,128)(2,1)S(1)}, bf16[256,1024]{1,0:T(8,128)(2,1)S(1)}, u32[]{:S(2)}, u32[]{:S(2)}) collective-permute-start(bf16[256,1024]{1,0:T(8,128)(2,1)S(1)} %pad_maximum_fusion.5.refs_8_), channel_id=1, source_target_pairs={{0,4},{1,5},{2,6},{3,7},{4,0},{5,1},{6,2},{7,3},{8,12},{9,13},{10,... | collective-permute-start | bytes 1572872 | tf_op jit(solution)/shard_map/ppermute | solution.py:59
  19.5 10.4 %collective-permute-done.9.refs_8_ = bf16[256,1024]{1,0:T(8,128)(2,1)S(1)} collective-permute-done((bf16[256,1024]{1,0:T(8,128)(2,1)S(1)}, bf16[256,1024]{1,0:T(8,128)(2,1)S(1)}, u32[]{:S(2)}, u32[]{:S(2)}) %collective-permute-start.9) | collective-permute-done | bytes 524320 | tf_op jit(solution)/shard_map/ppermute | solution.py:59
  29.8 1.5 %collective-permute-start.10 = (bf16[256,1024]{1,0:T(8,128)(2,1)S(1)}, bf16[256,1024]{1,0:T(8,128)(2,1)}, u32[]{:S(2)}, u32[]{:S(2)}) collective-permute-start(bf16[256,1024]{1,0:T(8,128)(2,1)S(1)} %collective-permute-done.9.refs_8_), channel_id=1, source_target_pairs={{4,8},{5,9},{6,10},{7,11},{8,4},{9,5},{10,6},{11,7},{20,24},{21,25... | collective-permute-start | bytes 1572872 | tf_op jit(solution)/shard_map/ppermute | solution.py:59
  31.3 1.3 %collective-permute-start.11 = (bf16[256,1024]{1,0:T(8,128)(2,1)}, bf16[256,1024]{1,0:T(8,128)(2,1)}, u32[]{:S(2)}, u32[]{:S(2)}) collective-permute-start(bf16[256,1024]{1,0:T(8,128)(2,1)} %collective-permute-done.5.refs_8_), channel_id=1, source_target_pairs={{4,0},{5,1},{6,2},{7,3},{8,12},{9,13},{10,14},{11,15},{20,16},{21,... | collective-permute-start | bytes 1572872 | tf_op jit(solution)/shard_map/ppermute | solution.py:59
  32.8 0.8 fusion.4
  33.7 0.1 copy.18
  34.0 0.4 collective-permute-done.2.refs_2_
  34.5 0.9 collective-permute-done.4.refs_6_
  35.4 0.5 collective-permute-start.7
  35.9 9.2 %collective-permute-done.11.refs_9_ = bf16[256,1024]{1,0:T(8,128)(2,1)} collective-permute-done((bf16[256,1024]{1,0:T(8,128)(2,1)}, bf16[256,1024]{1,0:T(8,128)(2,1)}, u32[]{:S(2)}, u32[]{:S(2)}) %collective-permute-start.11) | collective-permute-done | bytes 524320 | tf_op jit(solution)/shard_map/ppermute | solution.py:59
  45.1 1.3 %collective-permute-start.12 = (bf16[256,1024]{1,0:T(8,128)(2,1)}, bf16[256,1024]{1,0:T(8,128)(2,1)S(1)}, u32[]{:S(2)}, u32[]{:S(2)}) collective-permute-start(bf16[256,1024]{1,0:T(8,128)(2,1)} %collective-permute-done.10.refs_8_), channel_id=1, source_target_pairs={{4,0},{5,1},{6,2},{7,3},{8,12},{9,13},{10,14},{11,15},{20,16},{21,... | collective-permute-start | bytes 1572872 | tf_op jit(solution)/shard_map/ppermute | solution.py:59
  46.6 6.4 %shard_map.76 = (bf16[256,1024]{1,0:T(8,128)(2,1)S(1)}, bf16[8,160,128]{2,1,0:T(8,128)(2,1)S(1)}) custom-call(s32[5]{0:T(128)S(1)} %add_add_fusion.3.ids, bf16[128,2176]{1,0:T(8,128)(2,1)S(1)} %fusion.refs_0_, bf16[128,2176]{1,0:T(8,128)(2,1)S(1)} %collective-permute-done.1.refs_1_, bf16[128,2176]{1,0:T(8,128)(2,1)S(1)} %collective-permute-done.2.refs_2_, ...), custom_call_target="tpu_custom_call" | custom-call | tf_op jit(solution)/shard_map/pallas_call | solution.py:203
  52.9 4.6 %collective-permute-start.13 = (bf16[256,1024]{1,0:T(8,128)(2,1)S(1)}, bf16[256,1024]{1,0:T(8,128)(2,1)S(1)}, u32[]{:S(2)}, u32[]{:S(2)}) collective-permute-start(bf16[256,1024]{1,0:T(8,128)(2,1)S(1)} %get-tuple-element.71), channel_id=1, source_target_pairs={{0,4},{1,5},{2,6},{3,7},{12,8},{13,9},{14,10},{15,11},{16,20},{17,... | collective-permute-start | bytes 1572872 | tf_op jit(solution)/shard_map/ppermute | solution.py:59
  57.6 1.5 %collective-permute-done.12.refs_9_ = bf16[256,1024]{1,0:T(8,128)(2,1)S(1)} collective-permute-done((bf16[256,1024]{1,0:T(8,128)(2,1)}, bf16[256,1024]{1,0:T(8,128)(2,1)S(1)}, u32[]{:S(2)}, u32[]{:S(2)}) %collective-permute-start.12) | collective-permute-done | bytes 524320 | tf_op jit(solution)/shard_map/ppermute | solution.py:59
  59.1 6.2 %shard_map.77 = (bf16[256,1024]{1,0:T(8,128)(2,1)S(1)}, bf16[8,160,128]{2,1,0:T(8,128)(2,1)S(1)}) custom-call(s32[5]{0:T(128)S(1)} %get-tuple-element.66.ids, bf16[128,2176]{1,0:T(8,128)(2,1)S(1)} %fusion.refs_0_, bf16[128,2176]{1,0:T(8,128)(2,1)S(1)} %collective-permute-done.1.refs_1_, bf16[128,2176]{1,0:T(8,128)(2,1)S(1)} %collective-permute-done.2.refs_2_, ...), custom_call_target="tpu_custom_call" | custom-call | tf_op jit(solution)/shard_map/pallas_call | solution.py:203
  65.3 1.8 %collective-permute-start.16 = (bf16[256,1024]{1,0:T(8,128)(2,1)S(1)}, bf16[256,1024]{1,0:T(8,128)(2,1)S(1)}, u32[]{:S(2)}, u32[]{:S(2)}) collective-permute-start(bf16[256,1024]{1,0:T(8,128)(2,1)S(1)} %get-tuple-element.75), channel_id=1, source_target_pairs={{0,4},{1,5},{2,6},{3,7},{12,8},{13,9},{14,10},{15,11},{16,20},{17,... | collective-permute-start | bytes 1572872 | tf_op jit(solution)/shard_map/ppermute | solution.py:59
  67.0 5.9 %shard_map.78 = (bf16[256,1024]{1,0:T(8,128)(2,1)}, bf16[8,160,128]{2,1,0:T(8,128)(2,1)S(1)}) custom-call(s32[5]{0:T(128)S(1)} %get-tuple-element.69.ids, bf16[128,2176]{1,0:T(8,128)(2,1)S(1)} %fusion.refs_0_, bf16[128,2176]{1,0:T(8,128)(2,1)S(1)} %collective-permute-done.1.refs_1_, bf16[128,2176]{1,0:T(8,128)(2,1)S(1)} %collective-permute-done.2.refs_2_, ...), custom_call_target="tpu_custom_call" | custom-call | tf_op jit(solution)/shard_map/pallas_call | solution.py:203
  72.9 1.0 add.230
  73.9 1.5 %collective-permute-start.15 = (bf16[256,1024]{1,0:T(8,128)(2,1)}, bf16[256,1024]{1,0:T(8,128)(2,1)}, u32[]{:S(2)}, u32[]{:S(2)}) collective-permute-start(bf16[256,1024]{1,0:T(8,128)(2,1)} %add.230), channel_id=1, source_target_pairs={{4,8},{5,9},{6,10},{7,11},{8,4},{9,5},{10,6},{11,7},{20,24},{21,25... | collective-permute-start | bytes 1572872 | tf_op jit(solution)/shard_map/ppermute | solution.py:59
  75.4 5.1 %collective-permute-done.16 = bf16[256,1024]{1,0:T(8,128)(2,1)S(1)} collective-permute-done((bf16[256,1024]{1,0:T(8,128)(2,1)S(1)}, bf16[256,1024]{1,0:T(8,128)(2,1)S(1)}, u32[]{:S(2)}, u32[]{:S(2)}) %collective-permute-start.16) | collective-permute-done | bytes 524320 | tf_op jit(solution)/shard_map/ppermute | solution.py:59
  80.5 1.0 add.231
  81.5 1.3 %collective-permute-start.17 = (bf16[256,1024]{1,0:T(8,128)(2,1)}, bf16[256,1024]{1,0:T(8,128)(2,1)}, u32[]{:S(2)}, u32[]{:S(2)}) collective-permute-start(bf16[256,1024]{1,0:T(8,128)(2,1)} %add.231), channel_id=1, source_target_pairs={{4,12},{5,13},{6,14},{7,15},{8,0},{9,1},{10,2},{11,3},{20,28},{21,... | collective-permute-start | bytes 1572872 | tf_op jit(solution)/shard_map/ppermute | solution.py:59
  82.8 6.2 %shard_map.79 = (f32[256,1024]{1,0:T(8,128)S(1)}, bf16[640,128]{1,0:T(8,128)(2,1)S(1)}, bf16[640,128]{1,0:T(8,128)(2,1)}, bf16[640,128]{1,0:T(8,128)(2,1)}, bf16...) custom-call(s32[5]{0:T(128)S(1)} %get-tuple-element.72.ids, ...), custom_call_target="tpu_custom_call" | custom-call | tf_op jit(solution)/shard_map/pallas_call | solution.py:203
  89.0 1.0 copy-done
  90.0 0.7 copy-done.1
  90.6 0.7 copy-done.2
  91.3 0.5 collective-permute-start.19
  91.8 1.4 %collective-permute-start.20 = (bf16[640,128]{1,0:T(8,128)(2,1)}, bf16[640,128]{1,0:T(8,128)(2,1)S(1)}, u32[]{:S(2)}, u32[]{:S(2)}) collective-permute-start(bf16[640,128]{1,0:T(8,128)(2,1)} %copy-done.2), channel_id=1, source_target_pairs={{0,3},{1,2},{2,1},{3,0},{4,7},{5,6},{6,5},{7,4},{8,11},{9,10},{10,... | collective-permute-start | bytes 491528 | tf_op jit(solution)/shard_map/ppermute | solution.py:51
  93.2 1.5 %collective-permute-start.21 = (bf16[640,128]{1,0:T(8,128)(2,1)}, bf16[640,128]{1,0:T(8,128)(2,1)S(1)}, u32[]{:S(2)}, u32[]{:S(2)}) collective-permute-start(bf16[640,128]{1,0:T(8,128)(2,1)} %copy-done.1), channel_id=1, source_target_pairs={{0,16},{1,17},{2,18},{3,19},{4,20},{5,21},{6,22},{7,23},{8,24},{9,... | collective-permute-start | bytes 491528 | tf_op jit(solution)/shard_map/ppermute | solution.py:51
  94.7 0.1 collective-permute-start.22
  94.8 3.7 %collective-permute-done.19.refs_2_ = bf16[640,128]{1,0:T(8,128)(2,1)S(1)} collective-permute-done((bf16[640,128]{1,0:T(8,128)(2,1)}, bf16[640,128]{1,0:T(8,128)(2,1)S(1)}, u32[]{:S(2)}, u32[]{:S(2)}) %collective-permute-start.19) | collective-permute-done | bytes 163872 | tf_op jit(solution)/shard_map/ppermute | solution.py:51
  98.5 1.4 %collective-permute-start.23 = (bf16[640,128]{1,0:T(8,128)(2,1)S(1)}, bf16[640,128]{1,0:T(8,128)(2,1)S(1)}, u32[]{:S(2)}, u32[]{:S(2)}) collective-permute-start(bf16[640,128]{1,0:T(8,128)(2,1)S(1)} %get-tuple-element.94), channel_id=1, source_target_pairs={{0,18},{1,19},{2,16},{3,17},{4,22},{5,23},{6,20},{7,21},{8,26},{9,... | collective-permute-start | bytes 491528 | tf_op jit(solution)/shard_map/ppermute | solution.py:51
  100.0 0.2 collective-permute-start.24
  100.2 0.6 pad_add_fusion.1.starts
  100.8 0.7 pad_add_fusion.2.starts
  101.5 0.2 copy.21.gate_ref
  101.7 0.2 copy.22.place_ref
  102.0 2.7 %shard_map.80 = (f32[64,1024]{1,0:T(8,128)}, bf16[64,1024]{1,0:T(8,128)(2,1)}, bf16[64,1024]{1,0:T(8,128)(2,1)}, bf16[64,1024]{1,0:T(8,128)(2,1)}) custom-call(s32[4]{0:T(128)} %pad_add_fusion.1.starts, f32[256,1024]{1,0:T(8,128)} %copy-done, bf16[256,1024]{1,0:T(8,128)(2,1)} %collective-permute-done.14.refs_0_, ...), custom_call_target="tpu_custom_call" | custom-call | tf_op jit(solution)/shard_map/pallas_call | solution.py:233
  104.6 0.2 copy.20.target_ref
  104.9 1.3 %collective-permute-start.25 = (bf16[64,1024]{1,0:T(8,128)(2,1)}, bf16[64,1024]{1,0:T(8,128)(2,1)S(1)}, u32[]{:S(2)}, u32[]{:S(2)}) collective-permute-start(bf16[64,1024]{1,0:T(8,128)(2,1)} %get-tuple-element.98), channel_id=1, source_target_pairs={{0,2},{1,3},{2,0},{3,1},{4,6},{5,7},{6,4},{7,5},{8,10},{9,11},{10,... | collective-permute-start | bytes 393224 | tf_op jit(solution)/shard_map/ppermute | solution.py:51
  106.2 0.7 collective-permute-start.26
  107.0 1.5 %collective-permute-start.27 = (bf16[64,1024]{1,0:T(8,128)(2,1)}, bf16[64,1024]{1,0:T(8,128)(2,1)S(1)}, u32[]{:S(2)}, u32[]{:S(2)}) collective-permute-start(bf16[64,1024]{1,0:T(8,128)(2,1)} %get-tuple-element.100), channel_id=1, source_target_pairs={{0,18},{1,19},{2,16},{3,17},{4,22},{5,23},{6,20},{7,21},{8,26},{9,... | collective-permute-start | bytes 393224 | tf_op jit(solution)/shard_map/ppermute | solution.py:51
  108.4 1.6 %collective-permute-done.24.refs_7_ = bf16[640,128]{1,0:T(8,128)(2,1)S(1)} collective-permute-done((bf16[640,128]{1,0:T(8,128)(2,1)S(1)}, bf16[640,128]{1,0:T(8,128)(2,1)S(1)}, u32[]{:S(2)}, u32[]{:S(2)}) %collective-permute-start.24) | collective-permute-done | bytes 163872 | tf_op jit(solution)/shard_map/ppermute | solution.py:51
  110.0 2.2 %shard_map.81 = (bf16[1024,128]{1,0:T(8,128)(2,1)}, f32[1024,1]{1,0:T(8,128)S(1)}) custom-call(s32[1024,1]{1,0:T(8,128)S(1)} %copy.20.target_ref, s32[1024,1]{1,0:T(8,128)S(1)} %copy.21.gate_ref, s32[1024,1]{1,0:T(8,128)S(1)} %copy.22.place_ref, bf16[640,128]{1,0:T(8,128)(2,1)S(1)} %get-tuple-element.88.refs_0_, ...), custom_call_target="tpu_custom_call" | custom-call | tf_op jit(solution)/shard_map/pallas_call | solution.py:292
  112.3 0.2 convert_reduce_fusion
  112.5 0.1 convert_element_type.40
  112.6 0.7 copy.23
  113.2 0.6 collective-permute-done.26.refs_2_
  113.9 1.9 %collective-permute-done.27.refs_3_ = bf16[64,1024]{1,0:T(8,128)(2,1)S(1)} collective-permute-done((bf16[64,1024]{1,0:T(8,128)(2,1)}, bf16[64,1024]{1,0:T(8,128)(2,1)S(1)}, u32[]{:S(2)}, u32[]{:S(2)}) %collective-permute-start.27) | collective-permute-done | bytes 131104 | tf_op jit(solution)/shard_map/ppermute | solution.py:51
  115.8 0.7 copy-done.6
  116.5 2.2 %shard_map.82 = f32[64,4096]{1,0:T(8,128)} custom-call(s32[4]{0:T(128)} %pad_add_fusion.2.starts, f32[64,1024]{1,0:T(8,128)} %get-tuple-element.76.refs_0_, bf16[64,1024]{1,0:T(8,128)(2,1)} %copy-done.5, bf16[64,1024]{1,0:T(8,128)(2,1)} %collective-permute-done.26.refs_2_, bf16[64,1024]{1,0:T(8,128)(2,1)} %copy-done.6), custom_call_target="tpu_custom_call" | custom-call | tf_op jit(solution)/shard_map/pallas_call | solution.py:254
  (61 shorter events, 1.2 us)
Async XLA Ops:
  0.6 5.3 %copy-start.3 = (bf16[128,4096]{1,0:T(8,128)(2,1)S(1)}, bf16[128,4096]{1,0:T(8,128)(2,1)}, u32[]{:S(2)}) copy-start(bf16[128,4096]{1,0:T(8,128)(2,1)} %param.6) | copy-start | bytes 3145732
  0.6 5.3 %copy-start.7 = (s32[128,8]{0,1:T(8,128)S(1)}, s32[128,8]{0,1:T(8,128)}, u32[]{:S(2)}) copy-start(s32[128,8]{0,1:T(8,128)} %param.8) | copy-start | bytes 12292
  1.9 12.2 %collective-permute-start = (bf16[128,1024]{1,0:T(8,128)(2,1)S(1)}, bf16[128,1024]{1,0:T(8,128)(2,1)S(1)}, u32[]{:S(2)}, u32[]{:S(2)}) collective-permute-start(bf16[128,1024]{1,0:T(8,128)(2,1)S(1)} %get-tuple-element.54), channel_id=1, source_target_pairs={{0,2},{1,3},{2,0},{3,1},{4,6},{5,7},{6,4},{7,5},{8,10},{9,11},{10,... | collective-permute-start | bytes 786440 | tf_op jit(solution)/shard_map/ppermute | solution.py:51
  6.0 0.7 copy-start.8
  6.6 1.3 %copy-start.4 = (bf16[112,128]{1,0:T(8,128)(2,1)}, bf16[112,128]{1,0:T(8,128)(2,1)S(1)}, u32[]{:S(2)}) copy-start(bf16[112,128]{1,0:T(8,128)(2,1)S(1)} %broadcast_in_dim.46) | copy-start | bytes 86020
  7.9 26.5 %collective-permute-start.2 = (bf16[128,2176]{1,0:T(8,128)(2,1)}, bf16[128,2176]{1,0:T(8,128)(2,1)S(1)}, u32[]{:S(2)}, u32[]{:S(2)}) collective-permute-start(bf16[128,2176]{1,0:T(8,128)(2,1)} %get-tuple-element.119), channel_id=1, source_target_pairs={{0,2},{1,3},{2,0},{3,1},{4,6},{5,7},{6,4},{7,5},{8,10},{9,11},{10,... | collective-permute-start | bytes 1671176 | tf_op jit(solution)/shard_map/ppermute | solution.py:51
  8.0 26.5 %collective-permute-start.3 = (bf16[128,2176]{1,0:T(8,128)(2,1)}, bf16[128,2176]{1,0:T(8,128)(2,1)S(1)}, u32[]{:S(2)}, u32[]{:S(2)}) collective-permute-start(bf16[128,2176]{1,0:T(8,128)(2,1)} %get-tuple-element.120), channel_id=1, source_target_pairs={{0,16},{1,17},{2,18},{3,19},{4,20},{5,21},{6,22},{7,23},{8,24},{9,... | collective-permute-start | bytes 1671176 | tf_op jit(solution)/shard_map/ppermute | solution.py:51
  9.9 25.4 %collective-permute-start.4 = (bf16[128,2176]{1,0:T(8,128)(2,1)}, bf16[128,2176]{1,0:T(8,128)(2,1)S(1)}, u32[]{:S(2)}, u32[]{:S(2)}) collective-permute-start(bf16[128,2176]{1,0:T(8,128)(2,1)} %get-tuple-element.118), channel_id=1, source_target_pairs={{0,18},{1,19},{2,16},{3,17},{4,22},{5,23},{6,20},{7,21},{8,26},{9,... | collective-permute-start | bytes 1671176 | tf_op jit(solution)/shard_map/ppermute | solution.py:51
  13.3 6.0 %copy-start.10 = (s32[2]{0:T(128)S(1)}, s32[2]{0:T(128)}, u32[]{:S(2)}) copy-start(s32[2]{0:T(128)} %iota_multiply_fusion) | copy-start | bytes 28
  13.3 6.1 %copy-start.9 = (s32[2]{0:T(128)S(1)}, s32[2]{0:T(128)}, u32[]{:S(2)}) copy-start(s32[2]{0:T(128)} %fusion.16) | copy-start | bytes 28
  14.2 17.1 %collective-permute-start.5 = (bf16[256,1024]{1,0:T(8,128)(2,1)S(1)}, bf16[256,1024]{1,0:T(8,128)(2,1)}, u32[]{:S(2)}, u32[]{:S(2)}) collective-permute-start(bf16[256,1024]{1,0:T(8,128)(2,1)S(1)} %pad_maximum_fusion.5.refs_8_), channel_id=1, source_target_pairs={{4,8},{5,9},{6,10},{7,11},{8,4},{9,5},{10,6},{11,7},{20,24},{21,25... | collective-permute-start | bytes 1572872 | tf_op jit(solution)/shard_map/ppermute | solution.py:59
  15.6 14.2 %collective-permute-start.9 = (bf16[256,1024]{1,0:T(8,128)(2,1)S(1)}, bf16[256,1024]{1,0:T(8,128)(2,1)S(1)}, u32[]{:S(2)}, u32[]{:S(2)}) collective-permute-start(bf16[256,1024]{1,0:T(8,128)(2,1)S(1)} %pad_maximum_fusion.5.refs_8_), channel_id=1, source_target_pairs={{0,4},{1,5},{2,6},{3,7},{4,0},{5,1},{6,2},{7,3},{8,12},{9,13},{10,... | collective-permute-start | bytes 1572872 | tf_op jit(solution)/shard_map/ppermute | solution.py:59
  29.8 6.1 %collective-permute-start.10 = (bf16[256,1024]{1,0:T(8,128)(2,1)S(1)}, bf16[256,1024]{1,0:T(8,128)(2,1)}, u32[]{:S(2)}, u32[]{:S(2)}) collective-permute-start(bf16[256,1024]{1,0:T(8,128)(2,1)S(1)} %collective-permute-done.9.refs_8_), channel_id=1, source_target_pairs={{4,8},{5,9},{6,10},{7,11},{8,4},{9,5},{10,6},{11,7},{20,24},{21,25... | collective-permute-start | bytes 1572872 | tf_op jit(solution)/shard_map/ppermute | solution.py:59
  31.3 13.8 %collective-permute-start.11 = (bf16[256,1024]{1,0:T(8,128)(2,1)}, bf16[256,1024]{1,0:T(8,128)(2,1)}, u32[]{:S(2)}, u32[]{:S(2)}) collective-permute-start(bf16[256,1024]{1,0:T(8,128)(2,1)} %collective-permute-done.5.refs_8_), channel_id=1, source_target_pairs={{4,0},{5,1},{6,2},{7,3},{8,12},{9,13},{10,14},{11,15},{20,16},{21,... | collective-permute-start | bytes 1572872 | tf_op jit(solution)/shard_map/ppermute | solution.py:59
  34.5 12.1 %collective-permute-start.1 = (bf16[128,2176]{1,0:T(8,128)(2,1)S(1)}, bf16[128,2176]{1,0:T(8,128)(2,1)S(1)}, u32[]{:S(2)}, u32[]{:S(2)}) collective-permute-start(bf16[128,2176]{1,0:T(8,128)(2,1)S(1)} %fusion.refs_0_), channel_id=1, source_target_pairs={{0,1},{1,0},{2,3},{3,2},{4,5},{5,4},{6,7},{7,6},{8,9},{9,8},{10,11... | collective-permute-start | bytes 1671176 | tf_op jit(solution)/shard_map/ppermute | solution.py:51
  35.4 11.2 %collective-permute-start.6 = (bf16[128,2176]{1,0:T(8,128)(2,1)S(1)}, bf16[128,2176]{1,0:T(8,128)(2,1)S(1)}, u32[]{:S(2)}, u32[]{:S(2)}) collective-permute-start(bf16[128,2176]{1,0:T(8,128)(2,1)S(1)} %collective-permute-done.2.refs_2_), channel_id=1, source_target_pairs={{0,1},{1,0},{2,3},{3,2},{4,5},{5,4},{6,7},{7,6},{8,9},{9,8},{10,11... | collective-permute-start | bytes 1671176 | tf_op jit(solution)/shard_map/ppermute | solution.py:51
  35.4 11.2 %collective-permute-start.7 = (bf16[128,2176]{1,0:T(8,128)(2,1)S(1)}, bf16[128,2176]{1,0:T(8,128)(2,1)S(1)}, u32[]{:S(2)}, u32[]{:S(2)}) collective-permute-start(bf16[128,2176]{1,0:T(8,128)(2,1)S(1)} %collective-permute-done.3.refs_4_), channel_id=1, source_target_pairs={{0,1},{1,0},{2,3},{3,2},{4,5},{5,4},{6,7},{7,6},{8,9},{9,8},{10,11... | collective-permute-start | bytes 1671176 | tf_op jit(solution)/shard_map/ppermute | solution.py:51
  35.9 10.7 %collective-permute-start.8 = (bf16[128,2176]{1,0:T(8,128)(2,1)S(1)}, bf16[128,2176]{1,0:T(8,128)(2,1)S(1)}, u32[]{:S(2)}, u32[]{:S(2)}) collective-permute-start(bf16[128,2176]{1,0:T(8,128)(2,1)S(1)} %collective-permute-done.4.refs_6_), channel_id=1, source_target_pairs={{0,1},{1,0},{2,3},{3,2},{4,5},{5,4},{6,7},{7,6},{8,9},{9,8},{10,11... | collective-permute-start | bytes 1671176 | tf_op jit(solution)/shard_map/ppermute | solution.py:51
  45.1 14.0 %collective-permute-start.12 = (bf16[256,1024]{1,0:T(8,128)(2,1)}, bf16[256,1024]{1,0:T(8,128)(2,1)S(1)}, u32[]{:S(2)}, u32[]{:S(2)}) collective-permute-start(bf16[256,1024]{1,0:T(8,128)(2,1)} %collective-permute-done.10.refs_8_), channel_id=1, source_target_pairs={{4,0},{5,1},{6,2},{7,3},{8,12},{9,13},{10,14},{11,15},{20,16},{21,... | collective-permute-start | bytes 1572872 | tf_op jit(solution)/shard_map/ppermute | solution.py:59
  52.9 20.0 %collective-permute-start.13 = (bf16[256,1024]{1,0:T(8,128)(2,1)S(1)}, bf16[256,1024]{1,0:T(8,128)(2,1)S(1)}, u32[]{:S(2)}, u32[]{:S(2)}) collective-permute-start(bf16[256,1024]{1,0:T(8,128)(2,1)S(1)} %get-tuple-element.71), channel_id=1, source_target_pairs={{0,4},{1,5},{2,6},{3,7},{12,8},{13,9},{14,10},{15,11},{16,20},{17,... | collective-permute-start | bytes 1572872 | tf_op jit(solution)/shard_map/ppermute | solution.py:59
  65.3 15.2 %collective-permute-start.16 = (bf16[256,1024]{1,0:T(8,128)(2,1)S(1)}, bf16[256,1024]{1,0:T(8,128)(2,1)S(1)}, u32[]{:S(2)}, u32[]{:S(2)}) collective-permute-start(bf16[256,1024]{1,0:T(8,128)(2,1)S(1)} %get-tuple-element.75), channel_id=1, source_target_pairs={{0,4},{1,5},{2,6},{3,7},{12,8},{13,9},{14,10},{15,11},{16,20},{17,... | collective-permute-start | bytes 1572872 | tf_op jit(solution)/shard_map/ppermute | solution.py:59
  72.9 18.9 %collective-permute-start.14 = (bf16[256,1024]{1,0:T(8,128)(2,1)}, bf16[256,1024]{1,0:T(8,128)(2,1)}, u32[]{:S(2)}, u32[]{:S(2)}) collective-permute-start(bf16[256,1024]{1,0:T(8,128)(2,1)} %get-tuple-element.74), channel_id=1, source_target_pairs={{0,4},{1,5},{2,6},{3,7},{4,0},{5,1},{6,2},{7,3},{8,12},{9,13},{10,... | collective-permute-start | bytes 1572872 | tf_op jit(solution)/shard_map/ppermute | solution.py:59
  73.9 19.2 %collective-permute-start.15 = (bf16[256,1024]{1,0:T(8,128)(2,1)}, bf16[256,1024]{1,0:T(8,128)(2,1)}, u32[]{:S(2)}, u32[]{:S(2)}) collective-permute-start(bf16[256,1024]{1,0:T(8,128)(2,1)} %add.230), channel_id=1, source_target_pairs={{4,8},{5,9},{6,10},{7,11},{8,4},{9,5},{10,6},{11,7},{20,24},{21,25... | collective-permute-start | bytes 1572872 | tf_op jit(solution)/shard_map/ppermute | solution.py:59
  81.5 18.5 %collective-permute-start.17 = (bf16[256,1024]{1,0:T(8,128)(2,1)}, bf16[256,1024]{1,0:T(8,128)(2,1)}, u32[]{:S(2)}, u32[]{:S(2)}) collective-permute-start(bf16[256,1024]{1,0:T(8,128)(2,1)} %add.231), channel_id=1, source_target_pairs={{4,12},{5,13},{6,14},{7,15},{8,0},{9,1},{10,2},{11,3},{20,28},{21,... | collective-permute-start | bytes 1572872 | tf_op jit(solution)/shard_map/ppermute | solution.py:59
  89.0 1.0 copy-start
  90.0 0.7 copy-start.1
  90.6 0.7 copy-start.2
  91.3 3.4 %collective-permute-start.18 = (bf16[640,128]{1,0:T(8,128)(2,1)}, bf16[640,128]{1,0:T(8,128)(2,1)S(1)}, u32[]{:S(2)}, u32[]{:S(2)}) collective-permute-start(bf16[640,128]{1,0:T(8,128)(2,1)} %get-tuple-element.89), channel_id=1, source_target_pairs={{0,1},{1,0},{2,3},{3,2},{4,5},{5,4},{6,7},{7,6},{8,9},{9,8},{10,11... | collective-permute-start | bytes 491528 | tf_op jit(solution)/shard_map/ppermute | solution.py:51
  91.3 7.2 %collective-permute-start.19 = (bf16[640,128]{1,0:T(8,128)(2,1)}, bf16[640,128]{1,0:T(8,128)(2,1)S(1)}, u32[]{:S(2)}, u32[]{:S(2)}) collective-permute-start(bf16[640,128]{1,0:T(8,128)(2,1)} %get-tuple-element.90), channel_id=1, source_target_pairs={{0,2},{1,3},{2,0},{3,1},{4,6},{5,7},{6,4},{7,5},{8,10},{9,11},{10,... | collective-permute-start | bytes 491528 | tf_op jit(solution)/shard_map/ppermute | solution.py:51
  91.8 13.0 %collective-permute-start.20 = (bf16[640,128]{1,0:T(8,128)(2,1)}, bf16[640,128]{1,0:T(8,128)(2,1)S(1)}, u32[]{:S(2)}, u32[]{:S(2)}) collective-permute-start(bf16[640,128]{1,0:T(8,128)(2,1)} %copy-done.2), channel_id=1, source_target_pairs={{0,3},{1,2},{2,1},{3,0},{4,7},{5,6},{6,5},{7,4},{8,11},{9,10},{10,... | collective-permute-start | bytes 491528 | tf_op jit(solution)/shard_map/ppermute | solution.py:51
  93.2 13.0 %collective-permute-start.21 = (bf16[640,128]{1,0:T(8,128)(2,1)}, bf16[640,128]{1,0:T(8,128)(2,1)S(1)}, u32[]{:S(2)}, u32[]{:S(2)}) collective-permute-start(bf16[640,128]{1,0:T(8,128)(2,1)} %copy-done.1), channel_id=1, source_target_pairs={{0,16},{1,17},{2,18},{3,19},{4,20},{5,21},{6,22},{7,23},{8,24},{9,... | collective-permute-start | bytes 491528 | tf_op jit(solution)/shard_map/ppermute | solution.py:51
  94.7 12.3 %collective-permute-start.22 = (bf16[640,128]{1,0:T(8,128)(2,1)S(1)}, bf16[640,128]{1,0:T(8,128)(2,1)S(1)}, u32[]{:S(2)}, u32[]{:S(2)}) collective-permute-start(bf16[640,128]{1,0:T(8,128)(2,1)S(1)} %get-tuple-element.93), channel_id=1, source_target_pairs={{0,17},{1,16},{2,19},{3,18},{4,21},{5,20},{6,23},{7,22},{8,25},{9,... | collective-permute-start | bytes 491528 | tf_op jit(solution)/shard_map/ppermute | solution.py:51
  98.5 9.9 %collective-permute-start.23 = (bf16[640,128]{1,0:T(8,128)(2,1)S(1)}, bf16[640,128]{1,0:T(8,128)(2,1)S(1)}, u32[]{:S(2)}, u32[]{:S(2)}) collective-permute-start(bf16[640,128]{1,0:T(8,128)(2,1)S(1)} %get-tuple-element.94), channel_id=1, source_target_pairs={{0,18},{1,19},{2,16},{3,17},{4,22},{5,23},{6,20},{7,21},{8,26},{9,... | collective-permute-start | bytes 491528 | tf_op jit(solution)/shard_map/ppermute | solution.py:51
  100.0 10.0 %collective-permute-start.24 = (bf16[640,128]{1,0:T(8,128)(2,1)S(1)}, bf16[640,128]{1,0:T(8,128)(2,1)S(1)}, u32[]{:S(2)}, u32[]{:S(2)}) collective-permute-start(bf16[640,128]{1,0:T(8,128)(2,1)S(1)} %get-tuple-element.95), channel_id=1, source_target_pairs={{0,19},{1,18},{2,17},{3,16},{4,23},{5,22},{6,21},{7,20},{8,27},{9,... | collective-permute-start | bytes 491528 | tf_op jit(solution)/shard_map/ppermute | solution.py:51
  104.9 8.4 %collective-permute-start.25 = (bf16[64,1024]{1,0:T(8,128)(2,1)}, bf16[64,1024]{1,0:T(8,128)(2,1)S(1)}, u32[]{:S(2)}, u32[]{:S(2)}) collective-permute-start(bf16[64,1024]{1,0:T(8,128)(2,1)} %get-tuple-element.98), channel_id=1, source_target_pairs={{0,2},{1,3},{2,0},{3,1},{4,6},{5,7},{6,4},{7,5},{8,10},{9,11},{10,... | collective-permute-start | bytes 393224 | tf_op jit(solution)/shard_map/ppermute | solution.py:51
  106.2 7.7 %collective-permute-start.26 = (bf16[64,1024]{1,0:T(8,128)(2,1)}, bf16[64,1024]{1,0:T(8,128)(2,1)}, u32[]{:S(2)}, u32[]{:S(2)}) collective-permute-start(bf16[64,1024]{1,0:T(8,128)(2,1)} %get-tuple-element.99), channel_id=1, source_target_pairs={{0,16},{1,17},{2,18},{3,19},{4,20},{5,21},{6,22},{7,23},{8,24},{9,... | collective-permute-start | bytes 393224 | tf_op jit(solution)/shard_map/ppermute | solution.py:51
  107.0 8.9 %collective-permute-start.27 = (bf16[64,1024]{1,0:T(8,128)(2,1)}, bf16[64,1024]{1,0:T(8,128)(2,1)S(1)}, u32[]{:S(2)}, u32[]{:S(2)}) collective-permute-start(bf16[64,1024]{1,0:T(8,128)(2,1)} %get-tuple-element.100), channel_id=1, source_target_pairs={{0,18},{1,19},{2,16},{3,17},{4,22},{5,23},{6,20},{7,21},{8,26},{9,... | collective-permute-start | bytes 393224 | tf_op jit(solution)/shard_map/ppermute | solution.py:51
  113.2 2.6 %copy-start.5 = (bf16[64,1024]{1,0:T(8,128)(2,1)}, bf16[64,1024]{1,0:T(8,128)(2,1)S(1)}, u32[]{:S(2)}) copy-start(bf16[64,1024]{1,0:T(8,128)(2,1)S(1)} %collective-permute-done.25.refs_1_) | copy-start | bytes 393220
  115.8 0.7 copy-start.6

commit v5 on v4

--- a/solution.py
+++ b/solution.py
@@ -50,39 +50,51 @@
             return value
         return lax.ppermute(value, AXES, self.pairs(**by))
 
-    def along(self, value, moves):
+    def along(self, value, moves, dx=0, dy=0):
         out = []
         for x in range(self.dp):
             for a, b in moves:
-                for r in range(GROUP):
-                    out.append((self.index(x, a, 0, 0) + r, self.index(x, b, 0, 0) + r))
+                for y in range(self.rows):
+                    for c in range(2):
+                        target = self.index((x + dx) % self.dp, b, (y + dy) % self.rows, c)
+                        out.append((self.index(x, a, y, c), target))
         return lax.ppermute(value, AXES, out)
 
     def splits_list(self):
         return [(dx, dy) for dx in range(self.dp) for dy in range(self.rows)]
 
 
-def slot_kernel(plan, weight_count, earlier, ids, *refs):
+def slot_kernel(plan, weight_rows, earlier, ids, *refs):
+    weight_count = len(weight_rows)
     packs, rest = refs[: plan.sources], refs[plan.sources :]
     weight_refs, rest = rest[:weight_count], rest[weight_count:]
     earlier_refs, rest = rest[:earlier], rest[earlier:]
-    count = plan.sources if earlier else 1
+    count = plan.splits if earlier else 1
     p_ref, back_refs, (grads, heads, weights) = rest[0], rest[1 : 1 + count], rest[1 + count :]
     tokens, cap, part, top, head_dim = plan.tokens, plan.cap, plan.part, plan.top, plan.head_dim
     pair_rows = 2 * cap
     pair_total = plan.sources // 2
-    base = (plan.planes - 1) * plan.back if earlier else 0
+    length = plan.planes * plan.back
+
+    def put(s, slot, at, value):
+        if earlier:
+            start = (s % 2) * length + slot * plan.back + at
+            back_refs[s // 2][pl.ds(start, value.shape[0]), :] = value
+        else:
+            back_refs[0][s, pl.ds(at, value.shape[0]), :] = value
+
 
     for i in range(plan.rows):
-        at = pl.ds(pl.multiple_of(ids[plan.rows + i], head_dim), head_dim)
-        if weight_count == 1:
-            weights[i] = weight_refs[0][at, :]
-        else:
-            for j in range(2):
-
-                @pl.when(ids[2 * plan.rows] == j)
+        row = ids[plan.rows + i]
+        for ref, (first, where) in zip(weight_refs, weight_rows):
+            for r in range(ref.shape[0] // head_dim):
+                wanted = row == first + r
+                if where is not None:
+                    wanted = wanted & (ids[2 * plan.rows] == where)
+
+                @pl.when(wanted)
                 def _():
-                    weights[i] = weight_refs[j][at, :]
+                    weights[i] = ref[pl.ds(r * head_dim, head_dim), :]
 
     row_of = lax.broadcasted_iota(jnp.int32, (cap, tokens), 0)
     diagonal = (row_of == lax.broadcasted_iota(jnp.int32, (cap, tokens), 1)).astype(jnp.float32)
@@ -166,12 +178,7 @@
                 column = jnp.sum(sums[i][b * cap : (b + 1) * cap], axis=1, keepdims=True) * soft_cap
                 line = jnp.sum(diagonal * column, axis=0, keepdims=True)
                 block = jnp.where(block_row == i, line, block)
-            s = 2 * q + b
-            at = base + plan.rows * cap
-            if earlier:
-                back_refs[s][pl.ds(at, 16), :] = block.astype(jnp.bfloat16)
-            else:
-                back_refs[0][s, pl.ds(at, 16), :] = block.astype(jnp.bfloat16)
+            put(2 * q + b, plan.planes - 1, plan.rows * cap, block.astype(jnp.bfloat16))
     for i in range(plan.rows):
         grad_all = grads[i]
         p_ref[pl.ds(i * head_dim, head_dim), :] = lax.dot_general(
@@ -181,27 +188,23 @@
             grad_all, weights[i], (((1,), (1,)), ((), ())), preferred_element_type=jnp.float32
         ).astype(jnp.bfloat16)
         for s in range(plan.sources):
-            value = rows[s * cap : (s + 1) * cap]
-            if earlier:
-                back_refs[s][pl.ds(base + i * cap, cap), :] = value
-            else:
-                back_refs[0][s, pl.ds(i * cap, cap), :] = value
+            put(s, plan.planes - 1, i * cap, rows[s * cap : (s + 1) * cap])
     for j, ref in enumerate(earlier_refs):
         for s in range(plan.sources):
-            back_refs[s][pl.ds(j * plan.back, plan.back), :] = ref[s]
+            put(s, j, 0, ref[s])
 
 
 def slot_work(plan, ids, packs, weights, kind, earlier=()):
     rows = plan.sources * plan.cap
     if earlier:
         backs = (
-            jax.ShapeDtypeStruct((plan.planes * plan.back, LANES), jnp.bfloat16),
-        ) * plan.sources
+            jax.ShapeDtypeStruct((2 * plan.planes * plan.back, LANES), jnp.bfloat16),
+        ) * plan.splits
     else:
         backs = (jax.ShapeDtypeStruct((plan.sources, plan.back, LANES), jnp.bfloat16),)
     vmem = pl.BlockSpec(memory_space=pltpu.VMEM)
     return pl.pallas_call(
-        functools.partial(slot_kernel, plan, len(weights), len(earlier)),
+        functools.partial(slot_kernel, plan, [rows for _, *rows in weights], len(earlier)),
         out_shape=(jax.ShapeDtypeStruct((plan.rows * plan.head_dim, plan.part), kind), *backs),
         in_specs=[pl.BlockSpec(memory_space=pltpu.SMEM)]
         + [vmem] * (plan.sources + len(weights) + len(earlier)),
@@ -212,40 +215,43 @@
             pltpu.VMEM((plan.rows, plan.head_dim, plan.part), jnp.bfloat16),
         ],
         compiler_params=pltpu.CompilerParams(vmem_limit_bytes=20 * 1024 * 1024),
-    )(ids, *packs, *weights, *earlier)
-
-
-def sum_kernel(plan, starts, own_ref, *refs):
-    received = refs[: len(refs) - plan.splits]
-    pieces = refs[len(refs) - plan.splits :]
+    )(ids, *packs, *[array for array, *_ in weights], *earlier)
+
+
+def sum_kernel(plan, starts, *refs):
+    parts, pieces = refs[: len(refs) - plan.splits], refs[len(refs) - plan.splits :]
     rows = plan.head_dim // plan.dp
     for j, piece in enumerate(pieces):
         at = pl.ds(pl.multiple_of(starts[j], rows), rows)
-        total = own_ref[at, :]
-        for ref in received:
+        total = parts[0][at, :].astype(jnp.float32)
+        for ref in parts[1:]:
             total = total + ref[at, :].astype(jnp.float32)
         piece[...] = total.astype(piece.dtype)
 
 
-def sum_work(plan, starts, own, received):
+def sum_work(plan, starts, parts, own_kind):
     rows = plan.head_dim // plan.dp
     vmem = pl.BlockSpec(memory_space=pltpu.VMEM)
     return pl.pallas_call(
         functools.partial(sum_kernel, plan),
         out_shape=tuple(
-            jax.ShapeDtypeStruct((rows, plan.part), jnp.bfloat16 if j else jnp.float32)
+            jax.ShapeDtypeStruct((rows, plan.part), jnp.bfloat16 if j else own_kind)
             for j in range(plan.splits)
         ),
-        in_specs=[pl.BlockSpec(memory_space=pltpu.SMEM)] + [vmem] * (1 + len(received)),
+        in_specs=[pl.BlockSpec(memory_space=pltpu.SMEM)] + [vmem] * len(parts),
         out_specs=(vmem,) * plan.splits,
-    )(starts, own, *received)
+    )(starts, *parts)
 
 
 def layout_kernel(plan, starts, *refs):
     out_ref = refs[-1]
-    for j, piece in enumerate(refs[:-1]):
+    for j in range(plan.splits):
         at = pl.ds(pl.multiple_of(starts[j], plan.part), plan.part)
-        out_ref[:, at] = piece[...].astype(jnp.float32)
+        total = None
+        for ref in refs[j : -1 : plan.splits]:
+            piece = ref[...].astype(jnp.float32)
+            total = piece if total is None else total + piece
+        out_ref[:, at] = total
 
 
 def layout_work(plan, starts, pieces):
@@ -254,31 +260,46 @@
     return pl.pallas_call(
         functools.partial(layout_kernel, plan),
         out_shape=jax.ShapeDtypeStruct((rows, plan.part * plan.splits), jnp.float32),
-        in_specs=[pl.BlockSpec(memory_space=pltpu.SMEM)] + [vmem] * plan.splits,
+        in_specs=[pl.BlockSpec(memory_space=pltpu.SMEM)] + [vmem] * len(pieces),
         out_specs=vmem,
     )(starts, *pieces)
 
 
-def final_kernel(plan, target_ref, gate_ref, place_ref, *refs):
-    parts = refs[: plan.sources]
-    head_ref, out_gate_ref, table = refs[plan.sources :]
+def merge_kernel(plan, *refs):
+    parts, outs = refs[: plan.splits], refs[plan.splits :]
     length = plan.planes * plan.back
-    for dc in range(2):
+    for dc, out in enumerate(outs):
         total = None
-        for s in range(plan.splits):
-            piece = parts[2 * s + dc][...].astype(jnp.float32)
+        for ref in parts:
+            piece = ref[pl.ds(dc * length, length), :].astype(jnp.float32)
             total = piece if total is None else total + piece
-        table[pl.ds(dc * length, length), :] = total.astype(jnp.bfloat16)
+        out[...] = total.astype(out.dtype)
+
+
+def merge_work(plan, parts):
+    vmem = pl.BlockSpec(memory_space=pltpu.VMEM)
+    rows = jax.ShapeDtypeStruct((plan.planes * plan.back, LANES), jnp.bfloat16)
+    return pl.pallas_call(
+        functools.partial(merge_kernel, plan),
+        out_shape=(rows, rows),
+        in_specs=[vmem] * plan.splits,
+        out_specs=(vmem, vmem),
+    )(*parts)
+
+
+def final_kernel(plan, target_ref, gate_ref, place_ref, own_ref, other_ref, head_ref, out_gate_ref):
+    length = plan.planes * plan.back
+    table = jnp.concatenate([own_ref[...], other_ref[...]], axis=0)
     block = 256
     count = plan.tokens * plan.top
     for start in range(0, count, block):
         slot_of = lax.broadcasted_iota(jnp.int32, (block, 2 * length), 1)
         hot = (slot_of == target_ref[pl.ds(start, block), :]).astype(jnp.bfloat16)
         head_ref[pl.ds(start, block), :] = jnp.dot(
-            hot, table[...], preferred_element_type=jnp.float32
+            hot, table, preferred_element_type=jnp.float32
         ).astype(jnp.bfloat16)
         hot = (slot_of == gate_ref[pl.ds(start, block), :]).astype(jnp.bfloat16)
-        lines = jnp.dot(hot, table[...], preferred_element_type=jnp.float32)
+        lines = jnp.dot(hot, table, preferred_element_type=jnp.float32)
         lane_of = lax.broadcasted_iota(jnp.int32, (block, LANES), 1)
         out_gate_ref[pl.ds(start, block), :] = jnp.sum(
             jnp.where(lane_of == place_ref[pl.ds(start, block), :], lines, 0.0),
@@ -287,7 +308,7 @@
         )
 
 
-def final_work(plan, target, gate_line, place, parts):
+def final_work(plan, target, gate_line, place, own, other):
     count = plan.tokens * plan.top
     return pl.pallas_call(
         functools.partial(final_kernel, plan),
@@ -295,14 +316,13 @@
             jax.ShapeDtypeStruct((count, plan.head_dim), jnp.bfloat16),
             jax.ShapeDtypeStruct((count, 1), jnp.float32),
         ),
-        in_specs=[pl.BlockSpec(memory_space=pltpu.VMEM)] * (3 + plan.sources),
+        in_specs=[pl.BlockSpec(memory_space=pltpu.VMEM)] * 5,
         out_specs=(
             pl.BlockSpec(memory_space=pltpu.VMEM),
             pl.BlockSpec(memory_space=pltpu.VMEM),
         ),
-        scratch_shapes=[pltpu.VMEM((2 * plan.planes * plan.back, LANES), jnp.bfloat16)],
-        compiler_params=pltpu.CompilerParams(vmem_limit_bytes=48 * 1024 * 1024),
-    )(target, gate_line, place, *parts)
+        compiler_params=pltpu.CompilerParams(vmem_limit_bytes=24 * 1024 * 1024),
+    )(target, gate_line, place, own, other)
 
 
 def local(mesh, head_outputs, out_grad, gate_weights, route_ids, out_proj):
@@ -318,9 +338,8 @@
         split = x * plan.rows + (y + dy) % plan.rows
         weight_parts.append(lax.dynamic_slice_in_dim(out_proj[0], split * plan.part, plan.part, 1))
     out_grad, weight_parts = lax.optimization_barrier((out_grad, weight_parts))
-    own_weights = jnp.concatenate(
-        [plan.shift(piece, dy=dy) for dy, piece in enumerate(weight_parts)], axis=0
-    )
+    weight_parts = [plan.shift(piece, dy=dy) for dy, piece in enumerate(weight_parts)]
+    own_weights = jnp.concatenate(weight_parts, axis=0)
 
     meta = jnp.concatenate(
         [
@@ -346,19 +365,25 @@
         inner = (z == 1) | (z == 2)
         mates, middle = [(0, 1), (1, 0), (2, 3), (3, 2)], [(1, 2), (2, 1)]
         outward, inward, across = [(1, 0), (2, 3)], [(0, 1), (3, 2)], [(1, 3), (2, 0)]
-        plane_of = jnp.stack([jnp.where(z < 2, 2, 1), jnp.where(z < 2, 3, 0), z ^ 1, z])
+        plane_of = jnp.stack([z, jnp.where(z < 2, 2, 1), jnp.where(z < 2, 3, 0), z ^ 1])
         mate = plan.along(own_weights, mates)
-        near_in = plan.along(own_weights, middle)
-        near_out = plan.along(near_in, outward)
+        near_in = [plan.along(piece, middle) for piece in weight_parts]
+        near_out = [plan.along(piece, outward) for piece in near_in]
         far_in, near_out = lax.optimization_barrier((plan.along(mate, middle), near_out))
         far_out = plan.along(far_in, outward)
         near_packs[1:], near_in = lax.optimization_barrier((near_packs[1:], near_in))
-        weights = [(near_in, near_out), (far_in, far_out), (mate,), (own_weights,)]
+        weights = [
+            [(piece, dy, None) for dy, piece in enumerate(weight_parts)],
+            [(piece, dy, 0) for dy, piece in enumerate(near_in)]
+            + [(piece, dy, 1) for dy, piece in enumerate(near_out)],
+            [(far_in, 0, 0), (far_out, 0, 1)],
+            [(mate, 0, None)],
+        ]
         which = jnp.where(inner, 0, 1)
     else:
-        steps = [k % plan.planes for k in range(1, plan.planes + 1)]
+        steps = list(range(plan.planes))
         plane_of = (z + jnp.array(steps, jnp.int32)) % plan.planes
-        weights = [(plan.shift(own_weights, dz=-k % plan.planes),) for k in steps]
+        weights = [[(plan.shift(own_weights, dz=-k % plan.planes), 0, None)] for k in steps]
         which = z * 0
     packs = []
     for value in near_packs:
@@ -384,34 +409,21 @@
     place = place[:, None]
 
     rows_at = jnp.arange(plan.rows, dtype=jnp.int32)
-    weight_at = ((y - rows_at) % plan.rows) * head_dim
+    weight_at = (y - rows_at) % plan.rows
     expert_ids = (plane_of[:, None] * GROUP + rows_at[None, :] * 2 + c).astype(jnp.int32)
     sums, backs, done = [], [], (target, gate_line, place)
     for j in range(plan.planes):
         last = j == plan.planes - 1
         ids = jnp.concatenate([expert_ids[j], weight_at, which[None]]).astype(jnp.int32)
-        if last and plan.planes == 4:
-            near_sum = sums[0] + plan.along(sums[0], inward)
-            done = (done, near_sum)
         ids, done = lax.optimization_barrier((ids, done))
         if j == 0:
             target, gate_line, place = done
-        kind = jnp.float32 if last else jnp.bfloat16
+        kind = jnp.bfloat16 if j else jnp.float32
         part, *back = slot_work(plan, ids, packs, weights[j], kind, backs if last else ())
         sums.append(part)
         backs = back if last else backs + back
         done = back[0]
 
-    if plan.planes == 4:
-        far_sum = sums[1] + plan.along(sums[1], inward)
-        received = [
-            plan.along(sums[2], mates),
-            plan.along(near_sum, middle),
-            plan.along(far_sum, across),
-        ]
-        backs, _ = lax.optimization_barrier((backs, far_sum))
-    else:
-        received = [plan.shift(sums[j], dz=steps[j]) for j in range(plan.planes - 1)]
     own_rows = head_dim // plan.dp
     starts = jnp.stack(
         [
@@ -419,26 +431,43 @@
             for dx, dy in plan.splits_list()
         ]
     ).astype(jnp.int32)
-    pieces = sum_work(plan, starts, sums[-1], received)
-    target, _ = lax.optimization_barrier((target, pieces[0]))
+    far_pieces = []
+    if plan.planes == 4:
+        near_sum = sums[1] + plan.along(sums[1], inward)
+        backs, near_sum = lax.optimization_barrier((backs, near_sum))
+        received = [plan.along(sums[3], mates), plan.along(near_sum, middle)]
+        far_pieces = sum_work(plan, starts, [sums[2], plan.along(sums[2], inward)], jnp.bfloat16)
+    else:
+        received = [plan.shift(sums[j], dz=steps[j]) for j in range(1, plan.planes)]
+    pieces = sum_work(plan, starts, [sums[0]] + received, jnp.float32)
+    sent = (pieces, far_pieces)
+    if plan.planes == 4:
+        far_pieces = [
+            plan.along(piece, across, dx, dy)
+            for piece, (dx, dy) in zip(far_pieces, plan.splits_list())
+        ]
     pieces = [
         plan.shift(piece, dx=dx, dy=dy) for piece, (dx, dy) in zip(pieces, plan.splits_list())
     ]
+
+    parts = [
+        plan.shift(rows, dx=-dx % plan.dp, dy=-dy % plan.rows)
+        for rows, (dx, dy) in zip(backs, plan.splits_list())
+    ]
+    half = len(far_pieces) // 2
+    parts, far_pieces[:half], _ = lax.optimization_barrier((parts, far_pieces[:half], sent))
+    own, other = merge_work(plan, parts)
+    other = plan.shift(other, dc=1)
+    other, far_pieces = lax.optimization_barrier((other, far_pieces))
+    grad_head, grad_gate = final_work(plan, target, gate_line, place, own, other)
+
     starts = jnp.stack(
         [
             (((x - dx) % plan.dp) * plan.rows + (y - dy) % plan.rows) * plan.part
             for dx, dy in plan.splits_list()
         ]
     ).astype(jnp.int32)
-    grad_proj = layout_work(plan, starts, pieces)
-
-    parts = []
-    for dx, dy in plan.splits_list():
-        for dc in range(2):
-            parts.append(
-                plan.shift(backs[len(parts)], dx=-dx % plan.dp, dy=-dy % plan.rows, dc=dc)
-            )
-    grad_head, grad_gate = final_work(plan, target, gate_line, place, parts)
+    grad_proj = layout_work(plan, starts, pieces + far_pieces)
     return (
         grad_head.reshape(tokens, top, head_dim),
         grad_gate.reshape(tokens, top).astype(jnp.bfloat16),

time: 121 us -> 145 us (1.20)
  starting transfers between devices: 34.1 us -> 44.3 us
  local copies, waits for them, and re-layouts: 7.83 us -> 16 us
  Pallas kernels: 31.8 us -> 36.4 us
  other arithmetic: 7.68 us -> 11.2 us
  waiting for transfers between devices: 35.4 us -> 33.8 us
    ppermute x10 -> x15, waiting for transfers between devices: 26.2 us -> 14.6 us  [along(): return lax.ppermute(value, AXES, out)]
    ppermute x18 -> x15, waiting for transfers between devices: 9.25 us -> 19.2 us  [shift(): return lax.ppermute(value, AXES, self.pairs(**by))]
    ppermute x10 -> x15, starting transfers between devices: 18.3 us -> 27.9 us  [along(): return lax.ppermute(value, AXES, out)]
    convert_element_type x3, local copies, waits for them, and re-layouts: 0.29 us -> 4.45 us  [local(): place = jnp.sum(hot.reshape(tokens, top, plan.experts) * places[:, None,...]
    eq x2, local copies, waits for them, and re-layouts: 0.13 us -> 2.88 us  [local(): routes[:, None] == jnp.arange(plan.experts, dtype=jnp.int32)[None, :]]
    pallas_call x4 -> x5, Pallas kernels: 24.7 us -> 27.4 us  [the longest x4 25.2 us: slot_work(): pl.pallas_call(functools.partial(slot_kernel, plan, [rows for _, *rows in...]
    pallas_call x1 -> x2, Pallas kernels: 2.66 us -> 4.5 us  [sum_work(): pl.pallas_call(functools.partial(sum_kernel, plan), out_shape=tuple((jax....]
    ppermute x18 -> x15, starting transfers between devices: 15.8 us -> 16.4 us  [shift(): return lax.ppermute(value, AXES, self.pairs(**by))]
  transfers between devices with their start and end apart: 28 -> 30, of which waited for: 10 -> 10; matrix products, arithmetic and copies ran while one was open for 10% -> 14% of each run, Pallas kernels for 25% -> 22%
where the time goes in v5:
time: 145 us; the launch traced here: 144 us
  starting transfers between devices  44.3 us (31%)
  Pallas kernels  36.4 us (25%)
  waiting for transfers between devices  33.8 us (23%)
  local copies, waits for them, and re-layouts  16 us (11%)
  other arithmetic  11.2 us (8%)
    ppermute x15, starting transfers between devices, along(): return lax.ppermute(value, AXES, out)  27.9 us
    pallas_call x4, Pallas kernels, slot_work(): pl.pallas_call(functools.partial(slot_kernel, plan, [rows for _, *rows in...  25.2 us
    ppermute x15, waiting for transfers between devices, shift(): return lax.ppermute(value, AXES, self.pairs(**by))  19.2 us
    ppermute x15, starting transfers between devices, shift(): return lax.ppermute(value, AXES, self.pairs(**by))  16.4 us
    ppermute x15, waiting for transfers between devices, along(): return lax.ppermute(value, AXES, out)  14.6 us
    unnamed x61, local copies, waits for them, and re-layouts  5.56 us
    pallas_call x2, Pallas kernels, sum_work(): pl.pallas_call(functools.partial(sum_kernel, plan), out_shape=tuple((jax....  4.5 us
    convert_element_type x3, local copies, waits for them, and re-layouts, local(): place = jnp.sum(hot.reshape(tokens, top, plan.experts) * places[:, None,...  4.45 us
  transfers between devices with their start and end apart: 30, of which 10 were waited for; matrix products, arithmetic and copies ran while one was open for 14% of the time, Pallas kernels for 22%

profile of v5, /device:TPU:0, one launch (start us, length us, event | category | flops | bytes accessed | tf_op | source)
XLA Modules:
  0.0 144.0 jit_solution(12238864465858268644)
XLA Ops:
  0.8 1.1 dynamic-slice_bitcast_fusion
  1.8 1.0 copy.26
  3.6 1.3 fusion.3
  4.8 3.0 %collective-permute-start.2 = (bf16[128,2176]{1,0:T(8,128)(2,1)}, bf16[128,2176]{1,0:T(8,128)(2,1)S(1)}, u32[]{:S(2)}, u32[]{:S(2)}) collective-permute-start(bf16[128,2176]{1,0:T(8,128)(2,1)} %get-tuple-element.141), channel_id=1, source_target_pairs={{0,2},{1,3},{2,0},{3,1},{4,6},{5,7},{6,4},{7,5},{8,10},{9,11},{10,... | collective-permute-start | bytes 1671176 | tf_op jit(solution)/shard_map/ppermute | solution.py:51
  7.8 1.5 %collective-permute-start.3 = (bf16[128,2176]{1,0:T(8,128)(2,1)}, bf16[128,2176]{1,0:T(8,128)(2,1)S(1)}, u32[]{:S(2)}, u32[]{:S(2)}) collective-permute-start(bf16[128,2176]{1,0:T(8,128)(2,1)} %get-tuple-element.142), channel_id=1, source_target_pairs={{0,16},{1,17},{2,18},{3,19},{4,20},{5,21},{6,22},{7,23},{8,24},{9,... | collective-permute-start | bytes 1671176 | tf_op jit(solution)/shard_map/ppermute | solution.py:51
  9.8 0.7 collective-permute-start.5
  10.6 0.6 broadcast_multiply_fusion
  11.8 14.5 %collective-permute-done.refs_9_ = bf16[128,1024]{1,0:T(8,128)(2,1)S(1)} collective-permute-done((bf16[128,1024]{1,0:T(8,128)(2,1)S(1)}, bf16[128,1024]{1,0:T(8,128)(2,1)S(1)}, u32[]{:S(2)}, u32[]{:S(2)}) %collective-permute-start) | collective-permute-done | bytes 262176 | tf_op jit(solution)/shard_map/ppermute | solution.py:51
  26.3 0.8 pad_maximum_fusion.5
  27.1 1.8 %collective-permute-start.10 = (bf16[256,1024]{1,0:T(8,128)(2,1)}, bf16[256,1024]{1,0:T(8,128)(2,1)S(1)}, u32[]{:S(2)}, u32[]{:S(2)}) collective-permute-start(bf16[256,1024]{1,0:T(8,128)(2,1)} %pad_maximum_fusion.5), channel_id=1, source_target_pairs={{0,4},{1,5},{2,6},{3,7},{4,0},{5,1},{6,2},{7,3},{8,12},{9,13},{10,... | collective-permute-start | bytes 1572872 | tf_op jit(solution)/shard_map/ppermute | solution.py:61
  29.0 1.4 collective-permute-start.6
  31.0 0.7 reshape.86
  31.7 2.4 %collective-permute-start.4 = (bf16[128,2176]{1,0:T(8,128)(2,1)}, bf16[128,2176]{1,0:T(8,128)(2,1)S(1)}, u32[]{:S(2)}, u32[]{:S(2)}) collective-permute-start(bf16[128,2176]{1,0:T(8,128)(2,1)} %get-tuple-element.140), channel_id=1, source_target_pairs={{0,18},{1,19},{2,16},{3,17},{4,22},{5,23},{6,20},{7,21},{8,26},{9,... | collective-permute-start | bytes 1671176 | tf_op jit(solution)/shard_map/ppermute | solution.py:51
  34.1 0.7 add_add_fusion.3.ids
  34.8 1.4 eq.74
  36.2 1.5 %copy.17 = s32[128,8]{0,1:T(8,128)} copy(s32[128,8]{1,0:T(8,128)} %eq.74) | data formatting | bytes 8192 | tf_op jit(solution)/shard_map/eq | solution.py:393
  37.7 0.7 convert_reduce_fusion.1
  38.4 1.3 collective-permute-start.12
  39.7 1.3 collective-permute-start.13
  41.1 1.5 %collective-permute-start.11 = (bf16[256,1024]{1,0:T(8,128)(2,1)S(1)}, bf16[256,1024]{1,0:T(8,128)(2,1)}, u32[]{:S(2)}, u32[]{:S(2)}) collective-permute-start(bf16[256,1024]{1,0:T(8,128)(2,1)S(1)} %collective-permute-done.10.refs_8_), channel_id=1, source_target_pairs={{4,8},{5,9},{6,10},{7,11},{8,4},{9,5},{10,6},{11,7},{20,24},{21,25... | collective-permute-start | bytes 1572872 | tf_op jit(solution)/shard_map/ppermute | solution.py:61
  42.5 0.9 fusion.4
  43.4 0.7 select_reduce_fusion
  44.1 0.6 convert_element_type.36
  44.7 1.4 copy.18
  46.1 1.5 %convert_element_type.37 = s32[1024]{0:T(1024)} reshape(s32[128,8]{1,0:T(8,128)} %copy.18) | data formatting | bytes 8192 | tf_op jit(solution)/shard_map/convert_element_type | solution.py:399
  47.6 1.5 %convert_element_type.38 = s32[1024,1]{0,1:T(1,128)} reshape(s32[128,8]{1,0:T(8,128)} %copy.18) | data formatting | bytes 8192 | tf_op jit(solution)/shard_map/convert_element_type | solution.py:399
  49.7 1.1 collective-permute-done.12.refs_10_
  50.7 3.0 %collective-permute-done.13.refs_11_ = bf16[128,1024]{1,0:T(8,128)(2,1)} collective-permute-done((bf16[128,1024]{1,0:T(8,128)(2,1)}, bf16[128,1024]{1,0:T(8,128)(2,1)}, u32[]{:S(2)}, u32[]{:S(2)}) %collective-permute-start.13) | collective-permute-done | bytes 262176 | tf_op jit(solution)/shard_map/ppermute | solution.py:61
  53.7 0.7 add_select_fusion.2
  54.4 0.7 select_reduce_fusion.1
  55.1 1.3 collective-permute-start.14
  56.4 1.3 add_add_fusion
  57.7 5.7 %shard_map.76 = (f32[256,1024]{1,0:T(8,128)S(1)}, bf16[8,160,128]{2,1,0:T(8,128)(2,1)S(1)}) custom-call(s32[5]{0:T(128)S(1)} %add_add_fusion.3.ids, bf16[128,2176]{1,0:T(8,128)(2,1)S(1)} %fusion.refs_0_, bf16[128,2176]{1,0:T(8,128)(2,1)S(1)} %collective-permute-done.1.refs_1_, bf16[128,2176]{1,0:T(8,128)(2,1)S(1)} %collective-permute-done.2.refs_2_, ...), custom_call_target="tpu_custom_call" | custom-call | tf_op jit(solution)/shard_map/pallas_call | solution.py:206
  63.5 1.0 copy-done
  64.5 6.3 %shard_map.77 = (bf16[256,1024]{1,0:T(8,128)(2,1)S(1)}, bf16[8,160,128]{2,1,0:T(8,128)(2,1)S(1)}) custom-call(s32[5]{0:T(128)S(1)} %get-tuple-element.77.ids, bf16[128,2176]{1,0:T(8,128)(2,1)S(1)} %fusion.refs_0_, bf16[128,2176]{1,0:T(8,128)(2,1)S(1)} %collective-permute-done.1.refs_1_, bf16[128,2176]{1,0:T(8,128)(2,1)S(1)} %collective-permute-done.2.refs_2_, ...), custom_call_target="tpu_custom_call" | custom-call | tf_op jit(solution)/shard_map/pallas_call | solution.py:206
  70.8 6.9 %collective-permute-start.15 = (bf16[256,1024]{1,0:T(8,128)(2,1)S(1)}, bf16[256,1024]{1,0:T(8,128)(2,1)S(1)}, u32[]{:S(2)}, u32[]{:S(2)}) collective-permute-start(bf16[256,1024]{1,0:T(8,128)(2,1)S(1)} %get-tuple-element.91), channel_id=1, source_target_pairs={{0,4},{1,5},{2,6},{3,7},{12,8},{13,9},{14,10},{15,11},{16,20},{17,... | collective-permute-start | bytes 1572872 | tf_op jit(solution)/shard_map/ppermute | solution.py:61
  77.8 6.5 %shard_map.78 = (bf16[256,1024]{1,0:T(8,128)(2,1)S(1)}, bf16[8,160,128]{2,1,0:T(8,128)(2,1)S(1)}) custom-call(s32[5]{0:T(128)S(1)} %get-tuple-element.83.ids, bf16[128,2176]{1,0:T(8,128)(2,1)S(1)} %fusion.refs_0_, bf16[128,2176]{1,0:T(8,128)(2,1)S(1)} %collective-permute-done.1.refs_1_, bf16[128,2176]{1,0:T(8,128)(2,1)S(1)} %collective-permute-done.2.refs_2_, ...), custom_call_target="tpu_custom_call" | custom-call | tf_op jit(solution)/shard_map/pallas_call | solution.py:206
  84.2 1.3 collective-permute-start.19
  85.6 4.5 %collective-permute-done.15 = bf16[256,1024]{1,0:T(8,128)(2,1)S(1)} collective-permute-done((bf16[256,1024]{1,0:T(8,128)(2,1)S(1)}, bf16[256,1024]{1,0:T(8,128)(2,1)S(1)}, u32[]{:S(2)}, u32[]{:S(2)}) %collective-permute-start.15) | collective-permute-done | bytes 524320 | tf_op jit(solution)/shard_map/ppermute | solution.py:61
  90.1 1.0 add.223
  91.1 6.7 %shard_map.79 = (bf16[256,1024]{1,0:T(8,128)(2,1)S(1)}, bf16[1280,128]{1,0:T(8,128)(2,1)S(1)}, bf16[1280,128]{1,0:T(8,128)(2,1)}, bf16[1280,128]{1,0:T(8,128)(2,1)}, bf16[1280,128]{1,0:T(8,128)(2,1)}) custom-call(s32[5]{0:T(128)S(1)} %get-tuple-element.86.ids, bf16[128,2176]{1,0:T(8,128)(2,1)S(1)} %fusion.refs_0_, ...), custom_call_target="tpu_custom_call" | custom-call | tf_op jit(solution)/shard_map/pallas_call | solution.py:206
  97.8 0.7 copy-done.2
  98.5 0.7 collective-permute-start.23
  99.2 4.3 %collective-permute-start.22 = (bf16[256,1024]{1,0:T(8,128)(2,1)S(1)}, bf16[256,1024]{1,0:T(8,128)(2,1)S(1)}, u32[]{:S(2)}, u32[]{:S(2)}) collective-permute-start(bf16[256,1024]{1,0:T(8,128)(2,1)S(1)} %get-tuple-element.100), channel_id=1, source_target_pairs={{0,4},{1,5},{2,6},{3,7},{4,0},{5,1},{6,2},{7,3},{8,12},{9,13},{10,... | collective-permute-start | bytes 1572872 | tf_op jit(solution)/shard_map/ppermute | solution.py:61
  104.4 0.8 copy-done.7
  105.2 2.5 %collective-permute-start.18 = (bf16[1280,128]{1,0:T(8,128)(2,1)}, bf16[1280,128]{1,0:T(8,128)(2,1)S(1)}, u32[]{:S(2)}, u32[]{:S(2)}) collective-permute-start(bf16[1280,128]{1,0:T(8,128)(2,1)} %get-tuple-element.95), channel_id=1, source_target_pairs={{0,18},{1,19},{2,16},{3,17},{4,22},{5,23},{6,20},{7,21},{8,26},{9,... | collective-permute-start | bytes 983048 | tf_op jit(solution)/shard_map/ppermute | solution.py:51
  108.3 2.0 %shard_map.80 = (bf16[64,1024]{1,0:T(8,128)(2,1)}, bf16[64,1024]{1,0:T(8,128)(2,1)}, bf16[64,1024]{1,0:T(8,128)(2,1)}, bf16[64,1024]{1,0:T(8,128)(2,1)}) custom-call(s32[4]{0:T(128)} %pad_add_fusion.1.starts, bf16[256,1024]{1,0:T(8,128)(2,1)} %copy-done.1, bf16[256,1024]{1,0:T(8,128)(2,1)} %copy-done.7), custom_call_target="tpu_custom_call" | custom-call | tf_op jit(solution)/shard_map/pallas_call | solution.py:235
  110.4 1.3 collective-permute-start.20
  111.7 1.3 collective-permute-start.21
  113.0 2.5 %shard_map.81 = (f32[64,1024]{1,0:T(8,128)}, bf16[64,1024]{1,0:T(8,128)(2,1)}, bf16[64,1024]{1,0:T(8,128)(2,1)}, bf16[64,1024]{1,0:T(8,128)(2,1)}) custom-call(s32[4]{0:T(128)} %pad_add_fusion.1.starts, f32[256,1024]{1,0:T(8,128)} %copy-done, bf16[256,1024]{1,0:T(8,128)(2,1)} %copy-done.6, bf16[256,1024]{1,0:T(8,128)(2,1)} %copy-done.5), custom_call_target="tpu_custom_call" | custom-call | tf_op jit(solution)/shard_map/pallas_call | solution.py:235
  115.5 2.4 %collective-permute-done.18.refs_3_ = bf16[1280,128]{1,0:T(8,128)(2,1)S(1)} collective-permute-done((bf16[1280,128]{1,0:T(8,128)(2,1)}, bf16[1280,128]{1,0:T(8,128)(2,1)S(1)}, u32[]{:S(2)}, u32[]{:S(2)}) %collective-permute-start.18) | collective-permute-done | bytes 327712 | tf_op jit(solution)/shard_map/ppermute | solution.py:51
  118.4 2.2 %collective-permute-done.21.refs_5_ = bf16[64,1024]{1,0:T(8,128)(2,1)S(1)} collective-permute-done((bf16[64,1024]{1,0:T(8,128)(2,1)}, bf16[64,1024]{1,0:T(8,128)(2,1)S(1)}, u32[]{:S(2)}, u32[]{:S(2)}) %collective-permute-start.21) | collective-permute-done | bytes 131104 | tf_op jit(solution)/shard_map/ppermute | solution.py:61
  120.6 2.1 %shard_map.82 = (bf16[640,128]{1,0:T(8,128)(2,1)}, bf16[640,128]{1,0:T(8,128)(2,1)}) custom-call(bf16[1280,128]{1,0:T(8,128)(2,1)} %copy-done.2, bf16[1280,128]{1,0:T(8,128)(2,1)} %copy-done.8, bf16[1280,128]{1,0:T(8,128)(2,1)} %copy-done.9, bf16[1280,128]{1,0:T(8,128)(2,1)} %copy-done.10), custom_call_target="tpu_custom_call" | custom-call | tf_op jit(solution)/shard_map/pallas_call | solution.py:282
  122.8 1.4 collective-permute-start.25
  124.3 1.5 %collective-permute-start.26 = (bf16[64,1024]{1,0:T(8,128)(2,1)S(1)}, bf16[64,1024]{1,0:T(8,128)(2,1)S(1)}, u32[]{:S(2)}, u32[]{:S(2)}) collective-permute-start(bf16[64,1024]{1,0:T(8,128)(2,1)S(1)} %copy-done.27), channel_id=1, source_target_pairs={{4,30},{5,31},{6,28},{7,29},{8,18},{9,19},{10,16},{11,17},{20,14},... | collective-permute-start | bytes 393224 | tf_op jit(solution)/shard_map/ppermute | solution.py:61
  127.2 0.7 collective-permute-start.27
  127.9 2.0 %collective-permute-start.28 = (bf16[64,1024]{1,0:T(8,128)(2,1)S(1)}, bf16[64,1024]{1,0:T(8,128)(2,1)S(1)}, u32[]{:S(2)}, u32[]{:S(2)}) collective-permute-start(bf16[64,1024]{1,0:T(8,128)(2,1)S(1)} %copy-done.25), channel_id=1, source_target_pairs={{0,16},{1,17},{2,18},{3,19},{4,20},{5,21},{6,22},{7,23},{8,24},{9,... | collective-permute-start | bytes 393224 | tf_op jit(solution)/shard_map/ppermute | solution.py:51
  129.9 3.1 %collective-permute-done.25.refs_6_ = bf16[64,1024]{1,0:T(8,128)(2,1)S(1)} collective-permute-done((bf16[64,1024]{1,0:T(8,128)(2,1)S(1)}, bf16[64,1024]{1,0:T(8,128)(2,1)S(1)}, u32[]{:S(2)}, u32[]{:S(2)}) %collective-permute-start.25) | collective-permute-done | bytes 131104 | tf_op jit(solution)/shard_map/ppermute | solution.py:61
  133.1 2.1 %collective-permute-start.29 = (bf16[64,1024]{1,0:T(8,128)(2,1)S(1)}, bf16[64,1024]{1,0:T(8,128)(2,1)S(1)}, u32[]{:S(2)}, u32[]{:S(2)}) collective-permute-start(bf16[64,1024]{1,0:T(8,128)(2,1)S(1)} %copy-done.24), channel_id=1, source_target_pairs={{0,18},{1,19},{2,16},{3,17},{4,22},{5,23},{6,20},{7,21},{8,26},{9,... | collective-permute-start | bytes 393224 | tf_op jit(solution)/shard_map/ppermute | solution.py:51
  135.5 2.2 %shard_map.83 = (bf16[1024,128]{1,0:T(8,128)(2,1)}, f32[1024,1]{1,0:T(8,128)S(1)}) custom-call(s32[1024,1]{1,0:T(8,128)S(1)} %copy.20.target_ref, s32[1024,1]{1,0:T(8,128)S(1)} %copy.21.gate_ref, s32[1024,1]{1,0:T(8,128)S(1)} %copy.22.place_ref, bf16[640,128]{1,0:T(8,128)(2,1)S(1)} %copy-done.3, bf16[640,128]{1,0:T(8,128)(2,1)S(1)} %collective-permute-done.24.other_ref), custom_call_target="tpu_custom_call" | custom-call | tf_op jit(solution)/shard_map/pallas_call | solution.py:313
  138.0 0.7 copy.23
  138.7 2.2 %collective-permute-done.29.refs_3_ = bf16[64,1024]{1,0:T(8,128)(2,1)S(1)} collective-permute-done((bf16[64,1024]{1,0:T(8,128)(2,1)S(1)}, bf16[64,1024]{1,0:T(8,128)(2,1)S(1)}, u32[]{:S(2)}, u32[]{:S(2)}) %collective-permute-start.29) | collective-permute-done | bytes 131104 | tf_op jit(solution)/shard_map/ppermute | solution.py:51
  140.9 0.7 copy-done.17
  141.6 2.4 %shard_map.84 = f32[64,4096]{1,0:T(8,128)} custom-call(s32[4]{0:T(128)} %pad_add_fusion.2.starts, f32[64,1024]{1,0:T(8,128)} %get-tuple-element.102.refs_0_, bf16[64,1024]{1,0:T(8,128)(2,1)} %copy-done.15, bf16[64,1024]{1,0:T(8,128)(2,1)} %copy-done.16, bf16[64,1024]{1,0:T(8,128)(2,1)} %copy-done.17, bf16[64,1024]{1,0:T(8,128)(2,1)} %copy-done.11, ...), custom_call_target="tpu_custom_call" | custom-call | tf_op jit(solution)/shard_map/pallas_call | solution.py:260
  (102 shorter events, 7.0 us)
Async XLA Ops:
  0.6 2.3 %copy-start.4 = (bf16[128,4096]{1,0:T(8,128)(2,1)S(1)}, bf16[128,4096]{1,0:T(8,128)(2,1)}, u32[]{:S(2)}) copy-start(bf16[128,4096]{1,0:T(8,128)(2,1)} %param.6) | copy-start | bytes 3145732
  0.6 2.2 %copy-start.21 = (s32[128,8]{0,1:T(8,128)S(1)}, s32[128,8]{0,1:T(8,128)}, u32[]{:S(2)}) copy-start(s32[128,8]{0,1:T(8,128)} %param.8) | copy-start | bytes 12292
  2.9 0.7 copy-start.22
  4.8 34.9 %collective-permute-start.2 = (bf16[128,2176]{1,0:T(8,128)(2,1)}, bf16[128,2176]{1,0:T(8,128)(2,1)S(1)}, u32[]{:S(2)}, u32[]{:S(2)}) collective-permute-start(bf16[128,2176]{1,0:T(8,128)(2,1)} %get-tuple-element.141), channel_id=1, source_target_pairs={{0,2},{1,3},{2,0},{3,1},{4,6},{5,7},{6,4},{7,5},{8,10},{9,11},{10,... | collective-permute-start | bytes 1671176 | tf_op jit(solution)/shard_map/ppermute | solution.py:51
  7.8 41.3 %collective-permute-start.3 = (bf16[128,2176]{1,0:T(8,128)(2,1)}, bf16[128,2176]{1,0:T(8,128)(2,1)S(1)}, u32[]{:S(2)}, u32[]{:S(2)}) collective-permute-start(bf16[128,2176]{1,0:T(8,128)(2,1)} %get-tuple-element.142), channel_id=1, source_target_pairs={{0,16},{1,17},{2,18},{3,19},{4,20},{5,21},{6,22},{7,23},{8,24},{9,... | collective-permute-start | bytes 1671176 | tf_op jit(solution)/shard_map/ppermute | solution.py:51
  9.3 17.0 %collective-permute-start = (bf16[128,1024]{1,0:T(8,128)(2,1)S(1)}, bf16[128,1024]{1,0:T(8,128)(2,1)S(1)}, u32[]{:S(2)}, u32[]{:S(2)}) collective-permute-start(bf16[128,1024]{1,0:T(8,128)(2,1)S(1)} %get-tuple-element.65), channel_id=1, source_target_pairs={{0,2},{1,3},{2,0},{3,1},{4,6},{5,7},{6,4},{7,5},{8,10},{9,11},{10,... | collective-permute-start | bytes 786440 | tf_op jit(solution)/shard_map/ppermute | solution.py:51
  9.8 21.8 %collective-permute-start.5 = (bf16[128,1024]{1,0:T(8,128)(2,1)S(1)}, bf16[128,1024]{1,0:T(8,128)(2,1)S(1)}, u32[]{:S(2)}, u32[]{:S(2)}) collective-permute-start(bf16[128,1024]{1,0:T(8,128)(2,1)S(1)} %get-tuple-element.64.refs_8_), channel_id=1, source_target_pairs={{4,8},{5,9},{6,10},{7,11},{8,4},{9,5},{10,6},{11,7},{20,24},{21,25... | collective-permute-start | bytes 786440 | tf_op jit(solution)/shard_map/ppermute | solution.py:61
  27.1 14.0 %collective-permute-start.10 = (bf16[256,1024]{1,0:T(8,128)(2,1)}, bf16[256,1024]{1,0:T(8,128)(2,1)S(1)}, u32[]{:S(2)}, u32[]{:S(2)}) collective-permute-start(bf16[256,1024]{1,0:T(8,128)(2,1)} %pad_maximum_fusion.5), channel_id=1, source_target_pairs={{0,4},{1,5},{2,6},{3,7},{4,0},{5,1},{6,2},{7,3},{8,12},{9,13},{10,... | collective-permute-start | bytes 1572872 | tf_op jit(solution)/shard_map/ppermute | solution.py:61
  28.9 1.5 %copy-start.23 = (s32[2]{0:T(128)}, s32[2]{0:T(128)S(1)}, u32[]{:S(2)}) copy-start(s32[2]{0:T(128)S(1)} %and_select_fusion) | copy-start | bytes 28
  29.0 9.4 %collective-permute-start.6 = (bf16[128,1024]{1,0:T(8,128)(2,1)S(1)}, bf16[128,1024]{1,0:T(8,128)(2,1)}, u32[]{:S(2)}, u32[]{:S(2)}) collective-permute-start(bf16[128,1024]{1,0:T(8,128)(2,1)S(1)} %collective-permute-done.refs_9_), channel_id=1, source_target_pairs={{4,8},{5,9},{6,10},{7,11},{8,4},{9,5},{10,6},{11,7},{20,24},{21,25... | collective-permute-start | bytes 786440 | tf_op jit(solution)/shard_map/ppermute | solution.py:61
  31.7 17.5 %collective-permute-start.4 = (bf16[128,2176]{1,0:T(8,128)(2,1)}, bf16[128,2176]{1,0:T(8,128)(2,1)S(1)}, u32[]{:S(2)}, u32[]{:S(2)}) collective-permute-start(bf16[128,2176]{1,0:T(8,128)(2,1)} %get-tuple-element.140), channel_id=1, source_target_pairs={{0,18},{1,19},{2,16},{3,17},{4,22},{5,23},{6,20},{7,21},{8,26},{9,... | collective-permute-start | bytes 1671176 | tf_op jit(solution)/shard_map/ppermute | solution.py:51
  38.4 12.3 %collective-permute-start.12 = (bf16[128,1024]{1,0:T(8,128)(2,1)S(1)}, bf16[128,1024]{1,0:T(8,128)(2,1)}, u32[]{:S(2)}, u32[]{:S(2)}) collective-permute-start(bf16[128,1024]{1,0:T(8,128)(2,1)S(1)} %collective-permute-done.5.refs_8_), channel_id=1, source_target_pairs={{4,0},{5,1},{6,2},{7,3},{8,12},{9,13},{10,14},{11,15},{20,16},{21,... | collective-permute-start | bytes 786440 | tf_op jit(solution)/shard_map/ppermute | solution.py:61
  39.7 14.0 %collective-permute-start.13 = (bf16[128,1024]{1,0:T(8,128)(2,1)}, bf16[128,1024]{1,0:T(8,128)(2,1)}, u32[]{:S(2)}, u32[]{:S(2)}) collective-permute-start(bf16[128,1024]{1,0:T(8,128)(2,1)} %collective-permute-done.6.refs_9_), channel_id=1, source_target_pairs={{4,0},{5,1},{6,2},{7,3},{8,12},{9,13},{10,14},{11,15},{20,16},{21,... | collective-permute-start | bytes 786440 | tf_op jit(solution)/shard_map/ppermute | solution.py:61
  41.1 14.0 %collective-permute-start.11 = (bf16[256,1024]{1,0:T(8,128)(2,1)S(1)}, bf16[256,1024]{1,0:T(8,128)(2,1)}, u32[]{:S(2)}, u32[]{:S(2)}) collective-permute-start(bf16[256,1024]{1,0:T(8,128)(2,1)S(1)} %collective-permute-done.10.refs_8_), channel_id=1, source_target_pairs={{4,8},{5,9},{6,10},{7,11},{8,4},{9,5},{10,6},{11,7},{20,24},{21,25... | collective-permute-start | bytes 1572872 | tf_op jit(solution)/shard_map/ppermute | solution.py:61
  49.2 8.6 %collective-permute-start.1 = (bf16[128,2176]{1,0:T(8,128)(2,1)S(1)}, bf16[128,2176]{1,0:T(8,128)(2,1)S(1)}, u32[]{:S(2)}, u32[]{:S(2)}) collective-permute-start(bf16[128,2176]{1,0:T(8,128)(2,1)S(1)} %fusion.refs_0_), channel_id=1, source_target_pairs={{0,1},{1,0},{2,3},{3,2},{4,5},{5,4},{6,7},{7,6},{8,9},{9,8},{10,11... | collective-permute-start | bytes 1671176 | tf_op jit(solution)/shard_map/ppermute | solution.py:51
  49.2 8.5 %collective-permute-start.7 = (bf16[128,2176]{1,0:T(8,128)(2,1)S(1)}, bf16[128,2176]{1,0:T(8,128)(2,1)S(1)}, u32[]{:S(2)}, u32[]{:S(2)}) collective-permute-start(bf16[128,2176]{1,0:T(8,128)(2,1)S(1)} %collective-permute-done.2.refs_2_), channel_id=1, source_target_pairs={{0,1},{1,0},{2,3},{3,2},{4,5},{5,4},{6,7},{7,6},{8,9},{9,8},{10,11... | collective-permute-start | bytes 1671176 | tf_op jit(solution)/shard_map/ppermute | solution.py:51
  50.7 7.0 %collective-permute-start.8 = (bf16[128,2176]{1,0:T(8,128)(2,1)S(1)}, bf16[128,2176]{1,0:T(8,128)(2,1)S(1)}, u32[]{:S(2)}, u32[]{:S(2)}) collective-permute-start(bf16[128,2176]{1,0:T(8,128)(2,1)S(1)} %collective-permute-done.3.refs_4_), channel_id=1, source_target_pairs={{0,1},{1,0},{2,3},{3,2},{4,5},{5,4},{6,7},{7,6},{8,9},{9,8},{10,11... | collective-permute-start | bytes 1671176 | tf_op jit(solution)/shard_map/ppermute | solution.py:51
  53.7 4.0 %collective-permute-start.9 = (bf16[128,2176]{1,0:T(8,128)(2,1)S(1)}, bf16[128,2176]{1,0:T(8,128)(2,1)S(1)}, u32[]{:S(2)}, u32[]{:S(2)}) collective-permute-start(bf16[128,2176]{1,0:T(8,128)(2,1)S(1)} %collective-permute-done.4.refs_6_), channel_id=1, source_target_pairs={{0,1},{1,0},{2,3},{3,2},{4,5},{5,4},{6,7},{7,6},{8,9},{9,8},{10,11... | collective-permute-start | bytes 1671176 | tf_op jit(solution)/shard_map/ppermute | solution.py:51
  55.1 22.6 %collective-permute-start.14 = (bf16[256,1024]{1,0:T(8,128)(2,1)}, bf16[256,1024]{1,0:T(8,128)(2,1)S(1)}, u32[]{:S(2)}, u32[]{:S(2)}) collective-permute-start(bf16[256,1024]{1,0:T(8,128)(2,1)} %collective-permute-done.11.refs_8_), channel_id=1, source_target_pairs={{4,0},{5,1},{6,2},{7,3},{8,12},{9,13},{10,14},{11,15},{20,16},{21,... | collective-permute-start | bytes 1572872 | tf_op jit(solution)/shard_map/ppermute | solution.py:61
  63.5 1.0 copy-start
  70.8 19.3 %collective-permute-start.15 = (bf16[256,1024]{1,0:T(8,128)(2,1)S(1)}, bf16[256,1024]{1,0:T(8,128)(2,1)S(1)}, u32[]{:S(2)}, u32[]{:S(2)}) collective-permute-start(bf16[256,1024]{1,0:T(8,128)(2,1)S(1)} %get-tuple-element.91), channel_id=1, source_target_pairs={{0,4},{1,5},{2,6},{3,7},{12,8},{13,9},{14,10},{15,11},{16,20},{17,... | collective-permute-start | bytes 1572872 | tf_op jit(solution)/shard_map/ppermute | solution.py:61
  84.2 13.5 %copy-start.1 = (bf16[256,1024]{1,0:T(8,128)(2,1)}, bf16[256,1024]{1,0:T(8,128)(2,1)S(1)}, u32[]{:S(2)}) copy-start(bf16[256,1024]{1,0:T(8,128)(2,1)S(1)} %get-tuple-element.96.refs_0_) | copy-start | bytes 1572868
  84.2 20.2 %collective-permute-start.19 = (bf16[256,1024]{1,0:T(8,128)(2,1)S(1)}, bf16[256,1024]{1,0:T(8,128)(2,1)S(1)}, u32[]{:S(2)}, u32[]{:S(2)}) collective-permute-start(bf16[256,1024]{1,0:T(8,128)(2,1)S(1)} %get-tuple-element.96.refs_0_), channel_id=1, source_target_pairs={{0,4},{1,5},{2,6},{3,7},{12,8},{13,9},{14,10},{15,11},{16,20},{17,... | collective-permute-start | bytes 1572872 | tf_op jit(solution)/shard_map/ppermute | solution.py:61
  97.7 0.7 copy-start.2
  98.5 11.9 %collective-permute-start.23 = (bf16[256,1024]{1,0:T(8,128)(2,1)}, bf16[256,1024]{1,0:T(8,128)(2,1)S(1)}, u32[]{:S(2)}, u32[]{:S(2)}) collective-permute-start(bf16[256,1024]{1,0:T(8,128)(2,1)} %add.223), channel_id=1, source_target_pairs={{4,8},{5,9},{6,10},{7,11},{8,4},{9,5},{10,6},{11,7},{20,24},{21,25... | collective-permute-start | bytes 1572872 | tf_op jit(solution)/shard_map/ppermute | solution.py:61
  99.2 12.5 %collective-permute-start.22 = (bf16[256,1024]{1,0:T(8,128)(2,1)S(1)}, bf16[256,1024]{1,0:T(8,128)(2,1)S(1)}, u32[]{:S(2)}, u32[]{:S(2)}) collective-permute-start(bf16[256,1024]{1,0:T(8,128)(2,1)S(1)} %get-tuple-element.100), channel_id=1, source_target_pairs={{0,4},{1,5},{2,6},{3,7},{4,0},{5,1},{6,2},{7,3},{8,12},{9,13},{10,... | collective-permute-start | bytes 1572872 | tf_op jit(solution)/shard_map/ppermute | solution.py:61
  103.5 12.0 %collective-permute-start.16 = (bf16[1280,128]{1,0:T(8,128)(2,1)}, bf16[1280,128]{1,0:T(8,128)(2,1)S(1)}, u32[]{:S(2)}, u32[]{:S(2)}) collective-permute-start(bf16[1280,128]{1,0:T(8,128)(2,1)} %get-tuple-element.93), channel_id=1, source_target_pairs={{0,2},{1,3},{2,0},{3,1},{4,6},{5,7},{6,4},{7,5},{8,10},{9,11},{10,... | collective-permute-start | bytes 983048 | tf_op jit(solution)/shard_map/ppermute | solution.py:51
  103.9 11.6 %collective-permute-start.17 = (bf16[1280,128]{1,0:T(8,128)(2,1)}, bf16[1280,128]{1,0:T(8,128)(2,1)S(1)}, u32[]{:S(2)}, u32[]{:S(2)}) collective-permute-start(bf16[1280,128]{1,0:T(8,128)(2,1)} %get-tuple-element.94), channel_id=1, source_target_pairs={{0,16},{1,17},{2,18},{3,19},{4,20},{5,21},{6,22},{7,23},{8,24},{9,... | collective-permute-start | bytes 983048 | tf_op jit(solution)/shard_map/ppermute | solution.py:51
  104.4 0.8 copy-start.7
  105.2 12.8 %collective-permute-start.18 = (bf16[1280,128]{1,0:T(8,128)(2,1)}, bf16[1280,128]{1,0:T(8,128)(2,1)S(1)}, u32[]{:S(2)}, u32[]{:S(2)}) collective-permute-start(bf16[1280,128]{1,0:T(8,128)(2,1)} %get-tuple-element.95), channel_id=1, source_target_pairs={{0,18},{1,19},{2,16},{3,17},{4,22},{5,23},{6,20},{7,21},{8,26},{9,... | collective-permute-start | bytes 983048 | tf_op jit(solution)/shard_map/ppermute | solution.py:51
  110.4 2.6 %copy-start.5 = (bf16[256,1024]{1,0:T(8,128)(2,1)}, bf16[256,1024]{1,0:T(8,128)(2,1)S(1)}, u32[]{:S(2)}) copy-start(bf16[256,1024]{1,0:T(8,128)(2,1)S(1)} %collective-permute-done.23.refs_2_) | copy-start | bytes 1572868
  110.4 8.0 %collective-permute-start.20 = (bf16[64,1024]{1,0:T(8,128)(2,1)}, bf16[64,1024]{1,0:T(8,128)(2,1)S(1)}, u32[]{:S(2)}, u32[]{:S(2)}) collective-permute-start(bf16[64,1024]{1,0:T(8,128)(2,1)} %get-tuple-element.97), channel_id=1, source_target_pairs={{4,12},{5,13},{6,14},{7,15},{8,0},{9,1},{10,2},{11,3},{20,28},{21,... | collective-permute-start | bytes 393224 | tf_op jit(solution)/shard_map/ppermute | solution.py:61
  111.7 1.3 copy-start.6
  111.7 8.9 %collective-permute-start.21 = (bf16[64,1024]{1,0:T(8,128)(2,1)}, bf16[64,1024]{1,0:T(8,128)(2,1)S(1)}, u32[]{:S(2)}, u32[]{:S(2)}) collective-permute-start(bf16[64,1024]{1,0:T(8,128)(2,1)} %get-tuple-element.98), channel_id=1, source_target_pairs={{4,14},{5,15},{6,12},{7,13},{8,2},{9,3},{10,0},{11,1},{20,30},{21,... | collective-permute-start | bytes 393224 | tf_op jit(solution)/shard_map/ppermute | solution.py:61
  115.5 7.4 %copy-start.28 = (bf16[64,1024]{1,0:T(8,128)(2,1)S(1)}, bf16[64,1024]{1,0:T(8,128)(2,1)}, u32[]{:S(2)}) copy-start(bf16[64,1024]{1,0:T(8,128)(2,1)} %get-tuple-element.106) | copy-start | bytes 393220
  115.5 8.8 %copy-start.27 = (bf16[64,1024]{1,0:T(8,128)(2,1)S(1)}, bf16[64,1024]{1,0:T(8,128)(2,1)}, u32[]{:S(2)}) copy-start(bf16[64,1024]{1,0:T(8,128)(2,1)} %get-tuple-element.107) | copy-start | bytes 393220
  115.5 11.0 %copy-start.20 = (s32[1024]{0:T(1024)S(1)}, s32[1024]{0:T(1024)}, u32[]{:S(2)}) copy-start(s32[1024]{0:T(1024)} %get-tuple-element.144) | copy-start | bytes 12292
  115.5 11.2 %copy-start.19 = (s32[1024]{0:T(1024)S(1)}, s32[1024]{0:T(1024)}, u32[]{:S(2)}) copy-start(s32[1024]{0:T(1024)} %get-tuple-element.143) | copy-start | bytes 12292
  115.5 5.1 %copy-start.8 = (bf16[1280,128]{1,0:T(8,128)(2,1)}, bf16[1280,128]{1,0:T(8,128)(2,1)S(1)}, u32[]{:S(2)}) copy-start(bf16[1280,128]{1,0:T(8,128)(2,1)S(1)} %collective-permute-done.16.refs_1_) | copy-start | bytes 983044
  115.5 5.0 %copy-start.9 = (bf16[1280,128]{1,0:T(8,128)(2,1)}, bf16[1280,128]{1,0:T(8,128)(2,1)S(1)}, u32[]{:S(2)}) copy-start(bf16[1280,128]{1,0:T(8,128)(2,1)S(1)} %collective-permute-done.17.refs_2_) | copy-start | bytes 983044
  118.0 2.6 %copy-start.10 = (bf16[1280,128]{1,0:T(8,128)(2,1)}, bf16[1280,128]{1,0:T(8,128)(2,1)S(1)}, u32[]{:S(2)}) copy-start(bf16[1280,128]{1,0:T(8,128)(2,1)S(1)} %collective-permute-done.18.refs_3_) | copy-start | bytes 983044
  118.3 8.6 %copy-start.11 = (bf16[64,1024]{1,0:T(8,128)(2,1)}, bf16[64,1024]{1,0:T(8,128)(2,1)S(1)}, u32[]{:S(2)}) copy-start(bf16[64,1024]{1,0:T(8,128)(2,1)S(1)} %collective-permute-done.20.refs_4_) | copy-start | bytes 393220
  120.6 6.3 %copy-start.12 = (bf16[64,1024]{1,0:T(8,128)(2,1)}, bf16[64,1024]{1,0:T(8,128)(2,1)S(1)}, u32[]{:S(2)}) copy-start(bf16[64,1024]{1,0:T(8,128)(2,1)S(1)} %collective-permute-done.21.refs_5_) | copy-start | bytes 393220
  120.6 6.3 %copy-start.18 = (s32[1024,1]{0,1:T(1,128)S(1)}, s32[1024,1]{0,1:T(1,128)}, u32[]{:S(2)}) copy-start(s32[1024,1]{0,1:T(1,128)} %convert_element_type.38) | copy-start | bytes 12292
  122.7 4.4 %copy-start.26 = (bf16[64,1024]{1,0:T(8,128)(2,1)S(1)}, bf16[64,1024]{1,0:T(8,128)(2,1)}, u32[]{:S(2)}) copy-start(bf16[64,1024]{1,0:T(8,128)(2,1)} %get-tuple-element.103) | copy-start | bytes 393220
  122.7 5.2 %copy-start.25 = (bf16[64,1024]{1,0:T(8,128)(2,1)S(1)}, bf16[64,1024]{1,0:T(8,128)(2,1)}, u32[]{:S(2)}) copy-start(bf16[64,1024]{1,0:T(8,128)(2,1)} %get-tuple-element.104) | copy-start | bytes 393220
  122.7 10.3 %copy-start.24 = (bf16[64,1024]{1,0:T(8,128)(2,1)S(1)}, bf16[64,1024]{1,0:T(8,128)(2,1)}, u32[]{:S(2)}) copy-start(bf16[64,1024]{1,0:T(8,128)(2,1)} %get-tuple-element.105) | copy-start | bytes 393220
  122.7 12.8 %copy-start.3 = (bf16[640,128]{1,0:T(8,128)(2,1)S(1)}, bf16[640,128]{1,0:T(8,128)(2,1)}, u32[]{:S(2)}) copy-start(bf16[640,128]{1,0:T(8,128)(2,1)} %get-tuple-element.112.own_ref) | copy-start | bytes 491524
  122.8 12.8 %collective-permute-start.24 = (bf16[640,128]{1,0:T(8,128)(2,1)}, bf16[640,128]{1,0:T(8,128)(2,1)S(1)}, u32[]{:S(2)}, u32[]{:S(2)}) collective-permute-start(bf16[640,128]{1,0:T(8,128)(2,1)} %get-tuple-element.113), channel_id=1, source_target_pairs={{0,1},{1,0},{2,3},{3,2},{4,5},{5,4},{6,7},{7,6},{8,9},{9,8},{10,11... | collective-permute-start | bytes 491528 | tf_op jit(solution)/shard_map/ppermute | solution.py:51
  122.8 10.2 %collective-permute-start.25 = (bf16[64,1024]{1,0:T(8,128)(2,1)S(1)}, bf16[64,1024]{1,0:T(8,128)(2,1)S(1)}, u32[]{:S(2)}, u32[]{:S(2)}) collective-permute-start(bf16[64,1024]{1,0:T(8,128)(2,1)S(1)} %copy-done.28), channel_id=1, source_target_pairs={{4,28},{5,29},{6,30},{7,31},{8,16},{9,17},{10,18},{11,19},{20,12},... | collective-permute-start | bytes 393224 | tf_op jit(solution)/shard_map/ppermute | solution.py:61
  124.3 11.2 %collective-permute-start.26 = (bf16[64,1024]{1,0:T(8,128)(2,1)S(1)}, bf16[64,1024]{1,0:T(8,128)(2,1)S(1)}, u32[]{:S(2)}, u32[]{:S(2)}) collective-permute-start(bf16[64,1024]{1,0:T(8,128)(2,1)S(1)} %copy-done.27), channel_id=1, source_target_pairs={{4,30},{5,31},{6,28},{7,29},{8,18},{9,19},{10,16},{11,17},{20,14},... | collective-permute-start | bytes 393224 | tf_op jit(solution)/shard_map/ppermute | solution.py:61
  127.2 11.5 %collective-permute-start.27 = (bf16[64,1024]{1,0:T(8,128)(2,1)S(1)}, bf16[64,1024]{1,0:T(8,128)(2,1)S(1)}, u32[]{:S(2)}, u32[]{:S(2)}) collective-permute-start(bf16[64,1024]{1,0:T(8,128)(2,1)S(1)} %copy-done.26), channel_id=1, source_target_pairs={{0,2},{1,3},{2,0},{3,1},{4,6},{5,7},{6,4},{7,5},{8,10},{9,11},{10,... | collective-permute-start | bytes 393224 | tf_op jit(solution)/shard_map/ppermute | solution.py:51
  127.9 10.8 %collective-permute-start.28 = (bf16[64,1024]{1,0:T(8,128)(2,1)S(1)}, bf16[64,1024]{1,0:T(8,128)(2,1)S(1)}, u32[]{:S(2)}, u32[]{:S(2)}) collective-permute-start(bf16[64,1024]{1,0:T(8,128)(2,1)S(1)} %copy-done.25), channel_id=1, source_target_pairs={{0,16},{1,17},{2,18},{3,19},{4,20},{5,21},{6,22},{7,23},{8,24},{9,... | collective-permute-start | bytes 393224 | tf_op jit(solution)/shard_map/ppermute | solution.py:51
  133.1 4.8 %copy-start.13 = (bf16[64,1024]{1,0:T(8,128)(2,1)}, bf16[64,1024]{1,0:T(8,128)(2,1)S(1)}, u32[]{:S(2)}) copy-start(bf16[64,1024]{1,0:T(8,128)(2,1)S(1)} %collective-permute-done.25.refs_6_) | copy-start | bytes 393220
  133.1 7.8 %collective-permute-start.29 = (bf16[64,1024]{1,0:T(8,128)(2,1)S(1)}, bf16[64,1024]{1,0:T(8,128)(2,1)S(1)}, u32[]{:S(2)}, u32[]{:S(2)}) collective-permute-start(bf16[64,1024]{1,0:T(8,128)(2,1)S(1)} %copy-done.24), channel_id=1, source_target_pairs={{0,18},{1,19},{2,16},{3,17},{4,22},{5,23},{6,20},{7,21},{8,26},{9,... | collective-permute-start | bytes 393224 | tf_op jit(solution)/shard_map/ppermute | solution.py:51
  135.5 2.4 %copy-start.14 = (bf16[64,1024]{1,0:T(8,128)(2,1)}, bf16[64,1024]{1,0:T(8,128)(2,1)S(1)}, u32[]{:S(2)}) copy-start(bf16[64,1024]{1,0:T(8,128)(2,1)S(1)} %collective-permute-done.26.refs_7_) | copy-start | bytes 393220
  138.7 2.3 %copy-start.15 = (bf16[64,1024]{1,0:T(8,128)(2,1)}, bf16[64,1024]{1,0:T(8,128)(2,1)S(1)}, u32[]{:S(2)}) copy-start(bf16[64,1024]{1,0:T(8,128)(2,1)S(1)} %collective-permute-done.27.refs_1_) | copy-start | bytes 393220
  138.7 2.3 %copy-start.16 = (bf16[64,1024]{1,0:T(8,128)(2,1)}, bf16[64,1024]{1,0:T(8,128)(2,1)S(1)}, u32[]{:S(2)}) copy-start(bf16[64,1024]{1,0:T(8,128)(2,1)S(1)} %collective-permute-done.28.refs_2_) | copy-start | bytes 393220
  140.9 0.7 copy-start.17

commit v6 on v5

v6 whole, which is shorter than its diff:
```python
import functools

import jax
import jax.numpy as jnp
from jax import lax
from jax.experimental import pallas as pl
from jax.experimental.pallas import tpu as pltpu
from jax.sharding import PartitionSpec as P

soft_cap = 1.5
AXES = ("dp", "expert")
GROUP = 4
LANES = 128


class Plan:
    def __init__(self, mesh, tokens, top, head_dim, features):
        self.dp = mesh.shape["dp"]
        self.experts = mesh.shape["expert"]
        self.rows = GROUP // 2
        self.planes = self.experts // GROUP
        self.sources = self.dp * GROUP
        self.tokens, self.top, self.head_dim = tokens, top, head_dim
        self.part = features // self.dp
        self.own_rows = head_dim // self.dp
        cap = 9 * tokens * top // (8 * self.experts)
        self.cap = -(-cap // 8) * 8
        self.back = self.cap + 8
        self.width = self.part + top * head_dim + LANES

    def index(self, x, z, y, c):
        return x * self.experts + z * GROUP + y * 2 + c

    def pairs(self, dx=0, dz=0, dy=0, dc=0):
        out = []
        for x in range(self.dp):
            for z in range(self.planes):
                for y in range(self.rows):
                    for c in range(2):
                        target = self.index(
                            (x + dx) % self.dp,
                            (z + dz) % self.planes,
                            (y + dy) % self.rows,
                            c ^ dc,
                        )
                        out.append((self.index(x, z, y, c), target))
        return out

    def shift(self, value, **by):
        if not any(by.values()):
            return value
        return lax.ppermute(value, AXES, self.pairs(**by))

    def along(self, value, moves, dx=0, dy=0):
        out = []
        for x in range(self.dp):
            for a, b in moves:
                for y in range(self.rows):
                    for c in range(2):
                        target = self.index((x + dx) % self.dp, b, (y + dy) % self.rows, c)
                        out.append((self.index(x, a, y, c), target))
        return lax.ppermute(value, AXES, out)

    def info(self, x, z, y, c, plane_of, which):
        values = [((x + dx) % self.dp) * self.own_rows for dx in range(self.dp)]
        self.lanes_at = len(values)
        values += [((x - dx) % self.dp) * self.part for dx in range(self.dp)]
        self.which_at = len(values)
        values += [which]
        self.experts_at = len(values)
        values += [plane_of[j] * GROUP + y * 2 + c for j in range(self.planes)]
        self.planes_at = len(values)
        values += list(plane_of) + [y, c]
        return jnp.stack([jnp.asarray(value, jnp.int32) for value in values])

    def chips(self):
        return [(dx, dy) for dx in range(self.dp) for dy in range(self.rows)]


def slot_kernel(plan, index, where, earlier, info, *refs):
    packs, rest = refs[: plan.sources], refs[plan.sources :]
    weight_refs, rest = rest[: len(where)], rest[len(where) :]
    earlier_refs, rest = rest[:earlier], rest[earlier:]
    count = plan.sources // 2 if earlier else 1
    p_ref, back_refs, (grads, heads, weights) = rest[0], rest[1 : 1 + count], rest[1 + count :]
    tokens, cap, part, top, head_dim = plan.tokens, plan.cap, plan.part, plan.top, plan.head_dim
    pair_rows = 2 * cap
    pair_total = plan.sources // 2
    length = plan.planes * plan.back

    def put(s, slot, at, value):
        if earlier:
            start = (s % 2) * length + slot * plan.back + at
            back_refs[s // 2][pl.ds(start, value.shape[0]), :] = value
        else:
            back_refs[0][s, pl.ds(at, value.shape[0]), :] = value

    if len(where) > 1:
        for ref, kind in zip(weight_refs, where):

            @pl.when(info[plan.which_at] == kind)
            def _():
                weights[...] = ref[...]

        weight_ref = weights
    else:
        weight_ref = weight_refs[0]
    expert = info[plan.experts_at + index].astype(jnp.float32)
    row_of = lax.broadcasted_iota(jnp.int32, (cap, tokens), 0)
    diagonal = (row_of == lax.broadcasted_iota(jnp.int32, (cap, tokens), 1)).astype(jnp.float32)
    before = (
        lax.broadcasted_iota(jnp.int32, (tokens, tokens), 0)
        < lax.broadcasted_iota(jnp.int32, (tokens, tokens), 1)
    ).astype(jnp.bfloat16)
    block_row = lax.broadcasted_iota(jnp.int32, (8, LANES), 0)
    empty = jnp.zeros((cap, tokens), jnp.bfloat16)
    chunk = min(part, 512)

    masks, occupied, gate_rows = [], [], []
    for s in range(plan.sources):
        meta = packs[s][pl.ds(0, 2 * top), pl.ds(part + top * head_dim, LANES)].astype(jnp.float32)
        mask = (meta[top:] == expert).astype(jnp.float32)
        masks.append(mask)
        occupied.append(jnp.sum(mask, axis=0, keepdims=True))
        gate_rows.append(jnp.sum(mask * meta[:top], axis=0, keepdims=True))
    filled = occupied + [jnp.zeros((1, tokens), jnp.float32)] * (-plan.sources % 16)
    places = jnp.dot(
        jnp.concatenate(filled, axis=0).astype(jnp.bfloat16),
        before,
        preferred_element_type=jnp.float32,
    ).astype(jnp.int32)
    for q in range(pair_total):
        hots, gates = [], []
        for b in range(2):
            s = 2 * q + b
            hot = jnp.where(row_of == places[s : s + 1], occupied[s], 0.0)
            gates.append(jnp.sum(hot * gate_rows[s], axis=1, keepdims=True))
            hots.append(hot.astype(jnp.bfloat16))
            wide = jnp.concatenate(
                [(hot * masks[s][k : k + 1]).astype(jnp.bfloat16) for k in range(top)], axis=1
            )
            raw = jnp.concatenate(
                [packs[s][:, pl.ds(part + k * head_dim, head_dim)] for k in range(top)], axis=0
            )
            heads[pl.ds(s * cap, cap), :] = jnp.dot(
                wide, raw, preferred_element_type=jnp.float32
            ).astype(jnp.bfloat16)
        all_hots = jnp.concatenate(
            [
                jnp.concatenate([hots[0], empty], axis=1),
                jnp.concatenate([empty, hots[1]], axis=1),
            ],
            axis=0,
        )
        gate = jnp.broadcast_to(jnp.concatenate(gates, axis=0), (pair_rows, LANES))
        total = jnp.zeros((pair_rows, LANES), jnp.float32)
        rows_at = pl.ds(q * pair_rows, pair_rows)
        for start in range(0, part, chunk):
            both = jnp.concatenate(
                [packs[2 * q + b][:, pl.ds(start, chunk)] for b in range(2)], axis=0
            )
            grad = jnp.dot(all_hots, both, preferred_element_type=jnp.float32)
            pre = jnp.dot(
                heads[rows_at, :], weight_ref[:, pl.ds(start, chunk)], preferred_element_type=jnp.float32
            )
            for lane in range(0, chunk, LANES):
                grad_block = grad[:, lane : lane + LANES]
                capped = jnp.tanh(pre[:, lane : lane + LANES] * (1.0 / soft_cap))
                total = total + grad_block * capped
                grads[rows_at, pl.ds(start + lane, LANES)] = (
                    gate * grad_block * (1.0 - capped * capped)
                ).astype(jnp.bfloat16)
        for b in range(2):
            column = jnp.sum(total[b * cap : (b + 1) * cap], axis=1, keepdims=True) * soft_cap
            line = jnp.sum(diagonal * column, axis=0, keepdims=True)
            block = jnp.where(block_row == 0, line, 0.0).astype(jnp.bfloat16)
            put(2 * q + b, plan.planes - 1, cap, block)
    grad_all = grads[...]
    p_ref[...] = lax.dot_general(
        heads[...], grad_all, (((0,), (0,)), ((), ())), preferred_element_type=jnp.float32
    ).astype(p_ref.dtype)
    rows = lax.dot_general(
        grad_all, weight_ref[...], (((1,), (1,)), ((), ())), preferred_element_type=jnp.float32
    ).astype(jnp.bfloat16)
    for s in range(plan.sources):
        put(s, plan.planes - 1, 0, rows[s * cap : (s + 1) * cap])
    for j, ref in enumerate(earlier_refs):
        for s in range(plan.sources):
            put(s, j, 0, ref[s])


def slot_work(plan, index, info, packs, weights, kind, earlier=()):
    rows = plan.sources * plan.cap
    if earlier:
        backs = (
            jax.ShapeDtypeStruct((2 * plan.planes * plan.back, LANES), jnp.bfloat16),
        ) * (plan.sources // 2)
    else:
        backs = (jax.ShapeDtypeStruct((plan.sources, plan.back, LANES), jnp.bfloat16),)
    vmem = pl.BlockSpec(memory_space=pltpu.VMEM)
    return pl.pallas_call(
        functools.partial(slot_kernel, plan, index, [where for _, where in weights], len(earlier)),
        out_shape=(jax.ShapeDtypeStruct((plan.head_dim, plan.part), kind), *backs),
        in_specs=[pl.BlockSpec(memory_space=pltpu.SMEM)]
        + [vmem] * (plan.sources + len(weights) + len(earlier)),
        out_specs=(vmem,) * (1 + len(backs)),
        scratch_shapes=[
            pltpu.VMEM((rows, plan.part), jnp.bfloat16),
            pltpu.VMEM((rows, plan.head_dim), jnp.bfloat16),
            pltpu.VMEM((plan.head_dim, plan.part), jnp.bfloat16),
        ],
        compiler_params=pltpu.CompilerParams(vmem_limit_bytes=20 * 1024 * 1024),
    )(info, *packs, *[array for array, _ in weights], *earlier)


def sum_kernel(plan, info, *refs):
    parts, pieces = refs[: len(refs) - plan.dp], refs[len(refs) - plan.dp :]
    rows = plan.own_rows
    for j, piece in enumerate(pieces):
        at = pl.ds(pl.multiple_of(info[j], rows), rows)
        total = parts[0][at, :].astype(jnp.float32)
        for ref in parts[1:]:
            total = total + ref[at, :].astype(jnp.float32)
        piece[...] = total.astype(piece.dtype)


def sum_work(plan, info, parts, own_kind):
    rows = plan.head_dim // plan.dp
    vmem = pl.BlockSpec(memory_space=pltpu.VMEM)
    return pl.pallas_call(
        functools.partial(sum_kernel, plan),
        out_shape=tuple(
            jax.ShapeDtypeStruct((rows, plan.part), jnp.bfloat16 if j else own_kind)
            for j in range(plan.dp)
        ),
        in_specs=[pl.BlockSpec(memory_space=pltpu.SMEM)] + [vmem] * len(parts),
        out_specs=(vmem,) * plan.dp,
    )(info, *parts)


def layout_kernel(plan, info, *refs):
    out_ref = refs[-1]
    for j in range(plan.dp):
        at = pl.ds(pl.multiple_of(info[plan.lanes_at + j], plan.part), plan.part)
        total = None
        for ref in refs[j : -1 : plan.dp]:
            piece = ref[...].astype(jnp.float32)
            total = piece if total is None else total + piece
        out_ref[:, at] = total


def layout_work(plan, info, pieces):
    rows = plan.head_dim // plan.dp
    vmem = pl.BlockSpec(memory_space=pltpu.VMEM)
    return pl.pallas_call(
        functools.partial(layout_kernel, plan),
        out_shape=jax.ShapeDtypeStruct((rows, plan.part * plan.dp), jnp.float32),
        in_specs=[pl.BlockSpec(memory_space=pltpu.SMEM)] + [vmem] * len(pieces),
        out_specs=vmem,
    )(info, *pieces)


def merge_kernel(plan, *refs):
    parts, outs = refs[: len(refs) - 2], refs[len(refs) - 2 :]
    length = plan.planes * plan.back
    for dc, out in enumerate(outs):
        for dy in range(plan.rows):
            total = None
            for ref in parts[dy :: plan.rows]:
                piece = ref[pl.ds(dc * length, length), :].astype(jnp.float32)
                total = piece if total is None else total + piece
            out[pl.ds(dy * length, length), :] = total.astype(out.dtype)


def merge_work(plan, parts):
    vmem = pl.BlockSpec(memory_space=pltpu.VMEM)
    rows = jax.ShapeDtypeStruct((plan.rows * plan.planes * plan.back, LANES), jnp.bfloat16)
    return pl.pallas_call(
        functools.partial(merge_kernel, plan),
        cost_estimate=pl.CostEstimate(flops=1, bytes_accessed=1, transcendentals=0),
        out_shape=(rows, rows),
        in_specs=[vmem] * len(parts),
        out_specs=(vmem, vmem),
    )(*parts)


def target_kernel(plan, info, route_ref, out_ref):
    tokens, top = plan.tokens, plan.top
    count = tokens * top
    lane = lax.broadcasted_iota(jnp.int32, (tokens, LANES), 1)
    routes = route_ref[...]
    named = jnp.zeros((tokens, LANES), jnp.float32)
    listed = jnp.zeros((tokens, LANES), jnp.float32)
    for k in range(top):
        column = routes[:, k : k + 1]
        named = named + (column == lane).astype(jnp.float32)
        listed = listed + jnp.where(lane == k, column, 0).astype(jnp.float32)
    earlier = (
        lax.broadcasted_iota(jnp.int32, (tokens, tokens), 1)
        < lax.broadcasted_iota(jnp.int32, (tokens, tokens), 0)
    ).astype(jnp.bfloat16)
    places = jnp.dot(earlier, named.astype(jnp.bfloat16), preferred_element_type=jnp.float32)
    pair = lax.broadcasted_iota(jnp.int32, (count, LANES), 0)
    lane = lax.broadcasted_iota(jnp.int32, (count, LANES), 1)
    spread = (pair // top == lane).astype(jnp.bfloat16)
    route = jnp.dot(spread, listed.astype(jnp.bfloat16), preferred_element_type=jnp.float32)
    route = jnp.sum(jnp.where(lane == pair % top, route, 0.0), axis=1, keepdims=True)
    route = route.astype(jnp.int32)
    place = jnp.dot(spread, places.astype(jnp.bfloat16), preferred_element_type=jnp.float32)
    place = jnp.sum(jnp.where(lane == route, place, 0.0), axis=1, keepdims=True).astype(jnp.int32)
    slot = jnp.zeros_like(route)
    for j in range(plan.planes):
        slot = jnp.where(route // GROUP == info[plan.planes_at + j], j, slot)
    row = (route % GROUP) // 2 - info[plan.planes_at + plan.planes]
    row = jnp.where(row < 0, row + plan.rows, row)
    side = jnp.where(route % 2 == info[plan.planes_at + plan.planes + 1], 0, 1)
    base = ((side * plan.rows + row) * plan.planes + slot) * plan.back
    target = base + place
    gate_line = base + plan.cap
    out_ref[...] = jnp.where(lane == 0, target, jnp.where(lane == 1, gate_line, place))


def target_work(plan, info, route_ids):
    vmem = pl.BlockSpec(memory_space=pltpu.VMEM)
    return pl.pallas_call(
        functools.partial(target_kernel, plan),
        out_shape=jax.ShapeDtypeStruct((plan.tokens * plan.top, LANES), jnp.int32),
        in_specs=[pl.BlockSpec(memory_space=pltpu.SMEM), vmem],
        out_specs=vmem,
        compiler_params=pltpu.CompilerParams(vmem_limit_bytes=16 * 1024 * 1024),
    )(info, route_ids)


def final_kernel(plan, target_ref, own_ref, other_ref, head_ref, out_gate_ref):
    length = plan.rows * plan.planes * plan.back
    table = jnp.concatenate([own_ref[...], other_ref[...]], axis=0)
    block = 256
    for start in range(0, plan.tokens * plan.top, block):
        at = pl.ds(start, block)
        slot_of = lax.broadcasted_iota(jnp.int32, (block, 2 * length), 1)
        hot = (slot_of == target_ref[at, 0:1]).astype(jnp.bfloat16)
        head_ref[at, :] = jnp.dot(hot, table, preferred_element_type=jnp.float32).astype(jnp.bfloat16)
        hot = (slot_of == target_ref[at, 1:2]).astype(jnp.bfloat16)
        lines = jnp.dot(hot, table, preferred_element_type=jnp.float32)
        lane_of = lax.broadcasted_iota(jnp.int32, (block, LANES), 1)
        out_gate_ref[at, :] = jnp.sum(
            jnp.where(lane_of == target_ref[at, 2:3], lines, 0.0), axis=1, keepdims=True
        )


def final_work(plan, target, own, other):
    count = plan.tokens * plan.top
    vmem = pl.BlockSpec(memory_space=pltpu.VMEM)
    return pl.pallas_call(
        functools.partial(final_kernel, plan),
        cost_estimate=pl.CostEstimate(flops=1, bytes_accessed=1, transcendentals=0),
        out_shape=(
            jax.ShapeDtypeStruct((count, plan.head_dim), jnp.bfloat16),
            jax.ShapeDtypeStruct((count, 1), jnp.float32),
        ),
        in_specs=[vmem] * 3,
        out_specs=(vmem, vmem),
        compiler_params=pltpu.CompilerParams(vmem_limit_bytes=24 * 1024 * 1024),
    )(target, own, other)


def local(mesh, head_outputs, out_grad, gate_weights, route_ids, out_proj):
    tokens, top, head_dim = head_outputs.shape
    features = out_grad.shape[1]
    plan = Plan(mesh, tokens, top, head_dim, features)
    x = lax.axis_index("dp")
    me = lax.axis_index("expert")
    z, y, c = me // GROUP, (me % GROUP) // 2, me % 2

    if plan.planes == 4:
        inner = (z == 1) | (z == 2)
        mates, middle = [(0, 1), (1, 0), (2, 3), (3, 2)], [(1, 2), (2, 1)]
        outward, inward = [(1, 0), (2, 3)], [(0, 1), (3, 2)]
        across = [(1, 3), (2, 0)]
        plane_of = [jnp.where(z < 2, 2, 1), jnp.where(z < 2, 3, 0), z ^ 1, z]
        which = jnp.where(inner, 0, 1)
    else:
        steps = [k % plan.planes for k in range(1, plan.planes + 1)]
        plane_of = [(z + k) % plan.planes for k in steps]
        which = 0
    info = plan.info(x, z, y, c, plane_of, which)

    own_weights = lax.dynamic_slice_in_dim(out_proj[0], x * plan.part, plan.part, 1)
    if plan.planes == 4:
        mate = plan.along(own_weights, mates)
        near_in = plan.along(own_weights, middle)
        near_out = plan.along(near_in, outward)
        far_in, near_out = lax.optimization_barrier((plan.along(mate, middle), near_out))
        far_out = plan.along(far_in, outward)
    else:
        weights = [[(plan.shift(own_weights, dz=-k % plan.planes), None)] for k in steps]

    meta = jnp.concatenate(
        [
            gate_weights.T,
            route_ids.T.astype(jnp.bfloat16),
            jnp.zeros((LANES - 2 * top, tokens), jnp.bfloat16),
        ],
        axis=0,
    )
    flat_heads = head_outputs.reshape(tokens, top * head_dim)
    packs = []
    for dx, dy in plan.chips():
        piece = lax.dynamic_slice_in_dim(out_grad, ((x + dx) % plan.dp) * plan.part, plan.part, 1)
        value = jnp.concatenate([piece, flat_heads, meta], axis=1)
        value = plan.shift(value, dx=dx, dy=dy)
        if plan.planes == 4:
            if dx or dy:
                value, near_in, mate = lax.optimization_barrier((value, near_in, mate))
            else:
                value, near_out = lax.optimization_barrier((value, near_out))
        packs += [value, plan.shift(value, dc=1)]

    if plan.planes == 4:
        weights = [
            [(near_in, 0), (near_out, 1)],
            [(far_in, 0), (far_out, 1)],
            [(mate, None)],
            [(own_weights, None)],
        ]

    target = target_work(plan, info, route_ids)

    sums, backs, done = [], [], target
    for j in range(plan.planes):
        last = j == plan.planes - 1
        if last and plan.planes == 4:
            near_sum = sums[0] + plan.along(sums[0], inward)
            done = (done, near_sum)
        info, done = lax.optimization_barrier((info, done))
        target = target if j else done
        kind = jnp.float32 if last else jnp.bfloat16
        part, *back = slot_work(plan, j, info, packs, weights[j], kind, backs if last else ())
        sums.append(part)
        backs = back if last else backs + back
        done = back[0]

    far_pieces = []
    if plan.planes == 4:
        far_part = plan.along(sums[1], inward)
        far_part, done = lax.optimization_barrier((far_part, done))
        far_pieces = sum_work(plan, info, [sums[1], far_part], jnp.bfloat16)
        info, far_pieces = lax.optimization_barrier((info, far_pieces))
        far_pieces = [plan.along(piece, across, dx) for dx, piece in enumerate(far_pieces)]
        received = [plan.along(sums[2], mates), plan.along(near_sum, middle)]
    else:
        received = [plan.shift(sums[j], dz=steps[j]) for j in range(plan.planes - 1)]
    pieces = sum_work(plan, info, [sums[-1]] + received, jnp.float32)
    sent = pieces[0]
    pieces = [plan.shift(piece, dx=dx) for dx, piece in enumerate(pieces)]

    backs = [
        plan.shift(rows, dx=-dx % plan.dp, dy=-dy % plan.rows)
        for rows, (dx, dy) in zip(backs, plan.chips())
    ]
    half = len(far_pieces) // 2
    backs, far_pieces[:half], _ = lax.optimization_barrier((backs, far_pieces[:half], sent))
    own, other = merge_work(plan, backs)
    grad_head, grad_gate = final_work(plan, target, own, plan.shift(other, dc=1))
    grad_proj = layout_work(plan, info, pieces + far_pieces)
    return (
        grad_head.reshape(tokens, top, head_dim),
        grad_gate.reshape(tokens, top).astype(jnp.bfloat16),
        grad_proj[None],
    )


def solution(mesh):
    return jax.shard_map(
        functools.partial(local, mesh),
        mesh=mesh,
        in_specs=(
            P(("dp", "expert"), None, None),
            P(("dp", "expert"), None),
            P(("dp", "expert"), None),
            P(("dp", "expert"), None),
            P("expert", None, None),
        ),
        out_specs=(
            P(("dp", "expert"), None, None),
            P(("dp", "expert"), None),
            P("expert", "dp", None),
        ),
        check_vma=False,
    )
```

time: 145 us -> 132 us (0.910)
  starting transfers between devices: 44.3 us -> 30.7 us
  waiting for transfers between devices: 33.8 us -> 44.3 us
  other arithmetic: 11.2 us -> 1.27 us
  Pallas kernels: 36.4 us -> 39.4 us
  local copies, waits for them, and re-layouts: 16 us -> 14.5 us
    ppermute x15 -> x12, waiting for transfers between devices: 19.2 us -> 32.2 us  [shift(): return lax.ppermute(value, AXES, self.pairs(**by))]
    ppermute x15 -> x11, starting transfers between devices: 27.9 us -> 20 us  [along(): return lax.ppermute(value, AXES, out)]
    unnamed x61, local copies, waits for them, and re-layouts: 5.56 us -> 13.4 us
    ppermute x15 -> x12, starting transfers between devices: 16.4 us -> 10.7 us  [shift(): return lax.ppermute(value, AXES, self.pairs(**by))]
    convert_element_type x3 -> x0, local copies, waits for them, and re-layouts: 4.45 us -> none  [local(): place = jnp.sum(hot.reshape(tokens, top, plan.experts) * places[:, None,...]
    eq x2 -> x0, local copies, waits for them, and re-layouts: 2.88 us -> none  [local(): routes[:, None] == jnp.arange(plan.experts, dtype=jnp.int32)[None, :]]
    pallas_call x6 -> x7, Pallas kernels: 29.5 us -> 32.4 us  [the longest x4 25.9 us: slot_work(): pl.pallas_call(functools.partial(slot_kernel, plan, index, [where for _,...]
    ppermute x15 -> x11, waiting for transfers between devices: 14.6 us -> 12.1 us  [along(): return lax.ppermute(value, AXES, out)]
  transfers between devices with their start and end apart: 30 -> 23, of which waited for: 10 -> 8; matrix products, arithmetic and copies ran while one was open for 14% -> 2% of each run, Pallas kernels for 22% -> 27%
where the time goes in v6:
time: 132 us; the launch traced here: 131 us
  waiting for transfers between devices  44.3 us (34%)
  Pallas kernels  39.4 us (30%)
  starting transfers between devices  30.7 us (23%)
  local copies, waits for them, and re-layouts  14.5 us (11%)
    ppermute x12, waiting for transfers between devices, shift(): return lax.ppermute(value, AXES, self.pairs(**by))  32.2 us
    pallas_call x4, Pallas kernels, slot_work(): pl.pallas_call(functools.partial(slot_kernel, plan, index, [where for _,...  25.9 us
    ppermute x11, starting transfers between devices, along(): return lax.ppermute(value, AXES, out)  20 us
    unnamed x61, local copies, waits for them, and re-layouts  13.4 us
    ppermute x11, waiting for transfers between devices, along(): return lax.ppermute(value, AXES, out)  12.1 us
    ppermute x12, starting transfers between devices, shift(): return lax.ppermute(value, AXES, self.pairs(**by))  10.7 us
    pallas_call x2, Pallas kernels, sum_work(): pl.pallas_call(functools.partial(sum_kernel, plan), out_shape=tuple((jax....  4.72 us
  transfers between devices with their start and end apart: 23, of which 8 were waited for; matrix products, arithmetic and copies ran while one was open for 2% of the time, Pallas kernels for 27%

profile of v6, /device:TPU:0, one launch (start us, length us, event | category | flops | bytes accessed | tf_op | source)
XLA Modules:
  0.0 131.1 jit_solution(3344414096829472451)
XLA Ops:
  0.6 0.0 copy-start
  0.7 1.2 copy-done
  1.9 0.8 dynamic-slice_bitcast_fusion.refs_8_
  2.7 3.0 %collective-permute-start = (bf16[128,2048]{1,0:T(8,128)(2,1)}, bf16[128,2048]{1,0:T(8,128)(2,1)}, u32[]{:S(2)}, u32[]{:S(2)}) collective-permute-start(bf16[128,2048]{1,0:T(8,128)(2,1)} %dynamic-slice_bitcast_fusion.refs_8_), channel_id=1, source_target_pairs={{0,4},{1,5},{2,6},{3,7},{4,0},{5,1},{6,2},{7,3},{8,12},{9,13},{10,... | collective-permute-start | bytes 1572872 | tf_op jit(solution)/shard_map/ppermute | solution.py:62
  5.7 1.5 %collective-permute-start.2 = (bf16[128,2048]{1,0:T(8,128)(2,1)}, bf16[128,2048]{1,0:T(8,128)(2,1)}, u32[]{:S(2)}, u32[]{:S(2)}) collective-permute-start(bf16[128,2048]{1,0:T(8,128)(2,1)} %dynamic-slice_bitcast_fusion.refs_8_), channel_id=1, source_target_pairs={{4,8},{5,9},{6,10},{7,11},{8,4},{9,5},{10,6},{11,7},{20,24},{21,25... | collective-permute-start | bytes 1572872 | tf_op jit(solution)/shard_map/ppermute | solution.py:62
  7.3 0.0 copy-start.27
  7.3 0.1 constant_dynamic-slice_fusion
  7.4 0.5 copy-done.27
  8.0 0.1 fusion.1
  8.1 1.6 %collective-permute-start.5 = (bf16[128,3200]{1,0:T(8,128)(2,1)S(1)}, bf16[128,3200]{1,0:T(8,128)(2,1)S(1)}, u32[]{:S(2)}, u32[]{:S(2)}) collective-permute-start(bf16[128,3200]{1,0:T(8,128)(2,1)S(1)} %get-tuple-element.52.refs_0_), channel_id=1, source_target_pairs={{0,2},{1,3},{2,0},{3,1},{4,6},{5,7},{6,4},{7,5},{8,10},{9,11},{10,... | collective-permute-start | bytes 2457608 | tf_op jit(solution)/shard_map/ppermute | solution.py:52
  9.7 1.5 %collective-permute-start.7 = (bf16[128,3200]{1,0:T(8,128)(2,1)S(1)}, bf16[128,3200]{1,0:T(8,128)(2,1)S(1)}, u32[]{:S(2)}, u32[]{:S(2)}) collective-permute-start(bf16[128,3200]{1,0:T(8,128)(2,1)S(1)} %get-tuple-element.103), channel_id=1, source_target_pairs={{0,16},{1,17},{2,18},{3,19},{4,20},{5,21},{6,22},{7,23},{8,24},{9,... | collective-permute-start | bytes 2457608 | tf_op jit(solution)/shard_map/ppermute | solution.py:52
  11.2 0.5 collective-permute-start.9
  11.7 6.3 %collective-permute-done.refs_8_ = bf16[128,2048]{1,0:T(8,128)(2,1)} collective-permute-done((bf16[128,2048]{1,0:T(8,128)(2,1)}, bf16[128,2048]{1,0:T(8,128)(2,1)}, u32[]{:S(2)}, u32[]{:S(2)}) %collective-permute-start) | collective-permute-done | bytes 524320 | tf_op jit(solution)/shard_map/ppermute | solution.py:62
  18.0 1.4 %collective-permute-start.1 = (bf16[128,2048]{1,0:T(8,128)(2,1)}, bf16[128,2048]{1,0:T(8,128)(2,1)}, u32[]{:S(2)}, u32[]{:S(2)}) collective-permute-start(bf16[128,2048]{1,0:T(8,128)(2,1)} %collective-permute-done.refs_8_), channel_id=1, source_target_pairs={{4,8},{5,9},{6,10},{7,11},{8,4},{9,5},{10,6},{11,7},{20,24},{21,25... | collective-permute-start | bytes 1572872 | tf_op jit(solution)/shard_map/ppermute | solution.py:62
  19.4 1.3 collective-permute-start.3
  20.7 7.7 %collective-permute-done.5.refs_2_ = bf16[128,3200]{1,0:T(8,128)(2,1)S(1)} collective-permute-done((bf16[128,3200]{1,0:T(8,128)(2,1)S(1)}, bf16[128,3200]{1,0:T(8,128)(2,1)S(1)}, u32[]{:S(2)}, u32[]{:S(2)}) %collective-permute-start.5) | collective-permute-done | bytes 819232 | tf_op jit(solution)/shard_map/ppermute | solution.py:52
  28.4 2.4 %collective-permute-done.7.refs_4_ = bf16[128,3200]{1,0:T(8,128)(2,1)S(1)} collective-permute-done((bf16[128,3200]{1,0:T(8,128)(2,1)S(1)}, bf16[128,3200]{1,0:T(8,128)(2,1)S(1)}, u32[]{:S(2)}, u32[]{:S(2)}) %collective-permute-start.7) | collective-permute-done | bytes 819232 | tf_op jit(solution)/shard_map/ppermute | solution.py:52
  30.9 15.8 %collective-permute-done.9.refs_6_ = bf16[128,3200]{1,0:T(8,128)(2,1)} collective-permute-done((bf16[128,3200]{1,0:T(8,128)(2,1)S(1)}, bf16[128,3200]{1,0:T(8,128)(2,1)}, u32[]{:S(2)}, u32[]{:S(2)}) %collective-permute-start.9) | collective-permute-done | bytes 819232 | tf_op jit(solution)/shard_map/ppermute | solution.py:52
  46.7 0.0 collective-permute-start.10
  46.7 0.8 copy-done.5
  47.5 0.5 collective-permute-start.4
  48.0 1.3 collective-permute-start.11
  49.4 0.7 copy.10.route_ref
  50.1 0.1 stack.63.info
  50.2 0.0 copy-start.7
  50.2 0.8 copy-done.7
  51.0 2.4 %shard_map.76.target_ref = s32[1024,128]{1,0:T(8,128)S(1)} custom-call(s32[15]{0:T(128)S(1)} %stack.63.info, s32[128,8]{1,0:T(8,128)S(1)} %copy-done.7), custom_call_target="tpu_custom_call" | custom-call | tf_op jit(solution)/shard_map/pallas_call | solution.py:325
  53.4 0.8 copy-done.1
  54.3 1.0 copy-done.6
  55.3 6.4 %shard_map.77 = (bf16[128,2048]{1,0:T(8,128)(2,1)S(1)}, bf16[8,80,128]{2,1,0:T(8,128)(2,1)S(1)}) custom-call(s32[15]{0:T(128)S(1)} %stack.63.info, bf16[128,3200]{1,0:T(8,128)(2,1)S(1)} %get-tuple-element.52.refs_0_, bf16[128,3200]{1,0:T(8,128)(2,1)} %collective-permute-done.4.refs_1_, bf16[128,3200]{1,0:T(8,128)(2,1)S(1)} %collective-permute-done.5.refs_2_, ...), custom_call_target="tpu_custom_call" | custom-call | tf_op jit(solution)/shard_map/pallas_call | solution.py:201
  61.7 6.0 %collective-permute-start.12 = (bf16[128,2048]{1,0:T(8,128)(2,1)S(1)}, bf16[128,2048]{1,0:T(8,128)(2,1)S(1)}, u32[]{:S(2)}, u32[]{:S(2)}) collective-permute-start(bf16[128,2048]{1,0:T(8,128)(2,1)S(1)} %get-tuple-element.69), channel_id=1, source_target_pairs={{0,4},{1,5},{2,6},{3,7},{12,8},{13,9},{14,10},{15,11},{16,20},{17,... | collective-permute-start | bytes 1572872 | tf_op jit(solution)/shard_map/ppermute | solution.py:62
  67.7 6.6 %shard_map.78 = (bf16[128,2048]{1,0:T(8,128)(2,1)S(1)}, bf16[8,80,128]{2,1,0:T(8,128)(2,1)S(1)}) custom-call(s32[15]{0:T(128)S(1)} %stack.63.info, bf16[128,3200]{1,0:T(8,128)(2,1)S(1)} %get-tuple-element.52.refs_0_, bf16[128,3200]{1,0:T(8,128)(2,1)} %collective-permute-done.4.refs_1_, bf16[128,3200]{1,0:T(8,128)(2,1)S(1)} %collective-permute-done.5.refs_2_, ...), custom_call_target="tpu_custom_call" | custom-call | tf_op jit(solution)/shard_map/pallas_call | solution.py:201
  74.3 1.5 %collective-permute-start.16 = (bf16[128,2048]{1,0:T(8,128)(2,1)S(1)}, bf16[128,2048]{1,0:T(8,128)(2,1)S(1)}, u32[]{:S(2)}, u32[]{:S(2)}) collective-permute-start(bf16[128,2048]{1,0:T(8,128)(2,1)S(1)} %get-tuple-element.75.refs_0_), channel_id=1, source_target_pairs={{0,4},{1,5},{2,6},{3,7},{12,8},{13,9},{14,10},{15,11},{16,20},{17,... | collective-permute-start | bytes 1572872 | tf_op jit(solution)/shard_map/ppermute | solution.py:62
  75.8 6.5 %shard_map.79 = (bf16[128,2048]{1,0:T(8,128)(2,1)}, bf16[8,80,128]{2,1,0:T(8,128)(2,1)S(1)}) custom-call(s32[15]{0:T(128)S(1)} %stack.63.info, bf16[128,3200]{1,0:T(8,128)(2,1)S(1)} %get-tuple-element.52.refs_0_, bf16[128,3200]{1,0:T(8,128)(2,1)} %collective-permute-done.4.refs_1_, bf16[128,3200]{1,0:T(8,128)(2,1)S(1)} %collective-permute-done.5.refs_2_, ...), custom_call_target="tpu_custom_call" | custom-call | tf_op jit(solution)/shard_map/pallas_call | solution.py:201
  82.4 0.9 add.84
  83.3 1.5 %collective-permute-start.19 = (bf16[128,2048]{1,0:T(8,128)(2,1)}, bf16[128,2048]{1,0:T(8,128)(2,1)}, u32[]{:S(2)}, u32[]{:S(2)}) collective-permute-start(bf16[128,2048]{1,0:T(8,128)(2,1)} %add.84), channel_id=1, source_target_pairs={{4,8},{5,9},{6,10},{7,11},{8,4},{9,5},{10,6},{11,7},{20,24},{21,25... | collective-permute-start | bytes 1572872 | tf_op jit(solution)/shard_map/ppermute | solution.py:62
  84.8 6.4 %shard_map.80 = (f32[128,2048]{1,0:T(8,128)S(1)}, bf16[640,128]{1,0:T(8,128)(2,1)S(1)}, bf16[640,128]{1,0:T(8,128)(2,1)S(1)}, bf16[640,128]{1,0:T(8,128)(2,1)S(1)}, bf16[640,128]{1,0:T(8,128)(2,1)S(1)}) custom-call(s32[15]{0:T(128)S(1)} %stack.63.info, bf16[128,3200]{1,0:T(8,128)(2,1)S(1)} %get-tuple-element.52.refs_0_, ...), custom_call_target="tpu_custom_call" | custom-call | tf_op jit(solution)/shard_map/pallas_call | solution.py:201
  91.2 1.0 copy-done.3
  92.2 0.7 copy-done.8
  92.8 0.7 copy-done.11
  93.5 0.7 copy-done.13
  94.2 0.7 copy-done.15
  94.8 0.8 copy-done.18
  95.6 2.1 %shard_map.81 = (bf16[64,2048]{1,0:T(8,128)(2,1)}, bf16[64,2048]{1,0:T(8,128)(2,1)}) custom-call(s32[15]{0:T(128)} %copy-done.10, bf16[128,2048]{1,0:T(8,128)(2,1)} %copy-done.4, bf16[128,2048]{1,0:T(8,128)(2,1)} %copy-done.18), custom_call_target="tpu_custom_call" | custom-call | tf_op jit(solution)/shard_map/pallas_call | solution.py:230
  97.7 1.3 collective-permute-start.17
  99.0 1.6 %collective-permute-start.13 = (bf16[640,128]{1,0:T(8,128)(2,1)S(1)}, bf16[640,128]{1,0:T(8,128)(2,1)S(1)}, u32[]{:S(2)}, u32[]{:S(2)}) collective-permute-start(bf16[640,128]{1,0:T(8,128)(2,1)S(1)} %copy-done.16), channel_id=1, source_target_pairs={{0,2},{1,3},{2,0},{3,1},{4,6},{5,7},{6,4},{7,5},{8,10},{9,11},{10,... | collective-permute-start | bytes 491528 | tf_op jit(solution)/shard_map/ppermute | solution.py:52
  100.7 1.5 %collective-permute-start.14 = (bf16[640,128]{1,0:T(8,128)(2,1)S(1)}, bf16[640,128]{1,0:T(8,128)(2,1)S(1)}, u32[]{:S(2)}, u32[]{:S(2)}) collective-permute-start(bf16[640,128]{1,0:T(8,128)(2,1)S(1)} %copy-done.14), channel_id=1, source_target_pairs={{0,16},{1,17},{2,18},{3,19},{4,20},{5,21},{6,22},{7,23},{8,24},{9,... | collective-permute-start | bytes 491528 | tf_op jit(solution)/shard_map/ppermute | solution.py:52
  102.2 1.9 %collective-permute-start.15 = (bf16[640,128]{1,0:T(8,128)(2,1)S(1)}, bf16[640,128]{1,0:T(8,128)(2,1)S(1)}, u32[]{:S(2)}, u32[]{:S(2)}) collective-permute-start(bf16[640,128]{1,0:T(8,128)(2,1)S(1)} %copy-done.12), channel_id=1, source_target_pairs={{0,18},{1,19},{2,16},{3,17},{4,22},{5,23},{6,20},{7,21},{8,26},{9,... | collective-permute-start | bytes 491528 | tf_op jit(solution)/shard_map/ppermute | solution.py:52
  104.1 2.6 %shard_map.82 = (f32[64,2048]{1,0:T(8,128)}, bf16[64,2048]{1,0:T(8,128)(2,1)}) custom-call(s32[15]{0:T(128)} %copy-done.10, f32[128,2048]{1,0:T(8,128)} %copy-done.3, bf16[128,2048]{1,0:T(8,128)(2,1)} %collective-permute-done.18.refs_1_, bf16[128,2048]{1,0:T(8,128)(2,1)} %collective-permute-done.19.refs_2_), custom_call_target="tpu_custom_call" | custom-call | tf_op jit(solution)/shard_map/pallas_call | solution.py:230
  106.7 1.1 collective-permute-done.14.refs_2_
  107.8 1.8 %collective-permute-done.15.refs_3_ = bf16[640,128]{1,0:T(8,128)(2,1)S(1)} collective-permute-done((bf16[640,128]{1,0:T(8,128)(2,1)S(1)}, bf16[640,128]{1,0:T(8,128)(2,1)S(1)}, u32[]{:S(2)}, u32[]{:S(2)}) %collective-permute-start.15) | collective-permute-done | bytes 163872 | tf_op jit(solution)/shard_map/ppermute | solution.py:52
  109.6 0.6 copy-done.25
  110.3 1.9 %shard_map.83 = (bf16[640,128]{1,0:T(8,128)(2,1)}, bf16[640,128]{1,0:T(8,128)(2,1)}) custom-call(bf16[640,128]{1,0:T(8,128)(2,1)} %copy-done.8, bf16[640,128]{1,0:T(8,128)(2,1)} %copy-done.23, bf16[640,128]{1,0:T(8,128)(2,1)} %copy-done.24, bf16[640,128]{1,0:T(8,128)(2,1)} %copy-done.25), custom_call_target="tpu_custom_call" | custom-call | flops 1 | bytes 1 | tf_op jit(solution)/shard_map/pallas_call | solution.py:278
  112.2 1.3 collective-permute-start.22
  113.5 1.6 %collective-permute-start.21 = (bf16[64,2048]{1,0:T(8,128)(2,1)}, bf16[64,2048]{1,0:T(8,128)(2,1)S(1)}, u32[]{:S(2)}, u32[]{:S(2)}) collective-permute-start(bf16[64,2048]{1,0:T(8,128)(2,1)} %get-tuple-element.92), channel_id=1, source_target_pairs={{0,16},{1,17},{2,18},{3,19},{4,20},{5,21},{6,22},{7,23},{8,24},{9,... | collective-permute-start | bytes 786440 | tf_op jit(solution)/shard_map/ppermute | solution.py:52
  115.0 0.9 copy-done.9
  116.0 2.1 %shard_map.84 = (bf16[1024,128]{1,0:T(8,128)(2,1)}, f32[1024,1]{1,0:T(8,128)S(1)}) custom-call(s32[1024,128]{1,0:T(8,128)S(1)} %copy-done.2, bf16[640,128]{1,0:T(8,128)(2,1)S(1)} %copy-done.9, bf16[640,128]{1,0:T(8,128)(2,1)S(1)} %collective-permute-done.20.other_ref), custom_call_target="tpu_custom_call" | custom-call | flops 1 | bytes 1 | tf_op jit(solution)/shard_map/pallas_call | solution.py:354
  118.1 0.2 convert_reduce_fusion
  118.3 0.1 convert_element_type.15
  118.4 0.7 copy.11
  119.1 5.8 %collective-permute-done.22.refs_3_ = bf16[64,2048]{1,0:T(8,128)(2,1)S(1)} collective-permute-done((bf16[64,2048]{1,0:T(8,128)(2,1)S(1)}, bf16[64,2048]{1,0:T(8,128)(2,1)S(1)}, u32[]{:S(2)}, u32[]{:S(2)}) %collective-permute-start.22) | collective-permute-done | bytes 262176 | tf_op jit(solution)/shard_map/ppermute | solution.py:62
  124.9 3.2 %collective-permute-done.21.refs_1_ = bf16[64,2048]{1,0:T(8,128)(2,1)S(1)} collective-permute-done((bf16[64,2048]{1,0:T(8,128)(2,1)}, bf16[64,2048]{1,0:T(8,128)(2,1)S(1)}, u32[]{:S(2)}, u32[]{:S(2)}) %collective-permute-start.21) | collective-permute-done | bytes 262176 | tf_op jit(solution)/shard_map/ppermute | solution.py:52
  128.1 0.7 copy-done.21
  128.8 2.3 %shard_map.85 = f32[64,4096]{1,0:T(8,128)} custom-call(s32[15]{0:T(128)} %copy-done.10, f32[64,2048]{1,0:T(8,128)} %get-tuple-element.83.refs_0_, bf16[64,2048]{1,0:T(8,128)(2,1)} %copy-done.21, bf16[64,2048]{1,0:T(8,128)(2,1)} %copy-done.19, bf16[64,2048]{1,0:T(8,128)(2,1)} %copy-done.20), custom_call_target="tpu_custom_call" | custom-call | tf_op jit(solution)/shard_map/pallas_call | solution.py:255
  (62 shorter events, 0.2 us)
Async XLA Ops:
  0.6 1.2 copy-start
  0.6 6.5 %copy-start.22 = (bf16[128,8,128]{2,1,0:T(8,128)(2,1)S(1)}, bf16[128,8,128]{2,1,0:T(8,128)(2,1)}, u32[]{:S(2)}) copy-start(bf16[128,8,128]{2,1,0:T(8,128)(2,1)} %param.5) | copy-start | bytes 786436
  0.7 6.6 %copy-start.26 = (s32[128,8]{0,1:T(8,128)S(1)}, s32[128,8]{0,1:T(8,128)}, u32[]{:S(2)}) copy-start(s32[128,8]{0,1:T(8,128)} %param.8) | copy-start | bytes 12292
  0.7 6.6 %copy-start.17 = (bf16[128,4096]{1,0:T(8,128)(2,1)S(1)}, bf16[128,4096]{1,0:T(8,128)(2,1)}, u32[]{:S(2)}) copy-start(bf16[128,4096]{1,0:T(8,128)(2,1)} %param.6) | copy-start | bytes 3145732
  2.7 15.3 %collective-permute-start = (bf16[128,2048]{1,0:T(8,128)(2,1)}, bf16[128,2048]{1,0:T(8,128)(2,1)}, u32[]{:S(2)}, u32[]{:S(2)}) collective-permute-start(bf16[128,2048]{1,0:T(8,128)(2,1)} %dynamic-slice_bitcast_fusion.refs_8_), channel_id=1, source_target_pairs={{0,4},{1,5},{2,6},{3,7},{4,0},{5,1},{6,2},{7,3},{8,12},{9,13},{10,... | collective-permute-start | bytes 1572872 | tf_op jit(solution)/shard_map/ppermute | solution.py:62
  5.7 13.7 %collective-permute-start.2 = (bf16[128,2048]{1,0:T(8,128)(2,1)}, bf16[128,2048]{1,0:T(8,128)(2,1)}, u32[]{:S(2)}, u32[]{:S(2)}) collective-permute-start(bf16[128,2048]{1,0:T(8,128)(2,1)} %dynamic-slice_bitcast_fusion.refs_8_), channel_id=1, source_target_pairs={{4,8},{5,9},{6,10},{7,11},{8,4},{9,5},{10,6},{11,7},{20,24},{21,25... | collective-permute-start | bytes 1572872 | tf_op jit(solution)/shard_map/ppermute | solution.py:62
  7.3 0.7 copy-start.27
  8.1 20.3 %collective-permute-start.5 = (bf16[128,3200]{1,0:T(8,128)(2,1)S(1)}, bf16[128,3200]{1,0:T(8,128)(2,1)S(1)}, u32[]{:S(2)}, u32[]{:S(2)}) collective-permute-start(bf16[128,3200]{1,0:T(8,128)(2,1)S(1)} %get-tuple-element.52.refs_0_), channel_id=1, source_target_pairs={{0,2},{1,3},{2,0},{3,1},{4,6},{5,7},{6,4},{7,5},{8,10},{9,11},{10,... | collective-permute-start | bytes 2457608 | tf_op jit(solution)/shard_map/ppermute | solution.py:52
  9.7 21.2 %collective-permute-start.7 = (bf16[128,3200]{1,0:T(8,128)(2,1)S(1)}, bf16[128,3200]{1,0:T(8,128)(2,1)S(1)}, u32[]{:S(2)}, u32[]{:S(2)}) collective-permute-start(bf16[128,3200]{1,0:T(8,128)(2,1)S(1)} %get-tuple-element.103), channel_id=1, source_target_pairs={{0,16},{1,17},{2,18},{3,19},{4,20},{5,21},{6,22},{7,23},{8,24},{9,... | collective-permute-start | bytes 2457608 | tf_op jit(solution)/shard_map/ppermute | solution.py:52
  11.2 35.5 %collective-permute-start.9 = (bf16[128,3200]{1,0:T(8,128)(2,1)S(1)}, bf16[128,3200]{1,0:T(8,128)(2,1)}, u32[]{:S(2)}, u32[]{:S(2)}) collective-permute-start(bf16[128,3200]{1,0:T(8,128)(2,1)S(1)} %get-tuple-element.103), channel_id=1, source_target_pairs={{0,18},{1,19},{2,16},{3,17},{4,22},{5,23},{6,20},{7,21},{8,26},{9,... | collective-permute-start | bytes 2457608 | tf_op jit(solution)/shard_map/ppermute | solution.py:52
  18.0 28.8 %collective-permute-start.1 = (bf16[128,2048]{1,0:T(8,128)(2,1)}, bf16[128,2048]{1,0:T(8,128)(2,1)}, u32[]{:S(2)}, u32[]{:S(2)}) collective-permute-start(bf16[128,2048]{1,0:T(8,128)(2,1)} %collective-permute-done.refs_8_), channel_id=1, source_target_pairs={{4,8},{5,9},{6,10},{7,11},{8,4},{9,5},{10,6},{11,7},{20,24},{21,25... | collective-permute-start | bytes 1572872 | tf_op jit(solution)/shard_map/ppermute | solution.py:62
  19.4 27.3 %collective-permute-start.3 = (bf16[128,2048]{1,0:T(8,128)(2,1)}, bf16[128,2048]{1,0:T(8,128)(2,1)S(1)}, u32[]{:S(2)}, u32[]{:S(2)}) collective-permute-start(bf16[128,2048]{1,0:T(8,128)(2,1)} %collective-permute-done.2.refs_8_), channel_id=1, source_target_pairs={{4,0},{5,1},{6,2},{7,3},{8,12},{9,13},{10,14},{11,15},{20,16},{21,... | collective-permute-start | bytes 1572872 | tf_op jit(solution)/shard_map/ppermute | solution.py:62
  28.4 25.8 %collective-permute-start.6 = (bf16[128,3200]{1,0:T(8,128)(2,1)S(1)}, bf16[128,3200]{1,0:T(8,128)(2,1)}, u32[]{:S(2)}, u32[]{:S(2)}) collective-permute-start(bf16[128,3200]{1,0:T(8,128)(2,1)S(1)} %collective-permute-done.5.refs_2_), channel_id=1, source_target_pairs={{0,1},{1,0},{2,3},{3,2},{4,5},{5,4},{6,7},{7,6},{8,9},{9,8},{10,11... | collective-permute-start | bytes 2457608 | tf_op jit(solution)/shard_map/ppermute | solution.py:52
  30.9 23.4 %collective-permute-start.8 = (bf16[128,3200]{1,0:T(8,128)(2,1)S(1)}, bf16[128,3200]{1,0:T(8,128)(2,1)}, u32[]{:S(2)}, u32[]{:S(2)}) collective-permute-start(bf16[128,3200]{1,0:T(8,128)(2,1)S(1)} %collective-permute-done.7.refs_4_), channel_id=1, source_target_pairs={{0,1},{1,0},{2,3},{3,2},{4,5},{5,4},{6,7},{7,6},{8,9},{9,8},{10,11... | collective-permute-start | bytes 2457608 | tf_op jit(solution)/shard_map/ppermute | solution.py:52
  46.7 7.5 %collective-permute-start.10 = (bf16[128,3200]{1,0:T(8,128)(2,1)}, bf16[128,3200]{1,0:T(8,128)(2,1)}, u32[]{:S(2)}, u32[]{:S(2)}) collective-permute-start(bf16[128,3200]{1,0:T(8,128)(2,1)} %collective-permute-done.9.refs_6_), channel_id=1, source_target_pairs={{0,1},{1,0},{2,3},{3,2},{4,5},{5,4},{6,7},{7,6},{8,9},{9,8},{10,11... | collective-permute-start | bytes 2457608 | tf_op jit(solution)/shard_map/ppermute | solution.py:52
  46.7 0.8 copy-start.5
  47.5 6.7 %collective-permute-start.4 = (bf16[128,3200]{1,0:T(8,128)(2,1)S(1)}, bf16[128,3200]{1,0:T(8,128)(2,1)}, u32[]{:S(2)}, u32[]{:S(2)}) collective-permute-start(bf16[128,3200]{1,0:T(8,128)(2,1)S(1)} %get-tuple-element.52.refs_0_), channel_id=1, source_target_pairs={{0,1},{1,0},{2,3},{3,2},{4,5},{5,4},{6,7},{7,6},{8,9},{9,8},{10,11... | collective-permute-start | bytes 2457608 | tf_op jit(solution)/shard_map/ppermute | solution.py:52
  48.0 19.7 %collective-permute-start.11 = (bf16[128,2048]{1,0:T(8,128)(2,1)}, bf16[128,2048]{1,0:T(8,128)(2,1)}, u32[]{:S(2)}, u32[]{:S(2)}) collective-permute-start(bf16[128,2048]{1,0:T(8,128)(2,1)} %collective-permute-done.1.refs_8_), channel_id=1, source_target_pairs={{4,0},{5,1},{6,2},{7,3},{8,12},{9,13},{10,14},{11,15},{20,16},{21,... | collective-permute-start | bytes 1572872 | tf_op jit(solution)/shard_map/ppermute | solution.py:62
  50.2 0.8 copy-start.7
  51.0 33.8 %copy-start.10 = (s32[15]{0:T(128)}, s32[15]{0:T(128)S(1)}, u32[]{:S(2)}) copy-start(s32[15]{0:T(128)S(1)} %stack.63.info) | copy-start | bytes 184
  53.4 0.8 copy-start.1
  54.3 1.0 copy-start.6
  61.7 20.7 %collective-permute-start.12 = (bf16[128,2048]{1,0:T(8,128)(2,1)S(1)}, bf16[128,2048]{1,0:T(8,128)(2,1)S(1)}, u32[]{:S(2)}, u32[]{:S(2)}) collective-permute-start(bf16[128,2048]{1,0:T(8,128)(2,1)S(1)} %get-tuple-element.69), channel_id=1, source_target_pairs={{0,4},{1,5},{2,6},{3,7},{12,8},{13,9},{14,10},{15,11},{16,20},{17,... | collective-permute-start | bytes 1572872 | tf_op jit(solution)/shard_map/ppermute | solution.py:62
  74.3 8.1 %copy-start.4 = (bf16[128,2048]{1,0:T(8,128)(2,1)}, bf16[128,2048]{1,0:T(8,128)(2,1)S(1)}, u32[]{:S(2)}) copy-start(bf16[128,2048]{1,0:T(8,128)(2,1)S(1)} %get-tuple-element.75.refs_0_) | copy-start | bytes 1572868
  74.3 20.5 %collective-permute-start.16 = (bf16[128,2048]{1,0:T(8,128)(2,1)S(1)}, bf16[128,2048]{1,0:T(8,128)(2,1)S(1)}, u32[]{:S(2)}, u32[]{:S(2)}) collective-permute-start(bf16[128,2048]{1,0:T(8,128)(2,1)S(1)} %get-tuple-element.75.refs_0_), channel_id=1, source_target_pairs={{0,4},{1,5},{2,6},{3,7},{12,8},{13,9},{14,10},{15,11},{16,20},{17,... | collective-permute-start | bytes 1572872 | tf_op jit(solution)/shard_map/ppermute | solution.py:62
  82.4 19.8 %collective-permute-start.18 = (bf16[128,2048]{1,0:T(8,128)(2,1)}, bf16[128,2048]{1,0:T(8,128)(2,1)}, u32[]{:S(2)}, u32[]{:S(2)}) collective-permute-start(bf16[128,2048]{1,0:T(8,128)(2,1)} %get-tuple-element.82), channel_id=1, source_target_pairs={{0,4},{1,5},{2,6},{3,7},{4,0},{5,1},{6,2},{7,3},{8,12},{9,13},{10,... | collective-permute-start | bytes 1572872 | tf_op jit(solution)/shard_map/ppermute | solution.py:62
  83.3 20.7 %collective-permute-start.19 = (bf16[128,2048]{1,0:T(8,128)(2,1)}, bf16[128,2048]{1,0:T(8,128)(2,1)}, u32[]{:S(2)}, u32[]{:S(2)}) collective-permute-start(bf16[128,2048]{1,0:T(8,128)(2,1)} %add.84), channel_id=1, source_target_pairs={{4,8},{5,9},{6,10},{7,11},{8,4},{9,5},{10,6},{11,7},{20,24},{21,25... | collective-permute-start | bytes 1572872 | tf_op jit(solution)/shard_map/ppermute | solution.py:62
  91.2 1.0 copy-start.3
  92.2 0.7 copy-start.8
  92.8 0.7 copy-start.11
  93.5 0.7 copy-start.13
  94.2 0.7 copy-start.15
  94.8 0.8 copy-start.18
  95.6 3.4 %copy-start.16 = (bf16[640,128]{1,0:T(8,128)(2,1)S(1)}, bf16[640,128]{1,0:T(8,128)(2,1)}, u32[]{:S(2)}) copy-start(bf16[640,128]{1,0:T(8,128)(2,1)} %copy-done.15) | copy-start | bytes 491524
  95.6 5.0 %copy-start.14 = (bf16[640,128]{1,0:T(8,128)(2,1)S(1)}, bf16[640,128]{1,0:T(8,128)(2,1)}, u32[]{:S(2)}) copy-start(bf16[640,128]{1,0:T(8,128)(2,1)} %copy-done.13) | copy-start | bytes 491524
  95.6 6.5 %copy-start.12 = (bf16[640,128]{1,0:T(8,128)(2,1)S(1)}, bf16[640,128]{1,0:T(8,128)(2,1)}, u32[]{:S(2)}) copy-start(bf16[640,128]{1,0:T(8,128)(2,1)} %copy-done.11) | copy-start | bytes 491524
  97.7 11.9 %collective-permute-start.17 = (bf16[64,2048]{1,0:T(8,128)(2,1)}, bf16[64,2048]{1,0:T(8,128)(2,1)S(1)}, u32[]{:S(2)}, u32[]{:S(2)}) collective-permute-start(bf16[64,2048]{1,0:T(8,128)(2,1)} %get-tuple-element.79), channel_id=1, source_target_pairs={{4,12},{5,13},{6,14},{7,15},{8,0},{9,1},{10,2},{11,3},{20,28},{21,... | collective-permute-start | bytes 786440 | tf_op jit(solution)/shard_map/ppermute | solution.py:62
  99.0 7.6 %collective-permute-start.13 = (bf16[640,128]{1,0:T(8,128)(2,1)S(1)}, bf16[640,128]{1,0:T(8,128)(2,1)S(1)}, u32[]{:S(2)}, u32[]{:S(2)}) collective-permute-start(bf16[640,128]{1,0:T(8,128)(2,1)S(1)} %copy-done.16), channel_id=1, source_target_pairs={{0,2},{1,3},{2,0},{3,1},{4,6},{5,7},{6,4},{7,5},{8,10},{9,11},{10,... | collective-permute-start | bytes 491528 | tf_op jit(solution)/shard_map/ppermute | solution.py:52
  100.7 7.1 %collective-permute-start.14 = (bf16[640,128]{1,0:T(8,128)(2,1)S(1)}, bf16[640,128]{1,0:T(8,128)(2,1)S(1)}, u32[]{:S(2)}, u32[]{:S(2)}) collective-permute-start(bf16[640,128]{1,0:T(8,128)(2,1)S(1)} %copy-done.14), channel_id=1, source_target_pairs={{0,16},{1,17},{2,18},{3,19},{4,20},{5,21},{6,22},{7,23},{8,24},{9,... | collective-permute-start | bytes 491528 | tf_op jit(solution)/shard_map/ppermute | solution.py:52
  102.2 7.5 %collective-permute-start.15 = (bf16[640,128]{1,0:T(8,128)(2,1)S(1)}, bf16[640,128]{1,0:T(8,128)(2,1)S(1)}, u32[]{:S(2)}, u32[]{:S(2)}) collective-permute-start(bf16[640,128]{1,0:T(8,128)(2,1)S(1)} %copy-done.12), channel_id=1, source_target_pairs={{0,18},{1,19},{2,16},{3,17},{4,22},{5,23},{6,20},{7,21},{8,26},{9,... | collective-permute-start | bytes 491528 | tf_op jit(solution)/shard_map/ppermute | solution.py:52
  104.1 8.1 %copy-start.28 = (bf16[64,2048]{1,0:T(8,128)(2,1)S(1)}, bf16[64,2048]{1,0:T(8,128)(2,1)}, u32[]{:S(2)}) copy-start(bf16[64,2048]{1,0:T(8,128)(2,1)} %get-tuple-element.94) | copy-start | bytes 786436
  104.1 11.0 %copy-start.2 = (s32[1024,128]{1,0:T(8,128)S(1)}, s32[1024,128]{1,0:T(8,128)}, u32[]{:S(2)}) copy-start(s32[1024,128]{1,0:T(8,128)} %copy-done.1) | copy-start | bytes 1572868
  106.7 2.9 %copy-start.23 = (bf16[640,128]{1,0:T(8,128)(2,1)}, bf16[640,128]{1,0:T(8,128)(2,1)S(1)}, u32[]{:S(2)}) copy-start(bf16[640,128]{1,0:T(8,128)(2,1)S(1)} %collective-permute-done.13.refs_1_) | copy-start | bytes 491524
  107.8 1.8 %copy-start.24 = (bf16[640,128]{1,0:T(8,128)(2,1)}, bf16[640,128]{1,0:T(8,128)(2,1)S(1)}, u32[]{:S(2)}) copy-start(bf16[640,128]{1,0:T(8,128)(2,1)S(1)} %collective-permute-done.14.refs_2_) | copy-start | bytes 491524
  109.6 0.7 copy-start.25
  109.6 9.5 %copy-start.19 = (bf16[64,2048]{1,0:T(8,128)(2,1)}, bf16[64,2048]{1,0:T(8,128)(2,1)S(1)}, u32[]{:S(2)}) copy-start(bf16[64,2048]{1,0:T(8,128)(2,1)S(1)} %collective-permute-done.17.refs_2_) | copy-start | bytes 786436
  112.2 2.9 %collective-permute-start.20 = (bf16[640,128]{1,0:T(8,128)(2,1)}, bf16[640,128]{1,0:T(8,128)(2,1)S(1)}, u32[]{:S(2)}, u32[]{:S(2)}) collective-permute-start(bf16[640,128]{1,0:T(8,128)(2,1)} %get-tuple-element.89), channel_id=1, source_target_pairs={{0,1},{1,0},{2,3},{3,2},{4,5},{5,4},{6,7},{7,6},{8,9},{9,8},{10,11... | collective-permute-start | bytes 491528 | tf_op jit(solution)/shard_map/ppermute | solution.py:52
  112.2 12.7 %collective-permute-start.22 = (bf16[64,2048]{1,0:T(8,128)(2,1)S(1)}, bf16[64,2048]{1,0:T(8,128)(2,1)S(1)}, u32[]{:S(2)}, u32[]{:S(2)}) collective-permute-start(bf16[64,2048]{1,0:T(8,128)(2,1)S(1)} %copy-done.28), channel_id=1, source_target_pairs={{4,28},{5,29},{6,30},{7,31},{8,16},{9,17},{10,18},{11,19},{20,12},... | collective-permute-start | bytes 786440 | tf_op jit(solution)/shard_map/ppermute | solution.py:62
  113.5 14.6 %collective-permute-start.21 = (bf16[64,2048]{1,0:T(8,128)(2,1)}, bf16[64,2048]{1,0:T(8,128)(2,1)S(1)}, u32[]{:S(2)}, u32[]{:S(2)}) collective-permute-start(bf16[64,2048]{1,0:T(8,128)(2,1)} %get-tuple-element.92), channel_id=1, source_target_pairs={{0,16},{1,17},{2,18},{3,19},{4,20},{5,21},{6,22},{7,23},{8,24},{9,... | collective-permute-start | bytes 786440 | tf_op jit(solution)/shard_map/ppermute | solution.py:52
  115.0 0.9 copy-start.9
  124.9 3.2 %copy-start.20 = (bf16[64,2048]{1,0:T(8,128)(2,1)}, bf16[64,2048]{1,0:T(8,128)(2,1)S(1)}, u32[]{:S(2)}) copy-start(bf16[64,2048]{1,0:T(8,128)(2,1)S(1)} %collective-permute-done.22.refs_3_) | copy-start | bytes 786436
  128.1 0.7 copy-start.21

commit v7 on v6

--- a/solution.py
+++ b/solution.py
@@ -209,7 +209,7 @@
             pltpu.VMEM((rows, plan.head_dim), jnp.bfloat16),
             pltpu.VMEM((plan.head_dim, plan.part), jnp.bfloat16),
         ],
-        compiler_params=pltpu.CompilerParams(vmem_limit_bytes=20 * 1024 * 1024),
+        compiler_params=pltpu.CompilerParams(vmem_limit_bytes=14 * 1024 * 1024),
     )(info, *packs, *[array for array, _ in weights], *earlier)
 
 
@@ -229,6 +229,7 @@
     vmem = pl.BlockSpec(memory_space=pltpu.VMEM)
     return pl.pallas_call(
         functools.partial(sum_kernel, plan),
+        compiler_params=pltpu.CompilerParams(vmem_limit_bytes=6 * 1024 * 1024),
         out_shape=tuple(
             jax.ShapeDtypeStruct((rows, plan.part), jnp.bfloat16 if j else own_kind)
             for j in range(plan.dp)
@@ -254,6 +255,7 @@
     vmem = pl.BlockSpec(memory_space=pltpu.VMEM)
     return pl.pallas_call(
         functools.partial(layout_kernel, plan),
+        compiler_params=pltpu.CompilerParams(vmem_limit_bytes=6 * 1024 * 1024),
         out_shape=jax.ShapeDtypeStruct((rows, plan.part * plan.dp), jnp.float32),
         in_specs=[pl.BlockSpec(memory_space=pltpu.SMEM)] + [vmem] * len(pieces),
         out_specs=vmem,
@@ -277,6 +279,7 @@
     rows = jax.ShapeDtypeStruct((plan.rows * plan.planes * plan.back, LANES), jnp.bfloat16)
     return pl.pallas_call(
         functools.partial(merge_kernel, plan),
+        compiler_params=pltpu.CompilerParams(vmem_limit_bytes=6 * 1024 * 1024),
         cost_estimate=pl.CostEstimate(flops=1, bytes_accessed=1, transcendentals=0),
         out_shape=(rows, rows),
         in_specs=[vmem] * len(parts),
@@ -327,7 +330,7 @@
         out_shape=jax.ShapeDtypeStruct((plan.tokens * plan.top, LANES), jnp.int32),
         in_specs=[pl.BlockSpec(memory_space=pltpu.SMEM), vmem],
         out_specs=vmem,
-        compiler_params=pltpu.CompilerParams(vmem_limit_bytes=16 * 1024 * 1024),
+        compiler_params=pltpu.CompilerParams(vmem_limit_bytes=8 * 1024 * 1024),
     )(info, route_ids)
 
 
@@ -360,7 +363,7 @@
         ),
         in_specs=[vmem] * 3,
         out_specs=(vmem, vmem),
-        compiler_params=pltpu.CompilerParams(vmem_limit_bytes=24 * 1024 * 1024),
+        compiler_params=pltpu.CompilerParams(vmem_limit_bytes=8 * 1024 * 1024),
     )(target, own, other)
 
 
@@ -386,9 +389,11 @@
     info = plan.info(x, z, y, c, plane_of, which)
 
     own_weights = lax.dynamic_slice_in_dim(out_proj[0], x * plan.part, plan.part, 1)
+    target = target_work(plan, info, route_ids)
     if plan.planes == 4:
         mate = plan.along(own_weights, mates)
         near_in = plan.along(own_weights, middle)
+        mate, near_in, target = lax.optimization_barrier((mate, near_in, target))
         near_out = plan.along(near_in, outward)
         far_in, near_out = lax.optimization_barrier((plan.along(mate, middle), near_out))
         far_out = plan.along(far_in, outward)
@@ -424,8 +429,6 @@
             [(own_weights, None)],
         ]
 
-    target = target_work(plan, info, route_ids)
-
     sums, backs, done = [], [], target
     for j in range(plan.planes):
         last = j == plan.planes - 1
@@ -451,15 +454,13 @@
     else:
         received = [plan.shift(sums[j], dz=steps[j]) for j in range(plan.planes - 1)]
     pieces = sum_work(plan, info, [sums[-1]] + received, jnp.float32)
-    sent = pieces[0]
     pieces = [plan.shift(piece, dx=dx) for dx, piece in enumerate(pieces)]
 
     backs = [
         plan.shift(rows, dx=-dx % plan.dp, dy=-dy % plan.rows)
         for rows, (dx, dy) in zip(backs, plan.chips())
     ]
-    half = len(far_pieces) // 2
-    backs, far_pieces[:half], _ = lax.optimization_barrier((backs, far_pieces[:half], sent))
+    backs, far_pieces, pieces = lax.optimization_barrier((backs, far_pieces, pieces))
     own, other = merge_work(plan, backs)
     grad_head, grad_gate = final_work(plan, target, own, plan.shift(other, dc=1))
     grad_proj = layout_work(plan, info, pieces + far_pieces)

time: 132 us -> 123 us (0.932)
  waiting for transfers between devices: 44.3 us -> 57.7 us
  Pallas kernels: 39.4 us -> 29.4 us
  local copies, waits for them, and re-layouts: 14.5 us -> 5.15 us
  starting transfers between devices: 30.7 us -> 28.2 us
    ppermute x12, waiting for transfers between devices: 32.2 us -> 46.1 us  [shift(): return lax.ppermute(value, AXES, self.pairs(**by))]
    unnamed x61 -> x15, local copies, waits for them, and re-layouts: 13.4 us -> 4.01 us
    pallas_call x4, Pallas kernels: 8.96 us -> 3.05 us  [the longest x1 1.61 us: layout_work(): pl.pallas_call(functools.partial(layout_kernel, plan), compiler_params=pl...]
    pallas_call x4, Pallas kernels: 25.9 us -> 21.8 us  [slot_work(): pl.pallas_call(functools.partial(slot_kernel, plan, index, [where for _,...]
    ppermute x11, starting transfers between devices: 20 us -> 18 us  [along(): return lax.ppermute(value, AXES, out)]
  transfers between devices with their start and end apart: 23 -> 23, of which waited for: 8 -> 10; matrix products, arithmetic and copies ran while one was open for 2% -> 2% of each run, Pallas kernels for 27% -> 22%
where the time goes in v7:
time: 123 us
  waiting for transfers between devices  57.7 us (47%)
  Pallas kernels  29.4 us (24%)
  starting transfers between devices  28.2 us (23%)
  local copies, waits for them, and re-layouts  5.15 us (4%)
  other arithmetic  1.36 us (1%)
    ppermute x12, waiting for transfers between devices, shift(): return lax.ppermute(value, AXES, self.pairs(**by))  46.1 us
    pallas_call x4, Pallas kernels, slot_work(): pl.pallas_call(functools.partial(slot_kernel, plan, index, [where for _,...  21.8 us
    ppermute x11, starting transfers between devices, along(): return lax.ppermute(value, AXES, out)  18 us
    ppermute x11, waiting for transfers between devices, along(): return lax.ppermute(value, AXES, out)  11.6 us
    ppermute x12, starting transfers between devices, shift(): return lax.ppermute(value, AXES, self.pairs(**by))  10.2 us
    unnamed x15, local copies, waits for them, and re-layouts  4.01 us
  transfers between devices with their start and end apart: 23, of which 10 were waited for; matrix products, arithmetic and copies ran while one was open for 2% of the time, Pallas kernels for 22%

profile of v7, /device:TPU:0, one launch (start us, length us, event | category | flops | bytes accessed | tf_op | source)
XLA Modules:
  0.0 122.7 jit_solution(4529155873494909296)
XLA Ops:
  0.6 0.0 copy-start
  0.7 1.2 copy-done
  1.9 0.8 dynamic-slice_bitcast_fusion.refs_8_
  2.7 3.0 %collective-permute-start = (bf16[128,2048]{1,0:T(8,128)(2,1)}, bf16[128,2048]{1,0:T(8,128)(2,1)}, u32[]{:S(2)}, u32[]{:S(2)}) collective-permute-start(bf16[128,2048]{1,0:T(8,128)(2,1)} %dynamic-slice_bitcast_fusion.refs_8_), channel_id=1, source_target_pairs={{0,4},{1,5},{2,6},{3,7},{4,0},{5,1},{6,2},{7,3},{8,12},{9,13},{10,... | collective-permute-start | bytes 1572872 | tf_op jit(solution)/shard_map/ppermute | solution.py:62
  5.7 1.4 %collective-permute-start.1 = (bf16[128,2048]{1,0:T(8,128)(2,1)}, bf16[128,2048]{1,0:T(8,128)(2,1)}, u32[]{:S(2)}, u32[]{:S(2)}) collective-permute-start(bf16[128,2048]{1,0:T(8,128)(2,1)} %dynamic-slice_bitcast_fusion.refs_8_), channel_id=1, source_target_pairs={{4,8},{5,9},{6,10},{7,11},{8,4},{9,5},{10,6},{11,7},{20,24},{21,25... | collective-permute-start | bytes 1572872 | tf_op jit(solution)/shard_map/ppermute | solution.py:62
  7.3 0.0 copy-start.5
  7.3 0.1 constant_dynamic-slice_fusion
  7.4 0.5 copy-done.5
  7.9 1.0 fusion.1
  9.0 1.5 %collective-permute-start.5 = (bf16[128,3200]{1,0:T(8,128)(2,1)S(1)}, bf16[128,3200]{1,0:T(8,128)(2,1)S(1)}, u32[]{:S(2)}, u32[]{:S(2)}) collective-permute-start(bf16[128,3200]{1,0:T(8,128)(2,1)S(1)} %get-tuple-element.61.refs_0_), channel_id=1, source_target_pairs={{0,2},{1,3},{2,0},{3,1},{4,6},{5,7},{6,4},{7,5},{8,10},{9,11},{10,... | collective-permute-start | bytes 2457608 | tf_op jit(solution)/shard_map/ppermute | solution.py:52
  10.5 1.5 %collective-permute-start.7 = (bf16[128,3200]{1,0:T(8,128)(2,1)}, bf16[128,3200]{1,0:T(8,128)(2,1)S(1)}, u32[]{:S(2)}, u32[]{:S(2)}) collective-permute-start(bf16[128,3200]{1,0:T(8,128)(2,1)} %get-tuple-element.115), channel_id=1, source_target_pairs={{0,16},{1,17},{2,18},{3,19},{4,20},{5,21},{6,22},{7,23},{8,24},{9,... | collective-permute-start | bytes 2457608 | tf_op jit(solution)/shard_map/ppermute | solution.py:52
  12.0 0.5 collective-permute-start.9
  12.4 0.7 copy.10.route_ref
  13.2 0.1 stack.63.info
  13.3 0.0 copy-start.1
  13.3 0.8 copy-done.1
  14.1 2.4 %shard_map.76.target_ref = s32[1024,128]{1,0:T(8,128)S(1)} custom-call(s32[15]{0:T(128)S(1)} %stack.63.info, s32[128,8]{1,0:T(8,128)S(1)} %copy-done.1), custom_call_target="tpu_custom_call" | custom-call | tf_op jit(solution)/shard_map/pallas_call | solution.py:328
  16.5 1.5 %collective-permute-done.refs_8_ = bf16[128,2048]{1,0:T(8,128)(2,1)} collective-permute-done((bf16[128,2048]{1,0:T(8,128)(2,1)}, bf16[128,2048]{1,0:T(8,128)(2,1)}, u32[]{:S(2)}, u32[]{:S(2)}) %collective-permute-start) | collective-permute-done | bytes 524320 | tf_op jit(solution)/shard_map/ppermute | solution.py:62
  18.0 0.0 collective-permute-done.1.refs_8_
  18.0 0.7 collective-permute-start.2
  18.6 1.3 %collective-permute-start.3 = (bf16[128,2048]{1,0:T(8,128)(2,1)}, bf16[128,2048]{1,0:T(8,128)(2,1)S(1)}, u32[]{:S(2)}, u32[]{:S(2)}) collective-permute-start(bf16[128,2048]{1,0:T(8,128)(2,1)} %collective-permute-done.1.refs_8_), channel_id=1, source_target_pairs={{4,0},{5,1},{6,2},{7,3},{8,12},{9,13},{10,14},{11,15},{20,16},{21,... | collective-permute-start | bytes 1572872 | tf_op jit(solution)/shard_map/ppermute | solution.py:62
  19.9 9.1 %collective-permute-done.5.refs_2_ = bf16[128,3200]{1,0:T(8,128)(2,1)S(1)} collective-permute-done((bf16[128,3200]{1,0:T(8,128)(2,1)S(1)}, bf16[128,3200]{1,0:T(8,128)(2,1)S(1)}, u32[]{:S(2)}, u32[]{:S(2)}) %collective-permute-start.5) | collective-permute-done | bytes 819232 | tf_op jit(solution)/shard_map/ppermute | solution.py:52
  29.0 2.8 %collective-permute-done.7.refs_4_ = bf16[128,3200]{1,0:T(8,128)(2,1)S(1)} collective-permute-done((bf16[128,3200]{1,0:T(8,128)(2,1)}, bf16[128,3200]{1,0:T(8,128)(2,1)S(1)}, u32[]{:S(2)}, u32[]{:S(2)}) %collective-permute-start.7) | collective-permute-done | bytes 819232 | tf_op jit(solution)/shard_map/ppermute | solution.py:52
  31.9 0.0 collective-permute-start.8
  31.9 15.8 %collective-permute-done.9.refs_6_ = bf16[128,3200]{1,0:T(8,128)(2,1)} collective-permute-done((bf16[128,3200]{1,0:T(8,128)(2,1)}, bf16[128,3200]{1,0:T(8,128)(2,1)}, u32[]{:S(2)}, u32[]{:S(2)}) %collective-permute-start.9) | collective-permute-done | bytes 819232 | tf_op jit(solution)/shard_map/ppermute | solution.py:52
  47.7 0.0 collective-permute-done.2.refs_8_
  47.7 0.0 collective-permute-done.3.refs_9_
  47.7 0.5 collective-permute-start.4
  48.2 1.3 %collective-permute-start.11 = (bf16[128,2048]{1,0:T(8,128)(2,1)S(1)}, bf16[128,2048]{1,0:T(8,128)(2,1)S(1)}, u32[]{:S(2)}, u32[]{:S(2)}) collective-permute-start(bf16[128,2048]{1,0:T(8,128)(2,1)S(1)} %collective-permute-done.2.refs_8_), channel_id=1, source_target_pairs={{4,0},{5,1},{6,2},{7,3},{8,12},{9,13},{10,14},{11,15},{20,16},{21,... | collective-permute-start | bytes 1572872 | tf_op jit(solution)/shard_map/ppermute | solution.py:62
  49.5 0.0 collective-permute-done.8.refs_5_
  49.5 1.1 collective-permute-done.10.refs_7_
  50.7 0.6 collective-permute-done.4.refs_1_
  51.2 5.5 %shard_map.77 = (bf16[128,2048]{1,0:T(8,128)(2,1)S(1)}, bf16[8,80,128]{2,1,0:T(8,128)(2,1)S(1)}) custom-call(s32[15]{0:T(128)S(1)} %stack.63.info, bf16[128,3200]{1,0:T(8,128)(2,1)S(1)} %get-tuple-element.61.refs_0_, bf16[128,3200]{1,0:T(8,128)(2,1)S(1)} %collective-permute-done.4.refs_1_, bf16[128,3200]{1,0:T(8,128)(2,1)S(1)} %collective-permute-done.5.refs_2_, ...), custom_call_target="tpu_custom_call" | custom-call | tf_op jit(solution)/shard_map/pallas_call | solution.py:201
  56.7 5.3 %collective-permute-start.12 = (bf16[128,2048]{1,0:T(8,128)(2,1)S(1)}, bf16[128,2048]{1,0:T(8,128)(2,1)S(1)}, u32[]{:S(2)}, u32[]{:S(2)}) collective-permute-start(bf16[128,2048]{1,0:T(8,128)(2,1)S(1)} %get-tuple-element.78), channel_id=1, source_target_pairs={{0,4},{1,5},{2,6},{3,7},{12,8},{13,9},{14,10},{15,11},{16,20},{17,... | collective-permute-start | bytes 1572872 | tf_op jit(solution)/shard_map/ppermute | solution.py:62
  62.0 3.0 %collective-permute-done.11.refs_9_ = bf16[128,2048]{1,0:T(8,128)(2,1)S(1)} collective-permute-done((bf16[128,2048]{1,0:T(8,128)(2,1)S(1)}, bf16[128,2048]{1,0:T(8,128)(2,1)S(1)}, u32[]{:S(2)}, u32[]{:S(2)}) %collective-permute-start.11) | collective-permute-done | bytes 524320 | tf_op jit(solution)/shard_map/ppermute | solution.py:62
  65.0 5.4 %shard_map.78 = (bf16[128,2048]{1,0:T(8,128)(2,1)S(1)}, bf16[8,80,128]{2,1,0:T(8,128)(2,1)S(1)}) custom-call(s32[15]{0:T(128)S(1)} %stack.63.info, bf16[128,3200]{1,0:T(8,128)(2,1)S(1)} %get-tuple-element.61.refs_0_, bf16[128,3200]{1,0:T(8,128)(2,1)S(1)} %collective-permute-done.4.refs_1_, bf16[128,3200]{1,0:T(8,128)(2,1)S(1)} %collective-permute-done.5.refs_2_, ...), custom_call_target="tpu_custom_call" | custom-call | tf_op jit(solution)/shard_map/pallas_call | solution.py:201
  70.4 1.6 %collective-permute-start.16 = (bf16[128,2048]{1,0:T(8,128)(2,1)S(1)}, bf16[128,2048]{1,0:T(8,128)(2,1)S(1)}, u32[]{:S(2)}, u32[]{:S(2)}) collective-permute-start(bf16[128,2048]{1,0:T(8,128)(2,1)S(1)} %get-tuple-element.84.refs_0_), channel_id=1, source_target_pairs={{0,4},{1,5},{2,6},{3,7},{12,8},{13,9},{14,10},{15,11},{16,20},{17,... | collective-permute-start | bytes 1572872 | tf_op jit(solution)/shard_map/ppermute | solution.py:62
  72.0 5.5 %shard_map.79 = (bf16[128,2048]{1,0:T(8,128)(2,1)S(1)}, bf16[8,80,128]{2,1,0:T(8,128)(2,1)S(1)}) custom-call(s32[15]{0:T(128)S(1)} %stack.63.info, bf16[128,3200]{1,0:T(8,128)(2,1)S(1)} %get-tuple-element.61.refs_0_, bf16[128,3200]{1,0:T(8,128)(2,1)S(1)} %collective-permute-done.4.refs_1_, bf16[128,3200]{1,0:T(8,128)(2,1)S(1)} %collective-permute-done.5.refs_2_, ...), custom_call_target="tpu_custom_call" | custom-call | tf_op jit(solution)/shard_map/pallas_call | solution.py:201
  77.5 0.1 collective-permute-start.19
  77.6 0.0 collective-permute-done.12
  77.6 0.1 add.84
  77.7 0.7 collective-permute-start.20
  78.5 5.5 %shard_map.80 = (f32[128,2048]{1,0:T(8,128)S(1)}, bf16[640,128]{1,0:T(8,128)(2,1)S(1)}, bf16[640,128]{1,0:T(8,128)(2,1)S(1)}, bf16[640,128]{1,0:T(8,128)(2,1)S(1)}, bf16[640,128]{1,0:T(8,128)(2,1)S(1)}) custom-call(s32[15]{0:T(128)S(1)} %stack.63.info, bf16[128,3200]{1,0:T(8,128)(2,1)S(1)} %get-tuple-element.61.refs_0_, ...), custom_call_target="tpu_custom_call" | custom-call | tf_op jit(solution)/shard_map/pallas_call | solution.py:201
  83.9 1.6 %collective-permute-start.13 = (bf16[640,128]{1,0:T(8,128)(2,1)S(1)}, bf16[640,128]{1,0:T(8,128)(2,1)S(1)}, u32[]{:S(2)}, u32[]{:S(2)}) collective-permute-start(bf16[640,128]{1,0:T(8,128)(2,1)S(1)} %get-tuple-element.81), channel_id=1, source_target_pairs={{0,2},{1,3},{2,0},{3,1},{4,6},{5,7},{6,4},{7,5},{8,10},{9,11},{10,... | collective-permute-start | bytes 491528 | tf_op jit(solution)/shard_map/ppermute | solution.py:52
  85.5 0.0 collective-permute-done.16.refs_1_
  85.5 0.7 shard_map.81
  86.2 1.3 %collective-permute-start.17 = (bf16[64,2048]{1,0:T(8,128)(2,1)S(1)}, bf16[64,2048]{1,0:T(8,128)(2,1)S(1)}, u32[]{:S(2)}, u32[]{:S(2)}) collective-permute-start(bf16[64,2048]{1,0:T(8,128)(2,1)S(1)} %get-tuple-element.88), channel_id=1, source_target_pairs={{4,12},{5,13},{6,14},{7,15},{8,0},{9,1},{10,2},{11,3},{20,28},{21,... | collective-permute-start | bytes 786440 | tf_op jit(solution)/shard_map/ppermute | solution.py:62
  87.5 1.3 %collective-permute-start.18 = (bf16[64,2048]{1,0:T(8,128)(2,1)S(1)}, bf16[64,2048]{1,0:T(8,128)(2,1)S(1)}, u32[]{:S(2)}, u32[]{:S(2)}) collective-permute-start(bf16[64,2048]{1,0:T(8,128)(2,1)S(1)} %get-tuple-element.89), channel_id=1, source_target_pairs={{4,28},{5,29},{6,30},{7,31},{8,16},{9,17},{10,18},{11,19},{20,12},... | collective-permute-start | bytes 786440 | tf_op jit(solution)/shard_map/ppermute | solution.py:62
  88.8 7.1 %collective-permute-done.19.refs_1_ = bf16[128,2048]{1,0:T(8,128)(2,1)S(1)} collective-permute-done((bf16[128,2048]{1,0:T(8,128)(2,1)S(1)}, bf16[128,2048]{1,0:T(8,128)(2,1)S(1)}, u32[]{:S(2)}, u32[]{:S(2)}) %collective-permute-start.19) | collective-permute-done | bytes 524320 | tf_op jit(solution)/shard_map/ppermute | solution.py:62
  95.9 0.0 collective-permute-done.20.refs_2_
  95.9 0.7 shard_map.82
  96.6 1.6 %collective-permute-start.21 = (bf16[64,2048]{1,0:T(8,128)(2,1)S(1)}, bf16[64,2048]{1,0:T(8,128)(2,1)S(1)}, u32[]{:S(2)}, u32[]{:S(2)}) collective-permute-start(bf16[64,2048]{1,0:T(8,128)(2,1)S(1)} %get-tuple-element.94), channel_id=1, source_target_pairs={{0,16},{1,17},{2,18},{3,19},{4,20},{5,21},{6,22},{7,23},{8,24},{9,... | collective-permute-start | bytes 786440 | tf_op jit(solution)/shard_map/ppermute | solution.py:52
  98.2 0.5 collective-permute-start.14
  98.7 2.4 %collective-permute-start.15 = (bf16[640,128]{1,0:T(8,128)(2,1)S(1)}, bf16[640,128]{1,0:T(8,128)(2,1)S(1)}, u32[]{:S(2)}, u32[]{:S(2)}) collective-permute-start(bf16[640,128]{1,0:T(8,128)(2,1)S(1)} %get-tuple-element.83), channel_id=1, source_target_pairs={{0,18},{1,19},{2,16},{3,17},{4,22},{5,23},{6,20},{7,21},{8,26},{9,... | collective-permute-start | bytes 491528 | tf_op jit(solution)/shard_map/ppermute | solution.py:52
  101.2 13.1 %collective-permute-done.14.refs_2_ = bf16[640,128]{1,0:T(8,128)(2,1)S(1)} collective-permute-done((bf16[640,128]{1,0:T(8,128)(2,1)S(1)}, bf16[640,128]{1,0:T(8,128)(2,1)S(1)}, u32[]{:S(2)}, u32[]{:S(2)}) %collective-permute-start.14) | collective-permute-done | bytes 163872 | tf_op jit(solution)/shard_map/ppermute | solution.py:52
  114.2 3.6 %collective-permute-done.15.refs_3_ = bf16[640,128]{1,0:T(8,128)(2,1)S(1)} collective-permute-done((bf16[640,128]{1,0:T(8,128)(2,1)S(1)}, bf16[640,128]{1,0:T(8,128)(2,1)S(1)}, u32[]{:S(2)}, u32[]{:S(2)}) %collective-permute-start.15) | collective-permute-done | bytes 163872 | tf_op jit(solution)/shard_map/ppermute | solution.py:52
  117.8 0.0 collective-permute-done.18.refs_3_
  117.8 0.1 shard_map.83
  117.9 0.1 collective-permute-start.22
  118.0 1.6 %shard_map.85 = f32[64,4096]{1,0:T(8,128)} custom-call(s32[15]{0:T(128)S(1)} %stack.63.info, f32[64,2048]{1,0:T(8,128)S(1)} %get-tuple-element.103.refs_0_, bf16[64,2048]{1,0:T(8,128)(2,1)S(1)} %collective-permute-done.21.refs_1_, bf16[64,2048]{1,0:T(8,128)(2,1)S(1)} %collective-permute-done.17.refs_2_, bf16[64,2048]{1,0:T(8,128)(2,1)S(1)} %collective-permute-done.18.refs_3_), custom_call_target="tpu_custom_call" | custom-call | tf_op jit(solution)/shard_map/pallas_call | solution.py:256
  119.6 2.2 %shard_map.84 = (bf16[1024,128]{1,0:T(8,128)(2,1)}, f32[1024,1]{1,0:T(8,128)S(1)}) custom-call(s32[1024,128]{1,0:T(8,128)S(1)} %shard_map.76.target_ref, bf16[640,128]{1,0:T(8,128)(2,1)S(1)} %get-tuple-element.99.own_ref, bf16[640,128]{1,0:T(8,128)(2,1)S(1)} %collective-permute-done.22.other_ref), custom_call_target="tpu_custom_call" | custom-call | flops 1 | bytes 1 | tf_op jit(solution)/shard_map/pallas_call | solution.py:357
  121.7 0.2 convert_reduce_fusion
  122.0 0.1 convert_element_type.15
  122.1 0.7 copy.11
  (16 shorter events, 0.1 us)
Async XLA Ops:
  0.6 1.2 %copy-start = (bf16[1,128,4096]{2,1,0:T(8,128)(2,1)S(1)}, bf16[1,128,4096]{2,1,0:T(8,128)(2,1)}, u32[]{:S(2)}) copy-start(bf16[1,128,4096]{2,1,0:T(8,128)(2,1)} %param.9) | copy-start | bytes 3145732
  0.6 6.5 %copy-start.3 = (bf16[128,8,128]{2,1,0:T(8,128)(2,1)S(1)}, bf16[128,8,128]{2,1,0:T(8,128)(2,1)}, u32[]{:S(2)}) copy-start(bf16[128,8,128]{2,1,0:T(8,128)(2,1)} %param.5) | copy-start | bytes 786436
  0.7 6.6 %copy-start.4 = (s32[128,8]{0,1:T(8,128)S(1)}, s32[128,8]{0,1:T(8,128)}, u32[]{:S(2)}) copy-start(s32[128,8]{0,1:T(8,128)} %param.8) | copy-start | bytes 12292
  0.7 6.6 %copy-start.2 = (bf16[128,4096]{1,0:T(8,128)(2,1)S(1)}, bf16[128,4096]{1,0:T(8,128)(2,1)}, u32[]{:S(2)}) copy-start(bf16[128,4096]{1,0:T(8,128)(2,1)} %param.6) | copy-start | bytes 3145732
  2.7 15.3 %collective-permute-start = (bf16[128,2048]{1,0:T(8,128)(2,1)}, bf16[128,2048]{1,0:T(8,128)(2,1)}, u32[]{:S(2)}, u32[]{:S(2)}) collective-permute-start(bf16[128,2048]{1,0:T(8,128)(2,1)} %dynamic-slice_bitcast_fusion.refs_8_), channel_id=1, source_target_pairs={{0,4},{1,5},{2,6},{3,7},{4,0},{5,1},{6,2},{7,3},{8,12},{9,13},{10,... | collective-permute-start | bytes 1572872 | tf_op jit(solution)/shard_map/ppermute | solution.py:62
  5.7 12.2 %collective-permute-start.1 = (bf16[128,2048]{1,0:T(8,128)(2,1)}, bf16[128,2048]{1,0:T(8,128)(2,1)}, u32[]{:S(2)}, u32[]{:S(2)}) collective-permute-start(bf16[128,2048]{1,0:T(8,128)(2,1)} %dynamic-slice_bitcast_fusion.refs_8_), channel_id=1, source_target_pairs={{4,8},{5,9},{6,10},{7,11},{8,4},{9,5},{10,6},{11,7},{20,24},{21,25... | collective-permute-start | bytes 1572872 | tf_op jit(solution)/shard_map/ppermute | solution.py:62
  7.3 0.7 copy-start.5
  9.0 20.1 %collective-permute-start.5 = (bf16[128,3200]{1,0:T(8,128)(2,1)S(1)}, bf16[128,3200]{1,0:T(8,128)(2,1)S(1)}, u32[]{:S(2)}, u32[]{:S(2)}) collective-permute-start(bf16[128,3200]{1,0:T(8,128)(2,1)S(1)} %get-tuple-element.61.refs_0_), channel_id=1, source_target_pairs={{0,2},{1,3},{2,0},{3,1},{4,6},{5,7},{6,4},{7,5},{8,10},{9,11},{10,... | collective-permute-start | bytes 2457608 | tf_op jit(solution)/shard_map/ppermute | solution.py:52
  10.5 21.4 %collective-permute-start.7 = (bf16[128,3200]{1,0:T(8,128)(2,1)}, bf16[128,3200]{1,0:T(8,128)(2,1)S(1)}, u32[]{:S(2)}, u32[]{:S(2)}) collective-permute-start(bf16[128,3200]{1,0:T(8,128)(2,1)} %get-tuple-element.115), channel_id=1, source_target_pairs={{0,16},{1,17},{2,18},{3,19},{4,20},{5,21},{6,22},{7,23},{8,24},{9,... | collective-permute-start | bytes 2457608 | tf_op jit(solution)/shard_map/ppermute | solution.py:52
  12.0 35.7 %collective-permute-start.9 = (bf16[128,3200]{1,0:T(8,128)(2,1)}, bf16[128,3200]{1,0:T(8,128)(2,1)}, u32[]{:S(2)}, u32[]{:S(2)}) collective-permute-start(bf16[128,3200]{1,0:T(8,128)(2,1)} %get-tuple-element.115), channel_id=1, source_target_pairs={{0,18},{1,19},{2,16},{3,17},{4,22},{5,23},{6,20},{7,21},{8,26},{9,... | collective-permute-start | bytes 2457608 | tf_op jit(solution)/shard_map/ppermute | solution.py:52
  13.3 0.8 copy-start.1
  18.0 29.8 %collective-permute-start.2 = (bf16[128,2048]{1,0:T(8,128)(2,1)}, bf16[128,2048]{1,0:T(8,128)(2,1)S(1)}, u32[]{:S(2)}, u32[]{:S(2)}) collective-permute-start(bf16[128,2048]{1,0:T(8,128)(2,1)} %collective-permute-done.refs_8_), channel_id=1, source_target_pairs={{4,8},{5,9},{6,10},{7,11},{8,4},{9,5},{10,6},{11,7},{20,24},{21,25... | collective-permute-start | bytes 1572872 | tf_op jit(solution)/shard_map/ppermute | solution.py:62
  18.6 29.1 %collective-permute-start.3 = (bf16[128,2048]{1,0:T(8,128)(2,1)}, bf16[128,2048]{1,0:T(8,128)(2,1)S(1)}, u32[]{:S(2)}, u32[]{:S(2)}) collective-permute-start(bf16[128,2048]{1,0:T(8,128)(2,1)} %collective-permute-done.1.refs_8_), channel_id=1, source_target_pairs={{4,0},{5,1},{6,2},{7,3},{8,12},{9,13},{10,14},{11,15},{20,16},{21,... | collective-permute-start | bytes 1572872 | tf_op jit(solution)/shard_map/ppermute | solution.py:62
  29.0 20.5 %collective-permute-start.6 = (bf16[128,3200]{1,0:T(8,128)(2,1)S(1)}, bf16[128,3200]{1,0:T(8,128)(2,1)S(1)}, u32[]{:S(2)}, u32[]{:S(2)}) collective-permute-start(bf16[128,3200]{1,0:T(8,128)(2,1)S(1)} %collective-permute-done.5.refs_2_), channel_id=1, source_target_pairs={{0,1},{1,0},{2,3},{3,2},{4,5},{5,4},{6,7},{7,6},{8,9},{9,8},{10,11... | collective-permute-start | bytes 2457608 | tf_op jit(solution)/shard_map/ppermute | solution.py:52
  31.9 17.7 %collective-permute-start.8 = (bf16[128,3200]{1,0:T(8,128)(2,1)S(1)}, bf16[128,3200]{1,0:T(8,128)(2,1)S(1)}, u32[]{:S(2)}, u32[]{:S(2)}) collective-permute-start(bf16[128,3200]{1,0:T(8,128)(2,1)S(1)} %collective-permute-done.7.refs_4_), channel_id=1, source_target_pairs={{0,1},{1,0},{2,3},{3,2},{4,5},{5,4},{6,7},{7,6},{8,9},{9,8},{10,11... | collective-permute-start | bytes 2457608 | tf_op jit(solution)/shard_map/ppermute | solution.py:52
  47.7 2.9 %collective-permute-start.10 = (bf16[128,3200]{1,0:T(8,128)(2,1)}, bf16[128,3200]{1,0:T(8,128)(2,1)S(1)}, u32[]{:S(2)}, u32[]{:S(2)}) collective-permute-start(bf16[128,3200]{1,0:T(8,128)(2,1)} %collective-permute-done.9.refs_6_), channel_id=1, source_target_pairs={{0,1},{1,0},{2,3},{3,2},{4,5},{5,4},{6,7},{7,6},{8,9},{9,8},{10,11... | collective-permute-start | bytes 2457608 | tf_op jit(solution)/shard_map/ppermute | solution.py:52
  47.7 3.5 %collective-permute-start.4 = (bf16[128,3200]{1,0:T(8,128)(2,1)S(1)}, bf16[128,3200]{1,0:T(8,128)(2,1)S(1)}, u32[]{:S(2)}, u32[]{:S(2)}) collective-permute-start(bf16[128,3200]{1,0:T(8,128)(2,1)S(1)} %get-tuple-element.61.refs_0_), channel_id=1, source_target_pairs={{0,1},{1,0},{2,3},{3,2},{4,5},{5,4},{6,7},{7,6},{8,9},{9,8},{10,11... | collective-permute-start | bytes 2457608 | tf_op jit(solution)/shard_map/ppermute | solution.py:52
  48.2 16.8 %collective-permute-start.11 = (bf16[128,2048]{1,0:T(8,128)(2,1)S(1)}, bf16[128,2048]{1,0:T(8,128)(2,1)S(1)}, u32[]{:S(2)}, u32[]{:S(2)}) collective-permute-start(bf16[128,2048]{1,0:T(8,128)(2,1)S(1)} %collective-permute-done.2.refs_8_), channel_id=1, source_target_pairs={{4,0},{5,1},{6,2},{7,3},{8,12},{9,13},{10,14},{11,15},{20,16},{21,... | collective-permute-start | bytes 1572872 | tf_op jit(solution)/shard_map/ppermute | solution.py:62
  56.7 20.9 %collective-permute-start.12 = (bf16[128,2048]{1,0:T(8,128)(2,1)S(1)}, bf16[128,2048]{1,0:T(8,128)(2,1)S(1)}, u32[]{:S(2)}, u32[]{:S(2)}) collective-permute-start(bf16[128,2048]{1,0:T(8,128)(2,1)S(1)} %get-tuple-element.78), channel_id=1, source_target_pairs={{0,4},{1,5},{2,6},{3,7},{12,8},{13,9},{14,10},{15,11},{16,20},{17,... | collective-permute-start | bytes 1572872 | tf_op jit(solution)/shard_map/ppermute | solution.py:62
  70.4 15.1 %collective-permute-start.16 = (bf16[128,2048]{1,0:T(8,128)(2,1)S(1)}, bf16[128,2048]{1,0:T(8,128)(2,1)S(1)}, u32[]{:S(2)}, u32[]{:S(2)}) collective-permute-start(bf16[128,2048]{1,0:T(8,128)(2,1)S(1)} %get-tuple-element.84.refs_0_), channel_id=1, source_target_pairs={{0,4},{1,5},{2,6},{3,7},{12,8},{13,9},{14,10},{15,11},{16,20},{17,... | collective-permute-start | bytes 1572872 | tf_op jit(solution)/shard_map/ppermute | solution.py:62
  77.5 18.4 %collective-permute-start.19 = (bf16[128,2048]{1,0:T(8,128)(2,1)S(1)}, bf16[128,2048]{1,0:T(8,128)(2,1)S(1)}, u32[]{:S(2)}, u32[]{:S(2)}) collective-permute-start(bf16[128,2048]{1,0:T(8,128)(2,1)S(1)} %get-tuple-element.92), channel_id=1, source_target_pairs={{0,4},{1,5},{2,6},{3,7},{4,0},{5,1},{6,2},{7,3},{8,12},{9,13},{10,... | collective-permute-start | bytes 1572872 | tf_op jit(solution)/shard_map/ppermute | solution.py:62
  77.7 18.2 %collective-permute-start.20 = (bf16[128,2048]{1,0:T(8,128)(2,1)S(1)}, bf16[128,2048]{1,0:T(8,128)(2,1)S(1)}, u32[]{:S(2)}, u32[]{:S(2)}) collective-permute-start(bf16[128,2048]{1,0:T(8,128)(2,1)S(1)} %add.84), channel_id=1, source_target_pairs={{4,8},{5,9},{6,10},{7,11},{8,4},{9,5},{10,6},{11,7},{20,24},{21,25... | collective-permute-start | bytes 1572872 | tf_op jit(solution)/shard_map/ppermute | solution.py:62
  83.9 14.8 %collective-permute-start.13 = (bf16[640,128]{1,0:T(8,128)(2,1)S(1)}, bf16[640,128]{1,0:T(8,128)(2,1)S(1)}, u32[]{:S(2)}, u32[]{:S(2)}) collective-permute-start(bf16[640,128]{1,0:T(8,128)(2,1)S(1)} %get-tuple-element.81), channel_id=1, source_target_pairs={{0,2},{1,3},{2,0},{3,1},{4,6},{5,7},{6,4},{7,5},{8,10},{9,11},{10,... | collective-permute-start | bytes 491528 | tf_op jit(solution)/shard_map/ppermute | solution.py:52
  86.2 31.6 %collective-permute-start.17 = (bf16[64,2048]{1,0:T(8,128)(2,1)S(1)}, bf16[64,2048]{1,0:T(8,128)(2,1)S(1)}, u32[]{:S(2)}, u32[]{:S(2)}) collective-permute-start(bf16[64,2048]{1,0:T(8,128)(2,1)S(1)} %get-tuple-element.88), channel_id=1, source_target_pairs={{4,12},{5,13},{6,14},{7,15},{8,0},{9,1},{10,2},{11,3},{20,28},{21,... | collective-permute-start | bytes 786440 | tf_op jit(solution)/shard_map/ppermute | solution.py:62
  87.5 30.3 %collective-permute-start.18 = (bf16[64,2048]{1,0:T(8,128)(2,1)S(1)}, bf16[64,2048]{1,0:T(8,128)(2,1)S(1)}, u32[]{:S(2)}, u32[]{:S(2)}) collective-permute-start(bf16[64,2048]{1,0:T(8,128)(2,1)S(1)} %get-tuple-element.89), channel_id=1, source_target_pairs={{4,28},{5,29},{6,30},{7,31},{8,16},{9,17},{10,18},{11,19},{20,12},... | collective-permute-start | bytes 786440 | tf_op jit(solution)/shard_map/ppermute | solution.py:62
  96.6 21.2 %collective-permute-start.21 = (bf16[64,2048]{1,0:T(8,128)(2,1)S(1)}, bf16[64,2048]{1,0:T(8,128)(2,1)S(1)}, u32[]{:S(2)}, u32[]{:S(2)}) collective-permute-start(bf16[64,2048]{1,0:T(8,128)(2,1)S(1)} %get-tuple-element.94), channel_id=1, source_target_pairs={{0,16},{1,17},{2,18},{3,19},{4,20},{5,21},{6,22},{7,23},{8,24},{9,... | collective-permute-start | bytes 786440 | tf_op jit(solution)/shard_map/ppermute | solution.py:52
  98.2 16.1 %collective-permute-start.14 = (bf16[640,128]{1,0:T(8,128)(2,1)S(1)}, bf16[640,128]{1,0:T(8,128)(2,1)S(1)}, u32[]{:S(2)}, u32[]{:S(2)}) collective-permute-start(bf16[640,128]{1,0:T(8,128)(2,1)S(1)} %get-tuple-element.82), channel_id=1, source_target_pairs={{0,16},{1,17},{2,18},{3,19},{4,20},{5,21},{6,22},{7,23},{8,24},{9,... | collective-permute-start | bytes 491528 | tf_op jit(solution)/shard_map/ppermute | solution.py:52
  98.7 19.1 %collective-permute-start.15 = (bf16[640,128]{1,0:T(8,128)(2,1)S(1)}, bf16[640,128]{1,0:T(8,128)(2,1)S(1)}, u32[]{:S(2)}, u32[]{:S(2)}) collective-permute-start(bf16[640,128]{1,0:T(8,128)(2,1)S(1)} %get-tuple-element.83), channel_id=1, source_target_pairs={{0,18},{1,19},{2,16},{3,17},{4,22},{5,23},{6,20},{7,21},{8,26},{9,... | collective-permute-start | bytes 491528 | tf_op jit(solution)/shard_map/ppermute | solution.py:52
  117.9 1.7 %collective-permute-start.22 = (bf16[640,128]{1,0:T(8,128)(2,1)S(1)}, bf16[640,128]{1,0:T(8,128)(2,1)S(1)}, u32[]{:S(2)}, u32[]{:S(2)}) collective-permute-start(bf16[640,128]{1,0:T(8,128)(2,1)S(1)} %get-tuple-element.100), channel_id=1, source_target_pairs={{0,1},{1,0},{2,3},{3,2},{4,5},{5,4},{6,7},{7,6},{8,9},{9,8},{10,11... | collective-permute-start | bytes 491528 | tf_op jit(solution)/shard_map/ppermute | solution.py:52

commit v8 on v7

--- a/solution.py
+++ b/solution.py
@@ -81,7 +81,7 @@
     packs, rest = refs[: plan.sources], refs[plan.sources :]
     weight_refs, rest = rest[: len(where)], rest[len(where) :]
     earlier_refs, rest = rest[:earlier], rest[earlier:]
-    count = plan.sources // 2 if earlier else 1
+    count = plan.dp if earlier else 1
     p_ref, back_refs, (grads, heads, weights) = rest[0], rest[1 : 1 + count], rest[1 + count :]
     tokens, cap, part, top, head_dim = plan.tokens, plan.cap, plan.part, plan.top, plan.head_dim
     pair_rows = 2 * cap
@@ -90,8 +90,8 @@
 
     def put(s, slot, at, value):
         if earlier:
-            start = (s % 2) * length + slot * plan.back + at
-            back_refs[s // 2][pl.ds(start, value.shape[0]), :] = value
+            start = (s % GROUP) * length + slot * plan.back + at
+            back_refs[s // GROUP][pl.ds(start, value.shape[0]), :] = value
         else:
             back_refs[0][s, pl.ds(at, value.shape[0]), :] = value
 
@@ -193,8 +193,8 @@
     rows = plan.sources * plan.cap
     if earlier:
         backs = (
-            jax.ShapeDtypeStruct((2 * plan.planes * plan.back, LANES), jnp.bfloat16),
-        ) * (plan.sources // 2)
+            jax.ShapeDtypeStruct((GROUP * plan.planes * plan.back, LANES), jnp.bfloat16),
+        ) * plan.dp
     else:
         backs = (jax.ShapeDtypeStruct((plan.sources, plan.back, LANES), jnp.bfloat16),)
     vmem = pl.BlockSpec(memory_space=pltpu.VMEM)
@@ -263,27 +263,25 @@
 
 
 def merge_kernel(plan, *refs):
-    parts, outs = refs[: len(refs) - 2], refs[len(refs) - 2 :]
+    parts, outs = refs[: plan.dp], refs[plan.dp :]
     length = plan.planes * plan.back
-    for dc, out in enumerate(outs):
-        for dy in range(plan.rows):
-            total = None
-            for ref in parts[dy :: plan.rows]:
-                piece = ref[pl.ds(dc * length, length), :].astype(jnp.float32)
-                total = piece if total is None else total + piece
-            out[pl.ds(dy * length, length), :] = total.astype(out.dtype)
+    for j, out in enumerate(outs):
+        at = pl.ds(j * length, length)
+        total = parts[0][at, :].astype(jnp.float32)
+        for ref in parts[1:]:
+            total = total + ref[at, :].astype(jnp.float32)
+        out[...] = total.astype(out.dtype)
 
 
 def merge_work(plan, parts):
     vmem = pl.BlockSpec(memory_space=pltpu.VMEM)
-    rows = jax.ShapeDtypeStruct((plan.rows * plan.planes * plan.back, LANES), jnp.bfloat16)
+    rows = jax.ShapeDtypeStruct((plan.planes * plan.back, LANES), jnp.bfloat16)
     return pl.pallas_call(
         functools.partial(merge_kernel, plan),
         compiler_params=pltpu.CompilerParams(vmem_limit_bytes=6 * 1024 * 1024),
-        cost_estimate=pl.CostEstimate(flops=1, bytes_accessed=1, transcendentals=0),
-        out_shape=(rows, rows),
-        in_specs=[vmem] * len(parts),
-        out_specs=(vmem, vmem),
+        out_shape=(rows,) * GROUP,
+        in_specs=[vmem] * plan.dp,
+        out_specs=(vmem,) * GROUP,
     )(*parts)
 
 
@@ -334,9 +332,10 @@
     )(info, route_ids)
 
 
-def final_kernel(plan, target_ref, own_ref, other_ref, head_ref, out_gate_ref):
+def final_kernel(plan, target_ref, *refs):
+    head_ref, out_gate_ref = refs[GROUP:]
     length = plan.rows * plan.planes * plan.back
-    table = jnp.concatenate([own_ref[...], other_ref[...]], axis=0)
+    table = jnp.concatenate([ref[...] for ref in refs[:GROUP]], axis=0)
     block = 256
     for start in range(0, plan.tokens * plan.top, block):
         at = pl.ds(start, block)
@@ -351,7 +350,7 @@
         )
 
 
-def final_work(plan, target, own, other):
+def final_work(plan, target, tables):
     count = plan.tokens * plan.top
     vmem = pl.BlockSpec(memory_space=pltpu.VMEM)
     return pl.pallas_call(
@@ -361,10 +360,10 @@
             jax.ShapeDtypeStruct((count, plan.head_dim), jnp.bfloat16),
             jax.ShapeDtypeStruct((count, 1), jnp.float32),
         ),
-        in_specs=[vmem] * 3,
+        in_specs=[vmem] * (1 + GROUP),
         out_specs=(vmem, vmem),
         compiler_params=pltpu.CompilerParams(vmem_limit_bytes=8 * 1024 * 1024),
-    )(target, own, other)
+    )(target, *tables)
 
 
 def local(mesh, head_outputs, out_grad, gate_weights, route_ids, out_proj):
@@ -416,7 +415,7 @@
         value = plan.shift(value, dx=dx, dy=dy)
         if plan.planes == 4:
             if dx or dy:
-                value, near_in, mate = lax.optimization_barrier((value, near_in, mate))
+                value, far_in, near_out = lax.optimization_barrier((value, far_in, near_out))
             else:
                 value, near_out = lax.optimization_barrier((value, near_out))
         packs += [value, plan.shift(value, dc=1)]
@@ -447,22 +446,27 @@
     if plan.planes == 4:
         far_part = plan.along(sums[1], inward)
         far_part, done = lax.optimization_barrier((far_part, done))
-        far_pieces = sum_work(plan, info, [sums[1], far_part], jnp.bfloat16)
-        info, far_pieces = lax.optimization_barrier((info, far_pieces))
-        far_pieces = [plan.along(piece, across, dx) for dx, piece in enumerate(far_pieces)]
+        far_sums = sum_work(plan, info, [sums[1], far_part], jnp.bfloat16)
+        info, far_sums = lax.optimization_barrier((info, far_sums))
+        far_pieces = [plan.along(piece, across, dx) for dx, piece in enumerate(far_sums)]
         received = [plan.along(sums[2], mates), plan.along(near_sum, middle)]
     else:
         received = [plan.shift(sums[j], dz=steps[j]) for j in range(plan.planes - 1)]
     pieces = sum_work(plan, info, [sums[-1]] + received, jnp.float32)
     pieces = [plan.shift(piece, dx=dx) for dx, piece in enumerate(pieces)]
 
-    backs = [
-        plan.shift(rows, dx=-dx % plan.dp, dy=-dy % plan.rows)
-        for rows, (dx, dy) in zip(backs, plan.chips())
+    backs = [plan.shift(rows, dx=-dx % plan.dp) for dx, rows in enumerate(backs)]
+    if plan.planes == 4:
+        backs, far_sums = lax.optimization_barrier((backs, far_sums))
+    merged = merge_work(plan, backs)
+    tables = [
+        plan.shift(merged[2 * dy + dc], dy=-dy % plan.rows)
+        for dy in range(plan.rows)
+        for dc in range(2)
     ]
-    backs, far_pieces, pieces = lax.optimization_barrier((backs, far_pieces, pieces))
-    own, other = merge_work(plan, backs)
-    grad_head, grad_gate = final_work(plan, target, own, plan.shift(other, dc=1))
+    tables = tables[0::2] + [plan.shift(rows, dc=1) for rows in tables[1::2]]
+    tables, far_pieces, pieces = lax.optimization_barrier((tables, far_pieces, pieces))
+    grad_head, grad_gate = final_work(plan, target, tables)
     grad_proj = layout_work(plan, info, pieces + far_pieces)
     return (
         grad_head.reshape(tokens, top, head_dim),

time: 123 us -> 114 us (0.927)
  waiting for transfers between devices: 57.7 us -> 49.8 us
    ppermute x12 -> x13, waiting for transfers between devices: 46.1 us -> 13.4 us  [shift(): return lax.ppermute(value, AXES, self.pairs(**by))]
    ppermute x11, waiting for transfers between devices: 11.6 us -> 36.4 us  [along(): return lax.ppermute(value, AXES, out)]
    ppermute x12 -> x13, starting transfers between devices: 10.2 us -> 9.26 us  [shift(): return lax.ppermute(value, AXES, self.pairs(**by))]
  transfers between devices with their start and end apart: 23 -> 24, of which waited for: 10 -> 10; matrix products, arithmetic and copies ran while one was open for 2% -> 2% of each run, Pallas kernels for 22% -> 22%
where the time goes in v8:
time: 114 us
  waiting for transfers between devices  49.8 us (44%)
  Pallas kernels  29.4 us (26%)
  starting transfers between devices  27.3 us (24%)
  local copies, waits for them, and re-layouts  5.15 us (5%)
  other arithmetic  1.36 us (1%)
    ppermute x11, waiting for transfers between devices, along(): return lax.ppermute(value, AXES, out)  36.4 us
    pallas_call x4, Pallas kernels, slot_work(): pl.pallas_call(functools.partial(slot_kernel, plan, index, [where for _,...  21.8 us
    ppermute x11, starting transfers between devices, along(): return lax.ppermute(value, AXES, out)  18.1 us
    ppermute x13, waiting for transfers between devices, shift(): return lax.ppermute(value, AXES, self.pairs(**by))  13.4 us
    ppermute x13, starting transfers between devices, shift(): return lax.ppermute(value, AXES, self.pairs(**by))  9.26 us
    unnamed x15, local copies, waits for them, and re-layouts  4.01 us
    pallas_call x1, Pallas kernels, target_work(): pl.pallas_call(functools.partial(target_kernel, plan), out_shape=jax.Shap...  2.36 us
  transfers between devices with their start and end apart: 24, of which 10 were waited for; matrix products, arithmetic and copies ran while one was open for 2% of the time, Pallas kernels for 22%

profile of v8, /device:TPU:0, one launch (start us, length us, event | category | flops | bytes accessed | tf_op | source)
XLA Modules:
  0.0 113.9 jit_solution(11641532767940677940)
XLA Ops:
  0.6 0.0 copy-start
  0.7 1.2 %copy-done = bf16[1,128,4096]{2,1,0:T(8,128)(2,1)S(1)} copy-done((bf16[1,128,4096]{2,1,0:T(8,128)(2,1)S(1)}, bf16[1,128,4096]{2,1,0:T(8,128)(2,1)}, u32[]{:S(2)}) %copy-start) | copy-done | bytes 1048600
  1.9 0.8 dynamic-slice_bitcast_fusion.refs_8_
  2.7 3.0 %collective-permute-start = (bf16[128,2048]{1,0:T(8,128)(2,1)}, bf16[128,2048]{1,0:T(8,128)(2,1)}, u32[]{:S(2)}, u32[]{:S(2)}) collective-permute-start(bf16[128,2048]{1,0:T(8,128)(2,1)} %dynamic-slice_bitcast_fusion.refs_8_), channel_id=1, source_target_pairs={{0,4},{1,5},{2,6},{3,7},{4,0},{5,1},{6,2},{7,3},{8,12},{9,13},{10,... | collective-permute-start | bytes 1572872 | tf_op jit(solution)/shard_map/ppermute | solution.py:62
  5.7 1.4 %collective-permute-start.1 = (bf16[128,2048]{1,0:T(8,128)(2,1)}, bf16[128,2048]{1,0:T(8,128)(2,1)}, u32[]{:S(2)}, u32[]{:S(2)}) collective-permute-start(bf16[128,2048]{1,0:T(8,128)(2,1)} %dynamic-slice_bitcast_fusion.refs_8_), channel_id=1, source_target_pairs={{4,8},{5,9},{6,10},{7,11},{8,4},{9,5},{10,6},{11,7},{20,24},{21,25... | collective-permute-start | bytes 1572872 | tf_op jit(solution)/shard_map/ppermute | solution.py:62
  7.3 0.0 copy-start.5
  7.3 0.1 constant_dynamic-slice_fusion
  7.4 0.5 copy-done.5
  7.9 1.0 fusion.1
  9.0 1.5 %collective-permute-start.5 = (bf16[128,3200]{1,0:T(8,128)(2,1)S(1)}, bf16[128,3200]{1,0:T(8,128)(2,1)S(1)}, u32[]{:S(2)}, u32[]{:S(2)}) collective-permute-start(bf16[128,3200]{1,0:T(8,128)(2,1)S(1)} %get-tuple-element.63.refs_0_), channel_id=1, source_target_pairs={{0,2},{1,3},{2,0},{3,1},{4,6},{5,7},{6,4},{7,5},{8,10},{9,11},{10,... | collective-permute-start | bytes 2457608 | tf_op jit(solution)/shard_map/ppermute | solution.py:52
  10.5 1.5 %collective-permute-start.7 = (bf16[128,3200]{1,0:T(8,128)(2,1)}, bf16[128,3200]{1,0:T(8,128)(2,1)S(1)}, u32[]{:S(2)}, u32[]{:S(2)}) collective-permute-start(bf16[128,3200]{1,0:T(8,128)(2,1)} %get-tuple-element.119), channel_id=1, source_target_pairs={{0,16},{1,17},{2,18},{3,19},{4,20},{5,21},{6,22},{7,23},{8,24},{9,... | collective-permute-start | bytes 2457608 | tf_op jit(solution)/shard_map/ppermute | solution.py:52
  12.0 0.5 collective-permute-start.9
  12.5 0.7 copy.10.route_ref
  13.2 0.1 stack.63.info
  13.3 0.0 copy-start.1
  13.3 0.8 copy-done.1
  14.1 2.4 %shard_map.76.target_ref = s32[1024,128]{1,0:T(8,128)S(1)} custom-call(s32[15]{0:T(128)S(1)} %stack.63.info, s32[128,8]{1,0:T(8,128)S(1)} %copy-done.1), custom_call_target="tpu_custom_call" | custom-call | tf_op jit(solution)/shard_map/pallas_call | solution.py:326
  16.5 1.5 %collective-permute-done.refs_8_ = bf16[128,2048]{1,0:T(8,128)(2,1)} collective-permute-done((bf16[128,2048]{1,0:T(8,128)(2,1)}, bf16[128,2048]{1,0:T(8,128)(2,1)}, u32[]{:S(2)}, u32[]{:S(2)}) %collective-permute-start) | collective-permute-done | bytes 524320 | tf_op jit(solution)/shard_map/ppermute | solution.py:62
  18.0 0.7 collective-permute-start.2
  18.7 1.3 %collective-permute-start.3 = (bf16[128,2048]{1,0:T(8,128)(2,1)}, bf16[128,2048]{1,0:T(8,128)(2,1)S(1)}, u32[]{:S(2)}, u32[]{:S(2)}) collective-permute-start(bf16[128,2048]{1,0:T(8,128)(2,1)} %collective-permute-done.1.refs_8_), channel_id=1, source_target_pairs={{4,0},{5,1},{6,2},{7,3},{8,12},{9,13},{10,14},{11,15},{20,16},{21,... | collective-permute-start | bytes 1572872 | tf_op jit(solution)/shard_map/ppermute | solution.py:62
  20.0 18.3 %collective-permute-done.3.refs_9_ = bf16[128,2048]{1,0:T(8,128)(2,1)S(1)} collective-permute-done((bf16[128,2048]{1,0:T(8,128)(2,1)}, bf16[128,2048]{1,0:T(8,128)(2,1)S(1)}, u32[]{:S(2)}, u32[]{:S(2)}) %collective-permute-start.3) | collective-permute-done | bytes 524320 | tf_op jit(solution)/shard_map/ppermute | solution.py:62
  38.3 0.0 collective-permute-start.4
  38.3 0.0 collective-permute-done.5.refs_2_
  38.3 0.5 collective-permute-start.6
  38.8 0.0 collective-permute-done.7.refs_4_
  38.8 0.1 collective-permute-start.8
  38.9 8.8 %collective-permute-done.9.refs_6_ = bf16[128,3200]{1,0:T(8,128)(2,1)} collective-permute-done((bf16[128,3200]{1,0:T(8,128)(2,1)}, bf16[128,3200]{1,0:T(8,128)(2,1)}, u32[]{:S(2)}, u32[]{:S(2)}) %collective-permute-start.9) | collective-permute-done | bytes 819232 | tf_op jit(solution)/shard_map/ppermute | solution.py:52
  47.7 0.0 collective-permute-start.10
  47.7 1.3 %collective-permute-start.11 = (bf16[128,2048]{1,0:T(8,128)(2,1)S(1)}, bf16[128,2048]{1,0:T(8,128)(2,1)S(1)}, u32[]{:S(2)}, u32[]{:S(2)}) collective-permute-start(bf16[128,2048]{1,0:T(8,128)(2,1)S(1)} %collective-permute-done.2.refs_8_), channel_id=1, source_target_pairs={{4,0},{5,1},{6,2},{7,3},{8,12},{9,13},{10,14},{11,15},{20,16},{21,... | collective-permute-start | bytes 1572872 | tf_op jit(solution)/shard_map/ppermute | solution.py:62
  49.0 0.0 collective-permute-done.4.refs_1_
  49.0 0.0 collective-permute-done.8.refs_5_
  49.0 1.2 %collective-permute-done.10.refs_7_ = bf16[128,3200]{1,0:T(8,128)(2,1)S(1)} collective-permute-done((bf16[128,3200]{1,0:T(8,128)(2,1)}, bf16[128,3200]{1,0:T(8,128)(2,1)S(1)}, u32[]{:S(2)}, u32[]{:S(2)}) %collective-permute-start.10) | collective-permute-done | bytes 819232 | tf_op jit(solution)/shard_map/ppermute | solution.py:52
  50.3 5.5 %shard_map.77 = (bf16[128,2048]{1,0:T(8,128)(2,1)S(1)}, bf16[8,80,128]{2,1,0:T(8,128)(2,1)S(1)}) custom-call(s32[15]{0:T(128)S(1)} %stack.63.info, bf16[128,3200]{1,0:T(8,128)(2,1)S(1)} %get-tuple-element.63.refs_0_, bf16[128,3200]{1,0:T(8,128)(2,1)S(1)} %collective-permute-done.4.refs_1_, bf16[128,3200]{1,0:T(8,128)(2,1)S(1)} %collective-permute-done.5.refs_2_, ...), custom_call_target="tpu_custom_call" | custom-call | tf_op jit(solution)/shard_map/pallas_call | solution.py:201
  55.8 5.3 %collective-permute-start.12 = (bf16[128,2048]{1,0:T(8,128)(2,1)S(1)}, bf16[128,2048]{1,0:T(8,128)(2,1)S(1)}, u32[]{:S(2)}, u32[]{:S(2)}) collective-permute-start(bf16[128,2048]{1,0:T(8,128)(2,1)S(1)} %get-tuple-element.80), channel_id=1, source_target_pairs={{0,4},{1,5},{2,6},{3,7},{12,8},{13,9},{14,10},{15,11},{16,20},{17,... | collective-permute-start | bytes 1572872 | tf_op jit(solution)/shard_map/ppermute | solution.py:62
  61.1 3.9 %collective-permute-done.11.refs_9_ = bf16[128,2048]{1,0:T(8,128)(2,1)S(1)} collective-permute-done((bf16[128,2048]{1,0:T(8,128)(2,1)S(1)}, bf16[128,2048]{1,0:T(8,128)(2,1)S(1)}, u32[]{:S(2)}, u32[]{:S(2)}) %collective-permute-start.11) | collective-permute-done | bytes 524320 | tf_op jit(solution)/shard_map/ppermute | solution.py:62
  65.0 5.3 %shard_map.78 = (bf16[128,2048]{1,0:T(8,128)(2,1)S(1)}, bf16[8,80,128]{2,1,0:T(8,128)(2,1)S(1)}) custom-call(s32[15]{0:T(128)S(1)} %stack.63.info, bf16[128,3200]{1,0:T(8,128)(2,1)S(1)} %get-tuple-element.63.refs_0_, bf16[128,3200]{1,0:T(8,128)(2,1)S(1)} %collective-permute-done.4.refs_1_, bf16[128,3200]{1,0:T(8,128)(2,1)S(1)} %collective-permute-done.5.refs_2_, ...), custom_call_target="tpu_custom_call" | custom-call | tf_op jit(solution)/shard_map/pallas_call | solution.py:201
  70.3 1.7 %collective-permute-start.14 = (bf16[128,2048]{1,0:T(8,128)(2,1)S(1)}, bf16[128,2048]{1,0:T(8,128)(2,1)S(1)}, u32[]{:S(2)}, u32[]{:S(2)}) collective-permute-start(bf16[128,2048]{1,0:T(8,128)(2,1)S(1)} %get-tuple-element.84.refs_0_), channel_id=1, source_target_pairs={{0,4},{1,5},{2,6},{3,7},{12,8},{13,9},{14,10},{15,11},{16,20},{17,... | collective-permute-start | bytes 1572872 | tf_op jit(solution)/shard_map/ppermute | solution.py:62
  72.0 5.5 %shard_map.79 = (bf16[128,2048]{1,0:T(8,128)(2,1)S(1)}, bf16[8,80,128]{2,1,0:T(8,128)(2,1)S(1)}) custom-call(s32[15]{0:T(128)S(1)} %stack.63.info, bf16[128,3200]{1,0:T(8,128)(2,1)S(1)} %get-tuple-element.63.refs_0_, bf16[128,3200]{1,0:T(8,128)(2,1)S(1)} %collective-permute-done.4.refs_1_, bf16[128,3200]{1,0:T(8,128)(2,1)S(1)} %collective-permute-done.5.refs_2_, ...), custom_call_target="tpu_custom_call" | custom-call | tf_op jit(solution)/shard_map/pallas_call | solution.py:201
  77.5 0.1 collective-permute-start.21
  77.5 0.0 collective-permute-done.12
  77.5 0.1 add.84
  77.7 0.7 collective-permute-start.22
  78.4 5.5 %shard_map.80 = (f32[128,2048]{1,0:T(8,128)S(1)}, bf16[1280,128]{1,0:T(8,128)(2,1)S(1)}, bf16[1280,128]{1,0:T(8,128)(2,1)S(1)}) custom-call(s32[15]{0:T(128)S(1)} %stack.63.info, bf16[128,3200]{1,0:T(8,128)(2,1)S(1)} %get-tuple-element.63.refs_0_, bf16[128,3200]{1,0:T(8,128)(2,1)S(1)} %collective-permute-done.4.refs_1_, ...), custom_call_target="tpu_custom_call" | custom-call | tf_op jit(solution)/shard_map/pallas_call | solution.py:201
  83.9 1.5 %collective-permute-start.13 = (bf16[1280,128]{1,0:T(8,128)(2,1)S(1)}, bf16[1280,128]{1,0:T(8,128)(2,1)S(1)}, u32[]{:S(2)}, u32[]{:S(2)}) collective-permute-start(bf16[1280,128]{1,0:T(8,128)(2,1)S(1)} %get-tuple-element.83), channel_id=1, source_target_pairs={{0,16},{1,17},{2,18},{3,19},{4,20},{5,21},{6,22},{7,23},{8,24},{9,... | collective-permute-start | bytes 983048 | tf_op jit(solution)/shard_map/ppermute | solution.py:52
  85.4 0.7 shard_map.81
  86.1 1.3 %collective-permute-start.19 = (bf16[64,2048]{1,0:T(8,128)(2,1)S(1)}, bf16[64,2048]{1,0:T(8,128)(2,1)S(1)}, u32[]{:S(2)}, u32[]{:S(2)}) collective-permute-start(bf16[64,2048]{1,0:T(8,128)(2,1)S(1)} %get-tuple-element.88), channel_id=1, source_target_pairs={{4,12},{5,13},{6,14},{7,15},{8,0},{9,1},{10,2},{11,3},{20,28},{21,... | collective-permute-start | bytes 786440 | tf_op jit(solution)/shard_map/ppermute | solution.py:62
  87.4 1.3 %collective-permute-start.20 = (bf16[64,2048]{1,0:T(8,128)(2,1)S(1)}, bf16[64,2048]{1,0:T(8,128)(2,1)S(1)}, u32[]{:S(2)}, u32[]{:S(2)}) collective-permute-start(bf16[64,2048]{1,0:T(8,128)(2,1)S(1)} %get-tuple-element.89), channel_id=1, source_target_pairs={{4,28},{5,29},{6,30},{7,31},{8,16},{9,17},{10,18},{11,19},{20,12},... | collective-permute-start | bytes 786440 | tf_op jit(solution)/shard_map/ppermute | solution.py:62
  88.7 6.3 %collective-permute-done.21.refs_1_ = bf16[128,2048]{1,0:T(8,128)(2,1)S(1)} collective-permute-done((bf16[128,2048]{1,0:T(8,128)(2,1)S(1)}, bf16[128,2048]{1,0:T(8,128)(2,1)S(1)}, u32[]{:S(2)}, u32[]{:S(2)}) %collective-permute-start.21) | collective-permute-done | bytes 524320 | tf_op jit(solution)/shard_map/ppermute | solution.py:62
  95.0 0.7 shard_map.83
  95.7 1.6 %collective-permute-start.23 = (bf16[64,2048]{1,0:T(8,128)(2,1)S(1)}, bf16[64,2048]{1,0:T(8,128)(2,1)S(1)}, u32[]{:S(2)}, u32[]{:S(2)}) collective-permute-start(bf16[64,2048]{1,0:T(8,128)(2,1)S(1)} %get-tuple-element.100), channel_id=1, source_target_pairs={{0,16},{1,17},{2,18},{3,19},{4,20},{5,21},{6,22},{7,23},{8,24},{9,... | collective-permute-start | bytes 786440 | tf_op jit(solution)/shard_map/ppermute | solution.py:52
  97.2 0.1 shard_map.82
  97.3 1.6 %collective-permute-start.17 = (bf16[320,128]{1,0:T(8,128)(2,1)S(1)}, bf16[320,128]{1,0:T(8,128)(2,1)S(1)}, u32[]{:S(2)}, u32[]{:S(2)}) collective-permute-start(bf16[320,128]{1,0:T(8,128)(2,1)S(1)} %get-tuple-element.95), channel_id=1, source_target_pairs={{0,2},{1,3},{2,0},{3,1},{4,6},{5,7},{6,4},{7,5},{8,10},{9,11},{10,... | collective-permute-start | bytes 245768 | tf_op jit(solution)/shard_map/ppermute | solution.py:52
  98.9 0.5 collective-permute-start.15
  99.4 2.1 %collective-permute-done.19.refs_2_ = bf16[64,2048]{1,0:T(8,128)(2,1)S(1)} collective-permute-done((bf16[64,2048]{1,0:T(8,128)(2,1)S(1)}, bf16[64,2048]{1,0:T(8,128)(2,1)S(1)}, u32[]{:S(2)}, u32[]{:S(2)}) %collective-permute-start.19) | collective-permute-done | bytes 262176 | tf_op jit(solution)/shard_map/ppermute | solution.py:62
  101.5 0.0 collective-permute-start.16
  101.5 0.8 collective-permute-done.17
  102.3 4.3 %collective-permute-done.20.refs_3_ = bf16[64,2048]{1,0:T(8,128)(2,1)S(1)} collective-permute-done((bf16[64,2048]{1,0:T(8,128)(2,1)S(1)}, bf16[64,2048]{1,0:T(8,128)(2,1)S(1)}, u32[]{:S(2)}, u32[]{:S(2)}) %collective-permute-start.20) | collective-permute-done | bytes 262176 | tf_op jit(solution)/shard_map/ppermute | solution.py:62
  106.6 0.0 collective-permute-done.15.refs_1_
  106.6 2.5 %collective-permute-done.23.refs_1_ = bf16[64,2048]{1,0:T(8,128)(2,1)S(1)} collective-permute-done((bf16[64,2048]{1,0:T(8,128)(2,1)S(1)}, bf16[64,2048]{1,0:T(8,128)(2,1)S(1)}, u32[]{:S(2)}, u32[]{:S(2)}) %collective-permute-start.23) | collective-permute-done | bytes 262176 | tf_op jit(solution)/shard_map/ppermute | solution.py:52
  109.1 2.2 %shard_map.84 = (bf16[1024,128]{1,0:T(8,128)(2,1)}, f32[1024,1]{1,0:T(8,128)S(1)}) custom-call(s32[1024,128]{1,0:T(8,128)S(1)} %shard_map.76.target_ref, bf16[320,128]{1,0:T(8,128)(2,1)S(1)} %get-tuple-element.101.refs_0_, bf16[320,128]{1,0:T(8,128)(2,1)S(1)} %collective-permute-done.15.refs_1_, bf16[320,128]{1,0:T(8,128)(2,1)S(1)} %collective-permute-done.16.refs_2_, ...), custom_call_target="tpu_custom_call" | custom-call | flops 1 | bytes 1 | tf_op jit(solution)/shard_map/pallas_call | solution.py:356
  111.3 0.2 convert_reduce_fusion
  111.5 0.1 convert_element_type.15
  111.6 0.7 copy.11
  112.3 1.6 %shard_map.85 = f32[64,4096]{1,0:T(8,128)} custom-call(s32[15]{0:T(128)S(1)} %stack.63.info, f32[64,2048]{1,0:T(8,128)S(1)} %get-tuple-element.107.refs_0_, bf16[64,2048]{1,0:T(8,128)(2,1)S(1)} %collective-permute-done.23.refs_1_, bf16[64,2048]{1,0:T(8,128)(2,1)S(1)} %collective-permute-done.19.refs_2_, bf16[64,2048]{1,0:T(8,128)(2,1)S(1)} %collective-permute-done.20.refs_3_), custom_call_target="tpu_custom_call" | custom-call | tf_op jit(solution)/shard_map/pallas_call | solution.py:256
  (18 shorter events, 0.1 us)
Async XLA Ops:
  0.6 1.2 %copy-start = (bf16[1,128,4096]{2,1,0:T(8,128)(2,1)S(1)}, bf16[1,128,4096]{2,1,0:T(8,128)(2,1)}, u32[]{:S(2)}) copy-start(bf16[1,128,4096]{2,1,0:T(8,128)(2,1)} %param.9) | copy-start | bytes 3145732
  0.6 6.5 %copy-start.3 = (bf16[128,8,128]{2,1,0:T(8,128)(2,1)S(1)}, bf16[128,8,128]{2,1,0:T(8,128)(2,1)}, u32[]{:S(2)}) copy-start(bf16[128,8,128]{2,1,0:T(8,128)(2,1)} %param.5) | copy-start | bytes 786436
  0.7 6.6 %copy-start.4 = (s32[128,8]{0,1:T(8,128)S(1)}, s32[128,8]{0,1:T(8,128)}, u32[]{:S(2)}) copy-start(s32[128,8]{0,1:T(8,128)} %param.8) | copy-start | bytes 12292
  0.7 6.6 %copy-start.2 = (bf16[128,4096]{1,0:T(8,128)(2,1)S(1)}, bf16[128,4096]{1,0:T(8,128)(2,1)}, u32[]{:S(2)}) copy-start(bf16[128,4096]{1,0:T(8,128)(2,1)} %param.6) | copy-start | bytes 3145732
  2.7 15.3 %collective-permute-start = (bf16[128,2048]{1,0:T(8,128)(2,1)}, bf16[128,2048]{1,0:T(8,128)(2,1)}, u32[]{:S(2)}, u32[]{:S(2)}) collective-permute-start(bf16[128,2048]{1,0:T(8,128)(2,1)} %dynamic-slice_bitcast_fusion.refs_8_), channel_id=1, source_target_pairs={{0,4},{1,5},{2,6},{3,7},{4,0},{5,1},{6,2},{7,3},{8,12},{9,13},{10,... | collective-permute-start | bytes 1572872 | tf_op jit(solution)/shard_map/ppermute | solution.py:62
  5.7 12.2 %collective-permute-start.1 = (bf16[128,2048]{1,0:T(8,128)(2,1)}, bf16[128,2048]{1,0:T(8,128)(2,1)}, u32[]{:S(2)}, u32[]{:S(2)}) collective-permute-start(bf16[128,2048]{1,0:T(8,128)(2,1)} %dynamic-slice_bitcast_fusion.refs_8_), channel_id=1, source_target_pairs={{4,8},{5,9},{6,10},{7,11},{8,4},{9,5},{10,6},{11,7},{20,24},{21,25... | collective-permute-start | bytes 1572872 | tf_op jit(solution)/shard_map/ppermute | solution.py:62
  7.3 0.7 copy-start.5
  9.0 29.3 %collective-permute-start.5 = (bf16[128,3200]{1,0:T(8,128)(2,1)S(1)}, bf16[128,3200]{1,0:T(8,128)(2,1)S(1)}, u32[]{:S(2)}, u32[]{:S(2)}) collective-permute-start(bf16[128,3200]{1,0:T(8,128)(2,1)S(1)} %get-tuple-element.63.refs_0_), channel_id=1, source_target_pairs={{0,2},{1,3},{2,0},{3,1},{4,6},{5,7},{6,4},{7,5},{8,10},{9,11},{10,... | collective-permute-start | bytes 2457608 | tf_op jit(solution)/shard_map/ppermute | solution.py:52
  10.5 28.3 %collective-permute-start.7 = (bf16[128,3200]{1,0:T(8,128)(2,1)}, bf16[128,3200]{1,0:T(8,128)(2,1)S(1)}, u32[]{:S(2)}, u32[]{:S(2)}) collective-permute-start(bf16[128,3200]{1,0:T(8,128)(2,1)} %get-tuple-element.119), channel_id=1, source_target_pairs={{0,16},{1,17},{2,18},{3,19},{4,20},{5,21},{6,22},{7,23},{8,24},{9,... | collective-permute-start | bytes 2457608 | tf_op jit(solution)/shard_map/ppermute | solution.py:52
  12.0 35.7 %collective-permute-start.9 = (bf16[128,3200]{1,0:T(8,128)(2,1)}, bf16[128,3200]{1,0:T(8,128)(2,1)}, u32[]{:S(2)}, u32[]{:S(2)}) collective-permute-start(bf16[128,3200]{1,0:T(8,128)(2,1)} %get-tuple-element.119), channel_id=1, source_target_pairs={{0,18},{1,19},{2,16},{3,17},{4,22},{5,23},{6,20},{7,21},{8,26},{9,... | collective-permute-start | bytes 2457608 | tf_op jit(solution)/shard_map/ppermute | solution.py:52
  13.3 0.8 copy-start.1
  18.0 2.0 %collective-permute-start.2 = (bf16[128,2048]{1,0:T(8,128)(2,1)}, bf16[128,2048]{1,0:T(8,128)(2,1)S(1)}, u32[]{:S(2)}, u32[]{:S(2)}) collective-permute-start(bf16[128,2048]{1,0:T(8,128)(2,1)} %collective-permute-done.refs_8_), channel_id=1, source_target_pairs={{4,8},{5,9},{6,10},{7,11},{8,4},{9,5},{10,6},{11,7},{20,24},{21,25... | collective-permute-start | bytes 1572872 | tf_op jit(solution)/shard_map/ppermute | solution.py:62
  18.7 19.6 %collective-permute-start.3 = (bf16[128,2048]{1,0:T(8,128)(2,1)}, bf16[128,2048]{1,0:T(8,128)(2,1)S(1)}, u32[]{:S(2)}, u32[]{:S(2)}) collective-permute-start(bf16[128,2048]{1,0:T(8,128)(2,1)} %collective-permute-done.1.refs_8_), channel_id=1, source_target_pairs={{4,0},{5,1},{6,2},{7,3},{8,12},{9,13},{10,14},{11,15},{20,16},{21,... | collective-permute-start | bytes 1572872 | tf_op jit(solution)/shard_map/ppermute | solution.py:62
  38.3 10.7 %collective-permute-start.4 = (bf16[128,3200]{1,0:T(8,128)(2,1)S(1)}, bf16[128,3200]{1,0:T(8,128)(2,1)S(1)}, u32[]{:S(2)}, u32[]{:S(2)}) collective-permute-start(bf16[128,3200]{1,0:T(8,128)(2,1)S(1)} %get-tuple-element.63.refs_0_), channel_id=1, source_target_pairs={{0,1},{1,0},{2,3},{3,2},{4,5},{5,4},{6,7},{7,6},{8,9},{9,8},{10,11... | collective-permute-start | bytes 2457608 | tf_op jit(solution)/shard_map/ppermute | solution.py:52
  38.3 10.7 %collective-permute-start.6 = (bf16[128,3200]{1,0:T(8,128)(2,1)S(1)}, bf16[128,3200]{1,0:T(8,128)(2,1)S(1)}, u32[]{:S(2)}, u32[]{:S(2)}) collective-permute-start(bf16[128,3200]{1,0:T(8,128)(2,1)S(1)} %collective-permute-done.5.refs_2_), channel_id=1, source_target_pairs={{0,1},{1,0},{2,3},{3,2},{4,5},{5,4},{6,7},{7,6},{8,9},{9,8},{10,11... | collective-permute-start | bytes 2457608 | tf_op jit(solution)/shard_map/ppermute | solution.py:52
  38.8 10.2 %collective-permute-start.8 = (bf16[128,3200]{1,0:T(8,128)(2,1)S(1)}, bf16[128,3200]{1,0:T(8,128)(2,1)S(1)}, u32[]{:S(2)}, u32[]{:S(2)}) collective-permute-start(bf16[128,3200]{1,0:T(8,128)(2,1)S(1)} %collective-permute-done.7.refs_4_), channel_id=1, source_target_pairs={{0,1},{1,0},{2,3},{3,2},{4,5},{5,4},{6,7},{7,6},{8,9},{9,8},{10,11... | collective-permute-start | bytes 2457608 | tf_op jit(solution)/shard_map/ppermute | solution.py:52
  47.7 2.5 %collective-permute-start.10 = (bf16[128,3200]{1,0:T(8,128)(2,1)}, bf16[128,3200]{1,0:T(8,128)(2,1)S(1)}, u32[]{:S(2)}, u32[]{:S(2)}) collective-permute-start(bf16[128,3200]{1,0:T(8,128)(2,1)} %collective-permute-done.9.refs_6_), channel_id=1, source_target_pairs={{0,1},{1,0},{2,3},{3,2},{4,5},{5,4},{6,7},{7,6},{8,9},{9,8},{10,11... | collective-permute-start | bytes 2457608 | tf_op jit(solution)/shard_map/ppermute | solution.py:52
  47.7 17.2 %collective-permute-start.11 = (bf16[128,2048]{1,0:T(8,128)(2,1)S(1)}, bf16[128,2048]{1,0:T(8,128)(2,1)S(1)}, u32[]{:S(2)}, u32[]{:S(2)}) collective-permute-start(bf16[128,2048]{1,0:T(8,128)(2,1)S(1)} %collective-permute-done.2.refs_8_), channel_id=1, source_target_pairs={{4,0},{5,1},{6,2},{7,3},{8,12},{9,13},{10,14},{11,15},{20,16},{21,... | collective-permute-start | bytes 1572872 | tf_op jit(solution)/shard_map/ppermute | solution.py:62
  55.8 21.8 %collective-permute-start.12 = (bf16[128,2048]{1,0:T(8,128)(2,1)S(1)}, bf16[128,2048]{1,0:T(8,128)(2,1)S(1)}, u32[]{:S(2)}, u32[]{:S(2)}) collective-permute-start(bf16[128,2048]{1,0:T(8,128)(2,1)S(1)} %get-tuple-element.80), channel_id=1, source_target_pairs={{0,4},{1,5},{2,6},{3,7},{12,8},{13,9},{14,10},{15,11},{16,20},{17,... | collective-permute-start | bytes 1572872 | tf_op jit(solution)/shard_map/ppermute | solution.py:62
  70.3 15.1 %collective-permute-start.14 = (bf16[128,2048]{1,0:T(8,128)(2,1)S(1)}, bf16[128,2048]{1,0:T(8,128)(2,1)S(1)}, u32[]{:S(2)}, u32[]{:S(2)}) collective-permute-start(bf16[128,2048]{1,0:T(8,128)(2,1)S(1)} %get-tuple-element.84.refs_0_), channel_id=1, source_target_pairs={{0,4},{1,5},{2,6},{3,7},{12,8},{13,9},{14,10},{15,11},{16,20},{17,... | collective-permute-start | bytes 1572872 | tf_op jit(solution)/shard_map/ppermute | solution.py:62
  77.5 17.5 %collective-permute-start.21 = (bf16[128,2048]{1,0:T(8,128)(2,1)S(1)}, bf16[128,2048]{1,0:T(8,128)(2,1)S(1)}, u32[]{:S(2)}, u32[]{:S(2)}) collective-permute-start(bf16[128,2048]{1,0:T(8,128)(2,1)S(1)} %get-tuple-element.98), channel_id=1, source_target_pairs={{0,4},{1,5},{2,6},{3,7},{4,0},{5,1},{6,2},{7,3},{8,12},{9,13},{10,... | collective-permute-start | bytes 1572872 | tf_op jit(solution)/shard_map/ppermute | solution.py:62
  77.7 17.3 %collective-permute-start.22 = (bf16[128,2048]{1,0:T(8,128)(2,1)S(1)}, bf16[128,2048]{1,0:T(8,128)(2,1)S(1)}, u32[]{:S(2)}, u32[]{:S(2)}) collective-permute-start(bf16[128,2048]{1,0:T(8,128)(2,1)S(1)} %add.84), channel_id=1, source_target_pairs={{4,8},{5,9},{6,10},{7,11},{8,4},{9,5},{10,6},{11,7},{20,24},{21,25... | collective-permute-start | bytes 1572872 | tf_op jit(solution)/shard_map/ppermute | solution.py:62
  83.9 13.4 %collective-permute-start.13 = (bf16[1280,128]{1,0:T(8,128)(2,1)S(1)}, bf16[1280,128]{1,0:T(8,128)(2,1)S(1)}, u32[]{:S(2)}, u32[]{:S(2)}) collective-permute-start(bf16[1280,128]{1,0:T(8,128)(2,1)S(1)} %get-tuple-element.83), channel_id=1, source_target_pairs={{0,16},{1,17},{2,18},{3,19},{4,20},{5,21},{6,22},{7,23},{8,24},{9,... | collective-permute-start | bytes 983048 | tf_op jit(solution)/shard_map/ppermute | solution.py:52
  86.1 15.4 %collective-permute-start.19 = (bf16[64,2048]{1,0:T(8,128)(2,1)S(1)}, bf16[64,2048]{1,0:T(8,128)(2,1)S(1)}, u32[]{:S(2)}, u32[]{:S(2)}) collective-permute-start(bf16[64,2048]{1,0:T(8,128)(2,1)S(1)} %get-tuple-element.88), channel_id=1, source_target_pairs={{4,12},{5,13},{6,14},{7,15},{8,0},{9,1},{10,2},{11,3},{20,28},{21,... | collective-permute-start | bytes 786440 | tf_op jit(solution)/shard_map/ppermute | solution.py:62
  87.4 19.2 %collective-permute-start.20 = (bf16[64,2048]{1,0:T(8,128)(2,1)S(1)}, bf16[64,2048]{1,0:T(8,128)(2,1)S(1)}, u32[]{:S(2)}, u32[]{:S(2)}) collective-permute-start(bf16[64,2048]{1,0:T(8,128)(2,1)S(1)} %get-tuple-element.89), channel_id=1, source_target_pairs={{4,28},{5,29},{6,30},{7,31},{8,16},{9,17},{10,18},{11,19},{20,12},... | collective-permute-start | bytes 786440 | tf_op jit(solution)/shard_map/ppermute | solution.py:62
  95.7 13.5 %collective-permute-start.23 = (bf16[64,2048]{1,0:T(8,128)(2,1)S(1)}, bf16[64,2048]{1,0:T(8,128)(2,1)S(1)}, u32[]{:S(2)}, u32[]{:S(2)}) collective-permute-start(bf16[64,2048]{1,0:T(8,128)(2,1)S(1)} %get-tuple-element.100), channel_id=1, source_target_pairs={{0,16},{1,17},{2,18},{3,19},{4,20},{5,21},{6,22},{7,23},{8,24},{9,... | collective-permute-start | bytes 786440 | tf_op jit(solution)/shard_map/ppermute | solution.py:52
  97.3 5.0 %collective-permute-start.17 = (bf16[320,128]{1,0:T(8,128)(2,1)S(1)}, bf16[320,128]{1,0:T(8,128)(2,1)S(1)}, u32[]{:S(2)}, u32[]{:S(2)}) collective-permute-start(bf16[320,128]{1,0:T(8,128)(2,1)S(1)} %get-tuple-element.95), channel_id=1, source_target_pairs={{0,2},{1,3},{2,0},{3,1},{4,6},{5,7},{6,4},{7,5},{8,10},{9,11},{10,... | collective-permute-start | bytes 245768 | tf_op jit(solution)/shard_map/ppermute | solution.py:52
  98.9 7.7 %collective-permute-start.15 = (bf16[320,128]{1,0:T(8,128)(2,1)S(1)}, bf16[320,128]{1,0:T(8,128)(2,1)S(1)}, u32[]{:S(2)}, u32[]{:S(2)}) collective-permute-start(bf16[320,128]{1,0:T(8,128)(2,1)S(1)} %get-tuple-element.93), channel_id=1, source_target_pairs={{0,2},{1,3},{2,0},{3,1},{4,6},{5,7},{6,4},{7,5},{8,10},{9,11},{10,... | collective-permute-start | bytes 245768 | tf_op jit(solution)/shard_map/ppermute | solution.py:52
  101.5 5.1 %collective-permute-start.16 = (bf16[320,128]{1,0:T(8,128)(2,1)S(1)}, bf16[320,128]{1,0:T(8,128)(2,1)S(1)}, u32[]{:S(2)}, u32[]{:S(2)}) collective-permute-start(bf16[320,128]{1,0:T(8,128)(2,1)S(1)} %get-tuple-element.94), channel_id=1, source_target_pairs={{0,1},{1,0},{2,3},{3,2},{4,5},{5,4},{6,7},{7,6},{8,9},{9,8},{10,11... | collective-permute-start | bytes 245768 | tf_op jit(solution)/shard_map/ppermute | solution.py:52
  102.3 4.3 %collective-permute-start.18 = (bf16[320,128]{1,0:T(8,128)(2,1)S(1)}, bf16[320,128]{1,0:T(8,128)(2,1)S(1)}, u32[]{:S(2)}, u32[]{:S(2)}) collective-permute-start(bf16[320,128]{1,0:T(8,128)(2,1)S(1)} %collective-permute-done.17), channel_id=1, source_target_pairs={{0,1},{1,0},{2,3},{3,2},{4,5},{5,4},{6,7},{7,6},{8,9},{9,8},{10,11... | collective-permute-start | bytes 245768 | tf_op jit(solution)/shard_map/ppermute | solution.py:52

commit v9 on v8

--- a/solution.py
+++ b/solution.py
@@ -77,15 +77,17 @@
         return [(dx, dy) for dx in range(self.dp) for dy in range(self.rows)]
 
 
-def slot_kernel(plan, index, where, earlier, info, *refs):
-    packs, rest = refs[: plan.sources], refs[plan.sources :]
+def slot_kernel(plan, index, first, where, earlier, added, info, *refs):
+    count = plan.sources - 2 if first == 0 else 2
+    packs, rest = refs[:count], refs[count:]
     weight_refs, rest = rest[: len(where)], rest[len(where) :]
-    earlier_refs, rest = rest[:earlier], rest[earlier:]
-    count = plan.dp if earlier else 1
-    p_ref, back_refs, (grads, heads, weights) = rest[0], rest[1 : 1 + count], rest[1 + count :]
+    added_refs, rest = rest[:added], rest[added:]
+    earlier_refs, rest = rest[: len(earlier)], rest[len(earlier) :]
+    outs = plan.dp if earlier else 1
+    p_ref, back_refs, (grads, heads, weights) = rest[0], rest[1 : 1 + outs], rest[1 + outs :]
     tokens, cap, part, top, head_dim = plan.tokens, plan.cap, plan.part, plan.top, plan.head_dim
     pair_rows = 2 * cap
-    pair_total = plan.sources // 2
+    pair_total = count // 2
     length = plan.planes * plan.back
 
     def put(s, slot, at, value):
@@ -93,7 +95,7 @@
             start = (s % GROUP) * length + slot * plan.back + at
             back_refs[s // GROUP][pl.ds(start, value.shape[0]), :] = value
         else:
-            back_refs[0][s, pl.ds(at, value.shape[0]), :] = value
+            back_refs[0][s - first, pl.ds(at, value.shape[0]), :] = value
 
     if len(where) > 1:
         for ref, kind in zip(weight_refs, where):
@@ -117,13 +119,13 @@
     chunk = min(part, 512)
 
     masks, occupied, gate_rows = [], [], []
-    for s in range(plan.sources):
+    for s in range(count):
         meta = packs[s][pl.ds(0, 2 * top), pl.ds(part + top * head_dim, LANES)].astype(jnp.float32)
         mask = (meta[top:] == expert).astype(jnp.float32)
         masks.append(mask)
         occupied.append(jnp.sum(mask, axis=0, keepdims=True))
         gate_rows.append(jnp.sum(mask * meta[:top], axis=0, keepdims=True))
-    filled = occupied + [jnp.zeros((1, tokens), jnp.float32)] * (-plan.sources % 16)
+    filled = occupied + [jnp.zeros((1, tokens), jnp.float32)] * (-count % 16)
     places = jnp.dot(
         jnp.concatenate(filled, axis=0).astype(jnp.bfloat16),
         before,
@@ -174,35 +176,47 @@
             column = jnp.sum(total[b * cap : (b + 1) * cap], axis=1, keepdims=True) * soft_cap
             line = jnp.sum(diagonal * column, axis=0, keepdims=True)
             block = jnp.where(block_row == 0, line, 0.0).astype(jnp.bfloat16)
-            put(2 * q + b, plan.planes - 1, cap, block)
+            put(first + 2 * q + b, index, cap, block)
     grad_all = grads[...]
-    p_ref[...] = lax.dot_general(
+    total = lax.dot_general(
         heads[...], grad_all, (((0,), (0,)), ((), ())), preferred_element_type=jnp.float32
-    ).astype(p_ref.dtype)
+    )
+    for ref in added_refs:
+        total = total + ref[...]
+    p_ref[...] = total.astype(p_ref.dtype)
     rows = lax.dot_general(
         grad_all, weight_ref[...], (((1,), (1,)), ((), ())), preferred_element_type=jnp.float32
     ).astype(jnp.bfloat16)
-    for s in range(plan.sources):
-        put(s, plan.planes - 1, 0, rows[s * cap : (s + 1) * cap])
-    for j, ref in enumerate(earlier_refs):
-        for s in range(plan.sources):
-            put(s, j, 0, ref[s])
-
-
-def slot_work(plan, index, info, packs, weights, kind, earlier=()):
-    rows = plan.sources * plan.cap
+    for s in range(count):
+        put(first + s, index, 0, rows[s * cap : (s + 1) * cap])
+    for ref, (slot, start) in zip(earlier_refs, earlier):
+        for s in range(ref.shape[0]):
+            put(start + s, slot, 0, ref[s])
+
+
+def slot_work(plan, index, first, info, packs, weights, kind, added=(), earlier=()):
+    rows = len(packs) * plan.cap
     if earlier:
         backs = (
             jax.ShapeDtypeStruct((GROUP * plan.planes * plan.back, LANES), jnp.bfloat16),
         ) * plan.dp
     else:
-        backs = (jax.ShapeDtypeStruct((plan.sources, plan.back, LANES), jnp.bfloat16),)
+        backs = (jax.ShapeDtypeStruct((len(packs), plan.back, LANES), jnp.bfloat16),)
     vmem = pl.BlockSpec(memory_space=pltpu.VMEM)
+    body = functools.partial(
+        slot_kernel,
+        plan,
+        index,
+        first,
+        [where for _, where in weights],
+        [(slot, start) for slot, start, _ in earlier],
+        len(added),
+    )
+    operands = [*packs, *[array for array, _ in weights], *added, *[rows for _, _, rows in earlier]]
     return pl.pallas_call(
-        functools.partial(slot_kernel, plan, index, [where for _, where in weights], len(earlier)),
+        body,
         out_shape=(jax.ShapeDtypeStruct((plan.head_dim, plan.part), kind), *backs),
-        in_specs=[pl.BlockSpec(memory_space=pltpu.SMEM)]
-        + [vmem] * (plan.sources + len(weights) + len(earlier)),
+        in_specs=[pl.BlockSpec(memory_space=pltpu.SMEM)] + [vmem] * len(operands),
         out_specs=(vmem,) * (1 + len(backs)),
         scratch_shapes=[
             pltpu.VMEM((rows, plan.part), jnp.bfloat16),
@@ -210,7 +224,7 @@
             pltpu.VMEM((plan.head_dim, plan.part), jnp.bfloat16),
         ],
         compiler_params=pltpu.CompilerParams(vmem_limit_bytes=14 * 1024 * 1024),
-    )(info, *packs, *[array for array, _ in weights], *earlier)
+    )(info, *operands)
 
 
 def sum_kernel(plan, info, *refs):
@@ -408,17 +422,18 @@
         axis=0,
     )
     flat_heads = head_outputs.reshape(tokens, top * head_dim)
-    packs = []
+    packs, held = [], []
     for dx, dy in plan.chips():
         piece = lax.dynamic_slice_in_dim(out_grad, ((x + dx) % plan.dp) * plan.part, plan.part, 1)
         value = jnp.concatenate([piece, flat_heads, meta], axis=1)
+        if plan.planes == 4 and not (dx or dy):
+            value, near_in, mate = lax.optimization_barrier((value, near_in, mate))
+        if plan.planes == 4 and dx and dy:
+            value, far_in, near_out = lax.optimization_barrier((value, far_in, near_out))
         value = plan.shift(value, dx=dx, dy=dy)
-        if plan.planes == 4:
-            if dx or dy:
-                value, far_in, near_out = lax.optimization_barrier((value, far_in, near_out))
-            else:
-                value, near_out = lax.optimization_barrier((value, near_out))
-        packs += [value, plan.shift(value, dc=1)]
+        if len(packs) < plan.dp * plan.rows - 1:
+            held += [value, plan.shift(value, dc=1)]
+        packs.append(value)
 
     if plan.planes == 4:
         weights = [
@@ -428,18 +443,34 @@
             [(own_weights, None)],
         ]
 
-    sums, backs, done = [], [], target
-    for j in range(plan.planes):
-        last = j == plan.planes - 1
-        if last and plan.planes == 4:
+    last = plan.planes - 1
+    calls = [(j, 0) for j in [last, *range(last)]] + [(j, 1) for j in range(plan.planes)]
+    if plan.planes == 4:
+        calls = [(3, 0), (2, 0), (0, 0), (0, 1), (1, 0), (1, 1), (2, 1), (3, 1)]
+    sums, backs, done, far = {}, [], target, None
+    for j, late in calls:
+        final = (j, late) == (last, 1)
+        if late and far is None:
+            value, info, done = lax.optimization_barrier((packs[-1], info, done))
+            if plan.planes == 4:
+                value, far_out = lax.optimization_barrier((value, far_out))
+            far = [value, plan.shift(value, dc=1)]
+        if final and plan.planes == 4:
             near_sum = sums[0] + plan.along(sums[0], inward)
             done = (done, near_sum)
         info, done = lax.optimization_barrier((info, done))
-        target = target if j else done
-        kind = jnp.float32 if last else jnp.bfloat16
-        part, *back = slot_work(plan, j, info, packs, weights[j], kind, backs if last else ())
-        sums.append(part)
-        backs = back if last else backs + back
+        sums[j], *back = slot_work(
+            plan,
+            j,
+            plan.sources - 2 if late else 0,
+            info,
+            far if late else held,
+            weights[j],
+            jnp.bfloat16 if late and not final else jnp.float32,
+            [sums[j]] if late else [],
+            backs if final else [],
+        )
+        backs = back if final else backs + [(j, plan.sources - 2 if late else 0, back[0])]
         done = back[0]
 
     far_pieces = []
@@ -452,7 +483,7 @@
         received = [plan.along(sums[2], mates), plan.along(near_sum, middle)]
     else:
         received = [plan.shift(sums[j], dz=steps[j]) for j in range(plan.planes - 1)]
-    pieces = sum_work(plan, info, [sums[-1]] + received, jnp.float32)
+    pieces = sum_work(plan, info, [sums[last]] + received, jnp.float32)
     pieces = [plan.shift(piece, dx=dx) for dx, piece in enumerate(pieces)]
 
     backs = [plan.shift(rows, dx=-dx % plan.dp) for dx, rows in enumerate(backs)]

time: 114 us -> 115 us (level)
  Pallas kernels: 29.4 us -> 33.4 us
  waiting for transfers between devices: 49.8 us -> 46.1 us
    ppermute x11, waiting for transfers between devices: 36.4 us -> 24.9 us  [along(): return lax.ppermute(value, AXES, out)]
    ppermute x13, waiting for transfers between devices: 13.4 us -> 21.2 us  [shift(): return lax.ppermute(value, AXES, self.pairs(**by))]
    pallas_call x4 -> x8, Pallas kernels: 21.8 us -> 25.7 us  [slot_work(): pl.pallas_call(body, out_shape=(jax.ShapeDtypeStruct((plan.head_dim, plan...]
    ppermute x13, starting transfers between devices: 9.26 us -> 10.7 us  [shift(): return lax.ppermute(value, AXES, self.pairs(**by))]
    ppermute x11, starting transfers between devices: 18.1 us -> 16.6 us  [along(): return lax.ppermute(value, AXES, out)]
  transfers between devices with their start and end apart: 24 -> 24, of which waited for: 10 -> 12; matrix products, arithmetic and copies ran while one was open for 2% -> 2% of each run, Pallas kernels for 22% -> 24%
where the time goes in v9:
time: 115 us; the launch traced here: 114 us
  waiting for transfers between devices  46.1 us (40%)
  Pallas kernels  33.4 us (29%)
  starting transfers between devices  27.3 us (24%)
  local copies, waits for them, and re-layouts  5.13 us (4%)
  other arithmetic  1.36 us (1%)
    pallas_call x8, Pallas kernels, slot_work(): pl.pallas_call(body, out_shape=(jax.ShapeDtypeStruct((plan.head_dim, plan...  25.7 us
    ppermute x11, waiting for transfers between devices, along(): return lax.ppermute(value, AXES, out)  24.9 us
    ppermute x13, waiting for transfers between devices, shift(): return lax.ppermute(value, AXES, self.pairs(**by))  21.2 us
    ppermute x11, starting transfers between devices, along(): return lax.ppermute(value, AXES, out)  16.6 us
    ppermute x13, starting transfers between devices, shift(): return lax.ppermute(value, AXES, self.pairs(**by))  10.7 us
    unnamed x15, local copies, waits for them, and re-layouts  4.01 us
    pallas_call x1, Pallas kernels, target_work(): pl.pallas_call(functools.partial(target_kernel, plan), out_shape=jax.Shap...  2.36 us
  transfers between devices with their start and end apart: 24, of which 12 were waited for; matrix products, arithmetic and copies ran while one was open for 2% of the time, Pallas kernels for 24%

profile of v9, /device:TPU:0, one launch (start us, length us, event | category | flops | bytes accessed | tf_op | source)
XLA Modules:
  0.0 114.2 jit_solution(10170105050718275045)
XLA Ops:
  0.6 0.0 copy-start
  0.7 1.2 %copy-done = bf16[1,128,4096]{2,1,0:T(8,128)(2,1)S(1)} copy-done((bf16[1,128,4096]{2,1,0:T(8,128)(2,1)S(1)}, bf16[1,128,4096]{2,1,0:T(8,128)(2,1)}, u32[]{:S(2)}) %copy-start) | copy-done | bytes 1048600
  1.9 0.8 dynamic-slice_bitcast_fusion.refs_6_.refs_2_
  2.7 1.4 %collective-permute-start.1 = (bf16[128,2048]{1,0:T(8,128)(2,1)}, bf16[128,2048]{1,0:T(8,128)(2,1)}, u32[]{:S(2)}, u32[]{:S(2)}) collective-permute-start(bf16[128,2048]{1,0:T(8,128)(2,1)} %dynamic-slice_bitcast_fusion.refs_6_.refs_2_), channel_id=1, source_target_pairs={{4,8},{5,9},{6,10},{7,11},{8,4},{9,5},{10,6},{11,7},{20,24},{21,25... | collective-permute-start | bytes 1572872 | tf_op jit(solution)/shard_map/ppermute | solution.py:62
  4.1 5.1 %collective-permute-start = (bf16[128,2048]{1,0:T(8,128)(2,1)}, bf16[128,2048]{1,0:T(8,128)(2,1)}, u32[]{:S(2)}, u32[]{:S(2)}) collective-permute-start(bf16[128,2048]{1,0:T(8,128)(2,1)} %dynamic-slice_bitcast_fusion.refs_6_.refs_2_), channel_id=1, source_target_pairs={{0,4},{1,5},{2,6},{3,7},{4,0},{5,1},{6,2},{7,3},{8,12},{9,13},{10,... | collective-permute-start | bytes 1572872 | tf_op jit(solution)/shard_map/ppermute | solution.py:62
  9.3 0.0 copy-start.5
  9.3 0.1 constant_dynamic-slice_fusion
  9.5 0.5 copy-done.5
  10.0 1.0 fusion.1
  11.0 1.5 %collective-permute-start.6 = (bf16[128,3200]{1,0:T(8,128)(2,1)S(1)}, bf16[128,3200]{1,0:T(8,128)(2,1)S(1)}, u32[]{:S(2)}, u32[]{:S(2)}) collective-permute-start(bf16[128,3200]{1,0:T(8,128)(2,1)S(1)} %get-tuple-element.72.refs_0_), channel_id=1, source_target_pairs={{0,2},{1,3},{2,0},{3,1},{4,6},{5,7},{6,4},{7,5},{8,10},{9,11},{10,... | collective-permute-start | bytes 2457608 | tf_op jit(solution)/shard_map/ppermute | solution.py:52
  12.6 1.5 %collective-permute-start.8 = (bf16[128,3200]{1,0:T(8,128)(2,1)}, bf16[128,3200]{1,0:T(8,128)(2,1)S(1)}, u32[]{:S(2)}, u32[]{:S(2)}) collective-permute-start(bf16[128,3200]{1,0:T(8,128)(2,1)} %get-tuple-element.70), channel_id=1, source_target_pairs={{0,16},{1,17},{2,18},{3,19},{4,20},{5,21},{6,22},{7,23},{8,24},{9,... | collective-permute-start | bytes 2457608 | tf_op jit(solution)/shard_map/ppermute | solution.py:52
  14.0 0.7 copy.10.route_ref
  14.8 0.1 stack.63.info
  14.9 0.0 copy-start.1
  14.9 0.8 copy-done.1
  15.7 2.4 %shard_map.76.target_ref = s32[1024,128]{1,0:T(8,128)S(1)} custom-call(s32[15]{0:T(128)S(1)} %stack.63.info, s32[128,8]{1,0:T(8,128)S(1)} %copy-done.1), custom_call_target="tpu_custom_call" | custom-call | tf_op jit(solution)/shard_map/pallas_call | solution.py:340
  18.1 3.1 %collective-permute-done.refs_6_.refs_2_ = bf16[128,2048]{1,0:T(8,128)(2,1)} collective-permute-done((bf16[128,2048]{1,0:T(8,128)(2,1)}, bf16[128,2048]{1,0:T(8,128)(2,1)}, u32[]{:S(2)}, u32[]{:S(2)}) %collective-permute-start) | collective-permute-done | bytes 524320 | tf_op jit(solution)/shard_map/ppermute | solution.py:62
  21.2 0.7 collective-permute-start.2
  21.9 1.3 %collective-permute-start.3 = (bf16[128,2048]{1,0:T(8,128)(2,1)}, bf16[128,2048]{1,0:T(8,128)(2,1)S(1)}, u32[]{:S(2)}, u32[]{:S(2)}) collective-permute-start(bf16[128,2048]{1,0:T(8,128)(2,1)} %collective-permute-done.1.refs_6_.refs_2_), channel_id=1, source_target_pairs={{4,0},{5,1},{6,2},{7,3},{8,12},{9,13},{10,14},{11,15},{20,16},{21,... | collective-permute-start | bytes 1572872 | tf_op jit(solution)/shard_map/ppermute | solution.py:62
  23.2 0.1 collective-permute-start.5
  23.3 7.2 %collective-permute-done.6.refs_2_ = bf16[128,3200]{1,0:T(8,128)(2,1)S(1)} collective-permute-done((bf16[128,3200]{1,0:T(8,128)(2,1)S(1)}, bf16[128,3200]{1,0:T(8,128)(2,1)S(1)}, u32[]{:S(2)}, u32[]{:S(2)}) %collective-permute-start.6) | collective-permute-done | bytes 819232 | tf_op jit(solution)/shard_map/ppermute | solution.py:52
  30.5 1.4 %collective-permute-done.8.refs_4_ = bf16[128,3200]{1,0:T(8,128)(2,1)S(1)} collective-permute-done((bf16[128,3200]{1,0:T(8,128)(2,1)}, bf16[128,3200]{1,0:T(8,128)(2,1)S(1)}, u32[]{:S(2)}, u32[]{:S(2)}) %collective-permute-start.8) | collective-permute-done | bytes 819232 | tf_op jit(solution)/shard_map/ppermute | solution.py:52
  31.9 0.0 collective-permute-start.9
  31.9 0.0 collective-permute-done.2.refs_6_.refs_2_
  31.9 5.4 %collective-permute-done.3.refs_7_.refs_3_ = bf16[128,2048]{1,0:T(8,128)(2,1)S(1)} collective-permute-done((bf16[128,2048]{1,0:T(8,128)(2,1)}, bf16[128,2048]{1,0:T(8,128)(2,1)S(1)}, u32[]{:S(2)}, u32[]{:S(2)}) %collective-permute-start.3) | collective-permute-done | bytes 524320 | tf_op jit(solution)/shard_map/ppermute | solution.py:62
  37.3 2.4 %collective-permute-start.4 = (bf16[128,3200]{1,0:T(8,128)(2,1)}, bf16[128,3200]{1,0:T(8,128)(2,1)S(1)}, u32[]{:S(2)}, u32[]{:S(2)}) collective-permute-start(bf16[128,3200]{1,0:T(8,128)(2,1)} %get-tuple-element.70), channel_id=1, source_target_pairs={{0,18},{1,19},{2,16},{3,17},{4,22},{5,23},{6,20},{7,21},{8,26},{9,... | collective-permute-start | bytes 2457608 | tf_op jit(solution)/shard_map/ppermute | solution.py:52
  39.8 1.3 %collective-permute-start.10 = (bf16[128,2048]{1,0:T(8,128)(2,1)S(1)}, bf16[128,2048]{1,0:T(8,128)(2,1)S(1)}, u32[]{:S(2)}, u32[]{:S(2)}) collective-permute-start(bf16[128,2048]{1,0:T(8,128)(2,1)S(1)} %collective-permute-done.2.refs_6_.refs_2_), channel_id=1, source_target_pairs={{4,0},{5,1},{6,2},{7,3},{8,12},{9,13},{10,14},{11,15},{20,16},{21,... | collective-permute-start | bytes 1572872 | tf_op jit(solution)/shard_map/ppermute | solution.py:62
  41.0 0.0 collective-permute-done.5.refs_1_
  41.1 0.0 collective-permute-done.9.refs_5_
  41.1 4.2 %shard_map.77 = (f32[128,2048]{1,0:T(8,128)S(1)}, bf16[6,80,128]{2,1,0:T(8,128)(2,1)S(1)}) custom-call(s32[15]{0:T(128)S(1)} %stack.63.info, bf16[128,3200]{1,0:T(8,128)(2,1)S(1)} %get-tuple-element.72.refs_0_, bf16[128,3200]{1,0:T(8,128)(2,1)S(1)} %collective-permute-done.5.refs_1_, bf16[128,3200]{1,0:T(8,128)(2,1)S(1)} %collective-permute-done.6.refs_2_, ...), custom_call_target="tpu_custom_call" | custom-call | tf_op jit(solution)/shard_map/pallas_call | solution.py:216
  45.3 4.2 %shard_map.78 = (f32[128,2048]{1,0:T(8,128)S(1)}, bf16[6,80,128]{2,1,0:T(8,128)(2,1)S(1)}) custom-call(s32[15]{0:T(128)S(1)} %stack.63.info, bf16[128,3200]{1,0:T(8,128)(2,1)S(1)} %get-tuple-element.72.refs_0_, bf16[128,3200]{1,0:T(8,128)(2,1)S(1)} %collective-permute-done.5.refs_1_, bf16[128,3200]{1,0:T(8,128)(2,1)S(1)} %collective-permute-done.6.refs_2_, ...), custom_call_target="tpu_custom_call" | custom-call | tf_op jit(solution)/shard_map/pallas_call | solution.py:216
  49.5 4.2 %shard_map.79 = (f32[128,2048]{1,0:T(8,128)S(1)}, bf16[6,80,128]{2,1,0:T(8,128)(2,1)S(1)}) custom-call(s32[15]{0:T(128)S(1)} %stack.63.info, bf16[128,3200]{1,0:T(8,128)(2,1)S(1)} %get-tuple-element.72.refs_0_, bf16[128,3200]{1,0:T(8,128)(2,1)S(1)} %collective-permute-done.5.refs_1_, bf16[128,3200]{1,0:T(8,128)(2,1)S(1)} %collective-permute-done.6.refs_2_, ...), custom_call_target="tpu_custom_call" | custom-call | tf_op jit(solution)/shard_map/pallas_call | solution.py:216
  53.7 2.6 %collective-permute-done.4.refs_0_ = bf16[128,3200]{1,0:T(8,128)(2,1)S(1)} collective-permute-done((bf16[128,3200]{1,0:T(8,128)(2,1)}, bf16[128,3200]{1,0:T(8,128)(2,1)S(1)}, u32[]{:S(2)}, u32[]{:S(2)}) %collective-permute-start.4) | collective-permute-done | bytes 819232 | tf_op jit(solution)/shard_map/ppermute | solution.py:52
  56.4 2.3 %collective-permute-done.11.refs_1_ = bf16[128,3200]{1,0:T(8,128)(2,1)S(1)} collective-permute-done((bf16[128,3200]{1,0:T(8,128)(2,1)S(1)}, bf16[128,3200]{1,0:T(8,128)(2,1)S(1)}, u32[]{:S(2)}, u32[]{:S(2)}) %collective-permute-start.11) | collective-permute-done | bytes 819232 | tf_op jit(solution)/shard_map/ppermute | solution.py:52
  58.7 2.6 %shard_map.80 = (bf16[128,2048]{1,0:T(8,128)(2,1)S(1)}, bf16[2,80,128]{2,1,0:T(8,128)(2,1)S(1)}) custom-call(s32[15]{0:T(128)S(1)} %stack.63.info, bf16[128,3200]{1,0:T(8,128)(2,1)S(1)} %collective-permute-done.4.refs_0_, bf16[128,3200]{1,0:T(8,128)(2,1)S(1)} %collective-permute-done.11.refs_1_, bf16[128,2048]{1,0:T(8,128)(2,1)} %collective-permute-done.1.refs_6_.refs_2_, ...), custom_call_target="tpu_custom_call" | custom-call | tf_op jit(solution)/shard_map/pallas_call | solution.py:216
  61.3 2.1 %collective-permute-start.12 = (bf16[128,2048]{1,0:T(8,128)(2,1)S(1)}, bf16[128,2048]{1,0:T(8,128)(2,1)S(1)}, u32[]{:S(2)}, u32[]{:S(2)}) collective-permute-start(bf16[128,2048]{1,0:T(8,128)(2,1)S(1)} %get-tuple-element.95), channel_id=1, source_target_pairs={{0,4},{1,5},{2,6},{3,7},{12,8},{13,9},{14,10},{15,11},{16,20},{17,... | collective-permute-start | bytes 1572872 | tf_op jit(solution)/shard_map/ppermute | solution.py:62
  63.4 3.7 %shard_map.81 = (f32[128,2048]{1,0:T(8,128)S(1)}, bf16[6,80,128]{2,1,0:T(8,128)(2,1)S(1)}) custom-call(s32[15]{0:T(128)S(1)} %stack.63.info, bf16[128,3200]{1,0:T(8,128)(2,1)S(1)} %get-tuple-element.72.refs_0_, bf16[128,3200]{1,0:T(8,128)(2,1)S(1)} %collective-permute-done.5.refs_1_, bf16[128,3200]{1,0:T(8,128)(2,1)S(1)} %collective-permute-done.6.refs_2_, ...), custom_call_target="tpu_custom_call" | custom-call | tf_op jit(solution)/shard_map/pallas_call | solution.py:216
  67.1 1.9 %shard_map.82 = (bf16[128,2048]{1,0:T(8,128)(2,1)S(1)}, bf16[2,80,128]{2,1,0:T(8,128)(2,1)S(1)}) custom-call(s32[15]{0:T(128)S(1)} %stack.63.info, bf16[128,3200]{1,0:T(8,128)(2,1)S(1)} %collective-permute-done.4.refs_0_, bf16[128,3200]{1,0:T(8,128)(2,1)S(1)} %collective-permute-done.11.refs_1_, ...), custom_call_target="tpu_custom_call" | custom-call | tf_op jit(solution)/shard_map/pallas_call | solution.py:216
  69.1 1.3 %collective-permute-start.14 = (bf16[128,2048]{1,0:T(8,128)(2,1)S(1)}, bf16[128,2048]{1,0:T(8,128)(2,1)S(1)}, u32[]{:S(2)}, u32[]{:S(2)}) collective-permute-start(bf16[128,2048]{1,0:T(8,128)(2,1)S(1)} %get-tuple-element.100.refs_0_), channel_id=1, source_target_pairs={{0,4},{1,5},{2,6},{3,7},{12,8},{13,9},{14,10},{15,11},{16,20},{17,... | collective-permute-start | bytes 1572872 | tf_op jit(solution)/shard_map/ppermute | solution.py:62
  70.4 2.4 %shard_map.83 = (bf16[128,2048]{1,0:T(8,128)(2,1)S(1)}, bf16[2,80,128]{2,1,0:T(8,128)(2,1)S(1)}) custom-call(s32[15]{0:T(128)S(1)} %stack.63.info, bf16[128,3200]{1,0:T(8,128)(2,1)S(1)} %collective-permute-done.4.refs_0_, bf16[128,3200]{1,0:T(8,128)(2,1)S(1)} %collective-permute-done.11.refs_1_, bf16[128,2048]{1,0:T(8,128)(2,1)} %collective-permute-done.refs_6_.refs_2_, ...), custom_call_target="tpu_custom_call" | custom-call | tf_op jit(solution)/shard_map/pallas_call | solution.py:216
  72.8 0.1 collective-permute-start.21
  72.9 2.8 %collective-permute-done.12 = bf16[128,2048]{1,0:T(8,128)(2,1)S(1)} collective-permute-done((bf16[128,2048]{1,0:T(8,128)(2,1)S(1)}, bf16[128,2048]{1,0:T(8,128)(2,1)S(1)}, u32[]{:S(2)}, u32[]{:S(2)}) %collective-permute-start.12) | collective-permute-done | bytes 524320 | tf_op jit(solution)/shard_map/ppermute | solution.py:62
  75.7 0.1 add.84
  75.8 0.7 collective-permute-start.22
  76.5 2.4 %shard_map.84 = (f32[128,2048]{1,0:T(8,128)S(1)}, bf16[1280,128]{1,0:T(8,128)(2,1)S(1)}, bf16[1280,128]{1,0:T(8,128)(2,1)S(1)}) custom-call(s32[15]{0:T(128)S(1)} %stack.63.info, bf16[128,3200]{1,0:T(8,128)(2,1)S(1)} %collective-permute-done.4.refs_0_, bf16[128,3200]{1,0:T(8,128)(2,1)S(1)} %collective-permute-done.11.refs_1_, ...), custom_call_target="tpu_custom_call" | custom-call | tf_op jit(solution)/shard_map/pallas_call | solution.py:216
  78.9 1.6 %collective-permute-start.13 = (bf16[1280,128]{1,0:T(8,128)(2,1)S(1)}, bf16[1280,128]{1,0:T(8,128)(2,1)S(1)}, u32[]{:S(2)}, u32[]{:S(2)}) collective-permute-start(bf16[1280,128]{1,0:T(8,128)(2,1)S(1)} %get-tuple-element.99), channel_id=1, source_target_pairs={{0,16},{1,17},{2,18},{3,19},{4,20},{5,21},{6,22},{7,23},{8,24},{9,... | collective-permute-start | bytes 983048 | tf_op jit(solution)/shard_map/ppermute | solution.py:52
  80.5 6.4 %collective-permute-done.14.refs_1_ = bf16[128,2048]{1,0:T(8,128)(2,1)S(1)} collective-permute-done((bf16[128,2048]{1,0:T(8,128)(2,1)S(1)}, bf16[128,2048]{1,0:T(8,128)(2,1)S(1)}, u32[]{:S(2)}, u32[]{:S(2)}) %collective-permute-start.14) | collective-permute-done | bytes 524320 | tf_op jit(solution)/shard_map/ppermute | solution.py:62
  86.9 0.7 shard_map.85
  87.6 1.3 %collective-permute-start.19 = (bf16[64,2048]{1,0:T(8,128)(2,1)S(1)}, bf16[64,2048]{1,0:T(8,128)(2,1)S(1)}, u32[]{:S(2)}, u32[]{:S(2)}) collective-permute-start(bf16[64,2048]{1,0:T(8,128)(2,1)S(1)} %get-tuple-element.104), channel_id=1, source_target_pairs={{4,12},{5,13},{6,14},{7,15},{8,0},{9,1},{10,2},{11,3},{20,28},{21,... | collective-permute-start | bytes 786440 | tf_op jit(solution)/shard_map/ppermute | solution.py:62
  88.9 1.3 %collective-permute-start.20 = (bf16[64,2048]{1,0:T(8,128)(2,1)S(1)}, bf16[64,2048]{1,0:T(8,128)(2,1)S(1)}, u32[]{:S(2)}, u32[]{:S(2)}) collective-permute-start(bf16[64,2048]{1,0:T(8,128)(2,1)S(1)} %get-tuple-element.105), channel_id=1, source_target_pairs={{4,28},{5,29},{6,30},{7,31},{8,16},{9,17},{10,18},{11,19},{20,12},... | collective-permute-start | bytes 786440 | tf_op jit(solution)/shard_map/ppermute | solution.py:62
  90.2 7.2 %collective-permute-done.21.refs_1_ = bf16[128,2048]{1,0:T(8,128)(2,1)S(1)} collective-permute-done((bf16[128,2048]{1,0:T(8,128)(2,1)S(1)}, bf16[128,2048]{1,0:T(8,128)(2,1)S(1)}, u32[]{:S(2)}, u32[]{:S(2)}) %collective-permute-start.21) | collective-permute-done | bytes 524320 | tf_op jit(solution)/shard_map/ppermute | solution.py:62
  97.3 0.7 shard_map.87
  98.1 1.6 %collective-permute-start.23 = (bf16[64,2048]{1,0:T(8,128)(2,1)S(1)}, bf16[64,2048]{1,0:T(8,128)(2,1)S(1)}, u32[]{:S(2)}, u32[]{:S(2)}) collective-permute-start(bf16[64,2048]{1,0:T(8,128)(2,1)S(1)} %get-tuple-element.116), channel_id=1, source_target_pairs={{0,16},{1,17},{2,18},{3,19},{4,20},{5,21},{6,22},{7,23},{8,24},{9,... | collective-permute-start | bytes 786440 | tf_op jit(solution)/shard_map/ppermute | solution.py:52
  99.6 0.1 shard_map.86
  99.7 1.6 %collective-permute-start.17 = (bf16[320,128]{1,0:T(8,128)(2,1)S(1)}, bf16[320,128]{1,0:T(8,128)(2,1)S(1)}, u32[]{:S(2)}, u32[]{:S(2)}) collective-permute-start(bf16[320,128]{1,0:T(8,128)(2,1)S(1)} %get-tuple-element.111), channel_id=1, source_target_pairs={{0,2},{1,3},{2,0},{3,1},{4,6},{5,7},{6,4},{7,5},{8,10},{9,11},{10,... | collective-permute-start | bytes 245768 | tf_op jit(solution)/shard_map/ppermute | solution.py:52
  101.3 0.5 collective-permute-start.15
  101.8 2.6 %collective-permute-done.17 = bf16[320,128]{1,0:T(8,128)(2,1)S(1)} collective-permute-done((bf16[320,128]{1,0:T(8,128)(2,1)S(1)}, bf16[320,128]{1,0:T(8,128)(2,1)S(1)}, u32[]{:S(2)}, u32[]{:S(2)}) %collective-permute-start.17) | collective-permute-done | bytes 81952 | tf_op jit(solution)/shard_map/ppermute | solution.py:52
  104.4 1.3 %collective-permute-done.15.refs_1_ = bf16[320,128]{1,0:T(8,128)(2,1)S(1)} collective-permute-done((bf16[320,128]{1,0:T(8,128)(2,1)S(1)}, bf16[320,128]{1,0:T(8,128)(2,1)S(1)}, u32[]{:S(2)}, u32[]{:S(2)}) %collective-permute-start.15) | collective-permute-done | bytes 81952 | tf_op jit(solution)/shard_map/ppermute | solution.py:52
  105.7 3.7 %collective-permute-done.23.refs_1_ = bf16[64,2048]{1,0:T(8,128)(2,1)S(1)} collective-permute-done((bf16[64,2048]{1,0:T(8,128)(2,1)S(1)}, bf16[64,2048]{1,0:T(8,128)(2,1)S(1)}, u32[]{:S(2)}, u32[]{:S(2)}) %collective-permute-start.23) | collective-permute-done | bytes 262176 | tf_op jit(solution)/shard_map/ppermute | solution.py:52
  109.5 2.2 %shard_map.88 = (bf16[1024,128]{1,0:T(8,128)(2,1)}, f32[1024,1]{1,0:T(8,128)S(1)}) custom-call(s32[1024,128]{1,0:T(8,128)S(1)} %shard_map.76.target_ref, bf16[320,128]{1,0:T(8,128)(2,1)S(1)} %get-tuple-element.117.refs_0_, bf16[320,128]{1,0:T(8,128)(2,1)S(1)} %collective-permute-done.15.refs_1_, bf16[320,128]{1,0:T(8,128)(2,1)S(1)} %collective-permute-done.16.refs_2_, ...), custom_call_target="tpu_custom_call" | custom-call | flops 1 | bytes 1 | tf_op jit(solution)/shard_map/pallas_call | solution.py:370
  111.6 0.2 convert_reduce_fusion
  111.8 0.1 convert_element_type.15
  111.9 0.7 copy.11
  112.6 1.6 %shard_map.89 = f32[64,4096]{1,0:T(8,128)} custom-call(s32[15]{0:T(128)S(1)} %stack.63.info, f32[64,2048]{1,0:T(8,128)S(1)} %get-tuple-element.123.refs_0_, bf16[64,2048]{1,0:T(8,128)(2,1)S(1)} %collective-permute-done.23.refs_1_, bf16[64,2048]{1,0:T(8,128)(2,1)S(1)} %collective-permute-done.19.refs_2_, bf16[64,2048]{1,0:T(8,128)(2,1)S(1)} %collective-permute-done.20.refs_3_), custom_call_target="tpu_custom_call" | custom-call | tf_op jit(solution)/shard_map/pallas_call | solution.py:270
  (22 shorter events, 0.1 us)
Async XLA Ops:
  0.6 1.2 %copy-start = (bf16[1,128,4096]{2,1,0:T(8,128)(2,1)S(1)}, bf16[1,128,4096]{2,1,0:T(8,128)(2,1)}, u32[]{:S(2)}) copy-start(bf16[1,128,4096]{2,1,0:T(8,128)(2,1)} %param.9) | copy-start | bytes 3145732
  0.6 8.6 %copy-start.4 = (s32[128,8]{0,1:T(8,128)S(1)}, s32[128,8]{0,1:T(8,128)}, u32[]{:S(2)}) copy-start(s32[128,8]{0,1:T(8,128)} %param.8) | copy-start | bytes 12292
  0.7 8.6 %copy-start.3 = (bf16[128,8,128]{2,1,0:T(8,128)(2,1)S(1)}, bf16[128,8,128]{2,1,0:T(8,128)(2,1)}, u32[]{:S(2)}) copy-start(bf16[128,8,128]{2,1,0:T(8,128)(2,1)} %param.5) | copy-start | bytes 786436
  0.7 8.7 %copy-start.2 = (bf16[128,4096]{1,0:T(8,128)(2,1)S(1)}, bf16[128,4096]{1,0:T(8,128)(2,1)}, u32[]{:S(2)}) copy-start(bf16[128,4096]{1,0:T(8,128)(2,1)} %param.6) | copy-start | bytes 3145732
  2.7 15.4 %collective-permute-start.1 = (bf16[128,2048]{1,0:T(8,128)(2,1)}, bf16[128,2048]{1,0:T(8,128)(2,1)}, u32[]{:S(2)}, u32[]{:S(2)}) collective-permute-start(bf16[128,2048]{1,0:T(8,128)(2,1)} %dynamic-slice_bitcast_fusion.refs_6_.refs_2_), channel_id=1, source_target_pairs={{4,8},{5,9},{6,10},{7,11},{8,4},{9,5},{10,6},{11,7},{20,24},{21,25... | collective-permute-start | bytes 1572872 | tf_op jit(solution)/shard_map/ppermute | solution.py:62
  4.1 17.1 %collective-permute-start = (bf16[128,2048]{1,0:T(8,128)(2,1)}, bf16[128,2048]{1,0:T(8,128)(2,1)}, u32[]{:S(2)}, u32[]{:S(2)}) collective-permute-start(bf16[128,2048]{1,0:T(8,128)(2,1)} %dynamic-slice_bitcast_fusion.refs_6_.refs_2_), channel_id=1, source_target_pairs={{0,4},{1,5},{2,6},{3,7},{4,0},{5,1},{6,2},{7,3},{8,12},{9,13},{10,... | collective-permute-start | bytes 1572872 | tf_op jit(solution)/shard_map/ppermute | solution.py:62
  9.3 0.7 copy-start.5
  11.0 19.4 %collective-permute-start.6 = (bf16[128,3200]{1,0:T(8,128)(2,1)S(1)}, bf16[128,3200]{1,0:T(8,128)(2,1)S(1)}, u32[]{:S(2)}, u32[]{:S(2)}) collective-permute-start(bf16[128,3200]{1,0:T(8,128)(2,1)S(1)} %get-tuple-element.72.refs_0_), channel_id=1, source_target_pairs={{0,2},{1,3},{2,0},{3,1},{4,6},{5,7},{6,4},{7,5},{8,10},{9,11},{10,... | collective-permute-start | bytes 2457608 | tf_op jit(solution)/shard_map/ppermute | solution.py:52
  12.6 19.4 %collective-permute-start.8 = (bf16[128,3200]{1,0:T(8,128)(2,1)}, bf16[128,3200]{1,0:T(8,128)(2,1)S(1)}, u32[]{:S(2)}, u32[]{:S(2)}) collective-permute-start(bf16[128,3200]{1,0:T(8,128)(2,1)} %get-tuple-element.70), channel_id=1, source_target_pairs={{0,16},{1,17},{2,18},{3,19},{4,20},{5,21},{6,22},{7,23},{8,24},{9,... | collective-permute-start | bytes 2457608 | tf_op jit(solution)/shard_map/ppermute | solution.py:52
  14.9 0.8 copy-start.1
  21.2 10.7 %collective-permute-start.2 = (bf16[128,2048]{1,0:T(8,128)(2,1)}, bf16[128,2048]{1,0:T(8,128)(2,1)S(1)}, u32[]{:S(2)}, u32[]{:S(2)}) collective-permute-start(bf16[128,2048]{1,0:T(8,128)(2,1)} %collective-permute-done.refs_6_.refs_2_), channel_id=1, source_target_pairs={{4,8},{5,9},{6,10},{7,11},{8,4},{9,5},{10,6},{11,7},{20,24},{21,25... | collective-permute-start | bytes 1572872 | tf_op jit(solution)/shard_map/ppermute | solution.py:62
  21.9 15.4 %collective-permute-start.3 = (bf16[128,2048]{1,0:T(8,128)(2,1)}, bf16[128,2048]{1,0:T(8,128)(2,1)S(1)}, u32[]{:S(2)}, u32[]{:S(2)}) collective-permute-start(bf16[128,2048]{1,0:T(8,128)(2,1)} %collective-permute-done.1.refs_6_.refs_2_), channel_id=1, source_target_pairs={{4,0},{5,1},{6,2},{7,3},{8,12},{9,13},{10,14},{11,15},{20,16},{21,... | collective-permute-start | bytes 1572872 | tf_op jit(solution)/shard_map/ppermute | solution.py:62
  23.2 17.8 %collective-permute-start.5 = (bf16[128,3200]{1,0:T(8,128)(2,1)S(1)}, bf16[128,3200]{1,0:T(8,128)(2,1)S(1)}, u32[]{:S(2)}, u32[]{:S(2)}) collective-permute-start(bf16[128,3200]{1,0:T(8,128)(2,1)S(1)} %get-tuple-element.72.refs_0_), channel_id=1, source_target_pairs={{0,1},{1,0},{2,3},{3,2},{4,5},{5,4},{6,7},{7,6},{8,9},{9,8},{10,11... | collective-permute-start | bytes 2457608 | tf_op jit(solution)/shard_map/ppermute | solution.py:52
  30.5 10.6 %collective-permute-start.7 = (bf16[128,3200]{1,0:T(8,128)(2,1)S(1)}, bf16[128,3200]{1,0:T(8,128)(2,1)S(1)}, u32[]{:S(2)}, u32[]{:S(2)}) collective-permute-start(bf16[128,3200]{1,0:T(8,128)(2,1)S(1)} %collective-permute-done.6.refs_2_), channel_id=1, source_target_pairs={{0,1},{1,0},{2,3},{3,2},{4,5},{5,4},{6,7},{7,6},{8,9},{9,8},{10,11... | collective-permute-start | bytes 2457608 | tf_op jit(solution)/shard_map/ppermute | solution.py:52
  31.9 9.2 %collective-permute-start.9 = (bf16[128,3200]{1,0:T(8,128)(2,1)S(1)}, bf16[128,3200]{1,0:T(8,128)(2,1)S(1)}, u32[]{:S(2)}, u32[]{:S(2)}) collective-permute-start(bf16[128,3200]{1,0:T(8,128)(2,1)S(1)} %collective-permute-done.8.refs_4_), channel_id=1, source_target_pairs={{0,1},{1,0},{2,3},{3,2},{4,5},{5,4},{6,7},{7,6},{8,9},{9,8},{10,11... | collective-permute-start | bytes 2457608 | tf_op jit(solution)/shard_map/ppermute | solution.py:52
  37.3 19.0 %collective-permute-start.4 = (bf16[128,3200]{1,0:T(8,128)(2,1)}, bf16[128,3200]{1,0:T(8,128)(2,1)S(1)}, u32[]{:S(2)}, u32[]{:S(2)}) collective-permute-start(bf16[128,3200]{1,0:T(8,128)(2,1)} %get-tuple-element.70), channel_id=1, source_target_pairs={{0,18},{1,19},{2,16},{3,17},{4,22},{5,23},{6,20},{7,21},{8,26},{9,... | collective-permute-start | bytes 2457608 | tf_op jit(solution)/shard_map/ppermute | solution.py:52
  39.8 16.6 %collective-permute-start.10 = (bf16[128,2048]{1,0:T(8,128)(2,1)S(1)}, bf16[128,2048]{1,0:T(8,128)(2,1)S(1)}, u32[]{:S(2)}, u32[]{:S(2)}) collective-permute-start(bf16[128,2048]{1,0:T(8,128)(2,1)S(1)} %collective-permute-done.2.refs_6_.refs_2_), channel_id=1, source_target_pairs={{4,0},{5,1},{6,2},{7,3},{8,12},{9,13},{10,14},{11,15},{20,16},{21,... | collective-permute-start | bytes 1572872 | tf_op jit(solution)/shard_map/ppermute | solution.py:62
  56.4 2.3 %collective-permute-start.11 = (bf16[128,3200]{1,0:T(8,128)(2,1)S(1)}, bf16[128,3200]{1,0:T(8,128)(2,1)S(1)}, u32[]{:S(2)}, u32[]{:S(2)}) collective-permute-start(bf16[128,3200]{1,0:T(8,128)(2,1)S(1)} %collective-permute-done.4.refs_0_), channel_id=1, source_target_pairs={{0,1},{1,0},{2,3},{3,2},{4,5},{5,4},{6,7},{7,6},{8,9},{9,8},{10,11... | collective-permute-start | bytes 2457608 | tf_op jit(solution)/shard_map/ppermute | solution.py:52
  61.3 14.3 %collective-permute-start.12 = (bf16[128,2048]{1,0:T(8,128)(2,1)S(1)}, bf16[128,2048]{1,0:T(8,128)(2,1)S(1)}, u32[]{:S(2)}, u32[]{:S(2)}) collective-permute-start(bf16[128,2048]{1,0:T(8,128)(2,1)S(1)} %get-tuple-element.95), channel_id=1, source_target_pairs={{0,4},{1,5},{2,6},{3,7},{12,8},{13,9},{14,10},{15,11},{16,20},{17,... | collective-permute-start | bytes 1572872 | tf_op jit(solution)/shard_map/ppermute | solution.py:62
  69.1 17.8 %collective-permute-start.14 = (bf16[128,2048]{1,0:T(8,128)(2,1)S(1)}, bf16[128,2048]{1,0:T(8,128)(2,1)S(1)}, u32[]{:S(2)}, u32[]{:S(2)}) collective-permute-start(bf16[128,2048]{1,0:T(8,128)(2,1)S(1)} %get-tuple-element.100.refs_0_), channel_id=1, source_target_pairs={{0,4},{1,5},{2,6},{3,7},{12,8},{13,9},{14,10},{15,11},{16,20},{17,... | collective-permute-start | bytes 1572872 | tf_op jit(solution)/shard_map/ppermute | solution.py:62
  72.8 24.5 %collective-permute-start.21 = (bf16[128,2048]{1,0:T(8,128)(2,1)S(1)}, bf16[128,2048]{1,0:T(8,128)(2,1)S(1)}, u32[]{:S(2)}, u32[]{:S(2)}) collective-permute-start(bf16[128,2048]{1,0:T(8,128)(2,1)S(1)} %get-tuple-element.114), channel_id=1, source_target_pairs={{0,4},{1,5},{2,6},{3,7},{4,0},{5,1},{6,2},{7,3},{8,12},{9,13},{10,... | collective-permute-start | bytes 1572872 | tf_op jit(solution)/shard_map/ppermute | solution.py:62
  75.8 21.5 %collective-permute-start.22 = (bf16[128,2048]{1,0:T(8,128)(2,1)S(1)}, bf16[128,2048]{1,0:T(8,128)(2,1)S(1)}, u32[]{:S(2)}, u32[]{:S(2)}) collective-permute-start(bf16[128,2048]{1,0:T(8,128)(2,1)S(1)} %add.84), channel_id=1, source_target_pairs={{4,8},{5,9},{6,10},{7,11},{8,4},{9,5},{10,6},{11,7},{20,24},{21,25... | collective-permute-start | bytes 1572872 | tf_op jit(solution)/shard_map/ppermute | solution.py:62
  78.9 20.7 %collective-permute-start.13 = (bf16[1280,128]{1,0:T(8,128)(2,1)S(1)}, bf16[1280,128]{1,0:T(8,128)(2,1)S(1)}, u32[]{:S(2)}, u32[]{:S(2)}) collective-permute-start(bf16[1280,128]{1,0:T(8,128)(2,1)S(1)} %get-tuple-element.99), channel_id=1, source_target_pairs={{0,16},{1,17},{2,18},{3,19},{4,20},{5,21},{6,22},{7,23},{8,24},{9,... | collective-permute-start | bytes 983048 | tf_op jit(solution)/shard_map/ppermute | solution.py:52
  87.6 14.2 %collective-permute-start.19 = (bf16[64,2048]{1,0:T(8,128)(2,1)S(1)}, bf16[64,2048]{1,0:T(8,128)(2,1)S(1)}, u32[]{:S(2)}, u32[]{:S(2)}) collective-permute-start(bf16[64,2048]{1,0:T(8,128)(2,1)S(1)} %get-tuple-element.104), channel_id=1, source_target_pairs={{4,12},{5,13},{6,14},{7,15},{8,0},{9,1},{10,2},{11,3},{20,28},{21,... | collective-permute-start | bytes 786440 | tf_op jit(solution)/shard_map/ppermute | solution.py:62
  88.9 15.5 %collective-permute-start.20 = (bf16[64,2048]{1,0:T(8,128)(2,1)S(1)}, bf16[64,2048]{1,0:T(8,128)(2,1)S(1)}, u32[]{:S(2)}, u32[]{:S(2)}) collective-permute-start(bf16[64,2048]{1,0:T(8,128)(2,1)S(1)} %get-tuple-element.105), channel_id=1, source_target_pairs={{4,28},{5,29},{6,30},{7,31},{8,16},{9,17},{10,18},{11,19},{20,12},... | collective-permute-start | bytes 786440 | tf_op jit(solution)/shard_map/ppermute | solution.py:62
  98.1 11.4 %collective-permute-start.23 = (bf16[64,2048]{1,0:T(8,128)(2,1)S(1)}, bf16[64,2048]{1,0:T(8,128)(2,1)S(1)}, u32[]{:S(2)}, u32[]{:S(2)}) collective-permute-start(bf16[64,2048]{1,0:T(8,128)(2,1)S(1)} %get-tuple-element.116), channel_id=1, source_target_pairs={{0,16},{1,17},{2,18},{3,19},{4,20},{5,21},{6,22},{7,23},{8,24},{9,... | collective-permute-start | bytes 786440 | tf_op jit(solution)/shard_map/ppermute | solution.py:52
  99.7 4.7 %collective-permute-start.17 = (bf16[320,128]{1,0:T(8,128)(2,1)S(1)}, bf16[320,128]{1,0:T(8,128)(2,1)S(1)}, u32[]{:S(2)}, u32[]{:S(2)}) collective-permute-start(bf16[320,128]{1,0:T(8,128)(2,1)S(1)} %get-tuple-element.111), channel_id=1, source_target_pairs={{0,2},{1,3},{2,0},{3,1},{4,6},{5,7},{6,4},{7,5},{8,10},{9,11},{10,... | collective-permute-start | bytes 245768 | tf_op jit(solution)/shard_map/ppermute | solution.py:52
  101.3 4.4 %collective-permute-start.15 = (bf16[320,128]{1,0:T(8,128)(2,1)S(1)}, bf16[320,128]{1,0:T(8,128)(2,1)S(1)}, u32[]{:S(2)}, u32[]{:S(2)}) collective-permute-start(bf16[320,128]{1,0:T(8,128)(2,1)S(1)} %get-tuple-element.109), channel_id=1, source_target_pairs={{0,2},{1,3},{2,0},{3,1},{4,6},{5,7},{6,4},{7,5},{8,10},{9,11},{10,... | collective-permute-start | bytes 245768 | tf_op jit(solution)/shard_map/ppermute | solution.py:52
  101.8 3.9 %collective-permute-start.16 = (bf16[320,128]{1,0:T(8,128)(2,1)S(1)}, bf16[320,128]{1,0:T(8,128)(2,1)S(1)}, u32[]{:S(2)}, u32[]{:S(2)}) collective-permute-start(bf16[320,128]{1,0:T(8,128)(2,1)S(1)} %get-tuple-element.110), channel_id=1, source_target_pairs={{0,1},{1,0},{2,3},{3,2},{4,5},{5,4},{6,7},{7,6},{8,9},{9,8},{10,11... | collective-permute-start | bytes 245768 | tf_op jit(solution)/shard_map/ppermute | solution.py:52
  104.4 1.3 %collective-permute-start.18 = (bf16[320,128]{1,0:T(8,128)(2,1)S(1)}, bf16[320,128]{1,0:T(8,128)(2,1)S(1)}, u32[]{:S(2)}, u32[]{:S(2)}) collective-permute-start(bf16[320,128]{1,0:T(8,128)(2,1)S(1)} %collective-permute-done.17), channel_id=1, source_target_pairs={{0,1},{1,0},{2,3},{3,2},{4,5},{5,4},{6,7},{7,6},{8,9},{9,8},{10,11... | collective-permute-start | bytes 245768 | tf_op jit(solution)/shard_map/ppermute | solution.py:52

commit v10 on v9

--- a/solution.py
+++ b/solution.py
@@ -422,17 +422,13 @@
         axis=0,
     )
     flat_heads = head_outputs.reshape(tokens, top * head_dim)
-    packs, held = [], []
+    packs = []
     for dx, dy in plan.chips():
         piece = lax.dynamic_slice_in_dim(out_grad, ((x + dx) % plan.dp) * plan.part, plan.part, 1)
         value = jnp.concatenate([piece, flat_heads, meta], axis=1)
-        if plan.planes == 4 and not (dx or dy):
+        if plan.planes == 4 and dx and dy:
             value, near_in, mate = lax.optimization_barrier((value, near_in, mate))
-        if plan.planes == 4 and dx and dy:
-            value, far_in, near_out = lax.optimization_barrier((value, far_in, near_out))
         value = plan.shift(value, dx=dx, dy=dy)
-        if len(packs) < plan.dp * plan.rows - 1:
-            held += [value, plan.shift(value, dc=1)]
         packs.append(value)
 
     if plan.planes == 4:
@@ -442,6 +438,11 @@
             [(mate, None)],
             [(own_weights, None)],
         ]
+
+    if plan.planes == 4:
+        packs[:2] = lax.optimization_barrier(packs[:2])
+    held = [(value, plan.shift(value, dc=1)) for value in packs[:-1]]
+    held = [value for pair in held for value in pair]
 
     last = plan.planes - 1
     calls = [(j, 0) for j in [last, *range(last)]] + [(j, 1) for j in range(plan.planes)]
@@ -480,7 +481,9 @@
         far_sums = sum_work(plan, info, [sums[1], far_part], jnp.bfloat16)
         info, far_sums = lax.optimization_barrier((info, far_sums))
         far_pieces = [plan.along(piece, across, dx) for dx, piece in enumerate(far_sums)]
-        received = [plan.along(sums[2], mates), plan.along(near_sum, middle)]
+        mate_sums = sum_work(plan, info, [sums[2]], jnp.bfloat16)
+        far_pieces += [plan.along(piece, mates, dx) for dx, piece in enumerate(mate_sums)]
+        received = [plan.along(near_sum, middle)]
     else:
         received = [plan.shift(sums[j], dz=steps[j]) for j in range(plan.planes - 1)]
     pieces = sum_work(plan, info, [sums[last]] + received, jnp.float32)

time: 115 us -> 122 us (1.061)
  starting transfers between devices: 27.3 us -> 31 us
  waiting for transfers between devices: 46.1 us -> 48.9 us
    ppermute x11 -> x12, waiting for transfers between devices: 24.9 us -> 33.1 us  [along(): return lax.ppermute(value, AXES, out)]
    ppermute x13, waiting for transfers between devices: 21.2 us -> 15.8 us  [shift(): return lax.ppermute(value, AXES, self.pairs(**by))]
    ppermute x11 -> x12, starting transfers between devices: 16.6 us -> 19.6 us  [along(): return lax.ppermute(value, AXES, out)]
  transfers between devices with their start and end apart: 24 -> 25, of which waited for: 12 -> 11; matrix products, arithmetic and copies ran while one was open for 2% -> 2% of each run, Pallas kernels for 24% -> 23%
where the time goes in v10:
time: 122 us; the launch traced here: 121 us
  waiting for transfers between devices  48.9 us (40%)
  Pallas kernels  33.9 us (28%)
  starting transfers between devices  31 us (25%)
  local copies, waits for them, and re-layouts  5.13 us (4%)
  other arithmetic  1.36 us (1%)
    ppermute x12, waiting for transfers between devices, along(): return lax.ppermute(value, AXES, out)  33.1 us
    pallas_call x8, Pallas kernels, slot_work(): pl.pallas_call(body, out_shape=(jax.ShapeDtypeStruct((plan.head_dim, plan...  25.7 us
    ppermute x12, starting transfers between devices, along(): return lax.ppermute(value, AXES, out)  19.6 us
    ppermute x13, waiting for transfers between devices, shift(): return lax.ppermute(value, AXES, self.pairs(**by))  15.8 us
    ppermute x13, starting transfers between devices, shift(): return lax.ppermute(value, AXES, self.pairs(**by))  11.5 us
    unnamed x15, local copies, waits for them, and re-layouts  4.01 us
  transfers between devices with their start and end apart: 25, of which 11 were waited for; matrix products, arithmetic and copies ran while one was open for 2% of the time, Pallas kernels for 23%

profile of v10, /device:TPU:0, one launch (start us, length us, event | category | flops | bytes accessed | tf_op | source)
XLA Modules:
  0.0 121.3 jit_solution(1778934015631628471)
XLA Ops:
  0.6 0.0 copy-start
  0.7 1.2 copy-done
  1.9 0.8 dynamic-slice_bitcast_fusion.refs_6_.refs_2_
  2.7 1.5 %collective-permute-start.1 = (bf16[128,2048]{1,0:T(8,128)(2,1)}, bf16[128,2048]{1,0:T(8,128)(2,1)}, u32[]{:S(2)}, u32[]{:S(2)}) collective-permute-start(bf16[128,2048]{1,0:T(8,128)(2,1)} %dynamic-slice_bitcast_fusion.refs_6_.refs_2_), channel_id=1, source_target_pairs={{4,8},{5,9},{6,10},{7,11},{8,4},{9,5},{10,6},{11,7},{20,24},{21,25... | collective-permute-start | bytes 1572872 | tf_op jit(solution)/shard_map/ppermute | solution.py:62
  4.1 5.1 %collective-permute-start = (bf16[128,2048]{1,0:T(8,128)(2,1)}, bf16[128,2048]{1,0:T(8,128)(2,1)}, u32[]{:S(2)}, u32[]{:S(2)}) collective-permute-start(bf16[128,2048]{1,0:T(8,128)(2,1)} %dynamic-slice_bitcast_fusion.refs_6_.refs_2_), channel_id=1, source_target_pairs={{0,4},{1,5},{2,6},{3,7},{4,0},{5,1},{6,2},{7,3},{8,12},{9,13},{10,... | collective-permute-start | bytes 1572872 | tf_op jit(solution)/shard_map/ppermute | solution.py:62
  9.3 0.0 copy-start.5
  9.3 0.1 constant_dynamic-slice_fusion
  9.5 0.5 copy-done.5
  10.0 1.0 fusion.1
  11.0 1.5 %collective-permute-start.3 = (bf16[128,3200]{1,0:T(8,128)(2,1)S(1)}, bf16[128,3200]{1,0:T(8,128)(2,1)S(1)}, u32[]{:S(2)}, u32[]{:S(2)}) collective-permute-start(bf16[128,3200]{1,0:T(8,128)(2,1)S(1)} %get-tuple-element.73.refs_0_), channel_id=1, source_target_pairs={{0,2},{1,3},{2,0},{3,1},{4,6},{5,7},{6,4},{7,5},{8,10},{9,11},{10,... | collective-permute-start | bytes 2457608 | tf_op jit(solution)/shard_map/ppermute | solution.py:52
  12.6 1.5 %collective-permute-start.6 = (bf16[128,3200]{1,0:T(8,128)(2,1)}, bf16[128,3200]{1,0:T(8,128)(2,1)S(1)}, u32[]{:S(2)}, u32[]{:S(2)}) collective-permute-start(bf16[128,3200]{1,0:T(8,128)(2,1)} %get-tuple-element.71), channel_id=1, source_target_pairs={{0,16},{1,17},{2,18},{3,19},{4,20},{5,21},{6,22},{7,23},{8,24},{9,... | collective-permute-start | bytes 2457608 | tf_op jit(solution)/shard_map/ppermute | solution.py:52
  14.1 0.7 copy.10.route_ref
  14.8 0.1 stack.63.info
  14.9 0.0 copy-start.1
  14.9 0.8 copy-done.1
  15.7 2.4 %shard_map.76.target_ref = s32[1024,128]{1,0:T(8,128)S(1)} custom-call(s32[15]{0:T(128)S(1)} %stack.63.info, s32[128,8]{1,0:T(8,128)S(1)} %copy-done.1), custom_call_target="tpu_custom_call" | custom-call | tf_op jit(solution)/shard_map/pallas_call | solution.py:340
  18.1 0.0 collective-permute-done.1.refs_6_.refs_2_
  18.1 3.1 %collective-permute-done.refs_6_.refs_2_ = bf16[128,2048]{1,0:T(8,128)(2,1)} collective-permute-done((bf16[128,2048]{1,0:T(8,128)(2,1)}, bf16[128,2048]{1,0:T(8,128)(2,1)}, u32[]{:S(2)}, u32[]{:S(2)}) %collective-permute-start) | collective-permute-done | bytes 524320 | tf_op jit(solution)/shard_map/ppermute | solution.py:62
  21.2 1.3 %collective-permute-start.9 = (bf16[128,2048]{1,0:T(8,128)(2,1)}, bf16[128,2048]{1,0:T(8,128)(2,1)S(1)}, u32[]{:S(2)}, u32[]{:S(2)}) collective-permute-start(bf16[128,2048]{1,0:T(8,128)(2,1)} %collective-permute-done.1.refs_6_.refs_2_), channel_id=1, source_target_pairs={{4,0},{5,1},{6,2},{7,3},{8,12},{9,13},{10,14},{11,15},{20,16},{21,... | collective-permute-start | bytes 1572872 | tf_op jit(solution)/shard_map/ppermute | solution.py:62
  22.5 0.7 collective-permute-start.8
  23.2 7.3 %collective-permute-done.3.refs_2_ = bf16[128,3200]{1,0:T(8,128)(2,1)S(1)} collective-permute-done((bf16[128,3200]{1,0:T(8,128)(2,1)S(1)}, bf16[128,3200]{1,0:T(8,128)(2,1)S(1)}, u32[]{:S(2)}, u32[]{:S(2)}) %collective-permute-start.3) | collective-permute-done | bytes 819232 | tf_op jit(solution)/shard_map/ppermute | solution.py:52
  30.5 0.0 collective-permute-start.4
  30.5 0.5 collective-permute-start.5
  31.0 0.9 collective-permute-done.6.refs_4_
  31.9 4.2 %collective-permute-done.9.refs_7_.refs_3_ = bf16[128,2048]{1,0:T(8,128)(2,1)S(1)} collective-permute-done((bf16[128,2048]{1,0:T(8,128)(2,1)}, bf16[128,2048]{1,0:T(8,128)(2,1)S(1)}, u32[]{:S(2)}, u32[]{:S(2)}) %collective-permute-start.9) | collective-permute-done | bytes 524320 | tf_op jit(solution)/shard_map/ppermute | solution.py:62
  36.1 2.4 %collective-permute-start.2 = (bf16[128,3200]{1,0:T(8,128)(2,1)}, bf16[128,3200]{1,0:T(8,128)(2,1)S(1)}, u32[]{:S(2)}, u32[]{:S(2)}) collective-permute-start(bf16[128,3200]{1,0:T(8,128)(2,1)} %get-tuple-element.71), channel_id=1, source_target_pairs={{0,18},{1,19},{2,16},{3,17},{4,22},{5,23},{6,20},{7,21},{8,26},{9,... | collective-permute-start | bytes 2457608 | tf_op jit(solution)/shard_map/ppermute | solution.py:52
  38.5 1.3 %collective-permute-start.10 = (bf16[128,2048]{1,0:T(8,128)(2,1)S(1)}, bf16[128,2048]{1,0:T(8,128)(2,1)S(1)}, u32[]{:S(2)}, u32[]{:S(2)}) collective-permute-start(bf16[128,2048]{1,0:T(8,128)(2,1)S(1)} %collective-permute-done.8.refs_6_.refs_2_), channel_id=1, source_target_pairs={{4,0},{5,1},{6,2},{7,3},{8,12},{9,13},{10,14},{11,15},{20,16},{21,... | collective-permute-start | bytes 1572872 | tf_op jit(solution)/shard_map/ppermute | solution.py:62
  39.9 4.2 %shard_map.77 = (f32[128,2048]{1,0:T(8,128)S(1)}, bf16[6,80,128]{2,1,0:T(8,128)(2,1)S(1)}) custom-call(s32[15]{0:T(128)S(1)} %stack.63.info, bf16[128,3200]{1,0:T(8,128)(2,1)S(1)} %get-tuple-element.73.refs_0_, bf16[128,3200]{1,0:T(8,128)(2,1)S(1)} %collective-permute-done.4.refs_1_, bf16[128,3200]{1,0:T(8,128)(2,1)S(1)} %collective-permute-done.3.refs_2_, ...), custom_call_target="tpu_custom_call" | custom-call | tf_op jit(solution)/shard_map/pallas_call | solution.py:216
  44.1 4.2 %shard_map.78 = (f32[128,2048]{1,0:T(8,128)S(1)}, bf16[6,80,128]{2,1,0:T(8,128)(2,1)S(1)}) custom-call(s32[15]{0:T(128)S(1)} %stack.63.info, bf16[128,3200]{1,0:T(8,128)(2,1)S(1)} %get-tuple-element.73.refs_0_, bf16[128,3200]{1,0:T(8,128)(2,1)S(1)} %collective-permute-done.4.refs_1_, bf16[128,3200]{1,0:T(8,128)(2,1)S(1)} %collective-permute-done.3.refs_2_, ...), custom_call_target="tpu_custom_call" | custom-call | tf_op jit(solution)/shard_map/pallas_call | solution.py:216
  48.3 4.2 %shard_map.79 = (f32[128,2048]{1,0:T(8,128)S(1)}, bf16[6,80,128]{2,1,0:T(8,128)(2,1)S(1)}) custom-call(s32[15]{0:T(128)S(1)} %stack.63.info, bf16[128,3200]{1,0:T(8,128)(2,1)S(1)} %get-tuple-element.73.refs_0_, bf16[128,3200]{1,0:T(8,128)(2,1)S(1)} %collective-permute-done.4.refs_1_, bf16[128,3200]{1,0:T(8,128)(2,1)S(1)} %collective-permute-done.3.refs_2_, ...), custom_call_target="tpu_custom_call" | custom-call | tf_op jit(solution)/shard_map/pallas_call | solution.py:216
  52.5 2.9 %collective-permute-done.2.refs_0_ = bf16[128,3200]{1,0:T(8,128)(2,1)S(1)} collective-permute-done((bf16[128,3200]{1,0:T(8,128)(2,1)}, bf16[128,3200]{1,0:T(8,128)(2,1)S(1)}, u32[]{:S(2)}, u32[]{:S(2)}) %collective-permute-start.2) | collective-permute-done | bytes 819232 | tf_op jit(solution)/shard_map/ppermute | solution.py:52
  55.4 2.3 %collective-permute-done.11.refs_1_ = bf16[128,3200]{1,0:T(8,128)(2,1)S(1)} collective-permute-done((bf16[128,3200]{1,0:T(8,128)(2,1)S(1)}, bf16[128,3200]{1,0:T(8,128)(2,1)S(1)}, u32[]{:S(2)}, u32[]{:S(2)}) %collective-permute-start.11) | collective-permute-done | bytes 819232 | tf_op jit(solution)/shard_map/ppermute | solution.py:52
  57.7 2.6 %shard_map.80 = (bf16[128,2048]{1,0:T(8,128)(2,1)S(1)}, bf16[2,80,128]{2,1,0:T(8,128)(2,1)S(1)}) custom-call(s32[15]{0:T(128)S(1)} %stack.63.info, bf16[128,3200]{1,0:T(8,128)(2,1)S(1)} %collective-permute-done.2.refs_0_, bf16[128,3200]{1,0:T(8,128)(2,1)S(1)} %collective-permute-done.11.refs_1_, bf16[128,2048]{1,0:T(8,128)(2,1)} %collective-permute-done.1.refs_6_.refs_2_, ...), custom_call_target="tpu_custom_call" | custom-call | tf_op jit(solution)/shard_map/pallas_call | solution.py:216
  60.4 1.8 %collective-permute-start.12 = (bf16[128,2048]{1,0:T(8,128)(2,1)S(1)}, bf16[128,2048]{1,0:T(8,128)(2,1)S(1)}, u32[]{:S(2)}, u32[]{:S(2)}) collective-permute-start(bf16[128,2048]{1,0:T(8,128)(2,1)S(1)} %get-tuple-element.97), channel_id=1, source_target_pairs={{0,4},{1,5},{2,6},{3,7},{12,8},{13,9},{14,10},{15,11},{16,20},{17,... | collective-permute-start | bytes 1572872 | tf_op jit(solution)/shard_map/ppermute | solution.py:62
  62.2 3.7 %shard_map.81 = (f32[128,2048]{1,0:T(8,128)S(1)}, bf16[6,80,128]{2,1,0:T(8,128)(2,1)S(1)}) custom-call(s32[15]{0:T(128)S(1)} %stack.63.info, bf16[128,3200]{1,0:T(8,128)(2,1)S(1)} %get-tuple-element.73.refs_0_, bf16[128,3200]{1,0:T(8,128)(2,1)S(1)} %collective-permute-done.4.refs_1_, bf16[128,3200]{1,0:T(8,128)(2,1)S(1)} %collective-permute-done.3.refs_2_, ...), custom_call_target="tpu_custom_call" | custom-call | tf_op jit(solution)/shard_map/pallas_call | solution.py:216
  65.9 1.9 %shard_map.82 = (bf16[128,2048]{1,0:T(8,128)(2,1)S(1)}, bf16[2,80,128]{2,1,0:T(8,128)(2,1)S(1)}) custom-call(s32[15]{0:T(128)S(1)} %stack.63.info, bf16[128,3200]{1,0:T(8,128)(2,1)S(1)} %collective-permute-done.2.refs_0_, bf16[128,3200]{1,0:T(8,128)(2,1)S(1)} %collective-permute-done.11.refs_1_, ...), custom_call_target="tpu_custom_call" | custom-call | tf_op jit(solution)/shard_map/pallas_call | solution.py:216
  67.8 1.3 %collective-permute-start.14 = (bf16[128,2048]{1,0:T(8,128)(2,1)S(1)}, bf16[128,2048]{1,0:T(8,128)(2,1)S(1)}, u32[]{:S(2)}, u32[]{:S(2)}) collective-permute-start(bf16[128,2048]{1,0:T(8,128)(2,1)S(1)} %get-tuple-element.102.refs_0_), channel_id=1, source_target_pairs={{0,4},{1,5},{2,6},{3,7},{12,8},{13,9},{14,10},{15,11},{16,20},{17,... | collective-permute-start | bytes 1572872 | tf_op jit(solution)/shard_map/ppermute | solution.py:62
  69.2 5.3 %collective-permute-done.12 = bf16[128,2048]{1,0:T(8,128)(2,1)S(1)} collective-permute-done((bf16[128,2048]{1,0:T(8,128)(2,1)S(1)}, bf16[128,2048]{1,0:T(8,128)(2,1)S(1)}, u32[]{:S(2)}, u32[]{:S(2)}) %collective-permute-start.12) | collective-permute-done | bytes 524320 | tf_op jit(solution)/shard_map/ppermute | solution.py:62
  74.4 0.1 add.84
  74.6 0.7 collective-permute-start.23
  75.3 2.4 %shard_map.83 = (bf16[128,2048]{1,0:T(8,128)(2,1)S(1)}, bf16[2,80,128]{2,1,0:T(8,128)(2,1)S(1)}) custom-call(s32[15]{0:T(128)S(1)} %stack.63.info, bf16[128,3200]{1,0:T(8,128)(2,1)S(1)} %collective-permute-done.2.refs_0_, bf16[128,3200]{1,0:T(8,128)(2,1)S(1)} %collective-permute-done.11.refs_1_, bf16[128,2048]{1,0:T(8,128)(2,1)} %collective-permute-done.refs_6_.refs_2_, ...), custom_call_target="tpu_custom_call" | custom-call | tf_op jit(solution)/shard_map/pallas_call | solution.py:216
  77.7 2.4 %shard_map.84 = (f32[128,2048]{1,0:T(8,128)S(1)}, bf16[1280,128]{1,0:T(8,128)(2,1)S(1)}, bf16[1280,128]{1,0:T(8,128)(2,1)S(1)}) custom-call(s32[15]{0:T(128)S(1)} %stack.63.info, bf16[128,3200]{1,0:T(8,128)(2,1)S(1)} %collective-permute-done.2.refs_0_, bf16[128,3200]{1,0:T(8,128)(2,1)S(1)} %collective-permute-done.11.refs_1_, ...), custom_call_target="tpu_custom_call" | custom-call | tf_op jit(solution)/shard_map/pallas_call | solution.py:216
  80.1 1.3 %collective-permute-start.13 = (bf16[1280,128]{1,0:T(8,128)(2,1)S(1)}, bf16[1280,128]{1,0:T(8,128)(2,1)S(1)}, u32[]{:S(2)}, u32[]{:S(2)}) collective-permute-start(bf16[1280,128]{1,0:T(8,128)(2,1)S(1)} %get-tuple-element.101), channel_id=1, source_target_pairs={{0,16},{1,17},{2,18},{3,19},{4,20},{5,21},{6,22},{7,23},{8,24},{9,... | collective-permute-start | bytes 983048 | tf_op jit(solution)/shard_map/ppermute | solution.py:52
  81.4 3.4 %collective-permute-done.14.refs_1_ = bf16[128,2048]{1,0:T(8,128)(2,1)S(1)} collective-permute-done((bf16[128,2048]{1,0:T(8,128)(2,1)S(1)}, bf16[128,2048]{1,0:T(8,128)(2,1)S(1)}, u32[]{:S(2)}, u32[]{:S(2)}) %collective-permute-start.14) | collective-permute-done | bytes 524320 | tf_op jit(solution)/shard_map/ppermute | solution.py:62
  84.9 0.7 shard_map.85
  85.5 0.6 shard_map.87
  86.1 2.5 %collective-permute-start.21 = (bf16[64,2048]{1,0:T(8,128)(2,1)S(1)}, bf16[64,2048]{1,0:T(8,128)(2,1)S(1)}, u32[]{:S(2)}, u32[]{:S(2)}) collective-permute-start(bf16[64,2048]{1,0:T(8,128)(2,1)S(1)} %get-tuple-element.116), channel_id=1, source_target_pairs={{0,4},{1,5},{2,6},{3,7},{4,0},{5,1},{6,2},{7,3},{8,12},{9,13},{10,... | collective-permute-start | bytes 786440 | tf_op jit(solution)/shard_map/ppermute | solution.py:62
  88.7 0.8 collective-permute-start.22
  89.5 1.3 %collective-permute-start.19 = (bf16[64,2048]{1,0:T(8,128)(2,1)S(1)}, bf16[64,2048]{1,0:T(8,128)(2,1)S(1)}, u32[]{:S(2)}, u32[]{:S(2)}) collective-permute-start(bf16[64,2048]{1,0:T(8,128)(2,1)S(1)} %get-tuple-element.106), channel_id=1, source_target_pairs={{4,12},{5,13},{6,14},{7,15},{8,0},{9,1},{10,2},{11,3},{20,28},{21,... | collective-permute-start | bytes 786440 | tf_op jit(solution)/shard_map/ppermute | solution.py:62
  90.8 1.3 %collective-permute-start.20 = (bf16[64,2048]{1,0:T(8,128)(2,1)S(1)}, bf16[64,2048]{1,0:T(8,128)(2,1)S(1)}, u32[]{:S(2)}, u32[]{:S(2)}) collective-permute-start(bf16[64,2048]{1,0:T(8,128)(2,1)S(1)} %get-tuple-element.107), channel_id=1, source_target_pairs={{4,28},{5,29},{6,30},{7,31},{8,16},{9,17},{10,18},{11,19},{20,12},... | collective-permute-start | bytes 786440 | tf_op jit(solution)/shard_map/ppermute | solution.py:62
  92.1 0.7 shard_map.88
  92.7 0.8 collective-permute-start.24
  93.6 0.1 shard_map.86
  93.6 13.5 %collective-permute-done.21.refs_4_ = bf16[64,2048]{1,0:T(8,128)(2,1)S(1)} collective-permute-done((bf16[64,2048]{1,0:T(8,128)(2,1)S(1)}, bf16[64,2048]{1,0:T(8,128)(2,1)S(1)}, u32[]{:S(2)}, u32[]{:S(2)}) %collective-permute-start.21) | collective-permute-done | bytes 262176 | tf_op jit(solution)/shard_map/ppermute | solution.py:62
  107.1 1.3 %collective-permute-start.17 = (bf16[320,128]{1,0:T(8,128)(2,1)S(1)}, bf16[320,128]{1,0:T(8,128)(2,1)S(1)}, u32[]{:S(2)}, u32[]{:S(2)}) collective-permute-start(bf16[320,128]{1,0:T(8,128)(2,1)S(1)} %get-tuple-element.113), channel_id=1, source_target_pairs={{0,2},{1,3},{2,0},{3,1},{4,6},{5,7},{6,4},{7,5},{8,10},{9,11},{10,... | collective-permute-start | bytes 245768 | tf_op jit(solution)/shard_map/ppermute | solution.py:52
  108.4 3.6 %collective-permute-done.22.refs_5_ = bf16[64,2048]{1,0:T(8,128)(2,1)S(1)} collective-permute-done((bf16[64,2048]{1,0:T(8,128)(2,1)S(1)}, bf16[64,2048]{1,0:T(8,128)(2,1)S(1)}, u32[]{:S(2)}, u32[]{:S(2)}) %collective-permute-start.22) | collective-permute-done | bytes 262176 | tf_op jit(solution)/shard_map/ppermute | solution.py:62
  112.1 1.5 %collective-permute-start.15 = (bf16[320,128]{1,0:T(8,128)(2,1)S(1)}, bf16[320,128]{1,0:T(8,128)(2,1)S(1)}, u32[]{:S(2)}, u32[]{:S(2)}) collective-permute-start(bf16[320,128]{1,0:T(8,128)(2,1)S(1)} %get-tuple-element.111), channel_id=1, source_target_pairs={{0,2},{1,3},{2,0},{3,1},{4,6},{5,7},{6,4},{7,5},{8,10},{9,11},{10,... | collective-permute-start | bytes 245768 | tf_op jit(solution)/shard_map/ppermute | solution.py:52
  113.6 0.5 collective-permute-start.18
  114.1 2.4 %collective-permute-done.15.refs_1_ = bf16[320,128]{1,0:T(8,128)(2,1)S(1)} collective-permute-done((bf16[320,128]{1,0:T(8,128)(2,1)S(1)}, bf16[320,128]{1,0:T(8,128)(2,1)S(1)}, u32[]{:S(2)}, u32[]{:S(2)}) %collective-permute-start.15) | collective-permute-done | bytes 81952 | tf_op jit(solution)/shard_map/ppermute | solution.py:52
  116.5 2.2 %shard_map.89 = (bf16[1024,128]{1,0:T(8,128)(2,1)}, f32[1024,1]{1,0:T(8,128)S(1)}) custom-call(s32[1024,128]{1,0:T(8,128)S(1)} %shard_map.76.target_ref, bf16[320,128]{1,0:T(8,128)(2,1)S(1)} %get-tuple-element.121.refs_0_, bf16[320,128]{1,0:T(8,128)(2,1)S(1)} %collective-permute-done.15.refs_1_, bf16[320,128]{1,0:T(8,128)(2,1)S(1)} %collective-permute-done.16.refs_2_, ...), custom_call_target="tpu_custom_call" | custom-call | flops 1 | bytes 1 | tf_op jit(solution)/shard_map/pallas_call | solution.py:370
  118.7 0.2 convert_reduce_fusion
  118.9 0.1 convert_element_type.15
  119.0 0.7 copy.11
  119.7 1.7 %shard_map.90 = f32[64,4096]{1,0:T(8,128)} custom-call(s32[15]{0:T(128)S(1)} %stack.63.info, f32[64,2048]{1,0:T(8,128)S(1)} %get-tuple-element.127.refs_0_, bf16[64,2048]{1,0:T(8,128)(2,1)S(1)} %collective-permute-done.24.refs_1_, bf16[64,2048]{1,0:T(8,128)(2,1)S(1)} %collective-permute-done.19.refs_2_, ...), custom_call_target="tpu_custom_call" | custom-call | tf_op jit(solution)/shard_map/pallas_call | solution.py:270
  (25 shorter events, 0.1 us)
Async XLA Ops:
  0.6 1.2 %copy-start = (bf16[1,128,4096]{2,1,0:T(8,128)(2,1)S(1)}, bf16[1,128,4096]{2,1,0:T(8,128)(2,1)}, u32[]{:S(2)}) copy-start(bf16[1,128,4096]{2,1,0:T(8,128)(2,1)} %param.9) | copy-start | bytes 3145732
  0.6 8.6 %copy-start.4 = (s32[128,8]{0,1:T(8,128)S(1)}, s32[128,8]{0,1:T(8,128)}, u32[]{:S(2)}) copy-start(s32[128,8]{0,1:T(8,128)} %param.8) | copy-start | bytes 12292
  0.7 8.6 %copy-start.3 = (bf16[128,8,128]{2,1,0:T(8,128)(2,1)S(1)}, bf16[128,8,128]{2,1,0:T(8,128)(2,1)}, u32[]{:S(2)}) copy-start(bf16[128,8,128]{2,1,0:T(8,128)(2,1)} %param.5) | copy-start | bytes 786436
  0.7 8.7 %copy-start.2 = (bf16[128,4096]{1,0:T(8,128)(2,1)S(1)}, bf16[128,4096]{1,0:T(8,128)(2,1)}, u32[]{:S(2)}) copy-start(bf16[128,4096]{1,0:T(8,128)(2,1)} %param.6) | copy-start | bytes 3145732
  2.7 15.4 %collective-permute-start.1 = (bf16[128,2048]{1,0:T(8,128)(2,1)}, bf16[128,2048]{1,0:T(8,128)(2,1)}, u32[]{:S(2)}, u32[]{:S(2)}) collective-permute-start(bf16[128,2048]{1,0:T(8,128)(2,1)} %dynamic-slice_bitcast_fusion.refs_6_.refs_2_), channel_id=1, source_target_pairs={{4,8},{5,9},{6,10},{7,11},{8,4},{9,5},{10,6},{11,7},{20,24},{21,25... | collective-permute-start | bytes 1572872 | tf_op jit(solution)/shard_map/ppermute | solution.py:62
  4.1 17.1 %collective-permute-start = (bf16[128,2048]{1,0:T(8,128)(2,1)}, bf16[128,2048]{1,0:T(8,128)(2,1)}, u32[]{:S(2)}, u32[]{:S(2)}) collective-permute-start(bf16[128,2048]{1,0:T(8,128)(2,1)} %dynamic-slice_bitcast_fusion.refs_6_.refs_2_), channel_id=1, source_target_pairs={{0,4},{1,5},{2,6},{3,7},{4,0},{5,1},{6,2},{7,3},{8,12},{9,13},{10,... | collective-permute-start | bytes 1572872 | tf_op jit(solution)/shard_map/ppermute | solution.py:62
  9.3 0.7 copy-start.5
  11.0 19.4 %collective-permute-start.3 = (bf16[128,3200]{1,0:T(8,128)(2,1)S(1)}, bf16[128,3200]{1,0:T(8,128)(2,1)S(1)}, u32[]{:S(2)}, u32[]{:S(2)}) collective-permute-start(bf16[128,3200]{1,0:T(8,128)(2,1)S(1)} %get-tuple-element.73.refs_0_), channel_id=1, source_target_pairs={{0,2},{1,3},{2,0},{3,1},{4,6},{5,7},{6,4},{7,5},{8,10},{9,11},{10,... | collective-permute-start | bytes 2457608 | tf_op jit(solution)/shard_map/ppermute | solution.py:52
  12.6 19.4 %collective-permute-start.6 = (bf16[128,3200]{1,0:T(8,128)(2,1)}, bf16[128,3200]{1,0:T(8,128)(2,1)S(1)}, u32[]{:S(2)}, u32[]{:S(2)}) collective-permute-start(bf16[128,3200]{1,0:T(8,128)(2,1)} %get-tuple-element.71), channel_id=1, source_target_pairs={{0,16},{1,17},{2,18},{3,19},{4,20},{5,21},{6,22},{7,23},{8,24},{9,... | collective-permute-start | bytes 2457608 | tf_op jit(solution)/shard_map/ppermute | solution.py:52
  14.9 0.8 copy-start.1
  21.2 14.9 %collective-permute-start.9 = (bf16[128,2048]{1,0:T(8,128)(2,1)}, bf16[128,2048]{1,0:T(8,128)(2,1)S(1)}, u32[]{:S(2)}, u32[]{:S(2)}) collective-permute-start(bf16[128,2048]{1,0:T(8,128)(2,1)} %collective-permute-done.1.refs_6_.refs_2_), channel_id=1, source_target_pairs={{4,0},{5,1},{6,2},{7,3},{8,12},{9,13},{10,14},{11,15},{20,16},{21,... | collective-permute-start | bytes 1572872 | tf_op jit(solution)/shard_map/ppermute | solution.py:62
  22.5 16.0 %collective-permute-start.8 = (bf16[128,2048]{1,0:T(8,128)(2,1)}, bf16[128,2048]{1,0:T(8,128)(2,1)S(1)}, u32[]{:S(2)}, u32[]{:S(2)}) collective-permute-start(bf16[128,2048]{1,0:T(8,128)(2,1)} %collective-permute-done.refs_6_.refs_2_), channel_id=1, source_target_pairs={{4,8},{5,9},{6,10},{7,11},{8,4},{9,5},{10,6},{11,7},{20,24},{21,25... | collective-permute-start | bytes 1572872 | tf_op jit(solution)/shard_map/ppermute | solution.py:62
  30.5 9.4 %collective-permute-start.4 = (bf16[128,3200]{1,0:T(8,128)(2,1)S(1)}, bf16[128,3200]{1,0:T(8,128)(2,1)S(1)}, u32[]{:S(2)}, u32[]{:S(2)}) collective-permute-start(bf16[128,3200]{1,0:T(8,128)(2,1)S(1)} %get-tuple-element.73.refs_0_), channel_id=1, source_target_pairs={{0,1},{1,0},{2,3},{3,2},{4,5},{5,4},{6,7},{7,6},{8,9},{9,8},{10,11... | collective-permute-start | bytes 2457608 | tf_op jit(solution)/shard_map/ppermute | solution.py:52
  30.5 9.4 %collective-permute-start.5 = (bf16[128,3200]{1,0:T(8,128)(2,1)S(1)}, bf16[128,3200]{1,0:T(8,128)(2,1)S(1)}, u32[]{:S(2)}, u32[]{:S(2)}) collective-permute-start(bf16[128,3200]{1,0:T(8,128)(2,1)S(1)} %collective-permute-done.3.refs_2_), channel_id=1, source_target_pairs={{0,1},{1,0},{2,3},{3,2},{4,5},{5,4},{6,7},{7,6},{8,9},{9,8},{10,11... | collective-permute-start | bytes 2457608 | tf_op jit(solution)/shard_map/ppermute | solution.py:52
  31.9 7.9 %collective-permute-start.7 = (bf16[128,3200]{1,0:T(8,128)(2,1)S(1)}, bf16[128,3200]{1,0:T(8,128)(2,1)S(1)}, u32[]{:S(2)}, u32[]{:S(2)}) collective-permute-start(bf16[128,3200]{1,0:T(8,128)(2,1)S(1)} %collective-permute-done.6.refs_4_), channel_id=1, source_target_pairs={{0,1},{1,0},{2,3},{3,2},{4,5},{5,4},{6,7},{7,6},{8,9},{9,8},{10,11... | collective-permute-start | bytes 2457608 | tf_op jit(solution)/shard_map/ppermute | solution.py:52
  36.1 19.3 %collective-permute-start.2 = (bf16[128,3200]{1,0:T(8,128)(2,1)}, bf16[128,3200]{1,0:T(8,128)(2,1)S(1)}, u32[]{:S(2)}, u32[]{:S(2)}) collective-permute-start(bf16[128,3200]{1,0:T(8,128)(2,1)} %get-tuple-element.71), channel_id=1, source_target_pairs={{0,18},{1,19},{2,16},{3,17},{4,22},{5,23},{6,20},{7,21},{8,26},{9,... | collective-permute-start | bytes 2457608 | tf_op jit(solution)/shard_map/ppermute | solution.py:52
  38.5 16.9 %collective-permute-start.10 = (bf16[128,2048]{1,0:T(8,128)(2,1)S(1)}, bf16[128,2048]{1,0:T(8,128)(2,1)S(1)}, u32[]{:S(2)}, u32[]{:S(2)}) collective-permute-start(bf16[128,2048]{1,0:T(8,128)(2,1)S(1)} %collective-permute-done.8.refs_6_.refs_2_), channel_id=1, source_target_pairs={{4,0},{5,1},{6,2},{7,3},{8,12},{9,13},{10,14},{11,15},{20,16},{21,... | collective-permute-start | bytes 1572872 | tf_op jit(solution)/shard_map/ppermute | solution.py:62
  55.4 2.3 %collective-permute-start.11 = (bf16[128,3200]{1,0:T(8,128)(2,1)S(1)}, bf16[128,3200]{1,0:T(8,128)(2,1)S(1)}, u32[]{:S(2)}, u32[]{:S(2)}) collective-permute-start(bf16[128,3200]{1,0:T(8,128)(2,1)S(1)} %collective-permute-done.2.refs_0_), channel_id=1, source_target_pairs={{0,1},{1,0},{2,3},{3,2},{4,5},{5,4},{6,7},{7,6},{8,9},{9,8},{10,11... | collective-permute-start | bytes 2457608 | tf_op jit(solution)/shard_map/ppermute | solution.py:52
  60.4 14.1 %collective-permute-start.12 = (bf16[128,2048]{1,0:T(8,128)(2,1)S(1)}, bf16[128,2048]{1,0:T(8,128)(2,1)S(1)}, u32[]{:S(2)}, u32[]{:S(2)}) collective-permute-start(bf16[128,2048]{1,0:T(8,128)(2,1)S(1)} %get-tuple-element.97), channel_id=1, source_target_pairs={{0,4},{1,5},{2,6},{3,7},{12,8},{13,9},{14,10},{15,11},{16,20},{17,... | collective-permute-start | bytes 1572872 | tf_op jit(solution)/shard_map/ppermute | solution.py:62
  67.8 17.0 %collective-permute-start.14 = (bf16[128,2048]{1,0:T(8,128)(2,1)S(1)}, bf16[128,2048]{1,0:T(8,128)(2,1)S(1)}, u32[]{:S(2)}, u32[]{:S(2)}) collective-permute-start(bf16[128,2048]{1,0:T(8,128)(2,1)S(1)} %get-tuple-element.102.refs_0_), channel_id=1, source_target_pairs={{0,4},{1,5},{2,6},{3,7},{12,8},{13,9},{14,10},{15,11},{16,20},{17,... | collective-permute-start | bytes 1572872 | tf_op jit(solution)/shard_map/ppermute | solution.py:62
  74.6 16.2 %collective-permute-start.23 = (bf16[128,2048]{1,0:T(8,128)(2,1)S(1)}, bf16[128,2048]{1,0:T(8,128)(2,1)S(1)}, u32[]{:S(2)}, u32[]{:S(2)}) collective-permute-start(bf16[128,2048]{1,0:T(8,128)(2,1)S(1)} %add.84), channel_id=1, source_target_pairs={{4,8},{5,9},{6,10},{7,11},{8,4},{9,5},{10,6},{11,7},{20,24},{21,25... | collective-permute-start | bytes 1572872 | tf_op jit(solution)/shard_map/ppermute | solution.py:62
  80.1 12.6 %collective-permute-start.13 = (bf16[1280,128]{1,0:T(8,128)(2,1)S(1)}, bf16[1280,128]{1,0:T(8,128)(2,1)S(1)}, u32[]{:S(2)}, u32[]{:S(2)}) collective-permute-start(bf16[1280,128]{1,0:T(8,128)(2,1)S(1)} %get-tuple-element.101), channel_id=1, source_target_pairs={{0,16},{1,17},{2,18},{3,19},{4,20},{5,21},{6,22},{7,23},{8,24},{9,... | collective-permute-start | bytes 983048 | tf_op jit(solution)/shard_map/ppermute | solution.py:52
  86.1 21.0 %collective-permute-start.21 = (bf16[64,2048]{1,0:T(8,128)(2,1)S(1)}, bf16[64,2048]{1,0:T(8,128)(2,1)S(1)}, u32[]{:S(2)}, u32[]{:S(2)}) collective-permute-start(bf16[64,2048]{1,0:T(8,128)(2,1)S(1)} %get-tuple-element.116), channel_id=1, source_target_pairs={{0,4},{1,5},{2,6},{3,7},{4,0},{5,1},{6,2},{7,3},{8,12},{9,13},{10,... | collective-permute-start | bytes 786440 | tf_op jit(solution)/shard_map/ppermute | solution.py:62
  88.7 23.4 %collective-permute-start.22 = (bf16[64,2048]{1,0:T(8,128)(2,1)S(1)}, bf16[64,2048]{1,0:T(8,128)(2,1)S(1)}, u32[]{:S(2)}, u32[]{:S(2)}) collective-permute-start(bf16[64,2048]{1,0:T(8,128)(2,1)S(1)} %get-tuple-element.117), channel_id=1, source_target_pairs={{0,20},{1,21},{2,22},{3,23},{4,16},{5,17},{6,18},{7,19},{8,28},{9,... | collective-permute-start | bytes 786440 | tf_op jit(solution)/shard_map/ppermute | solution.py:62
  89.5 24.1 %collective-permute-start.19 = (bf16[64,2048]{1,0:T(8,128)(2,1)S(1)}, bf16[64,2048]{1,0:T(8,128)(2,1)S(1)}, u32[]{:S(2)}, u32[]{:S(2)}) collective-permute-start(bf16[64,2048]{1,0:T(8,128)(2,1)S(1)} %get-tuple-element.106), channel_id=1, source_target_pairs={{4,12},{5,13},{6,14},{7,15},{8,0},{9,1},{10,2},{11,3},{20,28},{21,... | collective-permute-start | bytes 786440 | tf_op jit(solution)/shard_map/ppermute | solution.py:62
  90.8 23.4 %collective-permute-start.20 = (bf16[64,2048]{1,0:T(8,128)(2,1)S(1)}, bf16[64,2048]{1,0:T(8,128)(2,1)S(1)}, u32[]{:S(2)}, u32[]{:S(2)}) collective-permute-start(bf16[64,2048]{1,0:T(8,128)(2,1)S(1)} %get-tuple-element.107), channel_id=1, source_target_pairs={{4,28},{5,29},{6,30},{7,31},{8,16},{9,17},{10,18},{11,19},{20,12},... | collective-permute-start | bytes 786440 | tf_op jit(solution)/shard_map/ppermute | solution.py:62
  92.7 23.8 %collective-permute-start.24 = (bf16[64,2048]{1,0:T(8,128)(2,1)S(1)}, bf16[64,2048]{1,0:T(8,128)(2,1)S(1)}, u32[]{:S(2)}, u32[]{:S(2)}) collective-permute-start(bf16[64,2048]{1,0:T(8,128)(2,1)S(1)} %get-tuple-element.120), channel_id=1, source_target_pairs={{0,16},{1,17},{2,18},{3,19},{4,20},{5,21},{6,22},{7,23},{8,24},{9,... | collective-permute-start | bytes 786440 | tf_op jit(solution)/shard_map/ppermute | solution.py:52
  107.1 6.5 %collective-permute-start.17 = (bf16[320,128]{1,0:T(8,128)(2,1)S(1)}, bf16[320,128]{1,0:T(8,128)(2,1)S(1)}, u32[]{:S(2)}, u32[]{:S(2)}) collective-permute-start(bf16[320,128]{1,0:T(8,128)(2,1)S(1)} %get-tuple-element.113), channel_id=1, source_target_pairs={{0,2},{1,3},{2,0},{3,1},{4,6},{5,7},{6,4},{7,5},{8,10},{9,11},{10,... | collective-permute-start | bytes 245768 | tf_op jit(solution)/shard_map/ppermute | solution.py:52
  112.1 4.4 %collective-permute-start.15 = (bf16[320,128]{1,0:T(8,128)(2,1)S(1)}, bf16[320,128]{1,0:T(8,128)(2,1)S(1)}, u32[]{:S(2)}, u32[]{:S(2)}) collective-permute-start(bf16[320,128]{1,0:T(8,128)(2,1)S(1)} %get-tuple-element.111), channel_id=1, source_target_pairs={{0,2},{1,3},{2,0},{3,1},{4,6},{5,7},{6,4},{7,5},{8,10},{9,11},{10,... | collective-permute-start | bytes 245768 | tf_op jit(solution)/shard_map/ppermute | solution.py:52
  113.6 2.9 %collective-permute-start.16 = (bf16[320,128]{1,0:T(8,128)(2,1)S(1)}, bf16[320,128]{1,0:T(8,128)(2,1)S(1)}, u32[]{:S(2)}, u32[]{:S(2)}) collective-permute-start(bf16[320,128]{1,0:T(8,128)(2,1)S(1)} %get-tuple-element.112), channel_id=1, source_target_pairs={{0,1},{1,0},{2,3},{3,2},{4,5},{5,4},{6,7},{7,6},{8,9},{9,8},{10,11... | collective-permute-start | bytes 245768 | tf_op jit(solution)/shard_map/ppermute | solution.py:52
  113.6 2.9 %collective-permute-start.18 = (bf16[320,128]{1,0:T(8,128)(2,1)S(1)}, bf16[320,128]{1,0:T(8,128)(2,1)S(1)}, u32[]{:S(2)}, u32[]{:S(2)}) collective-permute-start(bf16[320,128]{1,0:T(8,128)(2,1)S(1)} %collective-permute-done.17), channel_id=1, source_target_pairs={{0,1},{1,0},{2,3},{3,2},{4,5},{5,4},{6,7},{7,6},{8,9},{9,8},{10,11... | collective-permute-start | bytes 245768 | tf_op jit(solution)/shard_map/ppermute | solution.py:52

commit v11 on v8

--- a/solution.py
+++ b/solution.py
@@ -465,7 +465,7 @@
         for dc in range(2)
     ]
     tables = tables[0::2] + [plan.shift(rows, dc=1) for rows in tables[1::2]]
-    tables, far_pieces, pieces = lax.optimization_barrier((tables, far_pieces, pieces))
+    tables, far_pieces[:1] = lax.optimization_barrier((tables, far_pieces[:1]))
     grad_head, grad_gate = final_work(plan, target, tables)
     grad_proj = layout_work(plan, info, pieces + far_pieces)
     return (

time: 114 us -> 112 us (0.982)
  waiting for transfers between devices: 49.8 us -> 46.4 us
    ppermute x11, waiting for transfers between devices: 36.4 us -> 25.1 us  [along(): return lax.ppermute(value, AXES, out)]
    ppermute x13, waiting for transfers between devices: 13.4 us -> 21.4 us  [shift(): return lax.ppermute(value, AXES, self.pairs(**by))]
  transfers between devices with their start and end apart: 24 -> 24, of which waited for: 10 -> 10; matrix products, arithmetic and copies ran while one was open for 2% -> 3% of each run, Pallas kernels for 22% -> 25%
where the time goes in v11:
time: 112 us; the launch traced here: 111 us
  waiting for transfers between devices  46.4 us (41%)
  Pallas kernels  29.4 us (26%)
  starting transfers between devices  27.8 us (25%)
  local copies, waits for them, and re-layouts  5.15 us (5%)
  other arithmetic  1.36 us (1%)
    ppermute x11, waiting for transfers between devices, along(): return lax.ppermute(value, AXES, out)  25.1 us
    pallas_call x4, Pallas kernels, slot_work(): pl.pallas_call(functools.partial(slot_kernel, plan, index, [where for _,...  21.8 us
    ppermute x13, waiting for transfers between devices, shift(): return lax.ppermute(value, AXES, self.pairs(**by))  21.4 us
    ppermute x11, starting transfers between devices, along(): return lax.ppermute(value, AXES, out)  18 us
    ppermute x13, starting transfers between devices, shift(): return lax.ppermute(value, AXES, self.pairs(**by))  9.79 us
    unnamed x15, local copies, waits for them, and re-layouts  4.01 us
    pallas_call x1, Pallas kernels, target_work(): pl.pallas_call(functools.partial(target_kernel, plan), out_shape=jax.Shap...  2.36 us
  transfers between devices with their start and end apart: 24, of which 10 were waited for; matrix products, arithmetic and copies ran while one was open for 3% of the time, Pallas kernels for 25%

profile of v11, /device:TPU:0, one launch (start us, length us, event | category | flops | bytes accessed | tf_op | source)
XLA Modules:
  0.0 111.1 jit_solution(785695829885031981)
XLA Ops:
  0.6 0.0 copy-start
  0.7 1.2 %copy-done = bf16[1,128,4096]{2,1,0:T(8,128)(2,1)S(1)} copy-done((bf16[1,128,4096]{2,1,0:T(8,128)(2,1)S(1)}, bf16[1,128,4096]{2,1,0:T(8,128)(2,1)}, u32[]{:S(2)}) %copy-start) | copy-done | bytes 1048600
  1.9 0.8 dynamic-slice_bitcast_fusion.refs_8_
  2.7 3.0 %collective-permute-start = (bf16[128,2048]{1,0:T(8,128)(2,1)}, bf16[128,2048]{1,0:T(8,128)(2,1)}, u32[]{:S(2)}, u32[]{:S(2)}) collective-permute-start(bf16[128,2048]{1,0:T(8,128)(2,1)} %dynamic-slice_bitcast_fusion.refs_8_), channel_id=1, source_target_pairs={{0,4},{1,5},{2,6},{3,7},{4,0},{5,1},{6,2},{7,3},{8,12},{9,13},{10,... | collective-permute-start | bytes 1572872 | tf_op jit(solution)/shard_map/ppermute | solution.py:62
  5.7 1.4 %collective-permute-start.1 = (bf16[128,2048]{1,0:T(8,128)(2,1)}, bf16[128,2048]{1,0:T(8,128)(2,1)}, u32[]{:S(2)}, u32[]{:S(2)}) collective-permute-start(bf16[128,2048]{1,0:T(8,128)(2,1)} %dynamic-slice_bitcast_fusion.refs_8_), channel_id=1, source_target_pairs={{4,8},{5,9},{6,10},{7,11},{8,4},{9,5},{10,6},{11,7},{20,24},{21,25... | collective-permute-start | bytes 1572872 | tf_op jit(solution)/shard_map/ppermute | solution.py:62
  7.3 0.0 copy-start.5
  7.3 0.1 constant_dynamic-slice_fusion
  7.4 0.5 copy-done.5
  7.9 1.0 fusion.1
  9.0 1.5 %collective-permute-start.5 = (bf16[128,3200]{1,0:T(8,128)(2,1)S(1)}, bf16[128,3200]{1,0:T(8,128)(2,1)S(1)}, u32[]{:S(2)}, u32[]{:S(2)}) collective-permute-start(bf16[128,3200]{1,0:T(8,128)(2,1)S(1)} %get-tuple-element.60.refs_0_), channel_id=1, source_target_pairs={{0,2},{1,3},{2,0},{3,1},{4,6},{5,7},{6,4},{7,5},{8,10},{9,11},{10,... | collective-permute-start | bytes 2457608 | tf_op jit(solution)/shard_map/ppermute | solution.py:52
  10.5 1.5 %collective-permute-start.7 = (bf16[128,3200]{1,0:T(8,128)(2,1)}, bf16[128,3200]{1,0:T(8,128)(2,1)S(1)}, u32[]{:S(2)}, u32[]{:S(2)}) collective-permute-start(bf16[128,3200]{1,0:T(8,128)(2,1)} %get-tuple-element.113), channel_id=1, source_target_pairs={{0,16},{1,17},{2,18},{3,19},{4,20},{5,21},{6,22},{7,23},{8,24},{9,... | collective-permute-start | bytes 2457608 | tf_op jit(solution)/shard_map/ppermute | solution.py:52
  12.0 0.5 collective-permute-start.9
  12.5 0.7 copy.10.route_ref
  13.2 0.1 stack.63.info
  13.3 0.0 copy-start.1
  13.3 0.8 copy-done.1
  14.1 2.4 %shard_map.76.target_ref = s32[1024,128]{1,0:T(8,128)S(1)} custom-call(s32[15]{0:T(128)S(1)} %stack.63.info, s32[128,8]{1,0:T(8,128)S(1)} %copy-done.1), custom_call_target="tpu_custom_call" | custom-call | tf_op jit(solution)/shard_map/pallas_call | solution.py:326
  16.5 1.5 %collective-permute-done.refs_8_ = bf16[128,2048]{1,0:T(8,128)(2,1)} collective-permute-done((bf16[128,2048]{1,0:T(8,128)(2,1)}, bf16[128,2048]{1,0:T(8,128)(2,1)}, u32[]{:S(2)}, u32[]{:S(2)}) %collective-permute-start) | collective-permute-done | bytes 524320 | tf_op jit(solution)/shard_map/ppermute | solution.py:62
  18.0 0.0 collective-permute-done.1.refs_8_
  18.0 0.7 collective-permute-start.2
  18.7 1.3 %collective-permute-start.3 = (bf16[128,2048]{1,0:T(8,128)(2,1)}, bf16[128,2048]{1,0:T(8,128)(2,1)S(1)}, u32[]{:S(2)}, u32[]{:S(2)}) collective-permute-start(bf16[128,2048]{1,0:T(8,128)(2,1)} %collective-permute-done.1.refs_8_), channel_id=1, source_target_pairs={{4,0},{5,1},{6,2},{7,3},{8,12},{9,13},{10,14},{11,15},{20,16},{21,... | collective-permute-start | bytes 1572872 | tf_op jit(solution)/shard_map/ppermute | solution.py:62
  20.0 18.3 %collective-permute-done.3.refs_9_ = bf16[128,2048]{1,0:T(8,128)(2,1)S(1)} collective-permute-done((bf16[128,2048]{1,0:T(8,128)(2,1)}, bf16[128,2048]{1,0:T(8,128)(2,1)S(1)}, u32[]{:S(2)}, u32[]{:S(2)}) %collective-permute-start.3) | collective-permute-done | bytes 524320 | tf_op jit(solution)/shard_map/ppermute | solution.py:62
  38.3 0.5 collective-permute-start.6
  38.8 0.1 collective-permute-start.8
  38.9 8.8 %collective-permute-done.9.refs_6_ = bf16[128,3200]{1,0:T(8,128)(2,1)} collective-permute-done((bf16[128,3200]{1,0:T(8,128)(2,1)}, bf16[128,3200]{1,0:T(8,128)(2,1)}, u32[]{:S(2)}, u32[]{:S(2)}) %collective-permute-start.9) | collective-permute-done | bytes 819232 | tf_op jit(solution)/shard_map/ppermute | solution.py:52
  47.7 0.0 collective-permute-start.10
  47.7 1.3 %collective-permute-start.11 = (bf16[128,2048]{1,0:T(8,128)(2,1)S(1)}, bf16[128,2048]{1,0:T(8,128)(2,1)S(1)}, u32[]{:S(2)}, u32[]{:S(2)}) collective-permute-start(bf16[128,2048]{1,0:T(8,128)(2,1)S(1)} %collective-permute-done.2.refs_8_), channel_id=1, source_target_pairs={{4,0},{5,1},{6,2},{7,3},{8,12},{9,13},{10,14},{11,15},{20,16},{21,... | collective-permute-start | bytes 1572872 | tf_op jit(solution)/shard_map/ppermute | solution.py:62
  49.0 0.0 collective-permute-done.8.refs_5_
  49.0 1.2 %collective-permute-done.10.refs_7_ = bf16[128,3200]{1,0:T(8,128)(2,1)S(1)} collective-permute-done((bf16[128,3200]{1,0:T(8,128)(2,1)}, bf16[128,3200]{1,0:T(8,128)(2,1)S(1)}, u32[]{:S(2)}, u32[]{:S(2)}) %collective-permute-start.10) | collective-permute-done | bytes 819232 | tf_op jit(solution)/shard_map/ppermute | solution.py:52
  50.3 5.5 %shard_map.77 = (bf16[128,2048]{1,0:T(8,128)(2,1)S(1)}, bf16[8,80,128]{2,1,0:T(8,128)(2,1)S(1)}) custom-call(s32[15]{0:T(128)S(1)} %stack.63.info, bf16[128,3200]{1,0:T(8,128)(2,1)S(1)} %get-tuple-element.60.refs_0_, bf16[128,3200]{1,0:T(8,128)(2,1)S(1)} %collective-permute-done.4.refs_1_, bf16[128,3200]{1,0:T(8,128)(2,1)S(1)} %collective-permute-done.5.refs_2_, ...), custom_call_target="tpu_custom_call" | custom-call | tf_op jit(solution)/shard_map/pallas_call | solution.py:201
  55.8 5.3 %collective-permute-start.12 = (bf16[128,2048]{1,0:T(8,128)(2,1)S(1)}, bf16[128,2048]{1,0:T(8,128)(2,1)S(1)}, u32[]{:S(2)}, u32[]{:S(2)}) collective-permute-start(bf16[128,2048]{1,0:T(8,128)(2,1)S(1)} %get-tuple-element.77), channel_id=1, source_target_pairs={{0,4},{1,5},{2,6},{3,7},{12,8},{13,9},{14,10},{15,11},{16,20},{17,... | collective-permute-start | bytes 1572872 | tf_op jit(solution)/shard_map/ppermute | solution.py:62
  61.1 3.9 %collective-permute-done.11.refs_9_ = bf16[128,2048]{1,0:T(8,128)(2,1)S(1)} collective-permute-done((bf16[128,2048]{1,0:T(8,128)(2,1)S(1)}, bf16[128,2048]{1,0:T(8,128)(2,1)S(1)}, u32[]{:S(2)}, u32[]{:S(2)}) %collective-permute-start.11) | collective-permute-done | bytes 524320 | tf_op jit(solution)/shard_map/ppermute | solution.py:62
  65.0 5.3 %shard_map.78 = (bf16[128,2048]{1,0:T(8,128)(2,1)S(1)}, bf16[8,80,128]{2,1,0:T(8,128)(2,1)S(1)}) custom-call(s32[15]{0:T(128)S(1)} %stack.63.info, bf16[128,3200]{1,0:T(8,128)(2,1)S(1)} %get-tuple-element.60.refs_0_, bf16[128,3200]{1,0:T(8,128)(2,1)S(1)} %collective-permute-done.4.refs_1_, bf16[128,3200]{1,0:T(8,128)(2,1)S(1)} %collective-permute-done.5.refs_2_, ...), custom_call_target="tpu_custom_call" | custom-call | tf_op jit(solution)/shard_map/pallas_call | solution.py:201
  70.3 1.7 %collective-permute-start.14 = (bf16[128,2048]{1,0:T(8,128)(2,1)S(1)}, bf16[128,2048]{1,0:T(8,128)(2,1)S(1)}, u32[]{:S(2)}, u32[]{:S(2)}) collective-permute-start(bf16[128,2048]{1,0:T(8,128)(2,1)S(1)} %get-tuple-element.81.refs_0_), channel_id=1, source_target_pairs={{0,4},{1,5},{2,6},{3,7},{12,8},{13,9},{14,10},{15,11},{16,20},{17,... | collective-permute-start | bytes 1572872 | tf_op jit(solution)/shard_map/ppermute | solution.py:62
  72.0 5.5 %shard_map.79 = (bf16[128,2048]{1,0:T(8,128)(2,1)S(1)}, bf16[8,80,128]{2,1,0:T(8,128)(2,1)S(1)}) custom-call(s32[15]{0:T(128)S(1)} %stack.63.info, bf16[128,3200]{1,0:T(8,128)(2,1)S(1)} %get-tuple-element.60.refs_0_, bf16[128,3200]{1,0:T(8,128)(2,1)S(1)} %collective-permute-done.4.refs_1_, bf16[128,3200]{1,0:T(8,128)(2,1)S(1)} %collective-permute-done.5.refs_2_, ...), custom_call_target="tpu_custom_call" | custom-call | tf_op jit(solution)/shard_map/pallas_call | solution.py:201
  77.5 0.1 collective-permute-start.20
  77.5 0.0 collective-permute-done.12
  77.5 0.1 add.84
  77.7 0.7 collective-permute-start.21
  78.4 5.5 %shard_map.80 = (f32[128,2048]{1,0:T(8,128)S(1)}, bf16[1280,128]{1,0:T(8,128)(2,1)S(1)}, bf16[1280,128]{1,0:T(8,128)(2,1)S(1)}) custom-call(s32[15]{0:T(128)S(1)} %stack.63.info, bf16[128,3200]{1,0:T(8,128)(2,1)S(1)} %get-tuple-element.60.refs_0_, bf16[128,3200]{1,0:T(8,128)(2,1)S(1)} %collective-permute-done.4.refs_1_, ...), custom_call_target="tpu_custom_call" | custom-call | tf_op jit(solution)/shard_map/pallas_call | solution.py:201
  83.9 1.5 %collective-permute-start.13 = (bf16[1280,128]{1,0:T(8,128)(2,1)S(1)}, bf16[1280,128]{1,0:T(8,128)(2,1)S(1)}, u32[]{:S(2)}, u32[]{:S(2)}) collective-permute-start(bf16[1280,128]{1,0:T(8,128)(2,1)S(1)} %get-tuple-element.80), channel_id=1, source_target_pairs={{0,16},{1,17},{2,18},{3,19},{4,20},{5,21},{6,22},{7,23},{8,24},{9,... | collective-permute-start | bytes 983048 | tf_op jit(solution)/shard_map/ppermute | solution.py:52
  85.4 0.0 collective-permute-done.14.refs_1_
  85.4 0.7 shard_map.81
  86.1 1.3 %collective-permute-start.19 = (bf16[64,2048]{1,0:T(8,128)(2,1)S(1)}, bf16[64,2048]{1,0:T(8,128)(2,1)S(1)}, u32[]{:S(2)}, u32[]{:S(2)}) collective-permute-start(bf16[64,2048]{1,0:T(8,128)(2,1)S(1)} %get-tuple-element.85), channel_id=1, source_target_pairs={{4,12},{5,13},{6,14},{7,15},{8,0},{9,1},{10,2},{11,3},{20,28},{21,... | collective-permute-start | bytes 786440 | tf_op jit(solution)/shard_map/ppermute | solution.py:62
  87.4 5.9 %collective-permute-done.13.refs_1_ = bf16[1280,128]{1,0:T(8,128)(2,1)S(1)} collective-permute-done((bf16[1280,128]{1,0:T(8,128)(2,1)S(1)}, bf16[1280,128]{1,0:T(8,128)(2,1)S(1)}, u32[]{:S(2)}, u32[]{:S(2)}) %collective-permute-start.13) | collective-permute-done | bytes 327712 | tf_op jit(solution)/shard_map/ppermute | solution.py:52
  93.3 0.1 shard_map.82
  93.4 1.6 %collective-permute-start.17 = (bf16[320,128]{1,0:T(8,128)(2,1)S(1)}, bf16[320,128]{1,0:T(8,128)(2,1)S(1)}, u32[]{:S(2)}, u32[]{:S(2)}) collective-permute-start(bf16[320,128]{1,0:T(8,128)(2,1)S(1)} %get-tuple-element.92), channel_id=1, source_target_pairs={{0,2},{1,3},{2,0},{3,1},{4,6},{5,7},{6,4},{7,5},{8,10},{9,11},{10,... | collective-permute-start | bytes 245768 | tf_op jit(solution)/shard_map/ppermute | solution.py:52
  95.0 1.3 %collective-permute-start.23 = (bf16[64,2048]{1,0:T(8,128)(2,1)S(1)}, bf16[64,2048]{1,0:T(8,128)(2,1)S(1)}, u32[]{:S(2)}, u32[]{:S(2)}) collective-permute-start(bf16[64,2048]{1,0:T(8,128)(2,1)S(1)} %get-tuple-element.86), channel_id=1, source_target_pairs={{4,28},{5,29},{6,30},{7,31},{8,16},{9,17},{10,18},{11,19},{20,12},... | collective-permute-start | bytes 786440 | tf_op jit(solution)/shard_map/ppermute | solution.py:62
  96.2 0.0 collective-permute-done.21.refs_2_
  96.3 0.7 shard_map.84
  97.0 1.6 %collective-permute-start.22 = (bf16[64,2048]{1,0:T(8,128)(2,1)S(1)}, bf16[64,2048]{1,0:T(8,128)(2,1)S(1)}, u32[]{:S(2)}, u32[]{:S(2)}) collective-permute-start(bf16[64,2048]{1,0:T(8,128)(2,1)S(1)} %get-tuple-element.103), channel_id=1, source_target_pairs={{0,16},{1,17},{2,18},{3,19},{4,20},{5,21},{6,22},{7,23},{8,24},{9,... | collective-permute-start | bytes 786440 | tf_op jit(solution)/shard_map/ppermute | solution.py:52
  98.5 0.5 collective-permute-start.15
  99.0 0.9 collective-permute-done.19.refs_2_
  99.9 0.0 collective-permute-start.16
  99.9 0.0 collective-permute-done.17
  99.9 0.5 collective-permute-start.18
  100.4 2.5 %collective-permute-done.15.refs_1_ = bf16[320,128]{1,0:T(8,128)(2,1)S(1)} collective-permute-done((bf16[320,128]{1,0:T(8,128)(2,1)S(1)}, bf16[320,128]{1,0:T(8,128)(2,1)S(1)}, u32[]{:S(2)}, u32[]{:S(2)}) %collective-permute-start.15) | collective-permute-done | bytes 81952 | tf_op jit(solution)/shard_map/ppermute | solution.py:52
  103.0 2.2 %shard_map.83 = (bf16[1024,128]{1,0:T(8,128)(2,1)}, f32[1024,1]{1,0:T(8,128)S(1)}) custom-call(s32[1024,128]{1,0:T(8,128)S(1)} %shard_map.76.target_ref, bf16[320,128]{1,0:T(8,128)(2,1)S(1)} %get-tuple-element.93.refs_0_, bf16[320,128]{1,0:T(8,128)(2,1)S(1)} %collective-permute-done.15.refs_1_, bf16[320,128]{1,0:T(8,128)(2,1)S(1)} %collective-permute-done.16.refs_2_, ...), custom_call_target="tpu_custom_call" | custom-call | flops 1 | bytes 1 | tf_op jit(solution)/shard_map/pallas_call | solution.py:356
  105.2 0.2 convert_reduce_fusion
  105.4 0.1 convert_element_type.15
  105.5 0.7 copy.11
  106.1 0.5 collective-permute-done.23.refs_3_
  106.6 2.8 %collective-permute-done.22.refs_1_ = bf16[64,2048]{1,0:T(8,128)(2,1)S(1)} collective-permute-done((bf16[64,2048]{1,0:T(8,128)(2,1)S(1)}, bf16[64,2048]{1,0:T(8,128)(2,1)S(1)}, u32[]{:S(2)}, u32[]{:S(2)}) %collective-permute-start.22) | collective-permute-done | bytes 262176 | tf_op jit(solution)/shard_map/ppermute | solution.py:52
  109.4 1.6 %shard_map.85 = f32[64,4096]{1,0:T(8,128)} custom-call(s32[15]{0:T(128)S(1)} %stack.63.info, f32[64,2048]{1,0:T(8,128)S(1)} %get-tuple-element.102.refs_0_, bf16[64,2048]{1,0:T(8,128)(2,1)S(1)} %collective-permute-done.22.refs_1_, bf16[64,2048]{1,0:T(8,128)(2,1)S(1)} %collective-permute-done.19.refs_2_, bf16[64,2048]{1,0:T(8,128)(2,1)S(1)} %collective-permute-done.23.refs_3_), custom_call_target="tpu_custom_call" | custom-call | tf_op jit(solution)/shard_map/pallas_call | solution.py:256
  (18 shorter events, 0.1 us)
Async XLA Ops:
  0.6 1.2 %copy-start = (bf16[1,128,4096]{2,1,0:T(8,128)(2,1)S(1)}, bf16[1,128,4096]{2,1,0:T(8,128)(2,1)}, u32[]{:S(2)}) copy-start(bf16[1,128,4096]{2,1,0:T(8,128)(2,1)} %param.9) | copy-start | bytes 3145732
  0.6 6.5 %copy-start.3 = (bf16[128,8,128]{2,1,0:T(8,128)(2,1)S(1)}, bf16[128,8,128]{2,1,0:T(8,128)(2,1)}, u32[]{:S(2)}) copy-start(bf16[128,8,128]{2,1,0:T(8,128)(2,1)} %param.5) | copy-start | bytes 786436
  0.7 6.6 %copy-start.4 = (s32[128,8]{0,1:T(8,128)S(1)}, s32[128,8]{0,1:T(8,128)}, u32[]{:S(2)}) copy-start(s32[128,8]{0,1:T(8,128)} %param.8) | copy-start | bytes 12292
  0.7 6.6 %copy-start.2 = (bf16[128,4096]{1,0:T(8,128)(2,1)S(1)}, bf16[128,4096]{1,0:T(8,128)(2,1)}, u32[]{:S(2)}) copy-start(bf16[128,4096]{1,0:T(8,128)(2,1)} %param.6) | copy-start | bytes 3145732
  2.7 15.3 %collective-permute-start = (bf16[128,2048]{1,0:T(8,128)(2,1)}, bf16[128,2048]{1,0:T(8,128)(2,1)}, u32[]{:S(2)}, u32[]{:S(2)}) collective-permute-start(bf16[128,2048]{1,0:T(8,128)(2,1)} %dynamic-slice_bitcast_fusion.refs_8_), channel_id=1, source_target_pairs={{0,4},{1,5},{2,6},{3,7},{4,0},{5,1},{6,2},{7,3},{8,12},{9,13},{10,... | collective-permute-start | bytes 1572872 | tf_op jit(solution)/shard_map/ppermute | solution.py:62
  5.7 12.2 %collective-permute-start.1 = (bf16[128,2048]{1,0:T(8,128)(2,1)}, bf16[128,2048]{1,0:T(8,128)(2,1)}, u32[]{:S(2)}, u32[]{:S(2)}) collective-permute-start(bf16[128,2048]{1,0:T(8,128)(2,1)} %dynamic-slice_bitcast_fusion.refs_8_), channel_id=1, source_target_pairs={{4,8},{5,9},{6,10},{7,11},{8,4},{9,5},{10,6},{11,7},{20,24},{21,25... | collective-permute-start | bytes 1572872 | tf_op jit(solution)/shard_map/ppermute | solution.py:62
  7.3 0.7 copy-start.5
  9.0 29.3 %collective-permute-start.5 = (bf16[128,3200]{1,0:T(8,128)(2,1)S(1)}, bf16[128,3200]{1,0:T(8,128)(2,1)S(1)}, u32[]{:S(2)}, u32[]{:S(2)}) collective-permute-start(bf16[128,3200]{1,0:T(8,128)(2,1)S(1)} %get-tuple-element.60.refs_0_), channel_id=1, source_target_pairs={{0,2},{1,3},{2,0},{3,1},{4,6},{5,7},{6,4},{7,5},{8,10},{9,11},{10,... | collective-permute-start | bytes 2457608 | tf_op jit(solution)/shard_map/ppermute | solution.py:52
  10.5 28.3 %collective-permute-start.7 = (bf16[128,3200]{1,0:T(8,128)(2,1)}, bf16[128,3200]{1,0:T(8,128)(2,1)S(1)}, u32[]{:S(2)}, u32[]{:S(2)}) collective-permute-start(bf16[128,3200]{1,0:T(8,128)(2,1)} %get-tuple-element.113), channel_id=1, source_target_pairs={{0,16},{1,17},{2,18},{3,19},{4,20},{5,21},{6,22},{7,23},{8,24},{9,... | collective-permute-start | bytes 2457608 | tf_op jit(solution)/shard_map/ppermute | solution.py:52
  12.0 35.7 %collective-permute-start.9 = (bf16[128,3200]{1,0:T(8,128)(2,1)}, bf16[128,3200]{1,0:T(8,128)(2,1)}, u32[]{:S(2)}, u32[]{:S(2)}) collective-permute-start(bf16[128,3200]{1,0:T(8,128)(2,1)} %get-tuple-element.113), channel_id=1, source_target_pairs={{0,18},{1,19},{2,16},{3,17},{4,22},{5,23},{6,20},{7,21},{8,26},{9,... | collective-permute-start | bytes 2457608 | tf_op jit(solution)/shard_map/ppermute | solution.py:52
  13.3 0.8 copy-start.1
  18.0 2.0 %collective-permute-start.2 = (bf16[128,2048]{1,0:T(8,128)(2,1)}, bf16[128,2048]{1,0:T(8,128)(2,1)S(1)}, u32[]{:S(2)}, u32[]{:S(2)}) collective-permute-start(bf16[128,2048]{1,0:T(8,128)(2,1)} %collective-permute-done.refs_8_), channel_id=1, source_target_pairs={{4,8},{5,9},{6,10},{7,11},{8,4},{9,5},{10,6},{11,7},{20,24},{21,25... | collective-permute-start | bytes 1572872 | tf_op jit(solution)/shard_map/ppermute | solution.py:62
  18.7 19.6 %collective-permute-start.3 = (bf16[128,2048]{1,0:T(8,128)(2,1)}, bf16[128,2048]{1,0:T(8,128)(2,1)S(1)}, u32[]{:S(2)}, u32[]{:S(2)}) collective-permute-start(bf16[128,2048]{1,0:T(8,128)(2,1)} %collective-permute-done.1.refs_8_), channel_id=1, source_target_pairs={{4,0},{5,1},{6,2},{7,3},{8,12},{9,13},{10,14},{11,15},{20,16},{21,... | collective-permute-start | bytes 1572872 | tf_op jit(solution)/shard_map/ppermute | solution.py:62
  38.3 10.7 %collective-permute-start.4 = (bf16[128,3200]{1,0:T(8,128)(2,1)S(1)}, bf16[128,3200]{1,0:T(8,128)(2,1)S(1)}, u32[]{:S(2)}, u32[]{:S(2)}) collective-permute-start(bf16[128,3200]{1,0:T(8,128)(2,1)S(1)} %get-tuple-element.60.refs_0_), channel_id=1, source_target_pairs={{0,1},{1,0},{2,3},{3,2},{4,5},{5,4},{6,7},{7,6},{8,9},{9,8},{10,11... | collective-permute-start | bytes 2457608 | tf_op jit(solution)/shard_map/ppermute | solution.py:52
  38.3 10.7 %collective-permute-start.6 = (bf16[128,3200]{1,0:T(8,128)(2,1)S(1)}, bf16[128,3200]{1,0:T(8,128)(2,1)S(1)}, u32[]{:S(2)}, u32[]{:S(2)}) collective-permute-start(bf16[128,3200]{1,0:T(8,128)(2,1)S(1)} %collective-permute-done.5.refs_2_), channel_id=1, source_target_pairs={{0,1},{1,0},{2,3},{3,2},{4,5},{5,4},{6,7},{7,6},{8,9},{9,8},{10,11... | collective-permute-start | bytes 2457608 | tf_op jit(solution)/shard_map/ppermute | solution.py:52
  38.8 10.2 %collective-permute-start.8 = (bf16[128,3200]{1,0:T(8,128)(2,1)S(1)}, bf16[128,3200]{1,0:T(8,128)(2,1)S(1)}, u32[]{:S(2)}, u32[]{:S(2)}) collective-permute-start(bf16[128,3200]{1,0:T(8,128)(2,1)S(1)} %collective-permute-done.7.refs_4_), channel_id=1, source_target_pairs={{0,1},{1,0},{2,3},{3,2},{4,5},{5,4},{6,7},{7,6},{8,9},{9,8},{10,11... | collective-permute-start | bytes 2457608 | tf_op jit(solution)/shard_map/ppermute | solution.py:52
  47.7 2.5 %collective-permute-start.10 = (bf16[128,3200]{1,0:T(8,128)(2,1)}, bf16[128,3200]{1,0:T(8,128)(2,1)S(1)}, u32[]{:S(2)}, u32[]{:S(2)}) collective-permute-start(bf16[128,3200]{1,0:T(8,128)(2,1)} %collective-permute-done.9.refs_6_), channel_id=1, source_target_pairs={{0,1},{1,0},{2,3},{3,2},{4,5},{5,4},{6,7},{7,6},{8,9},{9,8},{10,11... | collective-permute-start | bytes 2457608 | tf_op jit(solution)/shard_map/ppermute | solution.py:52
  47.7 17.2 %collective-permute-start.11 = (bf16[128,2048]{1,0:T(8,128)(2,1)S(1)}, bf16[128,2048]{1,0:T(8,128)(2,1)S(1)}, u32[]{:S(2)}, u32[]{:S(2)}) collective-permute-start(bf16[128,2048]{1,0:T(8,128)(2,1)S(1)} %collective-permute-done.2.refs_8_), channel_id=1, source_target_pairs={{4,0},{5,1},{6,2},{7,3},{8,12},{9,13},{10,14},{11,15},{20,16},{21,... | collective-permute-start | bytes 1572872 | tf_op jit(solution)/shard_map/ppermute | solution.py:62
  55.8 21.8 %collective-permute-start.12 = (bf16[128,2048]{1,0:T(8,128)(2,1)S(1)}, bf16[128,2048]{1,0:T(8,128)(2,1)S(1)}, u32[]{:S(2)}, u32[]{:S(2)}) collective-permute-start(bf16[128,2048]{1,0:T(8,128)(2,1)S(1)} %get-tuple-element.77), channel_id=1, source_target_pairs={{0,4},{1,5},{2,6},{3,7},{12,8},{13,9},{14,10},{15,11},{16,20},{17,... | collective-permute-start | bytes 1572872 | tf_op jit(solution)/shard_map/ppermute | solution.py:62
  70.3 15.1 %collective-permute-start.14 = (bf16[128,2048]{1,0:T(8,128)(2,1)S(1)}, bf16[128,2048]{1,0:T(8,128)(2,1)S(1)}, u32[]{:S(2)}, u32[]{:S(2)}) collective-permute-start(bf16[128,2048]{1,0:T(8,128)(2,1)S(1)} %get-tuple-element.81.refs_0_), channel_id=1, source_target_pairs={{0,4},{1,5},{2,6},{3,7},{12,8},{13,9},{14,10},{15,11},{16,20},{17,... | collective-permute-start | bytes 1572872 | tf_op jit(solution)/shard_map/ppermute | solution.py:62
  77.5 18.8 %collective-permute-start.20 = (bf16[128,2048]{1,0:T(8,128)(2,1)S(1)}, bf16[128,2048]{1,0:T(8,128)(2,1)S(1)}, u32[]{:S(2)}, u32[]{:S(2)}) collective-permute-start(bf16[128,2048]{1,0:T(8,128)(2,1)S(1)} %get-tuple-element.101), channel_id=1, source_target_pairs={{0,4},{1,5},{2,6},{3,7},{4,0},{5,1},{6,2},{7,3},{8,12},{9,13},{10,... | collective-permute-start | bytes 1572872 | tf_op jit(solution)/shard_map/ppermute | solution.py:62
  77.7 18.6 %collective-permute-start.21 = (bf16[128,2048]{1,0:T(8,128)(2,1)S(1)}, bf16[128,2048]{1,0:T(8,128)(2,1)S(1)}, u32[]{:S(2)}, u32[]{:S(2)}) collective-permute-start(bf16[128,2048]{1,0:T(8,128)(2,1)S(1)} %add.84), channel_id=1, source_target_pairs={{4,8},{5,9},{6,10},{7,11},{8,4},{9,5},{10,6},{11,7},{20,24},{21,25... | collective-permute-start | bytes 1572872 | tf_op jit(solution)/shard_map/ppermute | solution.py:62
  83.9 9.4 %collective-permute-start.13 = (bf16[1280,128]{1,0:T(8,128)(2,1)S(1)}, bf16[1280,128]{1,0:T(8,128)(2,1)S(1)}, u32[]{:S(2)}, u32[]{:S(2)}) collective-permute-start(bf16[1280,128]{1,0:T(8,128)(2,1)S(1)} %get-tuple-element.80), channel_id=1, source_target_pairs={{0,16},{1,17},{2,18},{3,19},{4,20},{5,21},{6,22},{7,23},{8,24},{9,... | collective-permute-start | bytes 983048 | tf_op jit(solution)/shard_map/ppermute | solution.py:52
  86.1 13.9 %collective-permute-start.19 = (bf16[64,2048]{1,0:T(8,128)(2,1)S(1)}, bf16[64,2048]{1,0:T(8,128)(2,1)S(1)}, u32[]{:S(2)}, u32[]{:S(2)}) collective-permute-start(bf16[64,2048]{1,0:T(8,128)(2,1)S(1)} %get-tuple-element.85), channel_id=1, source_target_pairs={{4,12},{5,13},{6,14},{7,15},{8,0},{9,1},{10,2},{11,3},{20,28},{21,... | collective-permute-start | bytes 786440 | tf_op jit(solution)/shard_map/ppermute | solution.py:62
  93.4 6.6 %collective-permute-start.17 = (bf16[320,128]{1,0:T(8,128)(2,1)S(1)}, bf16[320,128]{1,0:T(8,128)(2,1)S(1)}, u32[]{:S(2)}, u32[]{:S(2)}) collective-permute-start(bf16[320,128]{1,0:T(8,128)(2,1)S(1)} %get-tuple-element.92), channel_id=1, source_target_pairs={{0,2},{1,3},{2,0},{3,1},{4,6},{5,7},{6,4},{7,5},{8,10},{9,11},{10,... | collective-permute-start | bytes 245768 | tf_op jit(solution)/shard_map/ppermute | solution.py:52
  95.0 11.7 %collective-permute-start.23 = (bf16[64,2048]{1,0:T(8,128)(2,1)S(1)}, bf16[64,2048]{1,0:T(8,128)(2,1)S(1)}, u32[]{:S(2)}, u32[]{:S(2)}) collective-permute-start(bf16[64,2048]{1,0:T(8,128)(2,1)S(1)} %get-tuple-element.86), channel_id=1, source_target_pairs={{4,28},{5,29},{6,30},{7,31},{8,16},{9,17},{10,18},{11,19},{20,12},... | collective-permute-start | bytes 786440 | tf_op jit(solution)/shard_map/ppermute | solution.py:62
  97.0 12.5 %collective-permute-start.22 = (bf16[64,2048]{1,0:T(8,128)(2,1)S(1)}, bf16[64,2048]{1,0:T(8,128)(2,1)S(1)}, u32[]{:S(2)}, u32[]{:S(2)}) collective-permute-start(bf16[64,2048]{1,0:T(8,128)(2,1)S(1)} %get-tuple-element.103), channel_id=1, source_target_pairs={{0,16},{1,17},{2,18},{3,19},{4,20},{5,21},{6,22},{7,23},{8,24},{9,... | collective-permute-start | bytes 786440 | tf_op jit(solution)/shard_map/ppermute | solution.py:52
  98.5 4.4 %collective-permute-start.15 = (bf16[320,128]{1,0:T(8,128)(2,1)S(1)}, bf16[320,128]{1,0:T(8,128)(2,1)S(1)}, u32[]{:S(2)}, u32[]{:S(2)}) collective-permute-start(bf16[320,128]{1,0:T(8,128)(2,1)S(1)} %get-tuple-element.90), channel_id=1, source_target_pairs={{0,2},{1,3},{2,0},{3,1},{4,6},{5,7},{6,4},{7,5},{8,10},{9,11},{10,... | collective-permute-start | bytes 245768 | tf_op jit(solution)/shard_map/ppermute | solution.py:52
  99.9 3.0 %collective-permute-start.16 = (bf16[320,128]{1,0:T(8,128)(2,1)S(1)}, bf16[320,128]{1,0:T(8,128)(2,1)S(1)}, u32[]{:S(2)}, u32[]{:S(2)}) collective-permute-start(bf16[320,128]{1,0:T(8,128)(2,1)S(1)} %get-tuple-element.91), channel_id=1, source_target_pairs={{0,1},{1,0},{2,3},{3,2},{4,5},{5,4},{6,7},{7,6},{8,9},{9,8},{10,11... | collective-permute-start | bytes 245768 | tf_op jit(solution)/shard_map/ppermute | solution.py:52
  99.9 3.0 %collective-permute-start.18 = (bf16[320,128]{1,0:T(8,128)(2,1)S(1)}, bf16[320,128]{1,0:T(8,128)(2,1)S(1)}, u32[]{:S(2)}, u32[]{:S(2)}) collective-permute-start(bf16[320,128]{1,0:T(8,128)(2,1)S(1)} %collective-permute-done.17), channel_id=1, source_target_pairs={{0,1},{1,0},{2,3},{3,2},{4,5},{5,4},{6,7},{7,6},{8,9},{9,8},{10,11... | collective-permute-start | bytes 245768 | tf_op jit(solution)/shard_map/ppermute | solution.py:52

commit v12 on v11

--- a/solution.py
+++ b/solution.py
@@ -465,7 +465,7 @@
         for dc in range(2)
     ]
     tables = tables[0::2] + [plan.shift(rows, dc=1) for rows in tables[1::2]]
-    tables, far_pieces[:1] = lax.optimization_barrier((tables, far_pieces[:1]))
+    tables, far_pieces[1:] = lax.optimization_barrier((tables, far_pieces[1:]))
     grad_head, grad_gate = final_work(plan, target, tables)
     grad_proj = layout_work(plan, info, pieces + far_pieces)
     return (

time: 112 us -> 109 us (0.973)
  waiting for transfers between devices: 46.4 us -> 43.1 us
    ppermute x13, waiting for transfers between devices: 21.4 us -> 17.5 us  [shift(): return lax.ppermute(value, AXES, self.pairs(**by))]
  transfers between devices with their start and end apart: 24 -> 24, of which waited for: 10 -> 8; matrix products, arithmetic and copies ran while one was open for 3% -> 3% of each run, Pallas kernels for 25% -> 26%
where the time goes in v12:
time: 109 us; the launch traced here: 108 us
  waiting for transfers between devices  43.1 us (40%)
  Pallas kernels  29.4 us (27%)
  starting transfers between devices  28.4 us (26%)
  local copies, waits for them, and re-layouts  5.15 us (5%)
  other arithmetic  1.36 us (1%)
    ppermute x11, waiting for transfers between devices, along(): return lax.ppermute(value, AXES, out)  25.6 us
    pallas_call x4, Pallas kernels, slot_work(): pl.pallas_call(functools.partial(slot_kernel, plan, index, [where for _,...  21.8 us
    ppermute x11, starting transfers between devices, along(): return lax.ppermute(value, AXES, out)  18 us
    ppermute x13, waiting for transfers between devices, shift(): return lax.ppermute(value, AXES, self.pairs(**by))  17.5 us
    ppermute x13, starting transfers between devices, shift(): return lax.ppermute(value, AXES, self.pairs(**by))  10.4 us
    unnamed x15, local copies, waits for them, and re-layouts  4.01 us
    pallas_call x1, Pallas kernels, target_work(): pl.pallas_call(functools.partial(target_kernel, plan), out_shape=jax.Shap...  2.36 us
  transfers between devices with their start and end apart: 24, of which 8 were waited for; matrix products, arithmetic and copies ran while one was open for 3% of the time, Pallas kernels for 26%

profile of v12, /device:TPU:0, one launch (start us, length us, event | category | flops | bytes accessed | tf_op | source)
XLA Modules:
  0.0 108.3 jit_solution(12149227608575592451)
XLA Ops:
  0.6 0.0 copy-start
  0.7 1.2 %copy-done = bf16[1,128,4096]{2,1,0:T(8,128)(2,1)S(1)} copy-done((bf16[1,128,4096]{2,1,0:T(8,128)(2,1)S(1)}, bf16[1,128,4096]{2,1,0:T(8,128)(2,1)}, u32[]{:S(2)}) %copy-start) | copy-done | bytes 1048600
  1.9 0.8 dynamic-slice_bitcast_fusion.refs_8_
  2.7 3.0 %collective-permute-start = (bf16[128,2048]{1,0:T(8,128)(2,1)}, bf16[128,2048]{1,0:T(8,128)(2,1)}, u32[]{:S(2)}, u32[]{:S(2)}) collective-permute-start(bf16[128,2048]{1,0:T(8,128)(2,1)} %dynamic-slice_bitcast_fusion.refs_8_), channel_id=1, source_target_pairs={{0,4},{1,5},{2,6},{3,7},{4,0},{5,1},{6,2},{7,3},{8,12},{9,13},{10,... | collective-permute-start | bytes 1572872 | tf_op jit(solution)/shard_map/ppermute | solution.py:62
  5.7 1.4 %collective-permute-start.1 = (bf16[128,2048]{1,0:T(8,128)(2,1)}, bf16[128,2048]{1,0:T(8,128)(2,1)}, u32[]{:S(2)}, u32[]{:S(2)}) collective-permute-start(bf16[128,2048]{1,0:T(8,128)(2,1)} %dynamic-slice_bitcast_fusion.refs_8_), channel_id=1, source_target_pairs={{4,8},{5,9},{6,10},{7,11},{8,4},{9,5},{10,6},{11,7},{20,24},{21,25... | collective-permute-start | bytes 1572872 | tf_op jit(solution)/shard_map/ppermute | solution.py:62
  7.3 0.0 copy-start.5
  7.3 0.1 constant_dynamic-slice_fusion
  7.4 0.5 copy-done.5
  7.9 1.0 fusion.1
  9.0 1.5 %collective-permute-start.5 = (bf16[128,3200]{1,0:T(8,128)(2,1)S(1)}, bf16[128,3200]{1,0:T(8,128)(2,1)S(1)}, u32[]{:S(2)}, u32[]{:S(2)}) collective-permute-start(bf16[128,3200]{1,0:T(8,128)(2,1)S(1)} %get-tuple-element.60.refs_0_), channel_id=1, source_target_pairs={{0,2},{1,3},{2,0},{3,1},{4,6},{5,7},{6,4},{7,5},{8,10},{9,11},{10,... | collective-permute-start | bytes 2457608 | tf_op jit(solution)/shard_map/ppermute | solution.py:52
  10.5 1.5 %collective-permute-start.7 = (bf16[128,3200]{1,0:T(8,128)(2,1)}, bf16[128,3200]{1,0:T(8,128)(2,1)S(1)}, u32[]{:S(2)}, u32[]{:S(2)}) collective-permute-start(bf16[128,3200]{1,0:T(8,128)(2,1)} %get-tuple-element.113), channel_id=1, source_target_pairs={{0,16},{1,17},{2,18},{3,19},{4,20},{5,21},{6,22},{7,23},{8,24},{9,... | collective-permute-start | bytes 2457608 | tf_op jit(solution)/shard_map/ppermute | solution.py:52
  12.0 0.5 collective-permute-start.9
  12.5 0.7 copy.10.route_ref
  13.2 0.1 stack.63.info
  13.3 0.0 copy-start.1
  13.3 0.8 copy-done.1
  14.1 2.4 %shard_map.76.target_ref = s32[1024,128]{1,0:T(8,128)S(1)} custom-call(s32[15]{0:T(128)S(1)} %stack.63.info, s32[128,8]{1,0:T(8,128)S(1)} %copy-done.1), custom_call_target="tpu_custom_call" | custom-call | tf_op jit(solution)/shard_map/pallas_call | solution.py:326
  16.5 1.5 %collective-permute-done.refs_8_ = bf16[128,2048]{1,0:T(8,128)(2,1)} collective-permute-done((bf16[128,2048]{1,0:T(8,128)(2,1)}, bf16[128,2048]{1,0:T(8,128)(2,1)}, u32[]{:S(2)}, u32[]{:S(2)}) %collective-permute-start) | collective-permute-done | bytes 524320 | tf_op jit(solution)/shard_map/ppermute | solution.py:62
  18.0 0.0 collective-permute-done.1.refs_8_
  18.0 0.7 collective-permute-start.2
  18.7 1.3 %collective-permute-start.3 = (bf16[128,2048]{1,0:T(8,128)(2,1)}, bf16[128,2048]{1,0:T(8,128)(2,1)S(1)}, u32[]{:S(2)}, u32[]{:S(2)}) collective-permute-start(bf16[128,2048]{1,0:T(8,128)(2,1)} %collective-permute-done.1.refs_8_), channel_id=1, source_target_pairs={{4,0},{5,1},{6,2},{7,3},{8,12},{9,13},{10,14},{11,15},{20,16},{21,... | collective-permute-start | bytes 1572872 | tf_op jit(solution)/shard_map/ppermute | solution.py:62
  20.0 0.0 collective-permute-done.2.refs_8_
  20.0 18.3 %collective-permute-done.3.refs_9_ = bf16[128,2048]{1,0:T(8,128)(2,1)S(1)} collective-permute-done((bf16[128,2048]{1,0:T(8,128)(2,1)}, bf16[128,2048]{1,0:T(8,128)(2,1)S(1)}, u32[]{:S(2)}, u32[]{:S(2)}) %collective-permute-start.3) | collective-permute-done | bytes 524320 | tf_op jit(solution)/shard_map/ppermute | solution.py:62
  38.3 0.5 collective-permute-start.6
  38.8 0.1 collective-permute-start.8
  38.9 8.8 %collective-permute-done.9.refs_6_ = bf16[128,3200]{1,0:T(8,128)(2,1)} collective-permute-done((bf16[128,3200]{1,0:T(8,128)(2,1)}, bf16[128,3200]{1,0:T(8,128)(2,1)}, u32[]{:S(2)}, u32[]{:S(2)}) %collective-permute-start.9) | collective-permute-done | bytes 819232 | tf_op jit(solution)/shard_map/ppermute | solution.py:52
  47.7 0.0 collective-permute-start.10
  47.7 1.3 %collective-permute-start.11 = (bf16[128,2048]{1,0:T(8,128)(2,1)S(1)}, bf16[128,2048]{1,0:T(8,128)(2,1)S(1)}, u32[]{:S(2)}, u32[]{:S(2)}) collective-permute-start(bf16[128,2048]{1,0:T(8,128)(2,1)S(1)} %collective-permute-done.2.refs_8_), channel_id=1, source_target_pairs={{4,0},{5,1},{6,2},{7,3},{8,12},{9,13},{10,14},{11,15},{20,16},{21,... | collective-permute-start | bytes 1572872 | tf_op jit(solution)/shard_map/ppermute | solution.py:62
  49.0 0.0 collective-permute-done.6.refs_3_
  49.0 0.0 collective-permute-done.8.refs_5_
  49.0 1.2 %collective-permute-done.10.refs_7_ = bf16[128,3200]{1,0:T(8,128)(2,1)S(1)} collective-permute-done((bf16[128,3200]{1,0:T(8,128)(2,1)}, bf16[128,3200]{1,0:T(8,128)(2,1)S(1)}, u32[]{:S(2)}, u32[]{:S(2)}) %collective-permute-start.10) | collective-permute-done | bytes 819232 | tf_op jit(solution)/shard_map/ppermute | solution.py:52
  50.3 5.5 %shard_map.77 = (bf16[128,2048]{1,0:T(8,128)(2,1)S(1)}, bf16[8,80,128]{2,1,0:T(8,128)(2,1)S(1)}) custom-call(s32[15]{0:T(128)S(1)} %stack.63.info, bf16[128,3200]{1,0:T(8,128)(2,1)S(1)} %get-tuple-element.60.refs_0_, bf16[128,3200]{1,0:T(8,128)(2,1)S(1)} %collective-permute-done.4.refs_1_, bf16[128,3200]{1,0:T(8,128)(2,1)S(1)} %collective-permute-done.5.refs_2_, ...), custom_call_target="tpu_custom_call" | custom-call | tf_op jit(solution)/shard_map/pallas_call | solution.py:201
  55.8 5.3 %collective-permute-start.12 = (bf16[128,2048]{1,0:T(8,128)(2,1)S(1)}, bf16[128,2048]{1,0:T(8,128)(2,1)S(1)}, u32[]{:S(2)}, u32[]{:S(2)}) collective-permute-start(bf16[128,2048]{1,0:T(8,128)(2,1)S(1)} %get-tuple-element.77), channel_id=1, source_target_pairs={{0,4},{1,5},{2,6},{3,7},{12,8},{13,9},{14,10},{15,11},{16,20},{17,... | collective-permute-start | bytes 1572872 | tf_op jit(solution)/shard_map/ppermute | solution.py:62
  61.1 3.9 %collective-permute-done.11.refs_9_ = bf16[128,2048]{1,0:T(8,128)(2,1)S(1)} collective-permute-done((bf16[128,2048]{1,0:T(8,128)(2,1)S(1)}, bf16[128,2048]{1,0:T(8,128)(2,1)S(1)}, u32[]{:S(2)}, u32[]{:S(2)}) %collective-permute-start.11) | collective-permute-done | bytes 524320 | tf_op jit(solution)/shard_map/ppermute | solution.py:62
  65.0 5.3 %shard_map.78 = (bf16[128,2048]{1,0:T(8,128)(2,1)S(1)}, bf16[8,80,128]{2,1,0:T(8,128)(2,1)S(1)}) custom-call(s32[15]{0:T(128)S(1)} %stack.63.info, bf16[128,3200]{1,0:T(8,128)(2,1)S(1)} %get-tuple-element.60.refs_0_, bf16[128,3200]{1,0:T(8,128)(2,1)S(1)} %collective-permute-done.4.refs_1_, bf16[128,3200]{1,0:T(8,128)(2,1)S(1)} %collective-permute-done.5.refs_2_, ...), custom_call_target="tpu_custom_call" | custom-call | tf_op jit(solution)/shard_map/pallas_call | solution.py:201
  70.3 1.7 %collective-permute-start.14 = (bf16[128,2048]{1,0:T(8,128)(2,1)S(1)}, bf16[128,2048]{1,0:T(8,128)(2,1)S(1)}, u32[]{:S(2)}, u32[]{:S(2)}) collective-permute-start(bf16[128,2048]{1,0:T(8,128)(2,1)S(1)} %get-tuple-element.81.refs_0_), channel_id=1, source_target_pairs={{0,4},{1,5},{2,6},{3,7},{12,8},{13,9},{14,10},{15,11},{16,20},{17,... | collective-permute-start | bytes 1572872 | tf_op jit(solution)/shard_map/ppermute | solution.py:62
  72.0 5.5 %shard_map.79 = (bf16[128,2048]{1,0:T(8,128)(2,1)S(1)}, bf16[8,80,128]{2,1,0:T(8,128)(2,1)S(1)}) custom-call(s32[15]{0:T(128)S(1)} %stack.63.info, bf16[128,3200]{1,0:T(8,128)(2,1)S(1)} %get-tuple-element.60.refs_0_, bf16[128,3200]{1,0:T(8,128)(2,1)S(1)} %collective-permute-done.4.refs_1_, bf16[128,3200]{1,0:T(8,128)(2,1)S(1)} %collective-permute-done.5.refs_2_, ...), custom_call_target="tpu_custom_call" | custom-call | tf_op jit(solution)/shard_map/pallas_call | solution.py:201
  77.5 0.1 collective-permute-start.20
  77.5 0.1 add.84
  77.7 0.7 collective-permute-start.21
  78.4 5.5 %shard_map.80 = (f32[128,2048]{1,0:T(8,128)S(1)}, bf16[1280,128]{1,0:T(8,128)(2,1)S(1)}, bf16[1280,128]{1,0:T(8,128)(2,1)S(1)}) custom-call(s32[15]{0:T(128)S(1)} %stack.63.info, bf16[128,3200]{1,0:T(8,128)(2,1)S(1)} %get-tuple-element.60.refs_0_, bf16[128,3200]{1,0:T(8,128)(2,1)S(1)} %collective-permute-done.4.refs_1_, ...), custom_call_target="tpu_custom_call" | custom-call | tf_op jit(solution)/shard_map/pallas_call | solution.py:201
  83.9 1.5 %collective-permute-start.13 = (bf16[1280,128]{1,0:T(8,128)(2,1)S(1)}, bf16[1280,128]{1,0:T(8,128)(2,1)S(1)}, u32[]{:S(2)}, u32[]{:S(2)}) collective-permute-start(bf16[1280,128]{1,0:T(8,128)(2,1)S(1)} %get-tuple-element.80), channel_id=1, source_target_pairs={{0,16},{1,17},{2,18},{3,19},{4,20},{5,21},{6,22},{7,23},{8,24},{9,... | collective-permute-start | bytes 983048 | tf_op jit(solution)/shard_map/ppermute | solution.py:52
  85.4 0.0 collective-permute-done.14.refs_1_
  85.4 0.7 shard_map.81
  86.1 1.3 %collective-permute-start.19 = (bf16[64,2048]{1,0:T(8,128)(2,1)S(1)}, bf16[64,2048]{1,0:T(8,128)(2,1)S(1)}, u32[]{:S(2)}, u32[]{:S(2)}) collective-permute-start(bf16[64,2048]{1,0:T(8,128)(2,1)S(1)} %get-tuple-element.86), channel_id=1, source_target_pairs={{4,28},{5,29},{6,30},{7,31},{8,16},{9,17},{10,18},{11,19},{20,12},... | collective-permute-start | bytes 786440 | tf_op jit(solution)/shard_map/ppermute | solution.py:62
  87.4 5.9 %collective-permute-done.13.refs_1_ = bf16[1280,128]{1,0:T(8,128)(2,1)S(1)} collective-permute-done((bf16[1280,128]{1,0:T(8,128)(2,1)S(1)}, bf16[1280,128]{1,0:T(8,128)(2,1)S(1)}, u32[]{:S(2)}, u32[]{:S(2)}) %collective-permute-start.13) | collective-permute-done | bytes 327712 | tf_op jit(solution)/shard_map/ppermute | solution.py:52
  93.3 0.1 shard_map.82
  93.4 1.6 %collective-permute-start.17 = (bf16[320,128]{1,0:T(8,128)(2,1)S(1)}, bf16[320,128]{1,0:T(8,128)(2,1)S(1)}, u32[]{:S(2)}, u32[]{:S(2)}) collective-permute-start(bf16[320,128]{1,0:T(8,128)(2,1)S(1)} %get-tuple-element.92), channel_id=1, source_target_pairs={{0,2},{1,3},{2,0},{3,1},{4,6},{5,7},{6,4},{7,5},{8,10},{9,11},{10,... | collective-permute-start | bytes 245768 | tf_op jit(solution)/shard_map/ppermute | solution.py:52
  95.0 1.3 %collective-permute-start.23 = (bf16[64,2048]{1,0:T(8,128)(2,1)S(1)}, bf16[64,2048]{1,0:T(8,128)(2,1)S(1)}, u32[]{:S(2)}, u32[]{:S(2)}) collective-permute-start(bf16[64,2048]{1,0:T(8,128)(2,1)S(1)} %get-tuple-element.85), channel_id=1, source_target_pairs={{4,12},{5,13},{6,14},{7,15},{8,0},{9,1},{10,2},{11,3},{20,28},{21,... | collective-permute-start | bytes 786440 | tf_op jit(solution)/shard_map/ppermute | solution.py:62
  96.2 0.0 collective-permute-done.21.refs_2_
  96.3 0.7 shard_map.84
  97.0 2.2 %collective-permute-start.22 = (bf16[64,2048]{1,0:T(8,128)(2,1)S(1)}, bf16[64,2048]{1,0:T(8,128)(2,1)S(1)}, u32[]{:S(2)}, u32[]{:S(2)}) collective-permute-start(bf16[64,2048]{1,0:T(8,128)(2,1)S(1)} %get-tuple-element.103), channel_id=1, source_target_pairs={{0,16},{1,17},{2,18},{3,19},{4,20},{5,21},{6,22},{7,23},{8,24},{9,... | collective-permute-start | bytes 786440 | tf_op jit(solution)/shard_map/ppermute | solution.py:52
  99.1 0.5 collective-permute-start.15
  99.6 1.9 %collective-permute-done.19.refs_3_ = bf16[64,2048]{1,0:T(8,128)(2,1)S(1)} collective-permute-done((bf16[64,2048]{1,0:T(8,128)(2,1)S(1)}, bf16[64,2048]{1,0:T(8,128)(2,1)S(1)}, u32[]{:S(2)}, u32[]{:S(2)}) %collective-permute-start.19) | collective-permute-done | bytes 262176 | tf_op jit(solution)/shard_map/ppermute | solution.py:62
  101.6 0.0 collective-permute-start.16
  101.6 0.0 collective-permute-done.17
  101.6 0.5 collective-permute-start.18
  102.1 1.5 %collective-permute-done.15.refs_1_ = bf16[320,128]{1,0:T(8,128)(2,1)S(1)} collective-permute-done((bf16[320,128]{1,0:T(8,128)(2,1)S(1)}, bf16[320,128]{1,0:T(8,128)(2,1)S(1)}, u32[]{:S(2)}, u32[]{:S(2)}) %collective-permute-start.15) | collective-permute-done | bytes 81952 | tf_op jit(solution)/shard_map/ppermute | solution.py:52
  103.6 0.0 collective-permute-done.16.refs_2_
  103.6 2.2 %shard_map.83 = (bf16[1024,128]{1,0:T(8,128)(2,1)}, f32[1024,1]{1,0:T(8,128)S(1)}) custom-call(s32[1024,128]{1,0:T(8,128)S(1)} %shard_map.76.target_ref, bf16[320,128]{1,0:T(8,128)(2,1)S(1)} %get-tuple-element.93.refs_0_, bf16[320,128]{1,0:T(8,128)(2,1)S(1)} %collective-permute-done.15.refs_1_, bf16[320,128]{1,0:T(8,128)(2,1)S(1)} %collective-permute-done.16.refs_2_, ...), custom_call_target="tpu_custom_call" | custom-call | flops 1 | bytes 1 | tf_op jit(solution)/shard_map/pallas_call | solution.py:356
  105.7 0.2 convert_reduce_fusion
  105.9 0.1 convert_element_type.15
  106.1 0.7 copy.11
  106.7 1.6 %shard_map.85 = f32[64,4096]{1,0:T(8,128)} custom-call(s32[15]{0:T(128)S(1)} %stack.63.info, f32[64,2048]{1,0:T(8,128)S(1)} %get-tuple-element.102.refs_0_, bf16[64,2048]{1,0:T(8,128)(2,1)S(1)} %collective-permute-done.22.refs_1_, bf16[64,2048]{1,0:T(8,128)(2,1)S(1)} %collective-permute-done.23.refs_2_, bf16[64,2048]{1,0:T(8,128)(2,1)S(1)} %collective-permute-done.19.refs_3_), custom_call_target="tpu_custom_call" | custom-call | tf_op jit(solution)/shard_map/pallas_call | solution.py:256
  (18 shorter events, 0.1 us)
Async XLA Ops:
  0.6 1.2 %copy-start = (bf16[1,128,4096]{2,1,0:T(8,128)(2,1)S(1)}, bf16[1,128,4096]{2,1,0:T(8,128)(2,1)}, u32[]{:S(2)}) copy-start(bf16[1,128,4096]{2,1,0:T(8,128)(2,1)} %param.9) | copy-start | bytes 3145732
  0.6 6.5 %copy-start.3 = (bf16[128,8,128]{2,1,0:T(8,128)(2,1)S(1)}, bf16[128,8,128]{2,1,0:T(8,128)(2,1)}, u32[]{:S(2)}) copy-start(bf16[128,8,128]{2,1,0:T(8,128)(2,1)} %param.5) | copy-start | bytes 786436
  0.7 6.6 %copy-start.4 = (s32[128,8]{0,1:T(8,128)S(1)}, s32[128,8]{0,1:T(8,128)}, u32[]{:S(2)}) copy-start(s32[128,8]{0,1:T(8,128)} %param.8) | copy-start | bytes 12292
  0.7 6.6 %copy-start.2 = (bf16[128,4096]{1,0:T(8,128)(2,1)S(1)}, bf16[128,4096]{1,0:T(8,128)(2,1)}, u32[]{:S(2)}) copy-start(bf16[128,4096]{1,0:T(8,128)(2,1)} %param.6) | copy-start | bytes 3145732
  2.7 15.3 %collective-permute-start = (bf16[128,2048]{1,0:T(8,128)(2,1)}, bf16[128,2048]{1,0:T(8,128)(2,1)}, u32[]{:S(2)}, u32[]{:S(2)}) collective-permute-start(bf16[128,2048]{1,0:T(8,128)(2,1)} %dynamic-slice_bitcast_fusion.refs_8_), channel_id=1, source_target_pairs={{0,4},{1,5},{2,6},{3,7},{4,0},{5,1},{6,2},{7,3},{8,12},{9,13},{10,... | collective-permute-start | bytes 1572872 | tf_op jit(solution)/shard_map/ppermute | solution.py:62
  5.7 12.2 %collective-permute-start.1 = (bf16[128,2048]{1,0:T(8,128)(2,1)}, bf16[128,2048]{1,0:T(8,128)(2,1)}, u32[]{:S(2)}, u32[]{:S(2)}) collective-permute-start(bf16[128,2048]{1,0:T(8,128)(2,1)} %dynamic-slice_bitcast_fusion.refs_8_), channel_id=1, source_target_pairs={{4,8},{5,9},{6,10},{7,11},{8,4},{9,5},{10,6},{11,7},{20,24},{21,25... | collective-permute-start | bytes 1572872 | tf_op jit(solution)/shard_map/ppermute | solution.py:62
  7.3 0.7 copy-start.5
  9.0 29.3 %collective-permute-start.5 = (bf16[128,3200]{1,0:T(8,128)(2,1)S(1)}, bf16[128,3200]{1,0:T(8,128)(2,1)S(1)}, u32[]{:S(2)}, u32[]{:S(2)}) collective-permute-start(bf16[128,3200]{1,0:T(8,128)(2,1)S(1)} %get-tuple-element.60.refs_0_), channel_id=1, source_target_pairs={{0,2},{1,3},{2,0},{3,1},{4,6},{5,7},{6,4},{7,5},{8,10},{9,11},{10,... | collective-permute-start | bytes 2457608 | tf_op jit(solution)/shard_map/ppermute | solution.py:52
  10.5 28.3 %collective-permute-start.7 = (bf16[128,3200]{1,0:T(8,128)(2,1)}, bf16[128,3200]{1,0:T(8,128)(2,1)S(1)}, u32[]{:S(2)}, u32[]{:S(2)}) collective-permute-start(bf16[128,3200]{1,0:T(8,128)(2,1)} %get-tuple-element.113), channel_id=1, source_target_pairs={{0,16},{1,17},{2,18},{3,19},{4,20},{5,21},{6,22},{7,23},{8,24},{9,... | collective-permute-start | bytes 2457608 | tf_op jit(solution)/shard_map/ppermute | solution.py:52
  12.0 35.7 %collective-permute-start.9 = (bf16[128,3200]{1,0:T(8,128)(2,1)}, bf16[128,3200]{1,0:T(8,128)(2,1)}, u32[]{:S(2)}, u32[]{:S(2)}) collective-permute-start(bf16[128,3200]{1,0:T(8,128)(2,1)} %get-tuple-element.113), channel_id=1, source_target_pairs={{0,18},{1,19},{2,16},{3,17},{4,22},{5,23},{6,20},{7,21},{8,26},{9,... | collective-permute-start | bytes 2457608 | tf_op jit(solution)/shard_map/ppermute | solution.py:52
  13.3 0.8 copy-start.1
  18.0 2.0 %collective-permute-start.2 = (bf16[128,2048]{1,0:T(8,128)(2,1)}, bf16[128,2048]{1,0:T(8,128)(2,1)S(1)}, u32[]{:S(2)}, u32[]{:S(2)}) collective-permute-start(bf16[128,2048]{1,0:T(8,128)(2,1)} %collective-permute-done.refs_8_), channel_id=1, source_target_pairs={{4,8},{5,9},{6,10},{7,11},{8,4},{9,5},{10,6},{11,7},{20,24},{21,25... | collective-permute-start | bytes 1572872 | tf_op jit(solution)/shard_map/ppermute | solution.py:62
  18.7 19.6 %collective-permute-start.3 = (bf16[128,2048]{1,0:T(8,128)(2,1)}, bf16[128,2048]{1,0:T(8,128)(2,1)S(1)}, u32[]{:S(2)}, u32[]{:S(2)}) collective-permute-start(bf16[128,2048]{1,0:T(8,128)(2,1)} %collective-permute-done.1.refs_8_), channel_id=1, source_target_pairs={{4,0},{5,1},{6,2},{7,3},{8,12},{9,13},{10,14},{11,15},{20,16},{21,... | collective-permute-start | bytes 1572872 | tf_op jit(solution)/shard_map/ppermute | solution.py:62
  38.3 10.7 %collective-permute-start.4 = (bf16[128,3200]{1,0:T(8,128)(2,1)S(1)}, bf16[128,3200]{1,0:T(8,128)(2,1)S(1)}, u32[]{:S(2)}, u32[]{:S(2)}) collective-permute-start(bf16[128,3200]{1,0:T(8,128)(2,1)S(1)} %get-tuple-element.60.refs_0_), channel_id=1, source_target_pairs={{0,1},{1,0},{2,3},{3,2},{4,5},{5,4},{6,7},{7,6},{8,9},{9,8},{10,11... | collective-permute-start | bytes 2457608 | tf_op jit(solution)/shard_map/ppermute | solution.py:52
  38.3 10.7 %collective-permute-start.6 = (bf16[128,3200]{1,0:T(8,128)(2,1)S(1)}, bf16[128,3200]{1,0:T(8,128)(2,1)S(1)}, u32[]{:S(2)}, u32[]{:S(2)}) collective-permute-start(bf16[128,3200]{1,0:T(8,128)(2,1)S(1)} %collective-permute-done.5.refs_2_), channel_id=1, source_target_pairs={{0,1},{1,0},{2,3},{3,2},{4,5},{5,4},{6,7},{7,6},{8,9},{9,8},{10,11... | collective-permute-start | bytes 2457608 | tf_op jit(solution)/shard_map/ppermute | solution.py:52
  38.8 10.2 %collective-permute-start.8 = (bf16[128,3200]{1,0:T(8,128)(2,1)S(1)}, bf16[128,3200]{1,0:T(8,128)(2,1)S(1)}, u32[]{:S(2)}, u32[]{:S(2)}) collective-permute-start(bf16[128,3200]{1,0:T(8,128)(2,1)S(1)} %collective-permute-done.7.refs_4_), channel_id=1, source_target_pairs={{0,1},{1,0},{2,3},{3,2},{4,5},{5,4},{6,7},{7,6},{8,9},{9,8},{10,11... | collective-permute-start | bytes 2457608 | tf_op jit(solution)/shard_map/ppermute | solution.py:52
  47.7 2.5 %collective-permute-start.10 = (bf16[128,3200]{1,0:T(8,128)(2,1)}, bf16[128,3200]{1,0:T(8,128)(2,1)S(1)}, u32[]{:S(2)}, u32[]{:S(2)}) collective-permute-start(bf16[128,3200]{1,0:T(8,128)(2,1)} %collective-permute-done.9.refs_6_), channel_id=1, source_target_pairs={{0,1},{1,0},{2,3},{3,2},{4,5},{5,4},{6,7},{7,6},{8,9},{9,8},{10,11... | collective-permute-start | bytes 2457608 | tf_op jit(solution)/shard_map/ppermute | solution.py:52
  47.7 17.2 %collective-permute-start.11 = (bf16[128,2048]{1,0:T(8,128)(2,1)S(1)}, bf16[128,2048]{1,0:T(8,128)(2,1)S(1)}, u32[]{:S(2)}, u32[]{:S(2)}) collective-permute-start(bf16[128,2048]{1,0:T(8,128)(2,1)S(1)} %collective-permute-done.2.refs_8_), channel_id=1, source_target_pairs={{4,0},{5,1},{6,2},{7,3},{8,12},{9,13},{10,14},{11,15},{20,16},{21,... | collective-permute-start | bytes 1572872 | tf_op jit(solution)/shard_map/ppermute | solution.py:62
  55.8 21.8 %collective-permute-start.12 = (bf16[128,2048]{1,0:T(8,128)(2,1)S(1)}, bf16[128,2048]{1,0:T(8,128)(2,1)S(1)}, u32[]{:S(2)}, u32[]{:S(2)}) collective-permute-start(bf16[128,2048]{1,0:T(8,128)(2,1)S(1)} %get-tuple-element.77), channel_id=1, source_target_pairs={{0,4},{1,5},{2,6},{3,7},{12,8},{13,9},{14,10},{15,11},{16,20},{17,... | collective-permute-start | bytes 1572872 | tf_op jit(solution)/shard_map/ppermute | solution.py:62
  70.3 15.1 %collective-permute-start.14 = (bf16[128,2048]{1,0:T(8,128)(2,1)S(1)}, bf16[128,2048]{1,0:T(8,128)(2,1)S(1)}, u32[]{:S(2)}, u32[]{:S(2)}) collective-permute-start(bf16[128,2048]{1,0:T(8,128)(2,1)S(1)} %get-tuple-element.81.refs_0_), channel_id=1, source_target_pairs={{0,4},{1,5},{2,6},{3,7},{12,8},{13,9},{14,10},{15,11},{16,20},{17,... | collective-permute-start | bytes 1572872 | tf_op jit(solution)/shard_map/ppermute | solution.py:62
  77.5 18.8 %collective-permute-start.20 = (bf16[128,2048]{1,0:T(8,128)(2,1)S(1)}, bf16[128,2048]{1,0:T(8,128)(2,1)S(1)}, u32[]{:S(2)}, u32[]{:S(2)}) collective-permute-start(bf16[128,2048]{1,0:T(8,128)(2,1)S(1)} %get-tuple-element.101), channel_id=1, source_target_pairs={{0,4},{1,5},{2,6},{3,7},{4,0},{5,1},{6,2},{7,3},{8,12},{9,13},{10,... | collective-permute-start | bytes 1572872 | tf_op jit(solution)/shard_map/ppermute | solution.py:62
  77.7 18.6 %collective-permute-start.21 = (bf16[128,2048]{1,0:T(8,128)(2,1)S(1)}, bf16[128,2048]{1,0:T(8,128)(2,1)S(1)}, u32[]{:S(2)}, u32[]{:S(2)}) collective-permute-start(bf16[128,2048]{1,0:T(8,128)(2,1)S(1)} %add.84), channel_id=1, source_target_pairs={{4,8},{5,9},{6,10},{7,11},{8,4},{9,5},{10,6},{11,7},{20,24},{21,25... | collective-permute-start | bytes 1572872 | tf_op jit(solution)/shard_map/ppermute | solution.py:62
  83.9 9.4 %collective-permute-start.13 = (bf16[1280,128]{1,0:T(8,128)(2,1)S(1)}, bf16[1280,128]{1,0:T(8,128)(2,1)S(1)}, u32[]{:S(2)}, u32[]{:S(2)}) collective-permute-start(bf16[1280,128]{1,0:T(8,128)(2,1)S(1)} %get-tuple-element.80), channel_id=1, source_target_pairs={{0,16},{1,17},{2,18},{3,19},{4,20},{5,21},{6,22},{7,23},{8,24},{9,... | collective-permute-start | bytes 983048 | tf_op jit(solution)/shard_map/ppermute | solution.py:52
  86.1 15.5 %collective-permute-start.19 = (bf16[64,2048]{1,0:T(8,128)(2,1)S(1)}, bf16[64,2048]{1,0:T(8,128)(2,1)S(1)}, u32[]{:S(2)}, u32[]{:S(2)}) collective-permute-start(bf16[64,2048]{1,0:T(8,128)(2,1)S(1)} %get-tuple-element.86), channel_id=1, source_target_pairs={{4,28},{5,29},{6,30},{7,31},{8,16},{9,17},{10,18},{11,19},{20,12},... | collective-permute-start | bytes 786440 | tf_op jit(solution)/shard_map/ppermute | solution.py:62
  93.4 8.2 %collective-permute-start.17 = (bf16[320,128]{1,0:T(8,128)(2,1)S(1)}, bf16[320,128]{1,0:T(8,128)(2,1)S(1)}, u32[]{:S(2)}, u32[]{:S(2)}) collective-permute-start(bf16[320,128]{1,0:T(8,128)(2,1)S(1)} %get-tuple-element.92), channel_id=1, source_target_pairs={{0,2},{1,3},{2,0},{3,1},{4,6},{5,7},{6,4},{7,5},{8,10},{9,11},{10,... | collective-permute-start | bytes 245768 | tf_op jit(solution)/shard_map/ppermute | solution.py:52
  95.0 11.8 %collective-permute-start.23 = (bf16[64,2048]{1,0:T(8,128)(2,1)S(1)}, bf16[64,2048]{1,0:T(8,128)(2,1)S(1)}, u32[]{:S(2)}, u32[]{:S(2)}) collective-permute-start(bf16[64,2048]{1,0:T(8,128)(2,1)S(1)} %get-tuple-element.85), channel_id=1, source_target_pairs={{4,12},{5,13},{6,14},{7,15},{8,0},{9,1},{10,2},{11,3},{20,28},{21,... | collective-permute-start | bytes 786440 | tf_op jit(solution)/shard_map/ppermute | solution.py:62
  97.0 9.8 %collective-permute-start.22 = (bf16[64,2048]{1,0:T(8,128)(2,1)S(1)}, bf16[64,2048]{1,0:T(8,128)(2,1)S(1)}, u32[]{:S(2)}, u32[]{:S(2)}) collective-permute-start(bf16[64,2048]{1,0:T(8,128)(2,1)S(1)} %get-tuple-element.103), channel_id=1, source_target_pairs={{0,16},{1,17},{2,18},{3,19},{4,20},{5,21},{6,22},{7,23},{8,24},{9,... | collective-permute-start | bytes 786440 | tf_op jit(solution)/shard_map/ppermute | solution.py:52
  99.1 4.4 %collective-permute-start.15 = (bf16[320,128]{1,0:T(8,128)(2,1)S(1)}, bf16[320,128]{1,0:T(8,128)(2,1)S(1)}, u32[]{:S(2)}, u32[]{:S(2)}) collective-permute-start(bf16[320,128]{1,0:T(8,128)(2,1)S(1)} %get-tuple-element.90), channel_id=1, source_target_pairs={{0,2},{1,3},{2,0},{3,1},{4,6},{5,7},{6,4},{7,5},{8,10},{9,11},{10,... | collective-permute-start | bytes 245768 | tf_op jit(solution)/shard_map/ppermute | solution.py:52
  101.6 2.0 %collective-permute-start.16 = (bf16[320,128]{1,0:T(8,128)(2,1)S(1)}, bf16[320,128]{1,0:T(8,128)(2,1)S(1)}, u32[]{:S(2)}, u32[]{:S(2)}) collective-permute-start(bf16[320,128]{1,0:T(8,128)(2,1)S(1)} %get-tuple-element.91), channel_id=1, source_target_pairs={{0,1},{1,0},{2,3},{3,2},{4,5},{5,4},{6,7},{7,6},{8,9},{9,8},{10,11... | collective-permute-start | bytes 245768 | tf_op jit(solution)/shard_map/ppermute | solution.py:52
  101.6 2.0 %collective-permute-start.18 = (bf16[320,128]{1,0:T(8,128)(2,1)S(1)}, bf16[320,128]{1,0:T(8,128)(2,1)S(1)}, u32[]{:S(2)}, u32[]{:S(2)}) collective-permute-start(bf16[320,128]{1,0:T(8,128)(2,1)S(1)} %collective-permute-done.17), channel_id=1, source_target_pairs={{0,1},{1,0},{2,3},{3,2},{4,5},{5,4},{6,7},{7,6},{8,9},{9,8},{10,11... | collective-permute-start | bytes 245768 | tf_op jit(solution)/shard_map/ppermute | solution.py:52

commit v13 on v12

--- a/solution.py
+++ b/solution.py
@@ -264,9 +264,9 @@
 
 def merge_kernel(plan, *refs):
     parts, outs = refs[: plan.dp], refs[plan.dp :]
-    length = plan.planes * plan.back
-    for j, out in enumerate(outs):
-        at = pl.ds(j * length, length)
+    length = 2 * plan.planes * plan.back
+    for dy, out in enumerate(outs):
+        at = pl.ds(dy * length, length)
         total = parts[0][at, :].astype(jnp.float32)
         for ref in parts[1:]:
             total = total + ref[at, :].astype(jnp.float32)
@@ -275,13 +275,13 @@
 
 def merge_work(plan, parts):
     vmem = pl.BlockSpec(memory_space=pltpu.VMEM)
-    rows = jax.ShapeDtypeStruct((plan.planes * plan.back, LANES), jnp.bfloat16)
+    rows = jax.ShapeDtypeStruct((2 * plan.planes * plan.back, LANES), jnp.bfloat16)
     return pl.pallas_call(
         functools.partial(merge_kernel, plan),
         compiler_params=pltpu.CompilerParams(vmem_limit_bytes=6 * 1024 * 1024),
-        out_shape=(rows,) * GROUP,
+        out_shape=(rows,) * plan.rows,
         in_specs=[vmem] * plan.dp,
-        out_specs=(vmem,) * GROUP,
+        out_specs=(vmem,) * plan.rows,
     )(*parts)
 
 
@@ -333,9 +333,14 @@
 
 
 def final_kernel(plan, target_ref, *refs):
-    head_ref, out_gate_ref = refs[GROUP:]
+    tables, (head_ref, out_gate_ref) = refs[:GROUP], refs[GROUP:]
     length = plan.rows * plan.planes * plan.back
-    table = jnp.concatenate([ref[...] for ref in refs[:GROUP]], axis=0)
+    part = plan.planes * plan.back
+    table = jnp.concatenate(
+        [ref[pl.ds(0, part), :] for ref in tables[: plan.rows]]
+        + [ref[pl.ds(part, part), :] for ref in tables[plan.rows :]],
+        axis=0,
+    )
     block = 256
     for start in range(0, plan.tokens * plan.top, block):
         at = pl.ds(start, block)
@@ -459,12 +464,8 @@
     if plan.planes == 4:
         backs, far_sums = lax.optimization_barrier((backs, far_sums))
     merged = merge_work(plan, backs)
-    tables = [
-        plan.shift(merged[2 * dy + dc], dy=-dy % plan.rows)
-        for dy in range(plan.rows)
-        for dc in range(2)
-    ]
-    tables = tables[0::2] + [plan.shift(rows, dc=1) for rows in tables[1::2]]
+    tables = [plan.shift(rows, dy=-dy % plan.rows) for dy, rows in enumerate(merged)]
+    tables = tables + [plan.shift(rows, dc=1) for rows in tables]
     tables, far_pieces[1:] = lax.optimization_barrier((tables, far_pieces[1:]))
     grad_head, grad_gate = final_work(plan, target, tables)
     grad_proj = layout_work(plan, info, pieces + far_pieces)

time: 109 us -> 114 us (1.046)
  waiting for transfers between devices: 43.1 us -> 50.3 us
  starting transfers between devices: 28.4 us -> 26.8 us
    ppermute x11, waiting for transfers between devices: 25.6 us -> 31.3 us  [along(): return lax.ppermute(value, AXES, out)]
    ppermute x13 -> x12, waiting for transfers between devices: 17.5 us -> 19 us  [shift(): return lax.ppermute(value, AXES, self.pairs(**by))]
    ppermute x13 -> x12, starting transfers between devices: 10.4 us -> 8.85 us  [shift(): return lax.ppermute(value, AXES, self.pairs(**by))]
  transfers between devices with their start and end apart: 24 -> 23, of which waited for: 8 -> 9; matrix products, arithmetic and copies ran while one was open for 3% -> 3% of each run, Pallas kernels for 26% -> 24%
where the time goes in v13:
time: 114 us
  waiting for transfers between devices  50.3 us (44%)
  Pallas kernels  29.4 us (26%)
  starting transfers between devices  26.8 us (24%)
  local copies, waits for them, and re-layouts  5.15 us (5%)
  other arithmetic  1.36 us (1%)
    ppermute x11, waiting for transfers between devices, along(): return lax.ppermute(value, AXES, out)  31.3 us
    pallas_call x4, Pallas kernels, slot_work(): pl.pallas_call(functools.partial(slot_kernel, plan, index, [where for _,...  21.8 us
    ppermute x12, waiting for transfers between devices, shift(): return lax.ppermute(value, AXES, self.pairs(**by))  19 us
    ppermute x11, starting transfers between devices, along(): return lax.ppermute(value, AXES, out)  17.9 us
    ppermute x12, starting transfers between devices, shift(): return lax.ppermute(value, AXES, self.pairs(**by))  8.85 us
    unnamed x15, local copies, waits for them, and re-layouts  4.01 us
    pallas_call x1, Pallas kernels, target_work(): pl.pallas_call(functools.partial(target_kernel, plan), out_shape=jax.Shap...  2.36 us
  transfers between devices with their start and end apart: 23, of which 9 were waited for; matrix products, arithmetic and copies ran while one was open for 3% of the time, Pallas kernels for 24%

profile of v13, /device:TPU:0, one launch (start us, length us, event | category | flops | bytes accessed | tf_op | source)
XLA Modules:
  0.0 113.9 jit_solution(5186060938078659900)
XLA Ops:
  0.6 0.0 copy-start
  0.7 1.2 %copy-done = bf16[1,128,4096]{2,1,0:T(8,128)(2,1)S(1)} copy-done((bf16[1,128,4096]{2,1,0:T(8,128)(2,1)S(1)}, bf16[1,128,4096]{2,1,0:T(8,128)(2,1)}, u32[]{:S(2)}) %copy-start) | copy-done | bytes 1048600
  1.9 0.8 dynamic-slice_bitcast_fusion.refs_8_
  2.7 3.0 %collective-permute-start = (bf16[128,2048]{1,0:T(8,128)(2,1)}, bf16[128,2048]{1,0:T(8,128)(2,1)}, u32[]{:S(2)}, u32[]{:S(2)}) collective-permute-start(bf16[128,2048]{1,0:T(8,128)(2,1)} %dynamic-slice_bitcast_fusion.refs_8_), channel_id=1, source_target_pairs={{0,4},{1,5},{2,6},{3,7},{4,0},{5,1},{6,2},{7,3},{8,12},{9,13},{10,... | collective-permute-start | bytes 1572872 | tf_op jit(solution)/shard_map/ppermute | solution.py:62
  5.7 1.4 %collective-permute-start.1 = (bf16[128,2048]{1,0:T(8,128)(2,1)}, bf16[128,2048]{1,0:T(8,128)(2,1)}, u32[]{:S(2)}, u32[]{:S(2)}) collective-permute-start(bf16[128,2048]{1,0:T(8,128)(2,1)} %dynamic-slice_bitcast_fusion.refs_8_), channel_id=1, source_target_pairs={{4,8},{5,9},{6,10},{7,11},{8,4},{9,5},{10,6},{11,7},{20,24},{21,25... | collective-permute-start | bytes 1572872 | tf_op jit(solution)/shard_map/ppermute | solution.py:62
  7.3 0.0 copy-start.5
  7.3 0.1 constant_dynamic-slice_fusion
  7.4 0.5 copy-done.5
  7.9 1.0 fusion.1
  9.0 1.5 %collective-permute-start.5 = (bf16[128,3200]{1,0:T(8,128)(2,1)S(1)}, bf16[128,3200]{1,0:T(8,128)(2,1)S(1)}, u32[]{:S(2)}, u32[]{:S(2)}) collective-permute-start(bf16[128,3200]{1,0:T(8,128)(2,1)S(1)} %get-tuple-element.58.refs_0_), channel_id=1, source_target_pairs={{0,2},{1,3},{2,0},{3,1},{4,6},{5,7},{6,4},{7,5},{8,10},{9,11},{10,... | collective-permute-start | bytes 2457608 | tf_op jit(solution)/shard_map/ppermute | solution.py:52
  10.5 1.5 %collective-permute-start.7 = (bf16[128,3200]{1,0:T(8,128)(2,1)}, bf16[128,3200]{1,0:T(8,128)(2,1)S(1)}, u32[]{:S(2)}, u32[]{:S(2)}) collective-permute-start(bf16[128,3200]{1,0:T(8,128)(2,1)} %get-tuple-element.109), channel_id=1, source_target_pairs={{0,16},{1,17},{2,18},{3,19},{4,20},{5,21},{6,22},{7,23},{8,24},{9,... | collective-permute-start | bytes 2457608 | tf_op jit(solution)/shard_map/ppermute | solution.py:52
  12.0 0.5 collective-permute-start.9
  12.4 0.7 copy.10.route_ref
  13.2 0.1 stack.63.info
  13.3 0.0 copy-start.1
  13.3 0.8 copy-done.1
  14.1 2.4 %shard_map.76.target_ref = s32[1024,128]{1,0:T(8,128)S(1)} custom-call(s32[15]{0:T(128)S(1)} %stack.63.info, s32[128,8]{1,0:T(8,128)S(1)} %copy-done.1), custom_call_target="tpu_custom_call" | custom-call | tf_op jit(solution)/shard_map/pallas_call | solution.py:326
  16.5 1.5 %collective-permute-done.refs_8_ = bf16[128,2048]{1,0:T(8,128)(2,1)} collective-permute-done((bf16[128,2048]{1,0:T(8,128)(2,1)}, bf16[128,2048]{1,0:T(8,128)(2,1)}, u32[]{:S(2)}, u32[]{:S(2)}) %collective-permute-start) | collective-permute-done | bytes 524320 | tf_op jit(solution)/shard_map/ppermute | solution.py:62
  18.0 0.0 collective-permute-done.1.refs_8_
  18.0 0.7 collective-permute-start.2
  18.6 1.3 %collective-permute-start.3 = (bf16[128,2048]{1,0:T(8,128)(2,1)}, bf16[128,2048]{1,0:T(8,128)(2,1)S(1)}, u32[]{:S(2)}, u32[]{:S(2)}) collective-permute-start(bf16[128,2048]{1,0:T(8,128)(2,1)} %collective-permute-done.1.refs_8_), channel_id=1, source_target_pairs={{4,0},{5,1},{6,2},{7,3},{8,12},{9,13},{10,14},{11,15},{20,16},{21,... | collective-permute-start | bytes 1572872 | tf_op jit(solution)/shard_map/ppermute | solution.py:62
  19.9 0.0 collective-permute-done.2.refs_8_
  20.0 18.3 %collective-permute-done.3.refs_9_ = bf16[128,2048]{1,0:T(8,128)(2,1)S(1)} collective-permute-done((bf16[128,2048]{1,0:T(8,128)(2,1)}, bf16[128,2048]{1,0:T(8,128)(2,1)S(1)}, u32[]{:S(2)}, u32[]{:S(2)}) %collective-permute-start.3) | collective-permute-done | bytes 524320 | tf_op jit(solution)/shard_map/ppermute | solution.py:62
  38.3 0.5 collective-permute-start.6
  38.8 0.1 collective-permute-start.8
  38.9 8.8 %collective-permute-done.9.refs_6_ = bf16[128,3200]{1,0:T(8,128)(2,1)} collective-permute-done((bf16[128,3200]{1,0:T(8,128)(2,1)}, bf16[128,3200]{1,0:T(8,128)(2,1)}, u32[]{:S(2)}, u32[]{:S(2)}) %collective-permute-start.9) | collective-permute-done | bytes 819232 | tf_op jit(solution)/shard_map/ppermute | solution.py:52
  47.7 0.0 collective-permute-start.10
  47.7 1.3 %collective-permute-start.11 = (bf16[128,2048]{1,0:T(8,128)(2,1)S(1)}, bf16[128,2048]{1,0:T(8,128)(2,1)S(1)}, u32[]{:S(2)}, u32[]{:S(2)}) collective-permute-start(bf16[128,2048]{1,0:T(8,128)(2,1)S(1)} %collective-permute-done.2.refs_8_), channel_id=1, source_target_pairs={{4,0},{5,1},{6,2},{7,3},{8,12},{9,13},{10,14},{11,15},{20,16},{21,... | collective-permute-start | bytes 1572872 | tf_op jit(solution)/shard_map/ppermute | solution.py:62
  49.0 0.0 collective-permute-done.6.refs_3_
  49.0 0.0 collective-permute-done.8.refs_5_
  49.0 1.2 %collective-permute-done.10.refs_7_ = bf16[128,3200]{1,0:T(8,128)(2,1)S(1)} collective-permute-done((bf16[128,3200]{1,0:T(8,128)(2,1)}, bf16[128,3200]{1,0:T(8,128)(2,1)S(1)}, u32[]{:S(2)}, u32[]{:S(2)}) %collective-permute-start.10) | collective-permute-done | bytes 819232 | tf_op jit(solution)/shard_map/ppermute | solution.py:52
  50.3 5.5 %shard_map.77 = (bf16[128,2048]{1,0:T(8,128)(2,1)S(1)}, bf16[8,80,128]{2,1,0:T(8,128)(2,1)S(1)}) custom-call(s32[15]{0:T(128)S(1)} %stack.63.info, bf16[128,3200]{1,0:T(8,128)(2,1)S(1)} %get-tuple-element.58.refs_0_, bf16[128,3200]{1,0:T(8,128)(2,1)S(1)} %collective-permute-done.4.refs_1_, bf16[128,3200]{1,0:T(8,128)(2,1)S(1)} %collective-permute-done.5.refs_2_, ...), custom_call_target="tpu_custom_call" | custom-call | tf_op jit(solution)/shard_map/pallas_call | solution.py:201
  55.8 5.3 %collective-permute-start.12 = (bf16[128,2048]{1,0:T(8,128)(2,1)S(1)}, bf16[128,2048]{1,0:T(8,128)(2,1)S(1)}, u32[]{:S(2)}, u32[]{:S(2)}) collective-permute-start(bf16[128,2048]{1,0:T(8,128)(2,1)S(1)} %get-tuple-element.75), channel_id=1, source_target_pairs={{0,4},{1,5},{2,6},{3,7},{12,8},{13,9},{14,10},{15,11},{16,20},{17,... | collective-permute-start | bytes 1572872 | tf_op jit(solution)/shard_map/ppermute | solution.py:62
  61.1 3.9 %collective-permute-done.11.refs_9_ = bf16[128,2048]{1,0:T(8,128)(2,1)S(1)} collective-permute-done((bf16[128,2048]{1,0:T(8,128)(2,1)S(1)}, bf16[128,2048]{1,0:T(8,128)(2,1)S(1)}, u32[]{:S(2)}, u32[]{:S(2)}) %collective-permute-start.11) | collective-permute-done | bytes 524320 | tf_op jit(solution)/shard_map/ppermute | solution.py:62
  64.9 5.3 %shard_map.78 = (bf16[128,2048]{1,0:T(8,128)(2,1)S(1)}, bf16[8,80,128]{2,1,0:T(8,128)(2,1)S(1)}) custom-call(s32[15]{0:T(128)S(1)} %stack.63.info, bf16[128,3200]{1,0:T(8,128)(2,1)S(1)} %get-tuple-element.58.refs_0_, bf16[128,3200]{1,0:T(8,128)(2,1)S(1)} %collective-permute-done.4.refs_1_, bf16[128,3200]{1,0:T(8,128)(2,1)S(1)} %collective-permute-done.5.refs_2_, ...), custom_call_target="tpu_custom_call" | custom-call | tf_op jit(solution)/shard_map/pallas_call | solution.py:201
  70.3 1.7 %collective-permute-start.14 = (bf16[128,2048]{1,0:T(8,128)(2,1)S(1)}, bf16[128,2048]{1,0:T(8,128)(2,1)S(1)}, u32[]{:S(2)}, u32[]{:S(2)}) collective-permute-start(bf16[128,2048]{1,0:T(8,128)(2,1)S(1)} %get-tuple-element.79.refs_0_), channel_id=1, source_target_pairs={{0,4},{1,5},{2,6},{3,7},{12,8},{13,9},{14,10},{15,11},{16,20},{17,... | collective-permute-start | bytes 1572872 | tf_op jit(solution)/shard_map/ppermute | solution.py:62
  72.0 5.5 %shard_map.79 = (bf16[128,2048]{1,0:T(8,128)(2,1)S(1)}, bf16[8,80,128]{2,1,0:T(8,128)(2,1)S(1)}) custom-call(s32[15]{0:T(128)S(1)} %stack.63.info, bf16[128,3200]{1,0:T(8,128)(2,1)S(1)} %get-tuple-element.58.refs_0_, bf16[128,3200]{1,0:T(8,128)(2,1)S(1)} %collective-permute-done.4.refs_1_, bf16[128,3200]{1,0:T(8,128)(2,1)S(1)} %collective-permute-done.5.refs_2_, ...), custom_call_target="tpu_custom_call" | custom-call | tf_op jit(solution)/shard_map/pallas_call | solution.py:201
  77.5 0.0 collective-permute-done.12
  77.5 0.1 add.84
  77.6 5.5 %shard_map.80 = (f32[128,2048]{1,0:T(8,128)S(1)}, bf16[1280,128]{1,0:T(8,128)(2,1)S(1)}, bf16[1280,128]{1,0:T(8,128)(2,1)S(1)}) custom-call(s32[15]{0:T(128)S(1)} %stack.63.info, bf16[128,3200]{1,0:T(8,128)(2,1)S(1)} %get-tuple-element.58.refs_0_, bf16[128,3200]{1,0:T(8,128)(2,1)S(1)} %collective-permute-done.4.refs_1_, ...), custom_call_target="tpu_custom_call" | custom-call | tf_op jit(solution)/shard_map/pallas_call | solution.py:201
  83.1 1.5 %collective-permute-start.13 = (bf16[1280,128]{1,0:T(8,128)(2,1)S(1)}, bf16[1280,128]{1,0:T(8,128)(2,1)S(1)}, u32[]{:S(2)}, u32[]{:S(2)}) collective-permute-start(bf16[1280,128]{1,0:T(8,128)(2,1)S(1)} %get-tuple-element.78), channel_id=1, source_target_pairs={{0,16},{1,17},{2,18},{3,19},{4,20},{5,21},{6,22},{7,23},{8,24},{9,... | collective-permute-start | bytes 983048 | tf_op jit(solution)/shard_map/ppermute | solution.py:52
  84.6 0.0 collective-permute-start.19
  84.6 0.7 collective-permute-start.20
  85.3 0.7 shard_map.81
  86.0 6.5 %collective-permute-done.13.refs_1_ = bf16[1280,128]{1,0:T(8,128)(2,1)S(1)} collective-permute-done((bf16[1280,128]{1,0:T(8,128)(2,1)S(1)}, bf16[1280,128]{1,0:T(8,128)(2,1)S(1)}, u32[]{:S(2)}, u32[]{:S(2)}) %collective-permute-start.13) | collective-permute-done | bytes 327712 | tf_op jit(solution)/shard_map/ppermute | solution.py:52
  92.5 0.1 shard_map.82
  92.6 1.6 %collective-permute-start.15 = (bf16[640,128]{1,0:T(8,128)(2,1)S(1)}, bf16[640,128]{1,0:T(8,128)(2,1)S(1)}, u32[]{:S(2)}, u32[]{:S(2)}) collective-permute-start(bf16[640,128]{1,0:T(8,128)(2,1)S(1)} %get-tuple-element.88), channel_id=1, source_target_pairs={{0,2},{1,3},{2,0},{3,1},{4,6},{5,7},{6,4},{7,5},{8,10},{9,11},{10,... | collective-permute-start | bytes 491528 | tf_op jit(solution)/shard_map/ppermute | solution.py:52
  94.2 1.3 %collective-permute-start.18 = (bf16[64,2048]{1,0:T(8,128)(2,1)S(1)}, bf16[64,2048]{1,0:T(8,128)(2,1)S(1)}, u32[]{:S(2)}, u32[]{:S(2)}) collective-permute-start(bf16[64,2048]{1,0:T(8,128)(2,1)S(1)} %get-tuple-element.84), channel_id=1, source_target_pairs={{4,28},{5,29},{6,30},{7,31},{8,16},{9,17},{10,18},{11,19},{20,12},... | collective-permute-start | bytes 786440 | tf_op jit(solution)/shard_map/ppermute | solution.py:62
  95.5 0.1 collective-permute-start.16
  95.5 2.4 %collective-permute-done.15.refs_1_ = bf16[640,128]{1,0:T(8,128)(2,1)S(1)} collective-permute-done((bf16[640,128]{1,0:T(8,128)(2,1)S(1)}, bf16[640,128]{1,0:T(8,128)(2,1)S(1)}, u32[]{:S(2)}, u32[]{:S(2)}) %collective-permute-start.15) | collective-permute-done | bytes 163872 | tf_op jit(solution)/shard_map/ppermute | solution.py:52
  98.0 0.0 collective-permute-start.17
  98.0 0.0 collective-permute-done.19.refs_1_
  98.0 1.3 %collective-permute-start.22 = (bf16[64,2048]{1,0:T(8,128)(2,1)S(1)}, bf16[64,2048]{1,0:T(8,128)(2,1)S(1)}, u32[]{:S(2)}, u32[]{:S(2)}) collective-permute-start(bf16[64,2048]{1,0:T(8,128)(2,1)S(1)} %get-tuple-element.83), channel_id=1, source_target_pairs={{4,12},{5,13},{6,14},{7,15},{8,0},{9,1},{10,2},{11,3},{20,28},{21,... | collective-permute-start | bytes 786440 | tf_op jit(solution)/shard_map/ppermute | solution.py:62
  99.3 0.0 collective-permute-done.20.refs_2_
  99.3 0.7 shard_map.84
  100.0 1.6 %collective-permute-start.21 = (bf16[64,2048]{1,0:T(8,128)(2,1)S(1)}, bf16[64,2048]{1,0:T(8,128)(2,1)S(1)}, u32[]{:S(2)}, u32[]{:S(2)}) collective-permute-start(bf16[64,2048]{1,0:T(8,128)(2,1)S(1)} %get-tuple-element.99), channel_id=1, source_target_pairs={{0,16},{1,17},{2,18},{3,19},{4,20},{5,21},{6,22},{7,23},{8,24},{9,... | collective-permute-start | bytes 786440 | tf_op jit(solution)/shard_map/ppermute | solution.py:52
  101.6 6.8 %collective-permute-done.18.refs_3_ = bf16[64,2048]{1,0:T(8,128)(2,1)S(1)} collective-permute-done((bf16[64,2048]{1,0:T(8,128)(2,1)S(1)}, bf16[64,2048]{1,0:T(8,128)(2,1)S(1)}, u32[]{:S(2)}, u32[]{:S(2)}) %collective-permute-start.18) | collective-permute-done | bytes 262176 | tf_op jit(solution)/shard_map/ppermute | solution.py:62
  108.3 0.0 collective-permute-done.16.refs_2_
  108.3 2.2 %shard_map.83 = (bf16[1024,128]{1,0:T(8,128)(2,1)}, f32[1024,1]{1,0:T(8,128)S(1)}) custom-call(s32[1024,128]{1,0:T(8,128)S(1)} %shard_map.76.target_ref, bf16[640,128]{1,0:T(8,128)(2,1)S(1)} %get-tuple-element.89.refs_0_, bf16[640,128]{1,0:T(8,128)(2,1)S(1)} %collective-permute-done.15.refs_1_, bf16[640,128]{1,0:T(8,128)(2,1)S(1)} %collective-permute-done.16.refs_2_, ...), custom_call_target="tpu_custom_call" | custom-call | flops 1 | bytes 1 | tf_op jit(solution)/shard_map/pallas_call | solution.py:361
  110.5 0.2 convert_reduce_fusion
  110.7 0.1 convert_element_type.15
  110.8 0.7 copy.11
  111.5 0.8 collective-permute-done.22.refs_2_
  112.3 1.6 %shard_map.85 = f32[64,4096]{1,0:T(8,128)} custom-call(s32[15]{0:T(128)S(1)} %stack.63.info, f32[64,2048]{1,0:T(8,128)S(1)} %get-tuple-element.98.refs_0_, bf16[64,2048]{1,0:T(8,128)(2,1)S(1)} %collective-permute-done.21.refs_1_, bf16[64,2048]{1,0:T(8,128)(2,1)S(1)} %collective-permute-done.22.refs_2_, bf16[64,2048]{1,0:T(8,128)(2,1)S(1)} %collective-permute-done.18.refs_3_), custom_call_target="tpu_custom_call" | custom-call | tf_op jit(solution)/shard_map/pallas_call | solution.py:256
  (16 shorter events, 0.1 us)
Async XLA Ops:
  0.6 1.2 %copy-start = (bf16[1,128,4096]{2,1,0:T(8,128)(2,1)S(1)}, bf16[1,128,4096]{2,1,0:T(8,128)(2,1)}, u32[]{:S(2)}) copy-start(bf16[1,128,4096]{2,1,0:T(8,128)(2,1)} %param.9) | copy-start | bytes 3145732
  0.6 6.5 %copy-start.3 = (bf16[128,8,128]{2,1,0:T(8,128)(2,1)S(1)}, bf16[128,8,128]{2,1,0:T(8,128)(2,1)}, u32[]{:S(2)}) copy-start(bf16[128,8,128]{2,1,0:T(8,128)(2,1)} %param.5) | copy-start | bytes 786436
  0.7 6.6 %copy-start.4 = (s32[128,8]{0,1:T(8,128)S(1)}, s32[128,8]{0,1:T(8,128)}, u32[]{:S(2)}) copy-start(s32[128,8]{0,1:T(8,128)} %param.8) | copy-start | bytes 12292
  0.7 6.6 %copy-start.2 = (bf16[128,4096]{1,0:T(8,128)(2,1)S(1)}, bf16[128,4096]{1,0:T(8,128)(2,1)}, u32[]{:S(2)}) copy-start(bf16[128,4096]{1,0:T(8,128)(2,1)} %param.6) | copy-start | bytes 3145732
  2.7 15.3 %collective-permute-start = (bf16[128,2048]{1,0:T(8,128)(2,1)}, bf16[128,2048]{1,0:T(8,128)(2,1)}, u32[]{:S(2)}, u32[]{:S(2)}) collective-permute-start(bf16[128,2048]{1,0:T(8,128)(2,1)} %dynamic-slice_bitcast_fusion.refs_8_), channel_id=1, source_target_pairs={{0,4},{1,5},{2,6},{3,7},{4,0},{5,1},{6,2},{7,3},{8,12},{9,13},{10,... | collective-permute-start | bytes 1572872 | tf_op jit(solution)/shard_map/ppermute | solution.py:62
  5.7 12.2 %collective-permute-start.1 = (bf16[128,2048]{1,0:T(8,128)(2,1)}, bf16[128,2048]{1,0:T(8,128)(2,1)}, u32[]{:S(2)}, u32[]{:S(2)}) collective-permute-start(bf16[128,2048]{1,0:T(8,128)(2,1)} %dynamic-slice_bitcast_fusion.refs_8_), channel_id=1, source_target_pairs={{4,8},{5,9},{6,10},{7,11},{8,4},{9,5},{10,6},{11,7},{20,24},{21,25... | collective-permute-start | bytes 1572872 | tf_op jit(solution)/shard_map/ppermute | solution.py:62
  7.3 0.7 copy-start.5
  9.0 29.3 %collective-permute-start.5 = (bf16[128,3200]{1,0:T(8,128)(2,1)S(1)}, bf16[128,3200]{1,0:T(8,128)(2,1)S(1)}, u32[]{:S(2)}, u32[]{:S(2)}) collective-permute-start(bf16[128,3200]{1,0:T(8,128)(2,1)S(1)} %get-tuple-element.58.refs_0_), channel_id=1, source_target_pairs={{0,2},{1,3},{2,0},{3,1},{4,6},{5,7},{6,4},{7,5},{8,10},{9,11},{10,... | collective-permute-start | bytes 2457608 | tf_op jit(solution)/shard_map/ppermute | solution.py:52
  10.5 28.3 %collective-permute-start.7 = (bf16[128,3200]{1,0:T(8,128)(2,1)}, bf16[128,3200]{1,0:T(8,128)(2,1)S(1)}, u32[]{:S(2)}, u32[]{:S(2)}) collective-permute-start(bf16[128,3200]{1,0:T(8,128)(2,1)} %get-tuple-element.109), channel_id=1, source_target_pairs={{0,16},{1,17},{2,18},{3,19},{4,20},{5,21},{6,22},{7,23},{8,24},{9,... | collective-permute-start | bytes 2457608 | tf_op jit(solution)/shard_map/ppermute | solution.py:52
  12.0 35.7 %collective-permute-start.9 = (bf16[128,3200]{1,0:T(8,128)(2,1)}, bf16[128,3200]{1,0:T(8,128)(2,1)}, u32[]{:S(2)}, u32[]{:S(2)}) collective-permute-start(bf16[128,3200]{1,0:T(8,128)(2,1)} %get-tuple-element.109), channel_id=1, source_target_pairs={{0,18},{1,19},{2,16},{3,17},{4,22},{5,23},{6,20},{7,21},{8,26},{9,... | collective-permute-start | bytes 2457608 | tf_op jit(solution)/shard_map/ppermute | solution.py:52
  13.3 0.8 copy-start.1
  18.0 2.0 %collective-permute-start.2 = (bf16[128,2048]{1,0:T(8,128)(2,1)}, bf16[128,2048]{1,0:T(8,128)(2,1)S(1)}, u32[]{:S(2)}, u32[]{:S(2)}) collective-permute-start(bf16[128,2048]{1,0:T(8,128)(2,1)} %collective-permute-done.refs_8_), channel_id=1, source_target_pairs={{4,8},{5,9},{6,10},{7,11},{8,4},{9,5},{10,6},{11,7},{20,24},{21,25... | collective-permute-start | bytes 1572872 | tf_op jit(solution)/shard_map/ppermute | solution.py:62
  18.6 19.6 %collective-permute-start.3 = (bf16[128,2048]{1,0:T(8,128)(2,1)}, bf16[128,2048]{1,0:T(8,128)(2,1)S(1)}, u32[]{:S(2)}, u32[]{:S(2)}) collective-permute-start(bf16[128,2048]{1,0:T(8,128)(2,1)} %collective-permute-done.1.refs_8_), channel_id=1, source_target_pairs={{4,0},{5,1},{6,2},{7,3},{8,12},{9,13},{10,14},{11,15},{20,16},{21,... | collective-permute-start | bytes 1572872 | tf_op jit(solution)/shard_map/ppermute | solution.py:62
  38.3 10.7 %collective-permute-start.4 = (bf16[128,3200]{1,0:T(8,128)(2,1)S(1)}, bf16[128,3200]{1,0:T(8,128)(2,1)S(1)}, u32[]{:S(2)}, u32[]{:S(2)}) collective-permute-start(bf16[128,3200]{1,0:T(8,128)(2,1)S(1)} %get-tuple-element.58.refs_0_), channel_id=1, source_target_pairs={{0,1},{1,0},{2,3},{3,2},{4,5},{5,4},{6,7},{7,6},{8,9},{9,8},{10,11... | collective-permute-start | bytes 2457608 | tf_op jit(solution)/shard_map/ppermute | solution.py:52
  38.3 10.7 %collective-permute-start.6 = (bf16[128,3200]{1,0:T(8,128)(2,1)S(1)}, bf16[128,3200]{1,0:T(8,128)(2,1)S(1)}, u32[]{:S(2)}, u32[]{:S(2)}) collective-permute-start(bf16[128,3200]{1,0:T(8,128)(2,1)S(1)} %collective-permute-done.5.refs_2_), channel_id=1, source_target_pairs={{0,1},{1,0},{2,3},{3,2},{4,5},{5,4},{6,7},{7,6},{8,9},{9,8},{10,11... | collective-permute-start | bytes 2457608 | tf_op jit(solution)/shard_map/ppermute | solution.py:52
  38.8 10.2 %collective-permute-start.8 = (bf16[128,3200]{1,0:T(8,128)(2,1)S(1)}, bf16[128,3200]{1,0:T(8,128)(2,1)S(1)}, u32[]{:S(2)}, u32[]{:S(2)}) collective-permute-start(bf16[128,3200]{1,0:T(8,128)(2,1)S(1)} %collective-permute-done.7.refs_4_), channel_id=1, source_target_pairs={{0,1},{1,0},{2,3},{3,2},{4,5},{5,4},{6,7},{7,6},{8,9},{9,8},{10,11... | collective-permute-start | bytes 2457608 | tf_op jit(solution)/shard_map/ppermute | solution.py:52
  47.7 2.5 %collective-permute-start.10 = (bf16[128,3200]{1,0:T(8,128)(2,1)}, bf16[128,3200]{1,0:T(8,128)(2,1)S(1)}, u32[]{:S(2)}, u32[]{:S(2)}) collective-permute-start(bf16[128,3200]{1,0:T(8,128)(2,1)} %collective-permute-done.9.refs_6_), channel_id=1, source_target_pairs={{0,1},{1,0},{2,3},{3,2},{4,5},{5,4},{6,7},{7,6},{8,9},{9,8},{10,11... | collective-permute-start | bytes 2457608 | tf_op jit(solution)/shard_map/ppermute | solution.py:52
  47.7 17.2 %collective-permute-start.11 = (bf16[128,2048]{1,0:T(8,128)(2,1)S(1)}, bf16[128,2048]{1,0:T(8,128)(2,1)S(1)}, u32[]{:S(2)}, u32[]{:S(2)}) collective-permute-start(bf16[128,2048]{1,0:T(8,128)(2,1)S(1)} %collective-permute-done.2.refs_8_), channel_id=1, source_target_pairs={{4,0},{5,1},{6,2},{7,3},{8,12},{9,13},{10,14},{11,15},{20,16},{21,... | collective-permute-start | bytes 1572872 | tf_op jit(solution)/shard_map/ppermute | solution.py:62
  55.8 21.7 %collective-permute-start.12 = (bf16[128,2048]{1,0:T(8,128)(2,1)S(1)}, bf16[128,2048]{1,0:T(8,128)(2,1)S(1)}, u32[]{:S(2)}, u32[]{:S(2)}) collective-permute-start(bf16[128,2048]{1,0:T(8,128)(2,1)S(1)} %get-tuple-element.75), channel_id=1, source_target_pairs={{0,4},{1,5},{2,6},{3,7},{12,8},{13,9},{14,10},{15,11},{16,20},{17,... | collective-permute-start | bytes 1572872 | tf_op jit(solution)/shard_map/ppermute | solution.py:62
  70.3 15.0 %collective-permute-start.14 = (bf16[128,2048]{1,0:T(8,128)(2,1)S(1)}, bf16[128,2048]{1,0:T(8,128)(2,1)S(1)}, u32[]{:S(2)}, u32[]{:S(2)}) collective-permute-start(bf16[128,2048]{1,0:T(8,128)(2,1)S(1)} %get-tuple-element.79.refs_0_), channel_id=1, source_target_pairs={{0,4},{1,5},{2,6},{3,7},{12,8},{13,9},{14,10},{15,11},{16,20},{17,... | collective-permute-start | bytes 1572872 | tf_op jit(solution)/shard_map/ppermute | solution.py:62
  83.1 9.4 %collective-permute-start.13 = (bf16[1280,128]{1,0:T(8,128)(2,1)S(1)}, bf16[1280,128]{1,0:T(8,128)(2,1)S(1)}, u32[]{:S(2)}, u32[]{:S(2)}) collective-permute-start(bf16[1280,128]{1,0:T(8,128)(2,1)S(1)} %get-tuple-element.78), channel_id=1, source_target_pairs={{0,16},{1,17},{2,18},{3,19},{4,20},{5,21},{6,22},{7,23},{8,24},{9,... | collective-permute-start | bytes 983048 | tf_op jit(solution)/shard_map/ppermute | solution.py:52
  84.6 13.4 %collective-permute-start.19 = (bf16[128,2048]{1,0:T(8,128)(2,1)S(1)}, bf16[128,2048]{1,0:T(8,128)(2,1)S(1)}, u32[]{:S(2)}, u32[]{:S(2)}) collective-permute-start(bf16[128,2048]{1,0:T(8,128)(2,1)S(1)} %get-tuple-element.97), channel_id=1, source_target_pairs={{0,4},{1,5},{2,6},{3,7},{4,0},{5,1},{6,2},{7,3},{8,12},{9,13},{10,... | collective-permute-start | bytes 1572872 | tf_op jit(solution)/shard_map/ppermute | solution.py:62
  84.6 14.6 %collective-permute-start.20 = (bf16[128,2048]{1,0:T(8,128)(2,1)S(1)}, bf16[128,2048]{1,0:T(8,128)(2,1)S(1)}, u32[]{:S(2)}, u32[]{:S(2)}) collective-permute-start(bf16[128,2048]{1,0:T(8,128)(2,1)S(1)} %add.84), channel_id=1, source_target_pairs={{4,8},{5,9},{6,10},{7,11},{8,4},{9,5},{10,6},{11,7},{20,24},{21,25... | collective-permute-start | bytes 1572872 | tf_op jit(solution)/shard_map/ppermute | solution.py:62
  92.6 5.4 %collective-permute-start.15 = (bf16[640,128]{1,0:T(8,128)(2,1)S(1)}, bf16[640,128]{1,0:T(8,128)(2,1)S(1)}, u32[]{:S(2)}, u32[]{:S(2)}) collective-permute-start(bf16[640,128]{1,0:T(8,128)(2,1)S(1)} %get-tuple-element.88), channel_id=1, source_target_pairs={{0,2},{1,3},{2,0},{3,1},{4,6},{5,7},{6,4},{7,5},{8,10},{9,11},{10,... | collective-permute-start | bytes 491528 | tf_op jit(solution)/shard_map/ppermute | solution.py:52
  94.2 14.1 %collective-permute-start.18 = (bf16[64,2048]{1,0:T(8,128)(2,1)S(1)}, bf16[64,2048]{1,0:T(8,128)(2,1)S(1)}, u32[]{:S(2)}, u32[]{:S(2)}) collective-permute-start(bf16[64,2048]{1,0:T(8,128)(2,1)S(1)} %get-tuple-element.84), channel_id=1, source_target_pairs={{4,28},{5,29},{6,30},{7,31},{8,16},{9,17},{10,18},{11,19},{20,12},... | collective-permute-start | bytes 786440 | tf_op jit(solution)/shard_map/ppermute | solution.py:62
  95.5 12.9 %collective-permute-start.16 = (bf16[640,128]{1,0:T(8,128)(2,1)S(1)}, bf16[640,128]{1,0:T(8,128)(2,1)S(1)}, u32[]{:S(2)}, u32[]{:S(2)}) collective-permute-start(bf16[640,128]{1,0:T(8,128)(2,1)S(1)} %get-tuple-element.89.refs_0_), channel_id=1, source_target_pairs={{0,1},{1,0},{2,3},{3,2},{4,5},{5,4},{6,7},{7,6},{8,9},{9,8},{10,11... | collective-permute-start | bytes 491528 | tf_op jit(solution)/shard_map/ppermute | solution.py:52
  98.0 10.4 %collective-permute-start.17 = (bf16[640,128]{1,0:T(8,128)(2,1)S(1)}, bf16[640,128]{1,0:T(8,128)(2,1)S(1)}, u32[]{:S(2)}, u32[]{:S(2)}) collective-permute-start(bf16[640,128]{1,0:T(8,128)(2,1)S(1)} %collective-permute-done.15.refs_1_), channel_id=1, source_target_pairs={{0,1},{1,0},{2,3},{3,2},{4,5},{5,4},{6,7},{7,6},{8,9},{9,8},{10,11... | collective-permute-start | bytes 491528 | tf_op jit(solution)/shard_map/ppermute | solution.py:52
  98.0 14.3 %collective-permute-start.22 = (bf16[64,2048]{1,0:T(8,128)(2,1)S(1)}, bf16[64,2048]{1,0:T(8,128)(2,1)S(1)}, u32[]{:S(2)}, u32[]{:S(2)}) collective-permute-start(bf16[64,2048]{1,0:T(8,128)(2,1)S(1)} %get-tuple-element.83), channel_id=1, source_target_pairs={{4,12},{5,13},{6,14},{7,15},{8,0},{9,1},{10,2},{11,3},{20,28},{21,... | collective-permute-start | bytes 786440 | tf_op jit(solution)/shard_map/ppermute | solution.py:62
  100.0 12.3 %collective-permute-start.21 = (bf16[64,2048]{1,0:T(8,128)(2,1)S(1)}, bf16[64,2048]{1,0:T(8,128)(2,1)S(1)}, u32[]{:S(2)}, u32[]{:S(2)}) collective-permute-start(bf16[64,2048]{1,0:T(8,128)(2,1)S(1)} %get-tuple-element.99), channel_id=1, source_target_pairs={{0,16},{1,17},{2,18},{3,19},{4,20},{5,21},{6,22},{7,23},{8,24},{9,... | collective-permute-start | bytes 786440 | tf_op jit(solution)/shard_map/ppermute | solution.py:52

commit v14 on v12

--- a/solution.py
+++ b/solution.py
@@ -379,7 +379,7 @@
         mates, middle = [(0, 1), (1, 0), (2, 3), (3, 2)], [(1, 2), (2, 1)]
         outward, inward = [(1, 0), (2, 3)], [(0, 1), (3, 2)]
         across = [(1, 3), (2, 0)]
-        plane_of = [jnp.where(z < 2, 2, 1), jnp.where(z < 2, 3, 0), z ^ 1, z]
+        plane_of = [jnp.where(z < 2, 2, 1), z, jnp.where(z < 2, 3, 0), z ^ 1]
         which = jnp.where(inner, 0, 1)
     else:
         steps = [k % plan.planes for k in range(1, plan.planes + 1)]
@@ -423,11 +423,12 @@
     if plan.planes == 4:
         weights = [
             [(near_in, 0), (near_out, 1)],
+            [(own_weights, None)],
             [(far_in, 0), (far_out, 1)],
             [(mate, None)],
-            [(own_weights, None)],
         ]
 
+    own_at = 1 if plan.planes == 4 else plan.planes - 1
     sums, backs, done = [], [], target
     for j in range(plan.planes):
         last = j == plan.planes - 1
@@ -436,7 +437,7 @@
             done = (done, near_sum)
         info, done = lax.optimization_barrier((info, done))
         target = target if j else done
-        kind = jnp.float32 if last else jnp.bfloat16
+        kind = jnp.float32 if j == own_at else jnp.bfloat16
         part, *back = slot_work(plan, j, info, packs, weights[j], kind, backs if last else ())
         sums.append(part)
         backs = back if last else backs + back
@@ -444,15 +445,15 @@
 
     far_pieces = []
     if plan.planes == 4:
-        far_part = plan.along(sums[1], inward)
+        far_part = plan.along(sums[2], inward)
         far_part, done = lax.optimization_barrier((far_part, done))
-        far_sums = sum_work(plan, info, [sums[1], far_part], jnp.bfloat16)
+        far_sums = sum_work(plan, info, [sums[2], far_part], jnp.bfloat16)
         info, far_sums = lax.optimization_barrier((info, far_sums))
         far_pieces = [plan.along(piece, across, dx) for dx, piece in enumerate(far_sums)]
-        received = [plan.along(sums[2], mates), plan.along(near_sum, middle)]
+        received = [plan.along(sums[3], mates), plan.along(near_sum, middle)]
     else:
         received = [plan.shift(sums[j], dz=steps[j]) for j in range(plan.planes - 1)]
-    pieces = sum_work(plan, info, [sums[-1]] + received, jnp.float32)
+    pieces = sum_work(plan, info, [sums[own_at]] + received, jnp.float32)
     pieces = [plan.shift(piece, dx=dx) for dx, piece in enumerate(pieces)]
 
     backs = [plan.shift(rows, dx=-dx % plan.dp) for dx, rows in enumerate(backs)]

time: 109 us -> 111 us (1.018)
  starting transfers between devices: 28.4 us -> 30 us
    ppermute x11, waiting for transfers between devices: 25.6 us -> 29.7 us  [along(): return lax.ppermute(value, AXES, out)]
    ppermute x13, waiting for transfers between devices: 17.5 us -> 13.4 us  [shift(): return lax.ppermute(value, AXES, self.pairs(**by))]
    ppermute x11, starting transfers between devices: 18 us -> 19.2 us  [along(): return lax.ppermute(value, AXES, out)]
  transfers between devices with their start and end apart: 24 -> 24, of which waited for: 8 -> 10; matrix products, arithmetic and copies ran while one was open for 3% -> 3% of each run, Pallas kernels for 26% -> 25%
where the time goes in v14:
time: 111 us; the launch traced here: 110 us
  waiting for transfers between devices  43.1 us (39%)
  starting transfers between devices  30 us (27%)
  Pallas kernels  29.6 us (27%)
  local copies, waits for them, and re-layouts  5.15 us (5%)
  other arithmetic  1.36 us (1%)
    ppermute x11, waiting for transfers between devices, along(): return lax.ppermute(value, AXES, out)  29.7 us
    pallas_call x4, Pallas kernels, slot_work(): pl.pallas_call(functools.partial(slot_kernel, plan, index, [where for _,...  22 us
    ppermute x11, starting transfers between devices, along(): return lax.ppermute(value, AXES, out)  19.2 us
    ppermute x13, waiting for transfers between devices, shift(): return lax.ppermute(value, AXES, self.pairs(**by))  13.4 us
    ppermute x13, starting transfers between devices, shift(): return lax.ppermute(value, AXES, self.pairs(**by))  10.8 us
    unnamed x15, local copies, waits for them, and re-layouts  4.01 us
    pallas_call x1, Pallas kernels, target_work(): pl.pallas_call(functools.partial(target_kernel, plan), out_shape=jax.Shap...  2.36 us
  transfers between devices with their start and end apart: 24, of which 10 were waited for; matrix products, arithmetic and copies ran while one was open for 3% of the time, Pallas kernels for 25%

profile of v14, /device:TPU:0, one launch (start us, length us, event | category | flops | bytes accessed | tf_op | source)
XLA Modules:
  0.0 110.1 jit_solution(13716621396003464117)
XLA Ops:
  0.6 0.0 copy-start
  0.7 1.2 %copy-done = bf16[1,128,4096]{2,1,0:T(8,128)(2,1)S(1)} copy-done((bf16[1,128,4096]{2,1,0:T(8,128)(2,1)S(1)}, bf16[1,128,4096]{2,1,0:T(8,128)(2,1)}, u32[]{:S(2)}) %copy-start) | copy-done | bytes 1048600
  1.9 0.8 dynamic-slice_bitcast_fusion.refs_8_
  2.7 3.0 %collective-permute-start = (bf16[128,2048]{1,0:T(8,128)(2,1)}, bf16[128,2048]{1,0:T(8,128)(2,1)}, u32[]{:S(2)}, u32[]{:S(2)}) collective-permute-start(bf16[128,2048]{1,0:T(8,128)(2,1)} %dynamic-slice_bitcast_fusion.refs_8_), channel_id=1, source_target_pairs={{0,4},{1,5},{2,6},{3,7},{4,0},{5,1},{6,2},{7,3},{8,12},{9,13},{10,... | collective-permute-start | bytes 1572872 | tf_op jit(solution)/shard_map/ppermute | solution.py:62
  5.7 1.4 %collective-permute-start.1 = (bf16[128,2048]{1,0:T(8,128)(2,1)}, bf16[128,2048]{1,0:T(8,128)(2,1)}, u32[]{:S(2)}, u32[]{:S(2)}) collective-permute-start(bf16[128,2048]{1,0:T(8,128)(2,1)} %dynamic-slice_bitcast_fusion.refs_8_), channel_id=1, source_target_pairs={{4,8},{5,9},{6,10},{7,11},{8,4},{9,5},{10,6},{11,7},{20,24},{21,25... | collective-permute-start | bytes 1572872 | tf_op jit(solution)/shard_map/ppermute | solution.py:62
  7.3 0.0 copy-start.5
  7.3 0.1 constant_dynamic-slice_fusion
  7.4 0.5 copy-done.5
  7.9 1.0 fusion.1
  9.0 1.5 %collective-permute-start.5 = (bf16[128,3200]{1,0:T(8,128)(2,1)S(1)}, bf16[128,3200]{1,0:T(8,128)(2,1)S(1)}, u32[]{:S(2)}, u32[]{:S(2)}) collective-permute-start(bf16[128,3200]{1,0:T(8,128)(2,1)S(1)} %get-tuple-element.60.refs_0_), channel_id=1, source_target_pairs={{0,2},{1,3},{2,0},{3,1},{4,6},{5,7},{6,4},{7,5},{8,10},{9,11},{10,... | collective-permute-start | bytes 2457608 | tf_op jit(solution)/shard_map/ppermute | solution.py:52
  10.5 1.5 %collective-permute-start.7 = (bf16[128,3200]{1,0:T(8,128)(2,1)}, bf16[128,3200]{1,0:T(8,128)(2,1)S(1)}, u32[]{:S(2)}, u32[]{:S(2)}) collective-permute-start(bf16[128,3200]{1,0:T(8,128)(2,1)} %get-tuple-element.113), channel_id=1, source_target_pairs={{0,16},{1,17},{2,18},{3,19},{4,20},{5,21},{6,22},{7,23},{8,24},{9,... | collective-permute-start | bytes 2457608 | tf_op jit(solution)/shard_map/ppermute | solution.py:52
  12.0 0.5 collective-permute-start.9
  12.5 0.7 copy.10.route_ref
  13.2 0.1 stack.63.info
  13.3 0.0 copy-start.1
  13.3 0.8 copy-done.1
  14.1 2.4 %shard_map.76.target_ref = s32[1024,128]{1,0:T(8,128)S(1)} custom-call(s32[15]{0:T(128)S(1)} %stack.63.info, s32[128,8]{1,0:T(8,128)S(1)} %copy-done.1), custom_call_target="tpu_custom_call" | custom-call | tf_op jit(solution)/shard_map/pallas_call | solution.py:326
  16.5 1.5 %collective-permute-done.refs_8_ = bf16[128,2048]{1,0:T(8,128)(2,1)} collective-permute-done((bf16[128,2048]{1,0:T(8,128)(2,1)}, bf16[128,2048]{1,0:T(8,128)(2,1)}, u32[]{:S(2)}, u32[]{:S(2)}) %collective-permute-start) | collective-permute-done | bytes 524320 | tf_op jit(solution)/shard_map/ppermute | solution.py:62
  18.0 0.0 collective-permute-done.1.refs_8_
  18.0 0.7 collective-permute-start.2
  18.7 1.3 %collective-permute-start.3 = (bf16[128,2048]{1,0:T(8,128)(2,1)}, bf16[128,2048]{1,0:T(8,128)(2,1)S(1)}, u32[]{:S(2)}, u32[]{:S(2)}) collective-permute-start(bf16[128,2048]{1,0:T(8,128)(2,1)} %collective-permute-done.1.refs_8_), channel_id=1, source_target_pairs={{4,0},{5,1},{6,2},{7,3},{8,12},{9,13},{10,14},{11,15},{20,16},{21,... | collective-permute-start | bytes 1572872 | tf_op jit(solution)/shard_map/ppermute | solution.py:62
  20.0 0.0 collective-permute-done.2.refs_8_
  20.0 18.3 %collective-permute-done.3.refs_9_ = bf16[128,2048]{1,0:T(8,128)(2,1)S(1)} collective-permute-done((bf16[128,2048]{1,0:T(8,128)(2,1)}, bf16[128,2048]{1,0:T(8,128)(2,1)S(1)}, u32[]{:S(2)}, u32[]{:S(2)}) %collective-permute-start.3) | collective-permute-done | bytes 524320 | tf_op jit(solution)/shard_map/ppermute | solution.py:62
  38.3 0.0 collective-permute-start.4
  38.3 0.5 collective-permute-start.6
  38.8 0.1 collective-permute-start.8
  38.9 8.8 %collective-permute-done.9.refs_6_ = bf16[128,3200]{1,0:T(8,128)(2,1)} collective-permute-done((bf16[128,3200]{1,0:T(8,128)(2,1)}, bf16[128,3200]{1,0:T(8,128)(2,1)}, u32[]{:S(2)}, u32[]{:S(2)}) %collective-permute-start.9) | collective-permute-done | bytes 819232 | tf_op jit(solution)/shard_map/ppermute | solution.py:52
  47.7 1.3 %collective-permute-start.11 = (bf16[128,2048]{1,0:T(8,128)(2,1)S(1)}, bf16[128,2048]{1,0:T(8,128)(2,1)S(1)}, u32[]{:S(2)}, u32[]{:S(2)}) collective-permute-start(bf16[128,2048]{1,0:T(8,128)(2,1)S(1)} %collective-permute-done.2.refs_8_), channel_id=1, source_target_pairs={{4,0},{5,1},{6,2},{7,3},{8,12},{9,13},{10,14},{11,15},{20,16},{21,... | collective-permute-start | bytes 1572872 | tf_op jit(solution)/shard_map/ppermute | solution.py:62
  49.0 0.0 collective-permute-done.6.refs_3_
  49.0 0.0 collective-permute-done.8.refs_5_
  49.0 1.2 %collective-permute-done.10.refs_7_ = bf16[128,3200]{1,0:T(8,128)(2,1)S(1)} collective-permute-done((bf16[128,3200]{1,0:T(8,128)(2,1)}, bf16[128,3200]{1,0:T(8,128)(2,1)S(1)}, u32[]{:S(2)}, u32[]{:S(2)}) %collective-permute-start.10) | collective-permute-done | bytes 819232 | tf_op jit(solution)/shard_map/ppermute | solution.py:52
  50.3 5.5 %shard_map.77 = (bf16[128,2048]{1,0:T(8,128)(2,1)S(1)}, bf16[8,80,128]{2,1,0:T(8,128)(2,1)S(1)}) custom-call(s32[15]{0:T(128)S(1)} %stack.63.info, bf16[128,3200]{1,0:T(8,128)(2,1)S(1)} %get-tuple-element.60.refs_0_, bf16[128,3200]{1,0:T(8,128)(2,1)S(1)} %collective-permute-done.4.refs_1_, bf16[128,3200]{1,0:T(8,128)(2,1)S(1)} %collective-permute-done.5.refs_2_, ...), custom_call_target="tpu_custom_call" | custom-call | tf_op jit(solution)/shard_map/pallas_call | solution.py:201
  55.8 5.3 %collective-permute-start.12 = (bf16[128,2048]{1,0:T(8,128)(2,1)S(1)}, bf16[128,2048]{1,0:T(8,128)(2,1)S(1)}, u32[]{:S(2)}, u32[]{:S(2)}) collective-permute-start(bf16[128,2048]{1,0:T(8,128)(2,1)S(1)} %get-tuple-element.77), channel_id=1, source_target_pairs={{0,4},{1,5},{2,6},{3,7},{12,8},{13,9},{14,10},{15,11},{16,20},{17,... | collective-permute-start | bytes 1572872 | tf_op jit(solution)/shard_map/ppermute | solution.py:62
  61.1 5.5 %shard_map.78 = (f32[128,2048]{1,0:T(8,128)S(1)}, bf16[8,80,128]{2,1,0:T(8,128)(2,1)S(1)}) custom-call(s32[15]{0:T(128)S(1)} %stack.63.info, bf16[128,3200]{1,0:T(8,128)(2,1)S(1)} %get-tuple-element.60.refs_0_, bf16[128,3200]{1,0:T(8,128)(2,1)S(1)} %collective-permute-done.4.refs_1_, bf16[128,3200]{1,0:T(8,128)(2,1)S(1)} %collective-permute-done.5.refs_2_, ...), custom_call_target="tpu_custom_call" | custom-call | tf_op jit(solution)/shard_map/pallas_call | solution.py:201
  66.6 0.0 collective-permute-done.11.refs_9_
  66.6 5.5 %shard_map.79 = (bf16[128,2048]{1,0:T(8,128)(2,1)S(1)}, bf16[8,80,128]{2,1,0:T(8,128)(2,1)S(1)}) custom-call(s32[15]{0:T(128)S(1)} %stack.63.info, bf16[128,3200]{1,0:T(8,128)(2,1)S(1)} %get-tuple-element.60.refs_0_, bf16[128,3200]{1,0:T(8,128)(2,1)S(1)} %collective-permute-done.4.refs_1_, bf16[128,3200]{1,0:T(8,128)(2,1)S(1)} %collective-permute-done.5.refs_2_, ...), custom_call_target="tpu_custom_call" | custom-call | tf_op jit(solution)/shard_map/pallas_call | solution.py:201
  72.1 1.3 %collective-permute-start.14 = (bf16[128,2048]{1,0:T(8,128)(2,1)S(1)}, bf16[128,2048]{1,0:T(8,128)(2,1)S(1)}, u32[]{:S(2)}, u32[]{:S(2)}) collective-permute-start(bf16[128,2048]{1,0:T(8,128)(2,1)S(1)} %get-tuple-element.81.refs_0_), channel_id=1, source_target_pairs={{0,4},{1,5},{2,6},{3,7},{12,8},{13,9},{14,10},{15,11},{16,20},{17,... | collective-permute-start | bytes 1572872 | tf_op jit(solution)/shard_map/ppermute | solution.py:62
  73.4 0.1 add.84
  73.6 5.5 %shard_map.80 = (bf16[128,2048]{1,0:T(8,128)(2,1)S(1)}, bf16[1280,128]{1,0:T(8,128)(2,1)S(1)}, bf16[1280,128]{1,0:T(8,128)(2,1)S(1)}) custom-call(s32[15]{0:T(128)S(1)} %stack.63.info, bf16[128,3200]{1,0:T(8,128)(2,1)S(1)} %get-tuple-element.60.refs_0_, bf16[128,3200]{1,0:T(8,128)(2,1)S(1)} %collective-permute-done.4.refs_1_, ...), custom_call_target="tpu_custom_call" | custom-call | tf_op jit(solution)/shard_map/pallas_call | solution.py:201
  79.1 1.6 %collective-permute-start.20 = (bf16[128,2048]{1,0:T(8,128)(2,1)S(1)}, bf16[128,2048]{1,0:T(8,128)(2,1)S(1)}, u32[]{:S(2)}, u32[]{:S(2)}) collective-permute-start(bf16[128,2048]{1,0:T(8,128)(2,1)S(1)} %get-tuple-element.101), channel_id=1, source_target_pairs={{0,4},{1,5},{2,6},{3,7},{4,0},{5,1},{6,2},{7,3},{8,12},{9,13},{10,... | collective-permute-start | bytes 1572872 | tf_op jit(solution)/shard_map/ppermute | solution.py:62
  80.7 0.7 collective-permute-start.21
  81.4 1.6 %collective-permute-start.13 = (bf16[1280,128]{1,0:T(8,128)(2,1)S(1)}, bf16[1280,128]{1,0:T(8,128)(2,1)S(1)}, u32[]{:S(2)}, u32[]{:S(2)}) collective-permute-start(bf16[1280,128]{1,0:T(8,128)(2,1)S(1)} %get-tuple-element.80), channel_id=1, source_target_pairs={{0,16},{1,17},{2,18},{3,19},{4,20},{5,21},{6,22},{7,23},{8,24},{9,... | collective-permute-start | bytes 983048 | tf_op jit(solution)/shard_map/ppermute | solution.py:52
  82.9 2.7 %collective-permute-done.14.refs_1_ = bf16[128,2048]{1,0:T(8,128)(2,1)S(1)} collective-permute-done((bf16[128,2048]{1,0:T(8,128)(2,1)S(1)}, bf16[128,2048]{1,0:T(8,128)(2,1)S(1)}, u32[]{:S(2)}, u32[]{:S(2)}) %collective-permute-start.14) | collective-permute-done | bytes 524320 | tf_op jit(solution)/shard_map/ppermute | solution.py:62
  85.7 0.7 shard_map.81
  86.3 1.3 %collective-permute-start.19 = (bf16[64,2048]{1,0:T(8,128)(2,1)S(1)}, bf16[64,2048]{1,0:T(8,128)(2,1)S(1)}, u32[]{:S(2)}, u32[]{:S(2)}) collective-permute-start(bf16[64,2048]{1,0:T(8,128)(2,1)S(1)} %get-tuple-element.86), channel_id=1, source_target_pairs={{4,28},{5,29},{6,30},{7,31},{8,16},{9,17},{10,18},{11,19},{20,12},... | collective-permute-start | bytes 786440 | tf_op jit(solution)/shard_map/ppermute | solution.py:62
  87.6 2.4 %collective-permute-done.13.refs_1_ = bf16[1280,128]{1,0:T(8,128)(2,1)S(1)} collective-permute-done((bf16[1280,128]{1,0:T(8,128)(2,1)S(1)}, bf16[1280,128]{1,0:T(8,128)(2,1)S(1)}, u32[]{:S(2)}, u32[]{:S(2)}) %collective-permute-start.13) | collective-permute-done | bytes 327712 | tf_op jit(solution)/shard_map/ppermute | solution.py:52
  90.1 0.1 shard_map.82
  90.2 1.6 %collective-permute-start.17 = (bf16[320,128]{1,0:T(8,128)(2,1)S(1)}, bf16[320,128]{1,0:T(8,128)(2,1)S(1)}, u32[]{:S(2)}, u32[]{:S(2)}) collective-permute-start(bf16[320,128]{1,0:T(8,128)(2,1)S(1)} %get-tuple-element.92), channel_id=1, source_target_pairs={{0,2},{1,3},{2,0},{3,1},{4,6},{5,7},{6,4},{7,5},{8,10},{9,11},{10,... | collective-permute-start | bytes 245768 | tf_op jit(solution)/shard_map/ppermute | solution.py:52
  91.7 1.3 %collective-permute-start.23 = (bf16[64,2048]{1,0:T(8,128)(2,1)S(1)}, bf16[64,2048]{1,0:T(8,128)(2,1)S(1)}, u32[]{:S(2)}, u32[]{:S(2)}) collective-permute-start(bf16[64,2048]{1,0:T(8,128)(2,1)S(1)} %get-tuple-element.85), channel_id=1, source_target_pairs={{4,12},{5,13},{6,14},{7,15},{8,0},{9,1},{10,2},{11,3},{20,28},{21,... | collective-permute-start | bytes 786440 | tf_op jit(solution)/shard_map/ppermute | solution.py:62
  93.0 3.1 %collective-permute-done.20.refs_1_ = bf16[128,2048]{1,0:T(8,128)(2,1)S(1)} collective-permute-done((bf16[128,2048]{1,0:T(8,128)(2,1)S(1)}, bf16[128,2048]{1,0:T(8,128)(2,1)S(1)}, u32[]{:S(2)}, u32[]{:S(2)}) %collective-permute-start.20) | collective-permute-done | bytes 524320 | tf_op jit(solution)/shard_map/ppermute | solution.py:62
  96.1 0.0 collective-permute-done.21.refs_2_
  96.1 0.7 shard_map.84
  96.8 1.6 %collective-permute-start.22 = (bf16[64,2048]{1,0:T(8,128)(2,1)S(1)}, bf16[64,2048]{1,0:T(8,128)(2,1)S(1)}, u32[]{:S(2)}, u32[]{:S(2)}) collective-permute-start(bf16[64,2048]{1,0:T(8,128)(2,1)S(1)} %get-tuple-element.103), channel_id=1, source_target_pairs={{0,16},{1,17},{2,18},{3,19},{4,20},{5,21},{6,22},{7,23},{8,24},{9,... | collective-permute-start | bytes 786440 | tf_op jit(solution)/shard_map/ppermute | solution.py:52
  98.4 1.5 %collective-permute-start.15 = (bf16[320,128]{1,0:T(8,128)(2,1)S(1)}, bf16[320,128]{1,0:T(8,128)(2,1)S(1)}, u32[]{:S(2)}, u32[]{:S(2)}) collective-permute-start(bf16[320,128]{1,0:T(8,128)(2,1)S(1)} %get-tuple-element.90), channel_id=1, source_target_pairs={{0,2},{1,3},{2,0},{3,1},{4,6},{5,7},{6,4},{7,5},{8,10},{9,11},{10,... | collective-permute-start | bytes 245768 | tf_op jit(solution)/shard_map/ppermute | solution.py:52
  99.9 4.0 %collective-permute-done.19.refs_3_ = bf16[64,2048]{1,0:T(8,128)(2,1)S(1)} collective-permute-done((bf16[64,2048]{1,0:T(8,128)(2,1)S(1)}, bf16[64,2048]{1,0:T(8,128)(2,1)S(1)}, u32[]{:S(2)}, u32[]{:S(2)}) %collective-permute-start.19) | collective-permute-done | bytes 262176 | tf_op jit(solution)/shard_map/ppermute | solution.py:62
  103.9 0.0 collective-permute-done.17
  103.9 0.5 collective-permute-start.18
  104.4 0.8 collective-permute-done.16.refs_2_
  105.2 0.2 collective-permute-done.18.refs_3_
  105.3 2.2 %shard_map.83 = (bf16[1024,128]{1,0:T(8,128)(2,1)}, f32[1024,1]{1,0:T(8,128)S(1)}) custom-call(s32[1024,128]{1,0:T(8,128)S(1)} %shard_map.76.target_ref, bf16[320,128]{1,0:T(8,128)(2,1)S(1)} %get-tuple-element.93.refs_0_, bf16[320,128]{1,0:T(8,128)(2,1)S(1)} %collective-permute-done.15.refs_1_, bf16[320,128]{1,0:T(8,128)(2,1)S(1)} %collective-permute-done.16.refs_2_, ...), custom_call_target="tpu_custom_call" | custom-call | flops 1 | bytes 1 | tf_op jit(solution)/shard_map/pallas_call | solution.py:356
  107.5 0.2 convert_reduce_fusion
  107.7 0.1 convert_element_type.15
  107.8 0.7 copy.11
  108.5 1.6 %shard_map.85 = f32[64,4096]{1,0:T(8,128)} custom-call(s32[15]{0:T(128)S(1)} %stack.63.info, f32[64,2048]{1,0:T(8,128)S(1)} %get-tuple-element.102.refs_0_, bf16[64,2048]{1,0:T(8,128)(2,1)S(1)} %collective-permute-done.22.refs_1_, bf16[64,2048]{1,0:T(8,128)(2,1)S(1)} %collective-permute-done.23.refs_2_, bf16[64,2048]{1,0:T(8,128)(2,1)S(1)} %collective-permute-done.19.refs_3_), custom_call_target="tpu_custom_call" | custom-call | tf_op jit(solution)/shard_map/pallas_call | solution.py:256
  (18 shorter events, 0.1 us)
Async XLA Ops:
  0.6 1.2 %copy-start = (bf16[1,128,4096]{2,1,0:T(8,128)(2,1)S(1)}, bf16[1,128,4096]{2,1,0:T(8,128)(2,1)}, u32[]{:S(2)}) copy-start(bf16[1,128,4096]{2,1,0:T(8,128)(2,1)} %param.9) | copy-start | bytes 3145732
  0.6 6.5 %copy-start.3 = (bf16[128,8,128]{2,1,0:T(8,128)(2,1)S(1)}, bf16[128,8,128]{2,1,0:T(8,128)(2,1)}, u32[]{:S(2)}) copy-start(bf16[128,8,128]{2,1,0:T(8,128)(2,1)} %param.5) | copy-start | bytes 786436
  0.7 6.6 %copy-start.4 = (s32[128,8]{0,1:T(8,128)S(1)}, s32[128,8]{0,1:T(8,128)}, u32[]{:S(2)}) copy-start(s32[128,8]{0,1:T(8,128)} %param.8) | copy-start | bytes 12292
  0.7 6.6 %copy-start.2 = (bf16[128,4096]{1,0:T(8,128)(2,1)S(1)}, bf16[128,4096]{1,0:T(8,128)(2,1)}, u32[]{:S(2)}) copy-start(bf16[128,4096]{1,0:T(8,128)(2,1)} %param.6) | copy-start | bytes 3145732
  2.7 15.3 %collective-permute-start = (bf16[128,2048]{1,0:T(8,128)(2,1)}, bf16[128,2048]{1,0:T(8,128)(2,1)}, u32[]{:S(2)}, u32[]{:S(2)}) collective-permute-start(bf16[128,2048]{1,0:T(8,128)(2,1)} %dynamic-slice_bitcast_fusion.refs_8_), channel_id=1, source_target_pairs={{0,4},{1,5},{2,6},{3,7},{4,0},{5,1},{6,2},{7,3},{8,12},{9,13},{10,... | collective-permute-start | bytes 1572872 | tf_op jit(solution)/shard_map/ppermute | solution.py:62
  5.7 12.2 %collective-permute-start.1 = (bf16[128,2048]{1,0:T(8,128)(2,1)}, bf16[128,2048]{1,0:T(8,128)(2,1)}, u32[]{:S(2)}, u32[]{:S(2)}) collective-permute-start(bf16[128,2048]{1,0:T(8,128)(2,1)} %dynamic-slice_bitcast_fusion.refs_8_), channel_id=1, source_target_pairs={{4,8},{5,9},{6,10},{7,11},{8,4},{9,5},{10,6},{11,7},{20,24},{21,25... | collective-permute-start | bytes 1572872 | tf_op jit(solution)/shard_map/ppermute | solution.py:62
  7.3 0.7 copy-start.5
  9.0 29.3 %collective-permute-start.5 = (bf16[128,3200]{1,0:T(8,128)(2,1)S(1)}, bf16[128,3200]{1,0:T(8,128)(2,1)S(1)}, u32[]{:S(2)}, u32[]{:S(2)}) collective-permute-start(bf16[128,3200]{1,0:T(8,128)(2,1)S(1)} %get-tuple-element.60.refs_0_), channel_id=1, source_target_pairs={{0,2},{1,3},{2,0},{3,1},{4,6},{5,7},{6,4},{7,5},{8,10},{9,11},{10,... | collective-permute-start | bytes 2457608 | tf_op jit(solution)/shard_map/ppermute | solution.py:52
  10.5 28.3 %collective-permute-start.7 = (bf16[128,3200]{1,0:T(8,128)(2,1)}, bf16[128,3200]{1,0:T(8,128)(2,1)S(1)}, u32[]{:S(2)}, u32[]{:S(2)}) collective-permute-start(bf16[128,3200]{1,0:T(8,128)(2,1)} %get-tuple-element.113), channel_id=1, source_target_pairs={{0,16},{1,17},{2,18},{3,19},{4,20},{5,21},{6,22},{7,23},{8,24},{9,... | collective-permute-start | bytes 2457608 | tf_op jit(solution)/shard_map/ppermute | solution.py:52
  12.0 35.7 %collective-permute-start.9 = (bf16[128,3200]{1,0:T(8,128)(2,1)}, bf16[128,3200]{1,0:T(8,128)(2,1)}, u32[]{:S(2)}, u32[]{:S(2)}) collective-permute-start(bf16[128,3200]{1,0:T(8,128)(2,1)} %get-tuple-element.113), channel_id=1, source_target_pairs={{0,18},{1,19},{2,16},{3,17},{4,22},{5,23},{6,20},{7,21},{8,26},{9,... | collective-permute-start | bytes 2457608 | tf_op jit(solution)/shard_map/ppermute | solution.py:52
  13.3 0.8 copy-start.1
  18.0 2.0 %collective-permute-start.2 = (bf16[128,2048]{1,0:T(8,128)(2,1)}, bf16[128,2048]{1,0:T(8,128)(2,1)S(1)}, u32[]{:S(2)}, u32[]{:S(2)}) collective-permute-start(bf16[128,2048]{1,0:T(8,128)(2,1)} %collective-permute-done.refs_8_), channel_id=1, source_target_pairs={{4,8},{5,9},{6,10},{7,11},{8,4},{9,5},{10,6},{11,7},{20,24},{21,25... | collective-permute-start | bytes 1572872 | tf_op jit(solution)/shard_map/ppermute | solution.py:62
  18.7 19.6 %collective-permute-start.3 = (bf16[128,2048]{1,0:T(8,128)(2,1)}, bf16[128,2048]{1,0:T(8,128)(2,1)S(1)}, u32[]{:S(2)}, u32[]{:S(2)}) collective-permute-start(bf16[128,2048]{1,0:T(8,128)(2,1)} %collective-permute-done.1.refs_8_), channel_id=1, source_target_pairs={{4,0},{5,1},{6,2},{7,3},{8,12},{9,13},{10,14},{11,15},{20,16},{21,... | collective-permute-start | bytes 1572872 | tf_op jit(solution)/shard_map/ppermute | solution.py:62
  38.3 10.7 %collective-permute-start.4 = (bf16[128,3200]{1,0:T(8,128)(2,1)S(1)}, bf16[128,3200]{1,0:T(8,128)(2,1)S(1)}, u32[]{:S(2)}, u32[]{:S(2)}) collective-permute-start(bf16[128,3200]{1,0:T(8,128)(2,1)S(1)} %get-tuple-element.60.refs_0_), channel_id=1, source_target_pairs={{0,1},{1,0},{2,3},{3,2},{4,5},{5,4},{6,7},{7,6},{8,9},{9,8},{10,11... | collective-permute-start | bytes 2457608 | tf_op jit(solution)/shard_map/ppermute | solution.py:52
  38.3 10.7 %collective-permute-start.6 = (bf16[128,3200]{1,0:T(8,128)(2,1)S(1)}, bf16[128,3200]{1,0:T(8,128)(2,1)S(1)}, u32[]{:S(2)}, u32[]{:S(2)}) collective-permute-start(bf16[128,3200]{1,0:T(8,128)(2,1)S(1)} %collective-permute-done.5.refs_2_), channel_id=1, source_target_pairs={{0,1},{1,0},{2,3},{3,2},{4,5},{5,4},{6,7},{7,6},{8,9},{9,8},{10,11... | collective-permute-start | bytes 2457608 | tf_op jit(solution)/shard_map/ppermute | solution.py:52
  38.8 10.2 %collective-permute-start.8 = (bf16[128,3200]{1,0:T(8,128)(2,1)S(1)}, bf16[128,3200]{1,0:T(8,128)(2,1)S(1)}, u32[]{:S(2)}, u32[]{:S(2)}) collective-permute-start(bf16[128,3200]{1,0:T(8,128)(2,1)S(1)} %collective-permute-done.7.refs_4_), channel_id=1, source_target_pairs={{0,1},{1,0},{2,3},{3,2},{4,5},{5,4},{6,7},{7,6},{8,9},{9,8},{10,11... | collective-permute-start | bytes 2457608 | tf_op jit(solution)/shard_map/ppermute | solution.py:52
  47.7 2.5 %collective-permute-start.10 = (bf16[128,3200]{1,0:T(8,128)(2,1)}, bf16[128,3200]{1,0:T(8,128)(2,1)S(1)}, u32[]{:S(2)}, u32[]{:S(2)}) collective-permute-start(bf16[128,3200]{1,0:T(8,128)(2,1)} %collective-permute-done.9.refs_6_), channel_id=1, source_target_pairs={{0,1},{1,0},{2,3},{3,2},{4,5},{5,4},{6,7},{7,6},{8,9},{9,8},{10,11... | collective-permute-start | bytes 2457608 | tf_op jit(solution)/shard_map/ppermute | solution.py:52
  47.7 18.8 %collective-permute-start.11 = (bf16[128,2048]{1,0:T(8,128)(2,1)S(1)}, bf16[128,2048]{1,0:T(8,128)(2,1)S(1)}, u32[]{:S(2)}, u32[]{:S(2)}) collective-permute-start(bf16[128,2048]{1,0:T(8,128)(2,1)S(1)} %collective-permute-done.2.refs_8_), channel_id=1, source_target_pairs={{4,0},{5,1},{6,2},{7,3},{8,12},{9,13},{10,14},{11,15},{20,16},{21,... | collective-permute-start | bytes 1572872 | tf_op jit(solution)/shard_map/ppermute | solution.py:62
  55.8 17.7 %collective-permute-start.12 = (bf16[128,2048]{1,0:T(8,128)(2,1)S(1)}, bf16[128,2048]{1,0:T(8,128)(2,1)S(1)}, u32[]{:S(2)}, u32[]{:S(2)}) collective-permute-start(bf16[128,2048]{1,0:T(8,128)(2,1)S(1)} %get-tuple-element.77), channel_id=1, source_target_pairs={{0,4},{1,5},{2,6},{3,7},{12,8},{13,9},{14,10},{15,11},{16,20},{17,... | collective-permute-start | bytes 1572872 | tf_op jit(solution)/shard_map/ppermute | solution.py:62
  72.1 13.6 %collective-permute-start.14 = (bf16[128,2048]{1,0:T(8,128)(2,1)S(1)}, bf16[128,2048]{1,0:T(8,128)(2,1)S(1)}, u32[]{:S(2)}, u32[]{:S(2)}) collective-permute-start(bf16[128,2048]{1,0:T(8,128)(2,1)S(1)} %get-tuple-element.81.refs_0_), channel_id=1, source_target_pairs={{0,4},{1,5},{2,6},{3,7},{12,8},{13,9},{14,10},{15,11},{16,20},{17,... | collective-permute-start | bytes 1572872 | tf_op jit(solution)/shard_map/ppermute | solution.py:62
  79.1 17.0 %collective-permute-start.20 = (bf16[128,2048]{1,0:T(8,128)(2,1)S(1)}, bf16[128,2048]{1,0:T(8,128)(2,1)S(1)}, u32[]{:S(2)}, u32[]{:S(2)}) collective-permute-start(bf16[128,2048]{1,0:T(8,128)(2,1)S(1)} %get-tuple-element.101), channel_id=1, source_target_pairs={{0,4},{1,5},{2,6},{3,7},{4,0},{5,1},{6,2},{7,3},{8,12},{9,13},{10,... | collective-permute-start | bytes 1572872 | tf_op jit(solution)/shard_map/ppermute | solution.py:62
  80.7 15.4 %collective-permute-start.21 = (bf16[128,2048]{1,0:T(8,128)(2,1)S(1)}, bf16[128,2048]{1,0:T(8,128)(2,1)S(1)}, u32[]{:S(2)}, u32[]{:S(2)}) collective-permute-start(bf16[128,2048]{1,0:T(8,128)(2,1)S(1)} %add.84), channel_id=1, source_target_pairs={{4,8},{5,9},{6,10},{7,11},{8,4},{9,5},{10,6},{11,7},{20,24},{21,25... | collective-permute-start | bytes 1572872 | tf_op jit(solution)/shard_map/ppermute | solution.py:62
  81.4 8.7 %collective-permute-start.13 = (bf16[1280,128]{1,0:T(8,128)(2,1)S(1)}, bf16[1280,128]{1,0:T(8,128)(2,1)S(1)}, u32[]{:S(2)}, u32[]{:S(2)}) collective-permute-start(bf16[1280,128]{1,0:T(8,128)(2,1)S(1)} %get-tuple-element.80), channel_id=1, source_target_pairs={{0,16},{1,17},{2,18},{3,19},{4,20},{5,21},{6,22},{7,23},{8,24},{9,... | collective-permute-start | bytes 983048 | tf_op jit(solution)/shard_map/ppermute | solution.py:52
  86.3 17.6 %collective-permute-start.19 = (bf16[64,2048]{1,0:T(8,128)(2,1)S(1)}, bf16[64,2048]{1,0:T(8,128)(2,1)S(1)}, u32[]{:S(2)}, u32[]{:S(2)}) collective-permute-start(bf16[64,2048]{1,0:T(8,128)(2,1)S(1)} %get-tuple-element.86), channel_id=1, source_target_pairs={{4,28},{5,29},{6,30},{7,31},{8,16},{9,17},{10,18},{11,19},{20,12},... | collective-permute-start | bytes 786440 | tf_op jit(solution)/shard_map/ppermute | solution.py:62
  90.2 13.8 %collective-permute-start.17 = (bf16[320,128]{1,0:T(8,128)(2,1)S(1)}, bf16[320,128]{1,0:T(8,128)(2,1)S(1)}, u32[]{:S(2)}, u32[]{:S(2)}) collective-permute-start(bf16[320,128]{1,0:T(8,128)(2,1)S(1)} %get-tuple-element.92), channel_id=1, source_target_pairs={{0,2},{1,3},{2,0},{3,1},{4,6},{5,7},{6,4},{7,5},{8,10},{9,11},{10,... | collective-permute-start | bytes 245768 | tf_op jit(solution)/shard_map/ppermute | solution.py:52
  91.7 16.8 %collective-permute-start.23 = (bf16[64,2048]{1,0:T(8,128)(2,1)S(1)}, bf16[64,2048]{1,0:T(8,128)(2,1)S(1)}, u32[]{:S(2)}, u32[]{:S(2)}) collective-permute-start(bf16[64,2048]{1,0:T(8,128)(2,1)S(1)} %get-tuple-element.85), channel_id=1, source_target_pairs={{4,12},{5,13},{6,14},{7,15},{8,0},{9,1},{10,2},{11,3},{20,28},{21,... | collective-permute-start | bytes 786440 | tf_op jit(solution)/shard_map/ppermute | solution.py:62
  96.8 11.7 %collective-permute-start.22 = (bf16[64,2048]{1,0:T(8,128)(2,1)S(1)}, bf16[64,2048]{1,0:T(8,128)(2,1)S(1)}, u32[]{:S(2)}, u32[]{:S(2)}) collective-permute-start(bf16[64,2048]{1,0:T(8,128)(2,1)S(1)} %get-tuple-element.103), channel_id=1, source_target_pairs={{0,16},{1,17},{2,18},{3,19},{4,20},{5,21},{6,22},{7,23},{8,24},{9,... | collective-permute-start | bytes 786440 | tf_op jit(solution)/shard_map/ppermute | solution.py:52
  98.4 6.1 %collective-permute-start.15 = (bf16[320,128]{1,0:T(8,128)(2,1)S(1)}, bf16[320,128]{1,0:T(8,128)(2,1)S(1)}, u32[]{:S(2)}, u32[]{:S(2)}) collective-permute-start(bf16[320,128]{1,0:T(8,128)(2,1)S(1)} %get-tuple-element.90), channel_id=1, source_target_pairs={{0,2},{1,3},{2,0},{3,1},{4,6},{5,7},{6,4},{7,5},{8,10},{9,11},{10,... | collective-permute-start | bytes 245768 | tf_op jit(solution)/shard_map/ppermute | solution.py:52
  103.9 1.3 %collective-permute-start.16 = (bf16[320,128]{1,0:T(8,128)(2,1)S(1)}, bf16[320,128]{1,0:T(8,128)(2,1)S(1)}, u32[]{:S(2)}, u32[]{:S(2)}) collective-permute-start(bf16[320,128]{1,0:T(8,128)(2,1)S(1)} %get-tuple-element.91), channel_id=1, source_target_pairs={{0,1},{1,0},{2,3},{3,2},{4,5},{5,4},{6,7},{7,6},{8,9},{9,8},{10,11... | collective-permute-start | bytes 245768 | tf_op jit(solution)/shard_map/ppermute | solution.py:52
  103.9 1.4 %collective-permute-start.18 = (bf16[320,128]{1,0:T(8,128)(2,1)S(1)}, bf16[320,128]{1,0:T(8,128)(2,1)S(1)}, u32[]{:S(2)}, u32[]{:S(2)}) collective-permute-start(bf16[320,128]{1,0:T(8,128)(2,1)S(1)} %collective-permute-done.17), channel_id=1, source_target_pairs={{0,1},{1,0},{2,3},{3,2},{4,5},{5,4},{6,7},{7,6},{8,9},{9,8},{10,11... | collective-permute-start | bytes 245768 | tf_op jit(solution)/shard_map/ppermute | solution.py:52
